TPU v7x, 32 devices: a whole 2x2x4 slice. The times are simulated.
32 devices in a mesh: grp: 2 (over y), orb: 4 (over z), row: 4 (over x, core).
Axes of the slice: x: 2, y: 2, z: 4, core: 2. Of those that a mesh axis runs over, the one named last changes fastest.
Arguments:
- half_tensor: bfloat16 [512, 64, 2048], P(('grp', 'orb'), 'row'), parts along dimension 0, may hold values from -0.75 to 0.75
- batch_owner: int32 [128, 1], P(('grp', 'row')), parts along dimension 0, may hold values from 0 to 3; in each aligned block of 16 rows (0 to 15, 16 to 31, ...) at most 8 rows name the same one
- pair_list: int32 [8, 64], P(('grp', 'orb')), parts along dimension 0, may hold values from 0 to 135, as said below
- live_pairs: int32 [8], P(('grp', 'orb')), parts along dimension 0, may hold values from 32 to 64, as said below
Outputs:
- exchange_blocks: bfloat16 [8, 64, 128, 128], P(('grp', 'orb'), 'row'), parts along dimension 0
There are 2 independent parts, one for each index of `grp`. A program takes and returns all parts, laid end to end along the dimension named above; each array names one. Nothing has to cross between parts.
Inputs may be any that keep to these rules, and one draw needn't show every extreme that they name: `batch_owner`: among the 16 orbitals of one index of row, no batch holds more than 8. `pair_list`: each batch lists 64 distinct pair codes. Only the first live_pairs[b] codes of batch b are used; some batch uses all 64.
All inputs are finite; a program needn't handle non-finite values.
Results may differ from a plain program's by a relative error of at most 0.008.
Values may be sent and summed in bfloat16 or wider, within the bound.
No kernel may reach another device: no remote copies, remote signals or barrier semaphores. Data moves between devices by JAX's collectives and lax.ppermute only.
A program may use at most 64 MiB of HBM per device.

v0:
```python
import math

import jax
import jax.numpy as jnp
from jax import lax
from jax.sharding import PartitionSpec as P

TILE = 128
CAP = 8


def block_pairs(pair_codes, blocks):
    row_grid = lax.broadcasted_iota(jnp.int32, (blocks, blocks), 0)
    col_grid = lax.broadcasted_iota(jnp.int32, (blocks, blocks), 1)
    code_grid = row_grid * blocks - row_grid * (row_grid - 1) // 2 + (col_grid - row_grid)
    upper_part = col_grid >= row_grid
    matches = (code_grid[None, :, :] == pair_codes[:, None, None]) & upper_part[None, :, :]
    first_blocks = jnp.sum(jnp.where(matches, row_grid[None], 0), axis=(1, 2))
    second_blocks = jnp.sum(jnp.where(matches, col_grid[None], 0), axis=(1, 2))
    return (first_blocks, second_blocks)


def slot_sources(owner_local, batches, capacity):
    local_count = owner_local.shape[0]
    batch_ids = lax.broadcasted_iota(jnp.int32, (local_count, batches), 1)
    onehot = (owner_local[:, None] == batch_ids).astype(jnp.int32)
    ranking = jnp.cumsum(onehot, axis=0) - 1
    slot_of = jnp.sum(ranking * onehot, axis=1)
    target = owner_local * capacity + slot_of
    slot_ids = lax.broadcasted_iota(jnp.int32, (local_count, batches * capacity), 1)
    orbital_ids = lax.broadcasted_iota(jnp.int32, (local_count, batches * capacity), 0)
    slot_hits = target[:, None] == slot_ids
    source_row = jnp.sum(jnp.where(slot_hits, orbital_ids, 0), axis=0)
    filled = jnp.any(slot_hits, axis=0)
    return jnp.where(filled, source_row, local_count)


def per_device(half_tensor, batch_owner, pair_list, live_pairs):
    batches = lax.axis_size("orb")
    aux_local, occ_local, domain = half_tensor.shape
    tile_width = TILE
    blocks = domain // tile_width
    sources = slot_sources(batch_owner[:, 0], batches, CAP)
    block_major = half_tensor.reshape(aux_local, occ_local, blocks, tile_width).transpose(
        2, 1, 0, 3
    )
    outgoing = jnp.take(block_major, sources, axis=1, mode="fill", fill_value=0)
    arrived = lax.all_to_all(outgoing, "orb", split_axis=1, concat_axis=2, tiled=True)
    pieces = [arrived.reshape(blocks, -1, tile_width)]
    first_blocks, second_blocks = block_pairs(pair_list[0], blocks)
    live_count = live_pairs[0]
    pair_total = pair_list.shape[1]
    contract = (((0,), (0,)), ((), ()))
    group_size = math.gcd(4, pair_total)
    group_turns = pair_total // group_size

    def one_group(group_index):
        pair_start = 0 + group_index * group_size
        tiles = []
        for offset in range(group_size):
            left_block = first_blocks[pair_start + offset]
            right_block = second_blocks[pair_start + offset]
            stacked_rows = pieces[0]
            left_part = lax.dynamic_index_in_dim(stacked_rows, left_block, 0, keepdims=False)
            right_part = lax.dynamic_index_in_dim(stacked_rows, right_block, 0, keepdims=False)
            tile_one = lax.dot_general(
                left_part, right_part, contract, preferred_element_type=jnp.float32
            )
            tiles.append(tile_one)
        tile_block = jnp.stack(tiles, axis=0)
        keep_mask = pair_start + lax.iota(jnp.int32, group_size) < live_count
        return jnp.where(keep_mask[:, None, None], tile_block, jnp.float32(0.0))

    grouped = lax.map(one_group, jnp.arange(group_turns, dtype=jnp.int32))
    terms = grouped.reshape(pair_total, tile_width, tile_width)
    mine = lax.psum_scatter(terms.astype(jnp.bfloat16), "row", scatter_dimension=0, tiled=True)
    return mine[None]


def solution(mesh):
    return jax.shard_map(
        per_device,
        mesh=mesh,
        in_specs=(
            P(("grp", "orb"), "row", None),
            P(("grp", "row"), None),
            P(("grp", "orb"), None),
            P(("grp", "orb")),
        ),
        out_specs=P(("grp", "orb"), "row", None, None),
        check_vma=False,
    )
```

profile of v0, /device:TPU:0, one launch (start us, length us, event | category | flops | bytes accessed | tf_op | source)
XLA Modules:
  0.0 657.2 jit_solution(14872112349458895811)
XLA Ops:
  9.0 3.6 copy.14
  12.6 4.7 copy.16
  17.3 7.1 %gather_fusion = bf16[32,16,64,128]{3,2,1,0:T(8,128)(2,1)} fusion(bf16[16,16,64,128]{3,2,1,0:T(8,128)(2,1)} %bitcast.112, s32[1024]{0:T(1024)S(1)} %pad_clamp_fusion), kind=kCustom, calls=%fused_computation | custom fusion | bytes 16777344 | tf_op jit(solution)/shard_map/jit(_take)/gather | solution.py:47
  24.4 7.2 %select_bitcast_fusion = bf16[16,32,64,128]{3,2,0,1:T(8,128)(2,1)} fusion(bf16[32,16,64,128]{3,2,1,0:T(8,128)(2,1)} %gather_fusion, pred[32]{0:T(512)(128)(4,1)S(1)} %compare_and_fusion.1), kind=kLoop, calls=%fused_computation.28 | loop fusion | flops 4194304 | bytes 16777248 | tf_op jit(solution)/shard_map/jit(_take)/select_n | solution.py:47
  31.6 6.4 all-to-all-start
  38.3 183.8 %all-to-all-done = bf16[16,32,64,128]{3,2,0,1:T(8,128)(2,1)} async-done(((bf16[16,32,64,128]{3,2,0,1:T(8,128)(2,1)}), bf16[16,32,64,128]{3,2,0,1:T(8,128)(2,1)}, u32[]{:S(2)}, u32[]{:S(2)}) %all-to-all-start) | async-done | bytes 8388640 | tf_op jit(solution)/shard_map/all_to_all | solution.py:48
  222.2 9.6 %copy.12 = bf16[16,8,4,64,128]{4,3,2,1,0:T(8,128)(2,1)} copy(bf16[16,8,4,64,128]{4,3,0,1,2:T(8,128)(2,1)} %bitcast.32) | data formatting | bytes 16777216 | tf_op jit(solution)/shard_map/all_to_all | solution.py:48
  231.8 387.7 %while.12 = (s32[]{:T(128)}, bf16[16,4,128,128]{3,2,1,0:T(8,128)(2,1)}, s32[16]{0:T(128)S(1)}, s32[]{:T(128)}, s32[64]{0:T(128)S(1)}, /*index=5*/bf16[16,2048,12...) while((s32[]{:T(128)}, ...), condition=%wide.region_7.8_spmd, body=%wide.region_6.7_spmd.sunk | while | flops 269025312 | bytes 4588785 | solution.py:74
  242.5 1.5 convolution_bitcast_fusion.10
  266.7 1.5 convolution_bitcast_fusion.10
  301.5 1.5 convolution_bitcast_fusion.8
  315.2 1.5 convolution_bitcast_fusion.10
  339.4 1.5 convolution_bitcast_fusion.10
  363.6 1.5 convolution_bitcast_fusion.10
  374.2 1.5 convolution_bitcast_fusion.8
  382.8 1.5 convolution_bitcast_fusion.11
  387.8 1.5 convolution_bitcast_fusion.10
  412.1 1.5 convolution_bitcast_fusion.10
  436.3 1.5 convolution_bitcast_fusion.10
  441.6 1.5 convolution_bitcast_fusion.9
  460.5 1.5 convolution_bitcast_fusion.10
  557.4 1.5 convolution_bitcast_fusion.10
  616.5 1.5 convolution_bitcast_fusion.8
  619.5 30.9 %reduce-scatter.2.cloned.1.call-done = bf16[16,128,128]{2,1,0:T(8,128)(2,1)} async-done(((bf16[64,128,128]{2,1,0:T(8,128)(2,1)}), bf16[16,128,128]{2,1,0:T(8,128)(2,1)}) %reduce-scatter.2.cloned.1.call-update) | async-done | bytes 524304 | tf_op jit(solution)/shard_map/reduce_scatter | solution.py:76
  (134 shorter events, 121.9 us)
Async XLA Ops:
  31.6 6.6 %copy-start = (s32[1,64]{1,0:T(1,128)S(1)}, s32[1,64]{1,0:T(1,128)}, u32[]{:S(2)}) copy-start(s32[1,64]{1,0:T(1,128)} %param.8) | copy-start | bytes 772
  31.6 190.6 %all-to-all-start = ((bf16[16,32,64,128]{3,2,0,1:T(8,128)(2,1)}), bf16[16,32,64,128]{3,2,0,1:T(8,128)(2,1)}, u32[]{:S(2)}, u32[]{:S(2)}) async-start(bf16[16,32,64,128]{3,2,0,1:T(8,128)(2,1)} %select_bitcast_fusion), calls=%async_computation | async-start | bytes 16777216 | tf_op jit(solution)/shard_map/all_to_all | solution.py:48
  38.0 612.3 %reduce-scatter.2.cloned.1.call-start = ((), (), s32[]{:S(2)}) async-start(), calls=%async_computation.2 | async-start | bytes 2621440 | tf_op jit(solution)/shard_map/reduce_scatter | solution.py:76
Sparse Core Ops, SparseCore 0:
  619.6 30.7 reduce-scatter.1
where the time goes:
time: 663 us; the launch traced here: 657 us
  loops' own time  245 us (37%)
  waiting for transfers between devices  215 us (32%)
  matrix products  98.7 us (15%)
  local copies, waits for them, and re-layouts  46.1 us (7%)
  other arithmetic  32.4 us (5%)
  between operations  13.4 us (2%)
    another operation x1, loops' own time, per_device(): grouped = lax.map(one_group, jnp.arange(group_turns, dtype=jnp.int32))  245 us
    all_to_all x1, waiting for transfers between devices, per_device(): lax.all_to_all(outgoing, 'orb', split_axis=1, concat_axis=2, tiled=True)  184 us
    dot_general x64, matrix products, one_group(): lax.dot_general(left_part, right_part, contract, preferred_element_type=j...  98.7 us
    reduce_scatter x1, waiting for transfers between devices, per_device(): lax.psum_scatter(terms.astype(jnp.bfloat16), 'row', scatter_dimension=0,...  30.9 us
  transfers between devices with their start and end apart: 2, of which 2 were waited for; matrix products, arithmetic and copies ran while one was open for 0% of the time, Pallas kernels for 0%

commit v1 on v0

--- a/solution.py
+++ b/solution.py
@@ -1,12 +1,16 @@
+import functools
 import math
 
 import jax
 import jax.numpy as jnp
 from jax import lax
+from jax.experimental import pallas as pl
+from jax.experimental.pallas import tpu as pltpu
 from jax.sharding import PartitionSpec as P
 
 TILE = 128
 CAP = 8
+GROUP = 256
 
 
 def block_pairs(pair_codes, blocks):
@@ -35,46 +39,199 @@
     return jnp.where(filled, source_row, local_count)
 
 
-def per_device(half_tensor, batch_owner, pair_list, live_pairs):
+def slab_plan(half_tensor, batch_owner, pair_list, live_pairs):
     batches = lax.axis_size("orb")
     aux_local, occ_local, domain = half_tensor.shape
-    tile_width = TILE
-    blocks = domain // tile_width
+    blocks = domain // TILE
     sources = slot_sources(batch_owner[:, 0], batches, CAP)
-    block_major = half_tensor.reshape(aux_local, occ_local, blocks, tile_width).transpose(
-        2, 1, 0, 3
-    )
+    block_major = half_tensor.reshape(aux_local, occ_local, blocks, TILE).transpose(2, 1, 0, 3)
     outgoing = jnp.take(block_major, sources, axis=1, mode="fill", fill_value=0)
     arrived = lax.all_to_all(outgoing, "orb", split_axis=1, concat_axis=2, tiled=True)
-    pieces = [arrived.reshape(blocks, -1, tile_width)]
+    stacked_rows = arrived.reshape(blocks, -1, TILE)
     first_blocks, second_blocks = block_pairs(pair_list[0], blocks)
     live_count = live_pairs[0]
     pair_total = pair_list.shape[1]
     contract = (((0,), (0,)), ((), ()))
     group_size = math.gcd(4, pair_total)
-    group_turns = pair_total // group_size
 
     def one_group(group_index):
-        pair_start = 0 + group_index * group_size
+        pair_start = group_index * group_size
         tiles = []
         for offset in range(group_size):
-            left_block = first_blocks[pair_start + offset]
-            right_block = second_blocks[pair_start + offset]
-            stacked_rows = pieces[0]
-            left_part = lax.dynamic_index_in_dim(stacked_rows, left_block, 0, keepdims=False)
-            right_part = lax.dynamic_index_in_dim(stacked_rows, right_block, 0, keepdims=False)
-            tile_one = lax.dot_general(
-                left_part, right_part, contract, preferred_element_type=jnp.float32
-            )
-            tiles.append(tile_one)
-        tile_block = jnp.stack(tiles, axis=0)
+            left = lax.dynamic_index_in_dim(
+                stacked_rows, first_blocks[pair_start + offset], 0, keepdims=False
+            )
+            right = lax.dynamic_index_in_dim(
+                stacked_rows, second_blocks[pair_start + offset], 0, keepdims=False
+            )
+            tiles.append(
+                lax.dot_general(left, right, contract, preferred_element_type=jnp.float32)
+            )
         keep_mask = pair_start + lax.iota(jnp.int32, group_size) < live_count
-        return jnp.where(keep_mask[:, None, None], tile_block, jnp.float32(0.0))
-
-    grouped = lax.map(one_group, jnp.arange(group_turns, dtype=jnp.int32))
-    terms = grouped.reshape(pair_total, tile_width, tile_width)
+        return jnp.where(keep_mask[:, None, None], jnp.stack(tiles, axis=0), jnp.float32(0.0))
+
+    grouped = lax.map(one_group, jnp.arange(pair_total // group_size, dtype=jnp.int32))
+    terms = grouped.reshape(pair_total, TILE, TILE)
     mine = lax.psum_scatter(terms.astype(jnp.bfloat16), "row", scatter_dimension=0, tiled=True)
     return mine[None]
+
+
+def chunk_kernel(
+    blocks, share, occ_local, place, pairs, own_row, own_col, other_row, other_col,
+    own_rows, other_rows, send_ref, keep_ref, rows_scratch, turned_scratch,
+):
+    step = pl.program_id(0)
+    half_steps = pl.num_programs(0) // 2
+    batch = place[0]
+    kept = GROUP // occ_local * CAP
+
+    def compact(row_ref, col_ref, data_ref):
+        owner_row = row_ref[...]
+        earlier = lax.broadcasted_iota(jnp.int32, (occ_local, GROUP), 0)
+        lane = lax.broadcasted_iota(jnp.int32, (occ_local, GROUP), 1)
+        before = (col_ref[...] == owner_row) & (earlier < lane % occ_local)
+        rank = jnp.sum(before.astype(jnp.int32), axis=0, keepdims=True)
+        lane_row = lax.broadcasted_iota(jnp.int32, (1, GROUP), 1)
+        target = jnp.where(owner_row == batch, lane_row // occ_local * CAP + rank, -1)
+        slot = lax.broadcasted_iota(jnp.int32, (kept, GROUP), 0)
+        pick = (slot == target).astype(jnp.bfloat16)
+        packed = jnp.dot(pick, data_ref[...], preferred_element_type=jnp.float32)
+        packed = packed.astype(jnp.bfloat16)
+        start = pl.multiple_of(step * kept, kept)
+        rows_scratch[pl.ds(start, kept), :] = packed
+        turned_scratch[:, pl.ds(start, kept)] = packed.T
+
+    @pl.when(step < half_steps)
+    def _():
+        compact(own_row, own_col, own_rows)
+
+    @pl.when(step >= half_steps)
+    def _():
+        compact(other_row, other_col, other_rows)
+
+    @pl.when(step == pl.num_programs(0) - 1)
+    def _():
+        def tile(pair):
+            code = pairs[batch, pair]
+            known = jnp.maximum(code, 0)
+            left = pl.multiple_of(known // blocks * TILE, TILE)
+            right = pl.multiple_of(known % blocks * TILE, TILE)
+            product = jnp.dot(
+                turned_scratch[pl.ds(left, TILE), :],
+                rows_scratch[:, pl.ds(right, TILE)],
+                preferred_element_type=jnp.float32,
+            )
+            return jnp.where(code >= 0, product, jnp.float32(0.0))
+
+        width = math.gcd(4, share)
+
+        def several(turn, carry):
+            for offset in range(width):
+                at = turn * width + offset
+                send_ref[at] = tile(place[1] + at).astype(jnp.bfloat16)
+                keep_ref[at] = tile(place[2] + at)
+            return carry
+
+        lax.fori_loop(0, share // width, several, 0)
+
+
+def tile_chunk(place, pairs, owners, own_rows, other_rows, share, occ_local):
+    rows_total, domain = own_rows.shape
+    half_steps = rows_total // GROUP
+    kept = GROUP // occ_local * CAP
+    depth = 2 * half_steps * kept
+    whole = lambda shape: pl.BlockSpec(shape, lambda step, *_: (0,) * len(shape))
+    return pl.pallas_call(
+        functools.partial(chunk_kernel, domain // TILE, share, occ_local),
+        grid_spec=pltpu.PrefetchScalarGridSpec(
+            num_scalar_prefetch=2,
+            grid=(2 * half_steps,),
+            in_specs=[
+                whole((1, GROUP)),
+                whole((occ_local, 1)),
+                whole((1, GROUP)),
+                whole((occ_local, 1)),
+                pl.BlockSpec(
+                    (GROUP, domain), lambda step, *_: (jnp.minimum(step, half_steps - 1), 0)
+                ),
+                pl.BlockSpec(
+                    (GROUP, domain), lambda step, *_: (jnp.maximum(step - half_steps, 0), 0)
+                ),
+            ],
+            out_specs=[whole((share, TILE, TILE)), whole((share, TILE, TILE))],
+            scratch_shapes=[
+                pltpu.VMEM((depth, domain), jnp.bfloat16),
+                pltpu.VMEM((domain, depth), jnp.bfloat16),
+            ],
+        ),
+        out_shape=[
+            jax.ShapeDtypeStruct((share, TILE, TILE), jnp.bfloat16),
+            jax.ShapeDtypeStruct((share, TILE, TILE), jnp.float32),
+        ],
+        compiler_params=pltpu.CompilerParams(vmem_limit_bytes=48 * 1024 * 1024),
+        cost_estimate=pl.CostEstimate(
+            flops=4 * share * TILE * TILE * depth + 2 * depth * GROUP * domain,
+            bytes_accessed=4 * rows_total * domain + 6 * share * TILE * TILE,
+            transcendentals=0,
+        ),
+        name="tile_chunk",
+    )(place, pairs, *owners, own_rows, other_rows)
+
+
+def tile_plan(half_tensor, batch_owner, pair_list, live_pairs):
+    batches = lax.axis_size("orb")
+    rows = lax.axis_size("row")
+    aux_local, occ_local, domain = half_tensor.shape
+    pair_total = pair_list.shape[1]
+    share = pair_total // rows
+    blocks = domain // TILE
+    row_at = lax.axis_index("row")
+    orb_at = lax.axis_index("orb")
+    swap_core = [(i, i ^ 1) for i in range(rows)]
+    swap_x = [(i, i ^ 2) for i in range(rows)]
+
+    own_rows = half_tensor.reshape(aux_local * occ_local, domain)
+    other_rows = lax.ppermute(own_rows, "row", swap_core)
+    other_owner = lax.ppermute(batch_owner, "row", swap_core)
+    first_blocks, second_blocks = block_pairs(pair_list[0], blocks)
+    live = lax.iota(jnp.int32, pair_total) < live_pairs[0]
+    own_pairs = jnp.where(live, first_blocks * blocks + second_blocks, -1)
+    pairs = lax.all_gather(own_pairs, "orb")
+
+    def lanes(owner):
+        return jnp.tile(owner[:, 0], GROUP // occ_local)[None]
+
+    owners = (lanes(batch_owner), batch_owner, lanes(other_owner), other_owner)
+    shifts = sorted(range(1, batches), key=lambda s: -min(s, batches - s)) + [0]
+    total = None
+    for shift in shifts:
+        batch = (orb_at + shift) % batches
+        place = jnp.stack([batch, (row_at ^ 2) * share, row_at * share]).astype(jnp.int32)
+        send, keep = tile_chunk(place, pairs, owners, own_rows, other_rows, share, occ_local)
+        term = keep + lax.ppermute(send, "row", swap_x).astype(jnp.float32)
+        if shift:
+            onward = [(i, (i + shift) % batches) for i in range(batches)]
+            term = lax.ppermute(term.astype(jnp.bfloat16), "orb", onward).astype(jnp.float32)
+        total = term if total is None else total + term
+    return total.astype(jnp.bfloat16)[None]
+
+
+def per_device(half_tensor, batch_owner, pair_list, live_pairs):
+    batches = lax.axis_size("orb")
+    rows = lax.axis_size("row")
+    aux_local, occ_local, domain = half_tensor.shape
+    pair_total = pair_list.shape[1]
+    tile_elements = batches * pair_total * TILE * TILE
+    slab_elements = batches * CAP * aux_local * domain
+    fits = (
+        rows == 4
+        and pair_total % rows == 0
+        and GROUP % occ_local == 0
+        and aux_local * occ_local % GROUP == 0
+        and tile_elements <= slab_elements
+    )
+    plan = tile_plan if fits else slab_plan
+    return plan(half_tensor, batch_owner, pair_list, live_pairs)
 
 
 def solution(mesh):

time: 663 us -> 109 us (0.16)
  the two profiles are of different devices: /device:TPU:0 before, /device:TPU:13 now
where the time goes in v1:
time: 109 us; the launch traced here: 108 us
  waiting for transfers between devices  43.8 us (40%)
  Pallas kernels  42.7 us (39%)
  starting transfers between devices  8.28 us (8%)
  blocking collectives  6.15 us (6%)
  local copies, waits for them, and re-layouts  3.75 us (3%)
  other arithmetic  2.81 us (3%)
    pallas_call x4, Pallas kernels, tile_chunk(): pl.pallas_call(functools.partial(chunk_kernel, domain // TILE, share, occ...  42.7 us
    ppermute x3, waiting for transfers between devices, tile_plan(): lax.ppermute(term.astype(jnp.bfloat16), 'orb', onward).astype(jnp.float32)  39.1 us
    all_gather x1, blocking collectives, tile_plan(): pairs = lax.all_gather(own_pairs, 'orb')  6.15 us
    ppermute x4, waiting for transfers between devices, tile_plan(): term = keep + lax.ppermute(send, 'row', swap_x).astype(jnp.float32)  4.76 us
    ppermute x3, starting transfers between devices, tile_plan(): lax.ppermute(term.astype(jnp.bfloat16), 'orb', onward).astype(jnp.float32)  4.44 us
    ppermute x4, starting transfers between devices, tile_plan(): term = keep + lax.ppermute(send, 'row', swap_x).astype(jnp.float32)  3.17 us
    unnamed x5, local copies, waits for them, and re-layouts  2.92 us
  transfers between devices with their start and end apart: 9, of which 4 were waited for; matrix products, arithmetic and copies ran while one was open for 3% of the time, Pallas kernels for 30%

profile of v1, /device:TPU:13, one launch (start us, length us, event | category | flops | bytes accessed | tf_op | source)
XLA Modules:
  0.0 108.3 jit_solution(17435240754080886691)
XLA Ops:
  0.0 0.7 collective-permute-start.1
  0.7 0.7 copy.23.own_col
  2.2 0.8 select_reduce_fusion.1
  3.0 6.2 %all-gather = s32[4,1,64]{2,1,0:T(1,128)S(1)} all-gather(s32[1,1,64]{2,1,0:T(1,128)S(1)} %fusion.1), channel_id=1, replica_groups=mesh['grp'=2,'orb'=4,'row'=4] {'orb'}, dimensions={0}, use_global_device_ids=true | all-gather | bytes 1280 | tf_op jit(solution)/shard_map/all_gather | solution.py:199
  9.3 0.7 tile.15
  10.3 2.2 %copy-done = bf16[64,16,2048]{2,1,0:T(8,128)(2,1)S(1)} copy-done((bf16[64,16,2048]{2,1,0:T(8,128)(2,1)S(1)}, bf16[64,16,2048]{2,1,0:T(8,128)(2,1)}, u32[]{:S(2)}) %copy-start) | copy-done | bytes 4194328
  12.5 10.6 %tile_chunk.4 = (bf16[16,128,128]{2,1,0:T(8,128)(2,1)S(1)}, f32[16,128,128]{2,1,0:T(8,128)S(1)}) custom-call(s32[3]{0:T(128)S(1)} %get-tuple-element.23.place, s32[4,64]{1,0:T(4,128)S(1)} %bitcast.23, s32[1,256]{1,0:T(1,128)S(1)} %broadcast_in_dim_tile.6.own_row, s32[16,1]{1,0:T(8,128)S(1)} %copy.23.own_col, s32[1,256]{1,0:T(1,128)S(1)} %broadcast_in_dim_tile.7.other_row, ...), custom_call_target="tpu_custom_call" | custom-call | flops 2147483648 | bytes 9961472 | tf_op jit(solution)/shard_map/tile_chunk/pallas_call | solution.py:144
  23.1 1.3 %collective-permute-start.2 = (bf16[16,128,128]{2,1,0:T(8,128)(2,1)S(1)}, bf16[16,128,128]{2,1,0:T(8,128)(2,1)S(1)}, u32[]{:S(2)}, u32[]{:S(2)}) collective-permute-start(bf16[16,128,128]{2,1,0:T(8,128)(2,1)S(1)} %get-tuple-element.14), channel_id=1, source_target_pairs={{0,2},{1,3},{2,0},{3,1},{4,6},{5,7},{6,4},{7,5},{8,10},{9,11},{10,... | collective-permute-start | bytes 1572872 | tf_op jit(solution)/shard_map/ppermute | solution.py:211
  24.3 10.6 %tile_chunk.5 = (bf16[16,128,128]{2,1,0:T(8,128)(2,1)S(1)}, f32[16,128,128]{2,1,0:T(8,128)S(1)}) custom-call(s32[3]{0:T(128)S(1)} %get-tuple-element.24.place, s32[4,64]{1,0:T(4,128)S(1)} %bitcast.24, s32[1,256]{1,0:T(1,128)S(1)} %broadcast_in_dim_tile.6.own_row, s32[16,1]{1,0:T(8,128)S(1)} %copy.23.own_col, s32[1,256]{1,0:T(1,128)S(1)} %broadcast_in_dim_tile.7.other_row, ...), custom_call_target="tpu_custom_call" | custom-call | flops 2147483648 | bytes 9961472 | tf_op jit(solution)/shard_map/tile_chunk/pallas_call | solution.py:144
  34.9 0.3 collective-permute-start.4
  35.3 10.9 %tile_chunk.6 = (bf16[16,128,128]{2,1,0:T(8,128)(2,1)S(1)}, f32[16,128,128]{2,1,0:T(8,128)S(1)}) custom-call(s32[3]{0:T(128)S(1)} %get-tuple-element.25.place, s32[4,64]{1,0:T(4,128)S(1)} %bitcast.25, s32[1,256]{1,0:T(1,128)S(1)} %broadcast_in_dim_tile.6.own_row, s32[16,1]{1,0:T(8,128)S(1)} %copy.23.own_col, s32[1,256]{1,0:T(1,128)S(1)} %broadcast_in_dim_tile.7.other_row, ...), custom_call_target="tpu_custom_call" | custom-call | flops 2147483648 | bytes 9961472 | tf_op jit(solution)/shard_map/tile_chunk/pallas_call | solution.py:144
  46.2 1.3 %collective-permute-start.6 = (bf16[16,128,128]{2,1,0:T(8,128)(2,1)S(1)}, bf16[16,128,128]{2,1,0:T(8,128)(2,1)S(1)}, u32[]{:S(2)}, u32[]{:S(2)}) collective-permute-start(bf16[16,128,128]{2,1,0:T(8,128)(2,1)S(1)} %get-tuple-element.18), channel_id=1, source_target_pairs={{0,2},{1,3},{2,0},{3,1},{4,6},{5,7},{6,4},{7,5},{8,10},{9,11},{10,... | collective-permute-start | bytes 1572872 | tf_op jit(solution)/shard_map/ppermute | solution.py:211
  47.5 10.6 %tile_chunk.7 = (bf16[16,128,128]{2,1,0:T(8,128)(2,1)S(1)}, f32[16,128,128]{2,1,0:T(8,128)S(1)}) custom-call(s32[3]{0:T(128)S(1)} %get-tuple-element.26.place, s32[4,64]{1,0:T(4,128)S(1)} %bitcast.26, s32[1,256]{1,0:T(1,128)S(1)} %broadcast_in_dim_tile.6.own_row, s32[16,1]{1,0:T(8,128)S(1)} %copy.23.own_col, s32[1,256]{1,0:T(1,128)S(1)} %broadcast_in_dim_tile.7.other_row, ...), custom_call_target="tpu_custom_call" | custom-call | flops 2147483648 | bytes 9961472 | tf_op jit(solution)/shard_map/tile_chunk/pallas_call | solution.py:144
  58.1 0.3 collective-permute-start.8
  58.4 0.2 add_convert_fusion.3
  58.6 1.8 %collective-permute-start.3 = (bf16[16,128,128]{2,1,0:T(8,128)(2,1)S(1)}, bf16[16,128,128]{2,1,0:T(8,128)(2,1)S(1)}, u32[]{:S(2)}, u32[]{:S(2)}) collective-permute-start(bf16[16,128,128]{2,1,0:T(8,128)(2,1)S(1)} %add_convert_fusion.3), channel_id=1, source_target_pairs={{0,8},{4,12},{8,0},{12,4},{1,9},{5,13},{9,1},{13,5},{2,10},{6,14},... | collective-permute-start | bytes 1572872 | tf_op jit(solution)/shard_map/ppermute | solution.py:214
  60.4 0.1 add_convert_fusion.2
  60.5 2.6 %collective-permute-start.5 = (bf16[16,128,128]{2,1,0:T(8,128)(2,1)S(1)}, bf16[16,128,128]{2,1,0:T(8,128)(2,1)S(1)}, u32[]{:S(2)}, u32[]{:S(2)}) collective-permute-start(bf16[16,128,128]{2,1,0:T(8,128)(2,1)S(1)} %add_convert_fusion.2), channel_id=1, source_target_pairs={{0,4},{4,8},{8,12},{12,0},{1,5},{5,9},{9,13},{13,1},{2,6},{6,10},{... | collective-permute-start | bytes 1572872 | tf_op jit(solution)/shard_map/ppermute | solution.py:214
  63.1 0.1 add_convert_fusion.1
  63.3 4.8 %collective-permute-done.8 = bf16[16,128,128]{2,1,0:T(8,128)(2,1)S(1)} collective-permute-done((bf16[16,128,128]{2,1,0:T(8,128)(2,1)S(1)}, bf16[16,128,128]{2,1,0:T(8,128)(2,1)S(1)}, u32[]{:S(2)}, u32[]{:S(2)}) %collective-permute-start.8) | collective-permute-done | bytes 524320 | tf_op jit(solution)/shard_map/ppermute | solution.py:211
  68.1 15.2 %collective-permute-done.3 = bf16[16,128,128]{2,1,0:T(8,128)(2,1)S(1)} collective-permute-done((bf16[16,128,128]{2,1,0:T(8,128)(2,1)S(1)}, bf16[16,128,128]{2,1,0:T(8,128)(2,1)S(1)}, u32[]{:S(2)}, u32[]{:S(2)}) %collective-permute-start.3) | collective-permute-done | bytes 524320 | tf_op jit(solution)/shard_map/ppermute | solution.py:214
  83.2 21.3 %collective-permute-done.5 = bf16[16,128,128]{2,1,0:T(8,128)(2,1)S(1)} collective-permute-done((bf16[16,128,128]{2,1,0:T(8,128)(2,1)S(1)}, bf16[16,128,128]{2,1,0:T(8,128)(2,1)S(1)}, u32[]{:S(2)}, u32[]{:S(2)}) %collective-permute-start.5) | collective-permute-done | bytes 524320 | tf_op jit(solution)/shard_map/ppermute | solution.py:214
  104.6 2.6 %collective-permute-done.7 = bf16[16,128,128]{2,1,0:T(8,128)(2,1)S(1)} collective-permute-done((bf16[16,128,128]{2,1,0:T(8,128)(2,1)S(1)}, bf16[16,128,128]{2,1,0:T(8,128)(2,1)S(1)}, u32[]{:S(2)}, u32[]{:S(2)}) %collective-permute-start.7) | collective-permute-done | bytes 524320 | tf_op jit(solution)/shard_map/ppermute | solution.py:214
  107.1 1.2 %fusion = bf16[1,16,128,128]{3,2,1,0:T(8,128)(2,1)} fusion(f32[16,128,128]{2,1,0:T(8,128)S(1)} %get-tuple-element.19, bf16[16,128,128]{2,1,0:T(8,128)(2,1)S(1)} %collective-permute-done.8, bf16[16,128,128]{2,1,0:T(8,128)(2,1)S(1)} %collective-permute-done.7, bf16[16,128,128]{2,1,0:T(8,128)(2,1)S(1)} %collective-permute-done.5, ...), kind=kLoop, calls=%fused_computation.4 | loop fusion | flops 2359296 | bytes 3670016 | tf_op jit(solution)/shard_map/broadcast_in_dim | solution.py:216
  (22 shorter events, 0.6 us)
Async XLA Ops:
  0.0 10.3 %collective-permute-start.1 = (bf16[1024,2048]{1,0:T(8,128)(2,1)}, bf16[1024,2048]{1,0:T(8,128)(2,1)}, u32[]{:S(2)}, u32[]{:S(2)}) collective-permute-start(bf16[1024,2048]{1,0:T(8,128)(2,1)} %bitcast.18), channel_id=1, source_target_pairs={{0,1},{1,0},{2,3},{3,2},{4,5},{5,4},{6,7},{7,6},{8,9},{9,8},{10,11... | collective-permute-start | bytes 12582920 | tf_op jit(solution)/shard_map/ppermute | solution.py:194
  1.4 8.7 %collective-permute-start = (s32[16,1]{1,0:T(8,128)S(1)}, s32[16,1]{1,0:T(8,128)S(1)}, u32[]{:S(2)}, u32[]{:S(2)}) collective-permute-start(s32[16,1]{1,0:T(8,128)S(1)} %copy.23.own_col), channel_id=1, source_target_pairs={{0,1},{1,0},{2,3},{3,2},{4,5},{5,4},{6,7},{7,6},{8,9},{9,8},{10,11... | collective-permute-start | bytes 200 | tf_op jit(solution)/shard_map/ppermute | solution.py:195
  10.3 2.2 %copy-start = (bf16[64,16,2048]{2,1,0:T(8,128)(2,1)S(1)}, bf16[64,16,2048]{2,1,0:T(8,128)(2,1)}, u32[]{:S(2)}) copy-start(bf16[64,16,2048]{2,1,0:T(8,128)(2,1)} %param.4) | copy-start | bytes 12582916
  23.1 35.3 %collective-permute-start.2 = (bf16[16,128,128]{2,1,0:T(8,128)(2,1)S(1)}, bf16[16,128,128]{2,1,0:T(8,128)(2,1)S(1)}, u32[]{:S(2)}, u32[]{:S(2)}) collective-permute-start(bf16[16,128,128]{2,1,0:T(8,128)(2,1)S(1)} %get-tuple-element.14), channel_id=1, source_target_pairs={{0,2},{1,3},{2,0},{3,1},{4,6},{5,7},{6,4},{7,5},{8,10},{9,11},{10,... | collective-permute-start | bytes 1572872 | tf_op jit(solution)/shard_map/ppermute | solution.py:211
  34.9 25.4 %collective-permute-start.4 = (bf16[16,128,128]{2,1,0:T(8,128)(2,1)S(1)}, bf16[16,128,128]{2,1,0:T(8,128)(2,1)S(1)}, u32[]{:S(2)}, u32[]{:S(2)}) collective-permute-start(bf16[16,128,128]{2,1,0:T(8,128)(2,1)S(1)} %get-tuple-element.16), channel_id=1, source_target_pairs={{0,2},{1,3},{2,0},{3,1},{4,6},{5,7},{6,4},{7,5},{8,10},{9,11},{10,... | collective-permute-start | bytes 1572872 | tf_op jit(solution)/shard_map/ppermute | solution.py:211
  35.3 12.2 %copy-start.1 = (bf16[64,16,2048]{2,1,0:T(8,128)(2,1)S(1)}, bf16[64,16,2048]{2,1,0:T(8,128)(2,1)}, u32[]{:S(2)}) copy-start(bf16[64,16,2048]{2,1,0:T(8,128)(2,1)} %param.4) | copy-start | bytes 12582916
  46.2 16.9 %collective-permute-start.6 = (bf16[16,128,128]{2,1,0:T(8,128)(2,1)S(1)}, bf16[16,128,128]{2,1,0:T(8,128)(2,1)S(1)}, u32[]{:S(2)}, u32[]{:S(2)}) collective-permute-start(bf16[16,128,128]{2,1,0:T(8,128)(2,1)S(1)} %get-tuple-element.18), channel_id=1, source_target_pairs={{0,2},{1,3},{2,0},{3,1},{4,6},{5,7},{6,4},{7,5},{8,10},{9,11},{10,... | collective-permute-start | bytes 1572872 | tf_op jit(solution)/shard_map/ppermute | solution.py:211
  58.1 10.0 %collective-permute-start.8 = (bf16[16,128,128]{2,1,0:T(8,128)(2,1)S(1)}, bf16[16,128,128]{2,1,0:T(8,128)(2,1)S(1)}, u32[]{:S(2)}, u32[]{:S(2)}) collective-permute-start(bf16[16,128,128]{2,1,0:T(8,128)(2,1)S(1)} %get-tuple-element.20), channel_id=1, source_target_pairs={{0,2},{1,3},{2,0},{3,1},{4,6},{5,7},{6,4},{7,5},{8,10},{9,11},{10,... | collective-permute-start | bytes 1572872 | tf_op jit(solution)/shard_map/ppermute | solution.py:211
  58.6 24.7 %collective-permute-start.3 = (bf16[16,128,128]{2,1,0:T(8,128)(2,1)S(1)}, bf16[16,128,128]{2,1,0:T(8,128)(2,1)S(1)}, u32[]{:S(2)}, u32[]{:S(2)}) collective-permute-start(bf16[16,128,128]{2,1,0:T(8,128)(2,1)S(1)} %add_convert_fusion.3), channel_id=1, source_target_pairs={{0,8},{4,12},{8,0},{12,4},{1,9},{5,13},{9,1},{13,5},{2,10},{6,14},... | collective-permute-start | bytes 1572872 | tf_op jit(solution)/shard_map/ppermute | solution.py:214
  60.5 44.1 %collective-permute-start.5 = (bf16[16,128,128]{2,1,0:T(8,128)(2,1)S(1)}, bf16[16,128,128]{2,1,0:T(8,128)(2,1)S(1)}, u32[]{:S(2)}, u32[]{:S(2)}) collective-permute-start(bf16[16,128,128]{2,1,0:T(8,128)(2,1)S(1)} %add_convert_fusion.2), channel_id=1, source_target_pairs={{0,4},{4,8},{8,12},{12,0},{1,5},{5,9},{9,13},{13,1},{2,6},{6,10},{... | collective-permute-start | bytes 1572872 | tf_op jit(solution)/shard_map/ppermute | solution.py:214
  63.3 43.9 %collective-permute-start.7 = (bf16[16,128,128]{2,1,0:T(8,128)(2,1)S(1)}, bf16[16,128,128]{2,1,0:T(8,128)(2,1)S(1)}, u32[]{:S(2)}, u32[]{:S(2)}) collective-permute-start(bf16[16,128,128]{2,1,0:T(8,128)(2,1)S(1)} %add_convert_fusion.1), channel_id=1, source_target_pairs={{0,12},{4,0},{8,4},{12,8},{1,13},{5,1},{9,5},{13,9},{2,14},{6,2},{... | collective-permute-start | bytes 1572872 | tf_op jit(solution)/shard_map/ppermute | solution.py:214

commit v2 on v0

--- a/solution.py
+++ b/solution.py
@@ -1,12 +1,16 @@
+import functools
 import math
 
 import jax
 import jax.numpy as jnp
 from jax import lax
+from jax.experimental import pallas as pl
+from jax.experimental.pallas import tpu as pltpu
 from jax.sharding import PartitionSpec as P
 
 TILE = 128
 CAP = 8
+GROUP = 256
 
 
 def block_pairs(pair_codes, blocks):
@@ -35,46 +39,256 @@
     return jnp.where(filled, source_row, local_count)
 
 
-def per_device(half_tensor, batch_owner, pair_list, live_pairs):
+def slab_plan(half_tensor, batch_owner, pair_list, live_pairs):
     batches = lax.axis_size("orb")
     aux_local, occ_local, domain = half_tensor.shape
-    tile_width = TILE
-    blocks = domain // tile_width
+    blocks = domain // TILE
     sources = slot_sources(batch_owner[:, 0], batches, CAP)
-    block_major = half_tensor.reshape(aux_local, occ_local, blocks, tile_width).transpose(
-        2, 1, 0, 3
-    )
+    block_major = half_tensor.reshape(aux_local, occ_local, blocks, TILE).transpose(2, 1, 0, 3)
     outgoing = jnp.take(block_major, sources, axis=1, mode="fill", fill_value=0)
     arrived = lax.all_to_all(outgoing, "orb", split_axis=1, concat_axis=2, tiled=True)
-    pieces = [arrived.reshape(blocks, -1, tile_width)]
+    stacked_rows = arrived.reshape(blocks, -1, TILE)
     first_blocks, second_blocks = block_pairs(pair_list[0], blocks)
     live_count = live_pairs[0]
     pair_total = pair_list.shape[1]
     contract = (((0,), (0,)), ((), ()))
     group_size = math.gcd(4, pair_total)
-    group_turns = pair_total // group_size
 
     def one_group(group_index):
-        pair_start = 0 + group_index * group_size
+        pair_start = group_index * group_size
         tiles = []
         for offset in range(group_size):
-            left_block = first_blocks[pair_start + offset]
-            right_block = second_blocks[pair_start + offset]
-            stacked_rows = pieces[0]
-            left_part = lax.dynamic_index_in_dim(stacked_rows, left_block, 0, keepdims=False)
-            right_part = lax.dynamic_index_in_dim(stacked_rows, right_block, 0, keepdims=False)
-            tile_one = lax.dot_general(
-                left_part, right_part, contract, preferred_element_type=jnp.float32
+            left = lax.dynamic_index_in_dim(
+                stacked_rows, first_blocks[pair_start + offset], 0, keepdims=False
             )
-            tiles.append(tile_one)
-        tile_block = jnp.stack(tiles, axis=0)
+            right = lax.dynamic_index_in_dim(
+                stacked_rows, second_blocks[pair_start + offset], 0, keepdims=False
+            )
+            tiles.append(
+                lax.dot_general(left, right, contract, preferred_element_type=jnp.float32)
+            )
         keep_mask = pair_start + lax.iota(jnp.int32, group_size) < live_count
-        return jnp.where(keep_mask[:, None, None], tile_block, jnp.float32(0.0))
-
-    grouped = lax.map(one_group, jnp.arange(group_turns, dtype=jnp.int32))
-    terms = grouped.reshape(pair_total, tile_width, tile_width)
+        return jnp.where(keep_mask[:, None, None], jnp.stack(tiles, axis=0), jnp.float32(0.0))
+
+    grouped = lax.map(one_group, jnp.arange(pair_total // group_size, dtype=jnp.int32))
+    terms = grouped.reshape(pair_total, TILE, TILE)
     mine = lax.psum_scatter(terms.astype(jnp.bfloat16), "row", scatter_dimension=0, tiled=True)
     return mine[None]
+
+
+def chunk_kernel(sources, started, occ_local, place, pairs, table, *refs):
+    owners, refs = refs[:sources], refs[sources:]
+    slabs, refs = refs[:sources], refs[sources:]
+    before, refs = (refs[:2], refs[2:]) if started else (None, refs)
+    send_ref, keep_ref, packed_rows, turned = refs
+    step = pl.program_id(0)
+    groups = pl.num_programs(0) // sources
+    batch = place[0]
+    share = send_ref.shape[0]
+    live = pairs[pairs.shape[0] - 1]
+    per_group = GROUP // occ_local
+    held = per_group * CAP
+
+    def count(owner):
+        number = jnp.int32(0)
+        for orbital in range(occ_local):
+            number = number + (owner[orbital] == batch).astype(jnp.int32)
+        return number
+
+    counts = [count(owner) for owner in owners]
+
+    def pack(owner, number, slab, first, group):
+        lane = lax.broadcasted_iota(jnp.int32, (1, GROUP), 1)
+        rank = jnp.int32(0)
+        target = jnp.full((1, GROUP), -1, jnp.int32)
+        for orbital in range(occ_local):
+            mine = owner[orbital] == batch
+            row = jnp.where(mine, lane // occ_local * number + rank, -1)
+            target = jnp.where(lane % occ_local == orbital, row, target)
+            rank = rank + mine.astype(jnp.int32)
+        slot = lax.broadcasted_iota(jnp.int32, (held, GROUP), 0)
+        pick = (slot == target).astype(jnp.bfloat16)
+        packed = jnp.dot(pick, slab[...], preferred_element_type=jnp.float32)
+        start = pl.multiple_of((first + group * number) * per_group, per_group)
+        packed_rows[pl.ds(start, held), :] = packed.astype(jnp.bfloat16)
+
+    first = jnp.int32(0)
+    for source in range(sources):
+        @pl.when((step >= source * groups) & (step < (source + 1) * groups))
+        def _(source=source, first=first):
+            pack(owners[source], counts[source], slabs[source], first, step - source * groups)
+
+        first = first + groups * counts[source]
+
+    @pl.when(step == pl.num_programs(0) - 1)
+    def _():
+        filled = pl.multiple_of(first * per_group, per_group)
+        domain = packed_rows.shape[1]
+        packed_rows[pl.ds(filled, GROUP), :] = jnp.zeros((GROUP, domain), jnp.bfloat16)
+        parts = (filled + GROUP - 1) // GROUP
+
+        def turn(part, carry):
+            at = pl.multiple_of(part * GROUP, GROUP)
+            for block in range(domain // TILE):
+                columns = slice(block * TILE, (block + 1) * TILE)
+                turned[columns, pl.ds(at, GROUP)] = packed_rows[pl.ds(at, GROUP), columns].T
+            return carry
+
+        lax.fori_loop(0, parts, turn, 0)
+
+        def tiles(depth):
+            def tile(pair, out, at, start):
+                value = jnp.zeros((TILE, TILE), jnp.float32)
+                if depth:
+                    code = pairs[pair]
+                    left = pl.multiple_of(table[2 * code], TILE)
+                    right = pl.multiple_of(table[2 * code + 1], TILE)
+                    product = jnp.dot(
+                        turned[pl.ds(left, TILE), :depth],
+                        packed_rows[:depth, pl.ds(right, TILE)],
+                        preferred_element_type=jnp.float32,
+                    )
+                    value = jnp.where(pair < live, product, value)
+                if start is not None:
+                    value = value + start[at]
+                out[at] = value.astype(out.dtype)
+
+            width = math.gcd(4, share)
+
+            def several(turn_at, carry):
+                for offset in range(width):
+                    at = turn_at * width + offset
+                    tile(place[1] + at, send_ref, at, before and before[0])
+                    tile(place[2] + at, keep_ref, at, before and before[1])
+                return carry
+
+            lax.fori_loop(0, share // width, several, 0)
+
+        for part_count in range(turned.shape[1] // GROUP + 1):
+            pl.when(parts == part_count)(functools.partial(tiles, part_count * GROUP))
+
+
+def tile_chunk(place, pairs, table, owners, slabs, share, send_type, before=()):
+    sources = len(slabs)
+    occ_local, = owners[0].shape
+    rows_total, domain = slabs[0].shape
+    groups = rows_total // GROUP
+    depth = sources * groups * GROUP // occ_local * CAP
+    depth = -(-depth // GROUP) * GROUP
+    tiles = (share, TILE, TILE)
+    whole = pl.BlockSpec(tiles, lambda step, *_: (0, 0, 0))
+
+    def slab_spec(source):
+        def block(step, *_):
+            return (jnp.clip(step - source * groups, 0, groups - 1), 0)
+
+        return pl.BlockSpec((GROUP, domain), block)
+
+    return pl.pallas_call(
+        functools.partial(chunk_kernel, sources, bool(before), occ_local),
+        grid_spec=pltpu.PrefetchScalarGridSpec(
+            num_scalar_prefetch=3 + sources,
+            grid=(sources * groups,),
+            in_specs=[slab_spec(source) for source in range(sources)] + [whole] * len(before),
+            out_specs=[whole, whole],
+            scratch_shapes=[
+                pltpu.VMEM((depth + GROUP, domain), jnp.bfloat16),
+                pltpu.VMEM((domain, depth), jnp.bfloat16),
+            ],
+        ),
+        out_shape=[
+            jax.ShapeDtypeStruct(tiles, send_type),
+            jax.ShapeDtypeStruct(tiles, jnp.float32),
+        ],
+        compiler_params=pltpu.CompilerParams(vmem_limit_bytes=56 * 1024 * 1024),
+        cost_estimate=pl.CostEstimate(
+            flops=4 * share * TILE * TILE * depth + 2 * depth * GROUP * domain,
+            bytes_accessed=2 * sources * rows_total * domain + 6 * share * TILE * TILE,
+            transcendentals=0,
+        ),
+        name="tile_chunk",
+    )(place, pairs, table, *owners, *slabs, *before)
+
+
+def pair_table(blocks):
+    return jnp.asarray(
+        [TILE * block for left in range(blocks) for right in range(left, blocks)
+         for block in (left, right)],
+        jnp.int32,
+    )
+
+
+def tile_plan(half_tensor, batch_owner, pair_list, live_pairs):
+    batches = lax.axis_size("orb")
+    rows = lax.axis_size("row")
+    aux_local, occ_local, domain = half_tensor.shape
+    share = pair_list.shape[1] // rows
+    row_at = lax.axis_index("row")
+    orb_at = lax.axis_index("orb")
+
+    def exchange(array, axis, bits):
+        size = lax.axis_size(axis)
+        return lax.ppermute(array, axis, [(i, i ^ bits) for i in range(size)])
+
+    own_rows = half_tensor.reshape(aux_local * occ_local, domain)
+    other_rows = exchange(own_rows, "row", 1)
+    own_owner = batch_owner[:, 0]
+    other_owner = exchange(own_owner, "row", 1)
+    own_pairs = jnp.concatenate([pair_list[0], live_pairs])
+    pairs = [own_pairs] + [exchange(own_pairs, "orb", bits) for bits in range(1, batches)]
+    table = pair_table(domain // TILE)
+
+    def place_of(bits):
+        return jnp.stack([orb_at ^ bits, (row_at ^ 2) * share, row_at * share]).astype(jnp.int32)
+
+    def chunk(bits, place):
+        both = (own_owner, other_owner), (own_rows, other_rows)
+        return tile_chunk(place, pairs[bits], table, *both, share, jnp.bfloat16)
+
+    def over_x(send, keep):
+        return keep + exchange(send, "row", 2).astype(jnp.float32)
+
+    def after(array, earlier):
+        return lax.optimization_barrier((array, earlier))
+
+    place = place_of(3)
+    started = tile_chunk(
+        place, pairs[3], table, (own_owner,), (own_rows,), share, jnp.float32
+    )
+    send_3, keep_3 = tile_chunk(
+        place, pairs[3], table, (other_owner,), (other_rows,), share, jnp.bfloat16, started
+    )
+    send_2, keep_2 = chunk(2, place_of(2))
+    far = over_x(send_3, keep_3).astype(jnp.bfloat16)
+    place, far = after(place_of(1), far)
+    far = exchange(far, "orb", 1)
+    send_1, keep_1 = chunk(1, place)
+    term_2 = over_x(send_2, keep_2)
+    place, term_2 = after(place_of(0), term_2)
+    across = exchange((term_2 + far.astype(jnp.float32)).astype(jnp.bfloat16), "orb", 2)
+    send_0, keep_0 = chunk(0, place)
+    near = exchange(over_x(send_1, keep_1).astype(jnp.bfloat16), "orb", 1)
+    total = over_x(send_0, keep_0) + near.astype(jnp.float32) + across.astype(jnp.float32)
+    return total.astype(jnp.bfloat16)[None]
+
+
+def per_device(half_tensor, batch_owner, pair_list, live_pairs):
+    batches = lax.axis_size("orb")
+    rows = lax.axis_size("row")
+    aux_local, occ_local, domain = half_tensor.shape
+    pair_total = pair_list.shape[1]
+    tile_elements = batches * pair_total * TILE * TILE
+    slab_elements = batches * CAP * aux_local * domain
+    fits = (
+        rows == 4
+        and batches == 4
+        and pair_total % rows == 0
+        and GROUP % occ_local == 0
+        and aux_local * occ_local % GROUP == 0
+        and tile_elements <= slab_elements
+    )
+    plan = tile_plan if fits else slab_plan
+    return plan(half_tensor, batch_owner, pair_list, live_pairs)
 
 
 def solution(mesh):

time: 663 us -> 104 us (0.16)
  loops' own time: 245 us -> 0 us
  waiting for transfers between devices: 215 us -> 22.2 us
  matrix products: 98.7 us -> 0 us
  Pallas kernels: 0 us -> 53.1 us
  local copies, waits for them, and re-layouts: 46.1 us -> 2.14 us
  other arithmetic: 32.4 us -> 4.8 us
  starting transfers between devices: 6.45 us -> 19.8 us
  between operations: 13.4 us -> 0.76 us
    another operation x1 -> x0, loops' own time: 245 us -> none  [per_device(): grouped = lax.map(one_group, jnp.arange(group_turns, dtype=jnp.int32))]
    all_to_all x1 -> x0, waiting for transfers between devices: 184 us -> none  [per_device(): lax.all_to_all(outgoing, 'orb', split_axis=1, concat_axis=2, tiled=True)]
    dot_general x64 -> x0, matrix products: 98.7 us -> none  [one_group(): lax.dot_general(left_part, right_part, contract, preferred_element_type=j...]
    pallas_call x0 -> x5, Pallas kernels: none -> 53.1 us  [tile_chunk(): pl.pallas_call(functools.partial(chunk_kernel, sources, bool(before), occ...]
    reduce_scatter x1 -> x0, waiting for transfers between devices: 30.9 us -> none  [per_device(): lax.psum_scatter(terms.astype(jnp.bfloat16), 'row', scatter_dimension=0,...]
    ppermute x0 -> x12, waiting for transfers between devices: none -> 22.2 us  [exchange(): return lax.ppermute(array, axis, [(i, i ^ bits) for i in range(size)])]
    dynamic_slice x32 -> x0, local copies, waits for them, and re-layouts: 21.1 us -> none  [the longest x16 10.8 us: one_group(): left_block = first_blocks[pair_start + offset]]
    ppermute x0 -> x12, starting transfers between devices: none -> 19.8 us  [exchange(): return lax.ppermute(array, axis, [(i, i ^ bits) for i in range(size)])]
  transfers between devices with their start and end apart: 2 -> 12, of which waited for: 2 -> 5; matrix products, arithmetic and copies ran while one was open for 0% -> 4% of each run, Pallas kernels for 0% -> 44%
where the time goes in v2:
time: 104 us; the launch traced here: 103 us
  Pallas kernels  53.1 us (51%)
  waiting for transfers between devices  22.2 us (21%)
  starting transfers between devices  19.8 us (19%)
  other arithmetic  4.8 us (5%)
  local copies, waits for them, and re-layouts  2.14 us (2%)
    pallas_call x5, Pallas kernels, tile_chunk(): pl.pallas_call(functools.partial(chunk_kernel, sources, bool(before), occ...  53.1 us
    ppermute x12, waiting for transfers between devices, exchange(): return lax.ppermute(array, axis, [(i, i ^ bits) for i in range(size)])  22.2 us
    ppermute x12, starting transfers between devices, exchange(): return lax.ppermute(array, axis, [(i, i ^ bits) for i in range(size)])  19.8 us
    another operation x4, other arithmetic, place_of(): jnp.stack([orb_at ^ bits, (row_at ^ 2) * share, row_at * share])  2.47 us
    unnamed x18, local copies, waits for them, and re-layouts  2.14 us
  transfers between devices with their start and end apart: 12, of which 5 were waited for; matrix products, arithmetic and copies ran while one was open for 4% of the time, Pallas kernels for 44%

profile of v2, /device:TPU:0, one launch (start us, length us, event | category | flops | bytes accessed | tf_op | source)
XLA Modules:
  0.0 102.8 jit_solution(9481295980021338334)
XLA Ops:
  1.1 0.7 pad_add_fusion.pairs
  1.8 4.6 %collective-permute-start.5 = (s32[65]{0:T(128)S(1)}, s32[65]{0:T(128)S(1)}, u32[]{:S(2)}, u32[]{:S(2)}) collective-permute-start(s32[65]{0:T(128)S(1)} %pad_add_fusion.pairs), channel_id=1, source_target_pairs={{0,12},{4,8},{8,4},{12,0},{1,13},{5,9},{9,5},{13,1},{2,14},{6,10},... | collective-permute-start | bytes 788 | tf_op jit(solution)/shard_map/ppermute | solution.py:231
  6.7 0.6 add_add_fusion.3.place
  7.3 0.7 collective-permute-done.5.pairs
  8.5 7.4 %tile_chunk.7 = (f32[16,128,128]{2,1,0:T(8,128)}, f32[16,128,128]{2,1,0:T(8,128)}) custom-call(s32[3]{0:T(128)} %add_add_fusion.3.place, s32[65]{0:T(128)} %copy-done.5, s32[272]{0:T(512)} %constant.17.clone.table, s32[16]{0:T(128)} %bitcast.17, bf16[1024,2048]{1,0:T(8,128)(2,1)} %bitcast.12), custom_call_target="tpu_custom_call" | custom-call | flops 1073741824 | bytes 5767168 | tf_op jit(solution)/shard_map/tile_chunk/pallas_call | solution.py:187
  15.9 0.5 copy-done.4
  16.4 7.9 %tile_chunk.8 = (bf16[16,128,128]{2,1,0:T(8,128)(2,1)}, f32[16,128,128]{2,1,0:T(8,128)}) custom-call(s32[3]{0:T(128)} %add_add_fusion.3.place, s32[65]{0:T(128)} %copy-done.5, s32[272]{0:T(512)} %constant.17.clone.table, s32[16]{0:T(128)} %copy-done.4, bf16[1024,2048]{1,0:T(8,128)(2,1)} %collective-permute-done.2.refs_3_.refs_1_, ...), custom_call_target="tpu_custom_call" | custom-call | flops 1073741824 | bytes 5767168 | tf_op jit(solution)/shard_map/tile_chunk/pallas_call | solution.py:187
  24.3 1.7 %collective-permute-start.6 = (bf16[16,128,128]{2,1,0:T(8,128)(2,1)}, bf16[16,128,128]{2,1,0:T(8,128)(2,1)S(1)}, u32[]{:S(2)}, u32[]{:S(2)}) collective-permute-start(bf16[16,128,128]{2,1,0:T(8,128)(2,1)} %get-tuple-element.27), channel_id=1, source_target_pairs={{0,2},{1,3},{2,0},{3,1},{4,6},{5,7},{6,4},{7,5},{8,10},{9,11},{10,... | collective-permute-start | bytes 1572872 | tf_op jit(solution)/shard_map/ppermute | solution.py:231
  26.0 6.0 %collective-permute-start = (s32[65]{0:T(128)S(1)}, s32[65]{0:T(128)S(1)}, u32[]{:S(2)}, u32[]{:S(2)}) collective-permute-start(s32[65]{0:T(128)S(1)} %pad_add_fusion.pairs), channel_id=1, source_target_pairs={{0,8},{4,12},{8,0},{12,4},{1,9},{5,13},{9,1},{13,5},{2,10},{6,14},... | collective-permute-start | bytes 788 | tf_op jit(solution)/shard_map/ppermute | solution.py:231
  32.1 0.6 add_add_fusion.2.place
  32.7 0.6 add_add_fusion.1.place
  33.6 0.6 copy-done.8
  34.2 11.8 %tile_chunk.5 = (bf16[16,128,128]{2,1,0:T(8,128)(2,1)}, f32[16,128,128]{2,1,0:T(8,128)}) custom-call(s32[3]{0:T(128)} %add_add_fusion.1.place, s32[65]{0:T(128)} %copy-done.8, s32[272]{0:T(512)} %constant.17.clone.table, s32[16]{0:T(128)} %bitcast.18, s32[16]{0:T(128)} %copy-done.4, bf16[1024,2048]{1,0:T(8,128)(2,1)} %bitcast.13, ...), custom_call_target="tpu_custom_call" | custom-call | flops 2147483648 | bytes 9961472 | tf_op jit(solution)/shard_map/tile_chunk/pallas_call | solution.py:187
  46.0 0.5 collective-permute-start.3
  47.2 11.9 %tile_chunk.9 = (bf16[16,128,128]{2,1,0:T(8,128)(2,1)}, f32[16,128,128]{2,1,0:T(8,128)}) custom-call(s32[3]{0:T(128)} %add_add_fusion.2.place, s32[65]{0:T(128)} %copy-done.7, s32[272]{0:T(512)} %constant.17.clone.table, s32[16]{0:T(128)} %bitcast.19, s32[16]{0:T(128)} %copy-done.4, bf16[1024,2048]{1,0:T(8,128)(2,1)} %bitcast.14, ...), custom_call_target="tpu_custom_call" | custom-call | flops 2147483648 | bytes 9961472 | tf_op jit(solution)/shard_map/tile_chunk/pallas_call | solution.py:187
  59.1 1.5 %collective-permute-start.8 = (bf16[16,128,128]{2,1,0:T(8,128)(2,1)}, bf16[16,128,128]{2,1,0:T(8,128)(2,1)S(1)}, u32[]{:S(2)}, u32[]{:S(2)}) collective-permute-start(bf16[16,128,128]{2,1,0:T(8,128)(2,1)} %get-tuple-element.30), channel_id=1, source_target_pairs={{0,2},{1,3},{2,0},{3,1},{4,6},{5,7},{6,4},{7,5},{8,10},{9,11},{10,... | collective-permute-start | bytes 1572872 | tf_op jit(solution)/shard_map/ppermute | solution.py:231
  60.6 0.6 add_add_fusion.place
  61.2 2.0 %collective-permute-start.10 = (bf16[16,128,128]{2,1,0:T(8,128)(2,1)S(1)}, bf16[16,128,128]{2,1,0:T(8,128)(2,1)S(1)}, u32[]{:S(2)}, u32[]{:S(2)}) collective-permute-start(bf16[16,128,128]{2,1,0:T(8,128)(2,1)S(1)} %add_convert_fusion.3), channel_id=1, source_target_pairs={{0,4},{4,0},{8,12},{12,8},{1,5},{5,1},{9,13},{13,9},{2,6},{6,2},{1... | collective-permute-start | bytes 1572872 | tf_op jit(solution)/shard_map/ppermute | solution.py:231
  63.3 14.1 %tile_chunk.6 = (bf16[16,128,128]{2,1,0:T(8,128)(2,1)}, f32[16,128,128]{2,1,0:T(8,128)}) custom-call(s32[3]{0:T(128)} %add_add_fusion.place, s32[65]{0:T(128)} %copy-done.6, s32[272]{0:T(512)} %constant.17.clone.table, s32[16]{0:T(128)} %bitcast.20, s32[16]{0:T(128)} %copy-done.4, bf16[1024,2048]{1,0:T(8,128)(2,1)} %bitcast.15, ...), custom_call_target="tpu_custom_call" | custom-call | flops 2147483648 | bytes 9961472 | tf_op jit(solution)/shard_map/tile_chunk/pallas_call | solution.py:187
  77.8 2.6 %collective-permute-start.11 = (bf16[16,128,128]{2,1,0:T(8,128)(2,1)S(1)}, bf16[16,128,128]{2,1,0:T(8,128)(2,1)S(1)}, u32[]{:S(2)}, u32[]{:S(2)}) collective-permute-start(bf16[16,128,128]{2,1,0:T(8,128)(2,1)S(1)} %add_convert_fusion.1), channel_id=1, source_target_pairs={{0,8},{4,12},{8,0},{12,4},{1,9},{5,13},{9,1},{13,5},{2,10},{6,14},... | collective-permute-start | bytes 1572872 | tf_op jit(solution)/shard_map/ppermute | solution.py:231
  80.4 8.8 %collective-permute-done.4 = bf16[16,128,128]{2,1,0:T(8,128)(2,1)S(1)} collective-permute-done((bf16[16,128,128]{2,1,0:T(8,128)(2,1)}, bf16[16,128,128]{2,1,0:T(8,128)(2,1)S(1)}, u32[]{:S(2)}, u32[]{:S(2)}) %collective-permute-start.4) | collective-permute-done | bytes 524320 | tf_op jit(solution)/shard_map/ppermute | solution.py:231
  89.2 10.2 %collective-permute-done.9 = bf16[16,128,128]{2,1,0:T(8,128)(2,1)S(1)} collective-permute-done((bf16[16,128,128]{2,1,0:T(8,128)(2,1)S(1)}, bf16[16,128,128]{2,1,0:T(8,128)(2,1)S(1)}, u32[]{:S(2)}, u32[]{:S(2)}) %collective-permute-start.9) | collective-permute-done | bytes 524320 | tf_op jit(solution)/shard_map/ppermute | solution.py:231
  99.4 2.2 %collective-permute-done.11 = bf16[16,128,128]{2,1,0:T(8,128)(2,1)S(1)} collective-permute-done((bf16[16,128,128]{2,1,0:T(8,128)(2,1)S(1)}, bf16[16,128,128]{2,1,0:T(8,128)(2,1)S(1)}, u32[]{:S(2)}, u32[]{:S(2)}) %collective-permute-start.11) | collective-permute-done | bytes 524320 | tf_op jit(solution)/shard_map/ppermute | solution.py:231
  101.7 1.1 %fusion = bf16[1,16,128,128]{3,2,1,0:T(8,128)(2,1)} fusion(bf16[16,128,128]{2,1,0:T(8,128)(2,1)S(1)} %collective-permute-done.11, bf16[16,128,128]{2,1,0:T(8,128)(2,1)S(1)} %collective-permute-done.9, f32[16,128,128]{2,1,0:T(8,128)S(1)} %copy-done, bf16[16,128,128]{2,1,0:T(8,128)(2,1)S(1)} %collective-permute-done.4), kind=kLoop, calls=%fused_computation.5 | loop fusion | flops 1835008 | bytes 3145728 | tf_op jit(solution)/shard_map/broadcast_in_dim | solution.py:272
  (33 shorter events, 2.6 us)
Async XLA Ops:
  0.0 15.9 %collective-permute-start.2 = (bf16[1024,2048]{1,0:T(8,128)(2,1)}, bf16[1024,2048]{1,0:T(8,128)(2,1)}, u32[]{:S(2)}, u32[]{:S(2)}) collective-permute-start(bf16[1024,2048]{1,0:T(8,128)(2,1)} %bitcast.11), channel_id=1, source_target_pairs={{0,1},{1,0},{2,3},{3,2},{4,5},{5,4},{6,7},{7,6},{8,9},{9,8},{10,11... | collective-permute-start | bytes 12582920 | tf_op jit(solution)/shard_map/ppermute | solution.py:231
  1.8 24.2 %copy-start.6 = (s32[65]{0:T(128)}, s32[65]{0:T(128)S(1)}, u32[]{:S(2)}) copy-start(s32[65]{0:T(128)S(1)} %pad_add_fusion.pairs) | copy-start | bytes 784
  1.8 6.1 %collective-permute-start.5 = (s32[65]{0:T(128)S(1)}, s32[65]{0:T(128)S(1)}, u32[]{:S(2)}, u32[]{:S(2)}) collective-permute-start(s32[65]{0:T(128)S(1)} %pad_add_fusion.pairs), channel_id=1, source_target_pairs={{0,12},{4,8},{8,4},{12,0},{1,13},{5,9},{9,5},{13,1},{2,14},{6,10},... | collective-permute-start | bytes 788 | tf_op jit(solution)/shard_map/ppermute | solution.py:231
  6.4 9.4 %collective-permute-start.1 = (s32[16]{0:T(128)}, s32[16]{0:T(128)S(1)}, u32[]{:S(2)}, u32[]{:S(2)}) collective-permute-start(s32[16]{0:T(128)} %bitcast.16), channel_id=1, source_target_pairs={{0,1},{1,0},{2,3},{3,2},{4,5},{5,4},{6,7},{7,6},{8,9},{9,8},{10,11... | collective-permute-start | bytes 200 | tf_op jit(solution)/shard_map/ppermute | solution.py:231
  8.0 0.5 copy-start.5
  15.9 0.5 copy-start.4
  24.3 22.2 %collective-permute-start.6 = (bf16[16,128,128]{2,1,0:T(8,128)(2,1)}, bf16[16,128,128]{2,1,0:T(8,128)(2,1)S(1)}, u32[]{:S(2)}, u32[]{:S(2)}) collective-permute-start(bf16[16,128,128]{2,1,0:T(8,128)(2,1)} %get-tuple-element.27), channel_id=1, source_target_pairs={{0,2},{1,3},{2,0},{3,1},{4,6},{5,7},{6,4},{7,5},{8,10},{9,11},{10,... | collective-permute-start | bytes 1572872 | tf_op jit(solution)/shard_map/ppermute | solution.py:231
  26.0 20.7 %collective-permute-start.7 = (s32[65]{0:T(128)S(1)}, s32[65]{0:T(128)S(1)}, u32[]{:S(2)}, u32[]{:S(2)}) collective-permute-start(s32[65]{0:T(128)S(1)} %pad_add_fusion.pairs), channel_id=1, source_target_pairs={{0,4},{4,0},{8,12},{12,8},{1,5},{5,1},{9,13},{13,9},{2,6},{6,2},{1... | collective-permute-start | bytes 788 | tf_op jit(solution)/shard_map/ppermute | solution.py:231
  26.0 7.6 %collective-permute-start = (s32[65]{0:T(128)S(1)}, s32[65]{0:T(128)S(1)}, u32[]{:S(2)}, u32[]{:S(2)}) collective-permute-start(s32[65]{0:T(128)S(1)} %pad_add_fusion.pairs), channel_id=1, source_target_pairs={{0,8},{4,12},{8,0},{12,4},{1,9},{5,13},{9,1},{13,5},{2,10},{6,14},... | collective-permute-start | bytes 788 | tf_op jit(solution)/shard_map/ppermute | solution.py:231
  33.3 13.3 %copy-start.1 = (f32[16,128,128]{2,1,0:T(8,128)S(1)}, f32[16,128,128]{2,1,0:T(8,128)}, u32[]{:S(2)}) copy-start(f32[16,128,128]{2,1,0:T(8,128)} %get-tuple-element.26) | copy-start | bytes 3145732
  33.6 0.6 copy-start.8
  46.0 17.2 %collective-permute-start.3 = (bf16[16,128,128]{2,1,0:T(8,128)(2,1)}, bf16[16,128,128]{2,1,0:T(8,128)(2,1)S(1)}, u32[]{:S(2)}, u32[]{:S(2)}) collective-permute-start(bf16[16,128,128]{2,1,0:T(8,128)(2,1)} %get-tuple-element.20), channel_id=1, source_target_pairs={{0,2},{1,3},{2,0},{3,1},{4,6},{5,7},{6,4},{7,5},{8,10},{9,11},{10,... | collective-permute-start | bytes 1572872 | tf_op jit(solution)/shard_map/ppermute | solution.py:231
  46.7 16.5 %copy-start.2 = (f32[16,128,128]{2,1,0:T(8,128)S(1)}, f32[16,128,128]{2,1,0:T(8,128)}, u32[]{:S(2)}) copy-start(f32[16,128,128]{2,1,0:T(8,128)} %get-tuple-element.19) | copy-start | bytes 3145732
  46.7 0.5 copy-start.7
  59.1 18.3 %collective-permute-start.8 = (bf16[16,128,128]{2,1,0:T(8,128)(2,1)}, bf16[16,128,128]{2,1,0:T(8,128)(2,1)S(1)}, u32[]{:S(2)}, u32[]{:S(2)}) collective-permute-start(bf16[16,128,128]{2,1,0:T(8,128)(2,1)} %get-tuple-element.30), channel_id=1, source_target_pairs={{0,2},{1,3},{2,0},{3,1},{4,6},{5,7},{6,4},{7,5},{8,10},{9,11},{10,... | collective-permute-start | bytes 1572872 | tf_op jit(solution)/shard_map/ppermute | solution.py:231
  61.2 16.5 %collective-permute-start.10 = (bf16[16,128,128]{2,1,0:T(8,128)(2,1)S(1)}, bf16[16,128,128]{2,1,0:T(8,128)(2,1)S(1)}, u32[]{:S(2)}, u32[]{:S(2)}) collective-permute-start(bf16[16,128,128]{2,1,0:T(8,128)(2,1)S(1)} %add_convert_fusion.3), channel_id=1, source_target_pairs={{0,4},{4,0},{8,12},{12,8},{1,5},{5,1},{9,13},{13,9},{2,6},{6,2},{1... | collective-permute-start | bytes 1572872 | tf_op jit(solution)/shard_map/ppermute | solution.py:231
  63.3 14.1 %copy-start.3 = (f32[16,128,128]{2,1,0:T(8,128)S(1)}, f32[16,128,128]{2,1,0:T(8,128)}, u32[]{:S(2)}) copy-start(f32[16,128,128]{2,1,0:T(8,128)} %get-tuple-element.29) | copy-start | bytes 3145732
  77.4 24.3 %copy-start = (f32[16,128,128]{2,1,0:T(8,128)S(1)}, f32[16,128,128]{2,1,0:T(8,128)}, u32[]{:S(2)}) copy-start(f32[16,128,128]{2,1,0:T(8,128)} %get-tuple-element.22) | copy-start | bytes 3145732
  77.4 11.8 %collective-permute-start.4 = (bf16[16,128,128]{2,1,0:T(8,128)(2,1)}, bf16[16,128,128]{2,1,0:T(8,128)(2,1)S(1)}, u32[]{:S(2)}, u32[]{:S(2)}) collective-permute-start(bf16[16,128,128]{2,1,0:T(8,128)(2,1)} %get-tuple-element.23), channel_id=1, source_target_pairs={{0,2},{1,3},{2,0},{3,1},{4,6},{5,7},{6,4},{7,5},{8,10},{9,11},{10,... | collective-permute-start | bytes 1572872 | tf_op jit(solution)/shard_map/ppermute | solution.py:231
  77.6 21.9 %collective-permute-start.9 = (bf16[16,128,128]{2,1,0:T(8,128)(2,1)S(1)}, bf16[16,128,128]{2,1,0:T(8,128)(2,1)S(1)}, u32[]{:S(2)}, u32[]{:S(2)}) collective-permute-start(bf16[16,128,128]{2,1,0:T(8,128)(2,1)S(1)} %add_convert_fusion.2), channel_id=1, source_target_pairs={{0,4},{4,0},{8,12},{12,8},{1,5},{5,1},{9,13},{13,9},{2,6},{6,2},{1... | collective-permute-start | bytes 1572872 | tf_op jit(solution)/shard_map/ppermute | solution.py:231
  77.8 23.9 %collective-permute-start.11 = (bf16[16,128,128]{2,1,0:T(8,128)(2,1)S(1)}, bf16[16,128,128]{2,1,0:T(8,128)(2,1)S(1)}, u32[]{:S(2)}, u32[]{:S(2)}) collective-permute-start(bf16[16,128,128]{2,1,0:T(8,128)(2,1)S(1)} %add_convert_fusion.1), channel_id=1, source_target_pairs={{0,8},{4,12},{8,0},{12,4},{1,9},{5,13},{9,1},{13,5},{2,10},{6,14},... | collective-permute-start | bytes 1572872 | tf_op jit(solution)/shard_map/ppermute | solution.py:231

commit v3 on v2

v3 whole, which is shorter than its diff:
```python
import functools
import math

import jax
import jax.numpy as jnp
from jax import lax
from jax.experimental import pallas as pl
from jax.experimental.pallas import tpu as pltpu
from jax.sharding import PartitionSpec as P

TILE = 128
CAP = 8
GROUP = 256
ROWS = 4


def block_pairs(pair_codes, blocks):
    row_grid = lax.broadcasted_iota(jnp.int32, (blocks, blocks), 0)
    col_grid = lax.broadcasted_iota(jnp.int32, (blocks, blocks), 1)
    code_grid = row_grid * blocks - row_grid * (row_grid - 1) // 2 + (col_grid - row_grid)
    upper_part = col_grid >= row_grid
    matches = (code_grid[None, :, :] == pair_codes[:, None, None]) & upper_part[None, :, :]
    first_blocks = jnp.sum(jnp.where(matches, row_grid[None], 0), axis=(1, 2))
    second_blocks = jnp.sum(jnp.where(matches, col_grid[None], 0), axis=(1, 2))
    return (first_blocks, second_blocks)


def slot_sources(owner_local, batches, capacity):
    local_count = owner_local.shape[0]
    batch_ids = lax.broadcasted_iota(jnp.int32, (local_count, batches), 1)
    onehot = (owner_local[:, None] == batch_ids).astype(jnp.int32)
    ranking = jnp.cumsum(onehot, axis=0) - 1
    slot_of = jnp.sum(ranking * onehot, axis=1)
    target = owner_local * capacity + slot_of
    slot_ids = lax.broadcasted_iota(jnp.int32, (local_count, batches * capacity), 1)
    orbital_ids = lax.broadcasted_iota(jnp.int32, (local_count, batches * capacity), 0)
    slot_hits = target[:, None] == slot_ids
    source_row = jnp.sum(jnp.where(slot_hits, orbital_ids, 0), axis=0)
    filled = jnp.any(slot_hits, axis=0)
    return jnp.where(filled, source_row, local_count)


def slab_plan(half_tensor, batch_owner, pair_list, live_pairs):
    batches = lax.axis_size("orb")
    aux_local, occ_local, domain = half_tensor.shape
    blocks = domain // TILE
    sources = slot_sources(batch_owner[:, 0], batches, CAP)
    block_major = half_tensor.reshape(aux_local, occ_local, blocks, TILE).transpose(2, 1, 0, 3)
    outgoing = jnp.take(block_major, sources, axis=1, mode="fill", fill_value=0)
    arrived = lax.all_to_all(outgoing, "orb", split_axis=1, concat_axis=2, tiled=True)
    stacked_rows = arrived.reshape(blocks, -1, TILE)
    first_blocks, second_blocks = block_pairs(pair_list[0], blocks)
    live_count = live_pairs[0]
    pair_total = pair_list.shape[1]
    contract = (((0,), (0,)), ((), ()))
    group_size = math.gcd(4, pair_total)

    def one_group(group_index):
        pair_start = group_index * group_size
        tiles = []
        for offset in range(group_size):
            left = lax.dynamic_index_in_dim(
                stacked_rows, first_blocks[pair_start + offset], 0, keepdims=False
            )
            right = lax.dynamic_index_in_dim(
                stacked_rows, second_blocks[pair_start + offset], 0, keepdims=False
            )
            tiles.append(
                lax.dot_general(left, right, contract, preferred_element_type=jnp.float32)
            )
        keep_mask = pair_start + lax.iota(jnp.int32, group_size) < live_count
        return jnp.where(keep_mask[:, None, None], jnp.stack(tiles, axis=0), jnp.float32(0.0))

    grouped = lax.map(one_group, jnp.arange(pair_total // group_size, dtype=jnp.int32))
    terms = grouped.reshape(pair_total, TILE, TILE)
    mine = lax.psum_scatter(terms.astype(jnp.bfloat16), "row", scatter_dimension=0, tiled=True)
    return mine[None]


def chunk_kernel(bits, sources, started, occ_local, info, table, *refs):
    slabs, refs = refs[:sources], refs[sources:]
    before, refs = (refs[:2], refs[2:]) if started else (None, refs)
    send_ref, keep_ref, stage, packed_rows, turned, pick, arrived = refs[:7]
    started_tiles, started_arrived = refs[7:] if started else (None, None)
    share = send_ref.shape[0]
    rows_total, domain = slabs[0].shape
    groups = rows_total // GROUP
    per_group = GROUP // occ_local
    held = per_group * CAP
    pair_total = share * ROWS
    batch = info[0] ^ bits
    send_first = (info[1] ^ 2) * share
    keep_first = info[1] * share
    owner_at = 2
    codes_at = owner_at + 2 * occ_local + bits * (pair_total + 1)
    live = info[codes_at + pair_total]

    def slab_copy(source, group):
        rows = pl.ds(pl.multiple_of(group * GROUP, GROUP), GROUP)
        place = source * groups + group
        staged = pl.ds(pl.multiple_of(place * GROUP, GROUP), GROUP)
        return pltpu.make_async_copy(
            slabs[source].at[rows, :], stage.at[staged, :], arrived.at[place]
        )

    for source in range(sources):
        for group in range(groups):
            slab_copy(source, group).start()
    if started:
        start_copies = [
            pltpu.make_async_copy(before[i], started_tiles.at[i], started_arrived.at[i])
            for i in range(2)
        ]
        for copy in start_copies:
            copy.start()

    first = jnp.int32(0)
    for source in range(sources):
        owners = owner_at + (source + (0 if sources == 2 else int(started))) * occ_local
        mine = [info[owners + orbital] == batch for orbital in range(occ_local)]
        number = sum(each.astype(jnp.int32) for each in mine)

        lane = lax.broadcasted_iota(jnp.int32, (1, GROUP), 1)
        orbital_of = lane & (occ_local - 1)
        base = (lane >> (occ_local.bit_length() - 1)) * number
        target = jnp.full((1, GROUP), -1, jnp.int32)
        rank = jnp.int32(0)
        for orbital in range(occ_local):
            shift = jnp.where(mine[orbital], rank, -GROUP * CAP)
            target = jnp.where(orbital_of == orbital, base + shift, target)
            rank = rank + mine[orbital].astype(jnp.int32)
        slot = lax.broadcasted_iota(jnp.int32, (held, GROUP), 0)
        pick[...] = (slot == target).astype(jnp.bfloat16)

        def pack(group, carry, source=source, number=number, first=first):
            slab_copy(source, group).wait()
            staged = pl.multiple_of((source * groups + group) * GROUP, GROUP)
            start = pl.multiple_of((first + group * number) * per_group, per_group)
            for column in range(0, domain, 2 * TILE):
                columns = slice(column, column + 2 * TILE)
                packed = jnp.dot(
                    pick[...], stage[pl.ds(staged, GROUP), columns],
                    preferred_element_type=jnp.float32,
                )
                packed_rows[pl.ds(start, held), columns] = packed.astype(jnp.bfloat16)
            return carry

        lax.fori_loop(0, groups, pack, 0)
        first = first + groups * number

    filled = pl.multiple_of(first * per_group, per_group)
    packed_rows[pl.ds(filled, GROUP), :] = jnp.zeros((GROUP, domain), jnp.bfloat16)
    parts = (filled + GROUP - 1) // GROUP

    def turn(part, carry):
        at = pl.multiple_of(part * GROUP, GROUP)
        for column in range(0, domain, TILE):
            columns = slice(column, column + TILE)
            turned[columns, pl.ds(at, GROUP)] = packed_rows[pl.ds(at, GROUP), columns].T
        return carry

    lax.fori_loop(0, parts, turn, 0)
    if started:
        for copy in start_copies:
            copy.wait()

    def tiles(depth):
        def tile(pair, out, at, side):
            value = jnp.zeros((TILE, TILE), jnp.float32)
            if depth:
                code = info[codes_at + pair]
                left = pl.multiple_of(table[2 * code], TILE)
                right = pl.multiple_of(table[2 * code + 1], TILE)
                product = jnp.dot(
                    turned[pl.ds(left, TILE), :depth],
                    packed_rows[:depth, pl.ds(right, TILE)],
                    preferred_element_type=jnp.float32,
                )
                value = jnp.where(pair < live, product, value)
            if started:
                value = value + started_tiles[side, at]
            out[at] = value.astype(out.dtype)

        width = math.gcd(4, share)

        def several(turn_at, carry):
            for offset in range(width):
                at = turn_at * width + offset
                tile(send_first + at, send_ref, at, 0)
                tile(keep_first + at, keep_ref, at, 1)
            return carry

        lax.fori_loop(0, share // width, several, 0)

    for part_count in range(turned.shape[1] // GROUP + 1):
        pl.when(parts == part_count)(functools.partial(tiles, part_count * GROUP))


def tile_chunk(bits, info, table, slabs, occ_local, share, send_type, before=()):
    sources = len(slabs)
    rows_total, domain = slabs[0].shape
    groups = rows_total // GROUP
    held = GROUP // occ_local * CAP
    depth = -(-sources * groups * held // GROUP) * GROUP
    tiles = (share, TILE, TILE)
    anywhere = pl.BlockSpec(memory_space=pl.ANY)
    in_vmem = pl.BlockSpec(memory_space=pltpu.VMEM)
    in_smem = pl.BlockSpec(memory_space=pltpu.SMEM)
    scratch = [
        pltpu.VMEM((sources * rows_total, domain), jnp.bfloat16),
        pltpu.VMEM((depth + GROUP, domain), jnp.bfloat16),
        pltpu.VMEM((domain, depth), jnp.bfloat16),
        pltpu.VMEM((held, GROUP), jnp.bfloat16),
        pltpu.SemaphoreType.DMA((sources * groups,)),
    ]
    if before:
        scratch += [pltpu.VMEM((2, *tiles), jnp.float32), pltpu.SemaphoreType.DMA((2,))]
    return pl.pallas_call(
        functools.partial(chunk_kernel, bits, sources, bool(before), occ_local),
        in_specs=[in_smem, in_smem] + [anywhere] * (sources + len(before)),
        out_specs=[in_vmem, in_vmem],
        scratch_shapes=scratch,
        out_shape=[
            jax.ShapeDtypeStruct(tiles, send_type),
            jax.ShapeDtypeStruct(tiles, jnp.float32),
        ],
        compiler_params=pltpu.CompilerParams(vmem_limit_bytes=56 * 1024 * 1024),
        cost_estimate=pl.CostEstimate(
            flops=4 * share * TILE * TILE * depth + 2 * depth * GROUP * domain,
            bytes_accessed=2 * sources * rows_total * domain + 6 * share * TILE * TILE,
            transcendentals=0,
        ),
        name="tile_chunk",
    )(info, table, *slabs, *before)


def pair_table(blocks):
    return jnp.asarray(
        [TILE * block for left in range(blocks) for right in range(left, blocks)
         for block in (left, right)],
        jnp.int32,
    )


def tile_plan(half_tensor, batch_owner, pair_list, live_pairs):
    batches = lax.axis_size("orb")
    rows = lax.axis_size("row")
    aux_local, occ_local, domain = half_tensor.shape
    share = pair_list.shape[1] // rows
    row_at = lax.axis_index("row")
    orb_at = lax.axis_index("orb")

    def exchange(array, axis, bits):
        size = lax.axis_size(axis)
        return lax.ppermute(array, axis, [(i, i ^ bits) for i in range(size)])

    own_rows = half_tensor.reshape(aux_local * occ_local, domain)
    other_rows = exchange(own_rows, "row", 1)
    own_owner = batch_owner[:, 0]
    own_pairs = jnp.concatenate([pair_list[0], live_pairs])
    info = jnp.concatenate(
        [jnp.stack([orb_at, row_at]), own_owner, exchange(own_owner, "row", 1), own_pairs]
        + [exchange(own_pairs, "orb", bits) for bits in range(1, batches)]
    )
    table = pair_table(domain // TILE)

    def chunk(bits, slabs, send_type=jnp.bfloat16, before=()):
        return tile_chunk(bits, info, table, slabs, occ_local, share, send_type, before)

    def over_x(send, keep):
        return keep + exchange(send, "row", 2).astype(jnp.float32)

    def after(array, earlier):
        return lax.optimization_barrier((array, earlier))

    started = chunk(3, (own_rows,), jnp.float32)
    send_3, keep_3 = chunk(3, (other_rows,), before=started)
    send_2, keep_2 = chunk(2, (own_rows, other_rows))
    send_1, keep_1 = chunk(1, (own_rows, other_rows))
    far = over_x(send_3, keep_3).astype(jnp.bfloat16)
    other_rows, far = after(other_rows, far)
    far = exchange(far, "orb", 1)
    send_0, keep_0 = chunk(0, (own_rows, other_rows))
    term_2 = over_x(send_2, keep_2)
    across = exchange((term_2 + far.astype(jnp.float32)).astype(jnp.bfloat16), "orb", 2)
    near = exchange(over_x(send_1, keep_1).astype(jnp.bfloat16), "orb", 1)
    total = over_x(send_0, keep_0) + near.astype(jnp.float32) + across.astype(jnp.float32)
    return total.astype(jnp.bfloat16)[None]


def per_device(half_tensor, batch_owner, pair_list, live_pairs):
    batches = lax.axis_size("orb")
    rows = lax.axis_size("row")
    aux_local, occ_local, domain = half_tensor.shape
    pair_total = pair_list.shape[1]
    tile_elements = batches * pair_total * TILE * TILE
    slab_elements = batches * CAP * aux_local * domain
    fits = (
        rows == ROWS
        and batches == 4
        and pair_total % rows == 0
        and occ_local & (occ_local - 1) == 0
        and GROUP % occ_local == 0
        and aux_local * occ_local % GROUP == 0
        and tile_elements <= slab_elements
    )
    plan = tile_plan if fits else slab_plan
    return plan(half_tensor, batch_owner, pair_list, live_pairs)


def solution(mesh):
    return jax.shard_map(
        per_device,
        mesh=mesh,
        in_specs=(
            P(("grp", "orb"), "row", None),
            P(("grp", "row"), None),
            P(("grp", "orb"), None),
            P(("grp", "orb")),
        ),
        out_specs=P(("grp", "orb"), "row", None, None),
        check_vma=False,
    )
```

time: 104 us -> 91 us (0.88)
  Pallas kernels: 53.1 us -> 40.2 us
  waiting for transfers between devices: 22.2 us -> 30.3 us
  starting transfers between devices: 19.8 us -> 13.6 us
  other arithmetic: 4.8 us -> 3.48 us
    pallas_call x5, Pallas kernels: 53.1 us -> 40.2 us  [tile_chunk(): pl.pallas_call(functools.partial(chunk_kernel, bits, sources, bool(before...]
    ppermute x12, waiting for transfers between devices: 22.2 us -> 30.3 us  [exchange(): return lax.ppermute(array, axis, [(i, i ^ bits) for i in range(size)])]
    ppermute x12, starting transfers between devices: 19.8 us -> 13.6 us  [exchange(): return lax.ppermute(array, axis, [(i, i ^ bits) for i in range(size)])]
    another operation x4 -> x0, other arithmetic: 2.47 us -> none  [place_of(): jnp.stack([orb_at ^ bits, (row_at ^ 2) * share, row_at * share])]
    unnamed x18 -> x6, local copies, waits for them, and re-layouts: 2.14 us -> 0.01 us
    concatenate x0 -> x1, local copies, waits for them, and re-layouts: none -> 1.34 us  [tile_plan(): jnp.concatenate([jnp.stack([orb_at, row_at]), own_owner, exchange(own_own...]
    broadcast_in_dim x1, other arithmetic: 1.1 us -> 2.3 us  [tile_plan(): return total.astype(jnp.bfloat16)[None]]
  transfers between devices with their start and end apart: 12 -> 12, of which waited for: 5 -> 6; matrix products, arithmetic and copies ran while one was open for 4% -> 3% of each run, Pallas kernels for 44% -> 37%
where the time goes in v3:
time: 91 us; the launch traced here: 89.7 us
  Pallas kernels  40.2 us (44%)
  waiting for transfers between devices  30.3 us (33%)
  starting transfers between devices  13.6 us (15%)
  other arithmetic  3.48 us (4%)
  local copies, waits for them, and re-layouts  1.35 us (1%)
    pallas_call x5, Pallas kernels, tile_chunk(): pl.pallas_call(functools.partial(chunk_kernel, bits, sources, bool(before...  40.2 us
    ppermute x12, waiting for transfers between devices, exchange(): return lax.ppermute(array, axis, [(i, i ^ bits) for i in range(size)])  30.3 us
    ppermute x12, starting transfers between devices, exchange(): return lax.ppermute(array, axis, [(i, i ^ bits) for i in range(size)])  13.6 us
    broadcast_in_dim x1, other arithmetic, tile_plan(): return total.astype(jnp.bfloat16)[None]  2.3 us
  transfers between devices with their start and end apart: 12, of which 6 were waited for; matrix products, arithmetic and copies ran while one was open for 3% of the time, Pallas kernels for 37%

profile of v3, /device:TPU:0, one launch (start us, length us, event | category | flops | bytes accessed | tf_op | source)
XLA Modules:
  0.0 89.7 jit_solution(3569059022182299048)
XLA Ops:
  0.0 0.5 collective-permute-start.4
  1.1 0.7 pad_add_fusion
  1.8 2.6 %collective-permute-start.1 = (s32[65]{0:T(128)S(1)}, s32[65]{0:T(128)S(1)}, u32[]{:S(2)}, u32[]{:S(2)}) collective-permute-start(s32[65]{0:T(128)S(1)} %pad_add_fusion), channel_id=1, source_target_pairs={{0,4},{4,0},{8,12},{12,8},{1,5},{5,1},{9,13},{13,9},{2,6},{6,2},{1... | collective-permute-start | bytes 788 | tf_op jit(solution)/shard_map/ppermute | solution.py:255
  4.4 2.6 %collective-permute-start.2 = (s32[65]{0:T(128)S(1)}, s32[65]{0:T(128)S(1)}, u32[]{:S(2)}, u32[]{:S(2)}) collective-permute-start(s32[65]{0:T(128)S(1)} %pad_add_fusion), channel_id=1, source_target_pairs={{0,8},{4,12},{8,0},{12,4},{1,9},{5,13},{9,1},{13,5},{2,10},{6,14},... | collective-permute-start | bytes 788 | tf_op jit(solution)/shard_map/ppermute | solution.py:255
  7.0 1.3 %collective-permute-done = s32[16]{0:T(128)S(1)} collective-permute-done((s32[16]{0:T(128)}, s32[16]{0:T(128)S(1)}, u32[]{:S(2)}, u32[]{:S(2)}) %collective-permute-start) | collective-permute-done | bytes 96 | tf_op jit(solution)/shard_map/ppermute | solution.py:255
  8.3 0.6 collective-permute-done.2
  8.9 3.5 %collective-permute-done.3 = s32[65]{0:T(128)S(1)} collective-permute-done((s32[65]{0:T(128)S(1)}, s32[65]{0:T(128)S(1)}, u32[]{:S(2)}, u32[]{:S(2)}) %collective-permute-start.3) | collective-permute-done | bytes 292 | tf_op jit(solution)/shard_map/ppermute | solution.py:255
  12.3 1.3 %concatenate.8.info = s32[294]{0:T(512)} concatenate(s32[1]{0:T(128)} %bitcast, s32[1]{0:T(128)} %bitcast.1, s32[16]{0:T(128)} %bitcast.13, s32[16]{0:T(128)S(1)} %collective-permute-done, s32[64]{0:T(128)} %bitcast.15, s32[1]{0:T(128)S(6)} %copy.6, s32[65]{0:T(128)S(1)} %collective-permute-done.1, s32[65]{0:T(128)S(1)} %collective-permute-done.2, s32[65]{0:T(128)S(1)} %collective-permute-done.3), dimensions={0} | concatenate | bytes 2352 | tf_op jit(solution)/shard_map/concatenate | solution.py:261
  13.7 6.4 %tile_chunk.5 = (f32[16,128,128]{2,1,0:T(8,128)}, f32[16,128,128]{2,1,0:T(8,128)}) custom-call(s32[294]{0:T(512)} %concatenate.8.info, s32[272]{0:T(512)} %constant.9.clone.table, bf16[1024,2048]{1,0:T(8,128)(2,1)} %bitcast.8), custom_call_target="tpu_custom_call" | custom-call | flops 1073741824 | bytes 5767168 | tf_op jit(solution)/shard_map/tile_chunk/pallas_call | solution.py:218
  20.1 6.6 %tile_chunk.6 = (bf16[16,128,128]{2,1,0:T(8,128)(2,1)}, f32[16,128,128]{2,1,0:T(8,128)}) custom-call(s32[294]{0:T(512)} %concatenate.8.info, s32[272]{0:T(512)} %constant.9.clone.table, bf16[1024,2048]{1,0:T(8,128)(2,1)} %collective-permute-done.4.refs_0_.refs_1_, f32[16,128,128]{2,1,0:T(8,128)} %get-tuple-element.17.refs_1_, ...), custom_call_target="tpu_custom_call" | custom-call | flops 1073741824 | bytes 5767168 | tf_op jit(solution)/shard_map/tile_chunk/pallas_call | solution.py:218
  26.7 1.6 %collective-permute-start.5 = (bf16[16,128,128]{2,1,0:T(8,128)(2,1)}, bf16[16,128,128]{2,1,0:T(8,128)(2,1)S(1)}, u32[]{:S(2)}, u32[]{:S(2)}) collective-permute-start(bf16[16,128,128]{2,1,0:T(8,128)(2,1)} %get-tuple-element.20), channel_id=1, source_target_pairs={{0,2},{1,3},{2,0},{3,1},{4,6},{5,7},{6,4},{7,5},{8,10},{9,11},{10,... | collective-permute-start | bytes 1572872 | tf_op jit(solution)/shard_map/ppermute | solution.py:255
  28.3 8.6 %tile_chunk.8 = (bf16[16,128,128]{2,1,0:T(8,128)(2,1)}, f32[16,128,128]{2,1,0:T(8,128)}) custom-call(s32[294]{0:T(512)} %concatenate.8.info, s32[272]{0:T(512)} %constant.9.clone.table, bf16[1024,2048]{1,0:T(8,128)(2,1)} %bitcast.9, bf16[1024,2048]{1,0:T(8,128)(2,1)} %collective-permute-done.4.refs_0_.refs_1_), custom_call_target="tpu_custom_call" | custom-call | flops 2147483648 | bytes 9961472 | tf_op jit(solution)/shard_map/tile_chunk/pallas_call | solution.py:218
  36.9 0.6 collective-permute-start.7
  37.5 7.8 %tile_chunk.9 = (bf16[16,128,128]{2,1,0:T(8,128)(2,1)}, f32[16,128,128]{2,1,0:T(8,128)}) custom-call(s32[294]{0:T(512)} %concatenate.8.info, s32[272]{0:T(512)} %constant.9.clone.table, bf16[1024,2048]{1,0:T(8,128)(2,1)} %bitcast.10, bf16[1024,2048]{1,0:T(8,128)(2,1)} %collective-permute-done.4.refs_0_.refs_1_), custom_call_target="tpu_custom_call" | custom-call | flops 2147483648 | bytes 9961472 | tf_op jit(solution)/shard_map/tile_chunk/pallas_call | solution.py:218
  45.3 1.4 %collective-permute-start.9 = (bf16[16,128,128]{2,1,0:T(8,128)(2,1)}, bf16[16,128,128]{2,1,0:T(8,128)(2,1)S(1)}, u32[]{:S(2)}, u32[]{:S(2)}) collective-permute-start(bf16[16,128,128]{2,1,0:T(8,128)(2,1)} %get-tuple-element.27), channel_id=1, source_target_pairs={{0,2},{1,3},{2,0},{3,1},{4,6},{5,7},{6,4},{7,5},{8,10},{9,11},{10,... | collective-permute-start | bytes 1572872 | tf_op jit(solution)/shard_map/ppermute | solution.py:255
  46.9 1.7 %collective-permute-start.10 = (bf16[16,128,128]{2,1,0:T(8,128)(2,1)S(1)}, bf16[16,128,128]{2,1,0:T(8,128)(2,1)S(1)}, u32[]{:S(2)}, u32[]{:S(2)}) collective-permute-start(bf16[16,128,128]{2,1,0:T(8,128)(2,1)S(1)} %add_convert_fusion.3), channel_id=1, source_target_pairs={{0,4},{4,0},{8,12},{12,8},{1,5},{5,1},{9,13},{13,9},{2,6},{6,2},{1... | collective-permute-start | bytes 1572872 | tf_op jit(solution)/shard_map/ppermute | solution.py:255
  48.6 3.6 %collective-permute-done.7 = bf16[16,128,128]{2,1,0:T(8,128)(2,1)S(1)} collective-permute-done((bf16[16,128,128]{2,1,0:T(8,128)(2,1)}, bf16[16,128,128]{2,1,0:T(8,128)(2,1)S(1)}, u32[]{:S(2)}, u32[]{:S(2)}) %collective-permute-start.7) | collective-permute-done | bytes 524320 | tf_op jit(solution)/shard_map/ppermute | solution.py:255
  52.3 0.5 collective-permute-start.8
  52.9 10.8 %tile_chunk.7 = (bf16[16,128,128]{2,1,0:T(8,128)(2,1)}, f32[16,128,128]{2,1,0:T(8,128)}) custom-call(s32[294]{0:T(512)} %concatenate.8.info, s32[272]{0:T(512)} %constant.9.clone.table, bf16[1024,2048]{1,0:T(8,128)(2,1)} %bitcast.11, bf16[1024,2048]{1,0:T(8,128)(2,1)} %collective-permute-done.4.refs_0_.refs_1_), custom_call_target="tpu_custom_call" | custom-call | flops 2147483648 | bytes 9961472 | tf_op jit(solution)/shard_map/tile_chunk/pallas_call | solution.py:218
  63.7 2.1 %collective-permute-start.6 = (bf16[16,128,128]{2,1,0:T(8,128)(2,1)}, bf16[16,128,128]{2,1,0:T(8,128)(2,1)S(1)}, u32[]{:S(2)}, u32[]{:S(2)}) collective-permute-start(bf16[16,128,128]{2,1,0:T(8,128)(2,1)} %get-tuple-element.23), channel_id=1, source_target_pairs={{0,2},{1,3},{2,0},{3,1},{4,6},{5,7},{6,4},{7,5},{8,10},{9,11},{10,... | collective-permute-start | bytes 1572872 | tf_op jit(solution)/shard_map/ppermute | solution.py:255
  65.8 0.2 add_convert_fusion.1
  66.1 12.3 %collective-permute-done.8 = bf16[16,128,128]{2,1,0:T(8,128)(2,1)S(1)} collective-permute-done((bf16[16,128,128]{2,1,0:T(8,128)(2,1)S(1)}, bf16[16,128,128]{2,1,0:T(8,128)(2,1)S(1)}, u32[]{:S(2)}, u32[]{:S(2)}) %collective-permute-start.8) | collective-permute-done | bytes 524320 | tf_op jit(solution)/shard_map/ppermute | solution.py:255
  78.4 9.0 %collective-permute-done.11 = bf16[16,128,128]{2,1,0:T(8,128)(2,1)S(1)} collective-permute-done((bf16[16,128,128]{2,1,0:T(8,128)(2,1)S(1)}, bf16[16,128,128]{2,1,0:T(8,128)(2,1)S(1)}, u32[]{:S(2)}, u32[]{:S(2)}) %collective-permute-start.11) | collective-permute-done | bytes 524320 | tf_op jit(solution)/shard_map/ppermute | solution.py:255
  87.4 2.3 %fusion = bf16[1,16,128,128]{3,2,1,0:T(8,128)(2,1)} fusion(bf16[16,128,128]{2,1,0:T(8,128)(2,1)S(1)} %collective-permute-done.11, bf16[16,128,128]{2,1,0:T(8,128)(2,1)S(1)} %collective-permute-done.8, f32[16,128,128]{2,1,0:T(8,128)} %get-tuple-element.22, bf16[16,128,128]{2,1,0:T(8,128)(2,1)S(1)} %collective-permute-done.6), kind=kLoop, calls=%fused_computation.4 | loop fusion | flops 1835008 | bytes 3145728 | tf_op jit(solution)/shard_map/broadcast_in_dim | solution.py:288
  (17 shorter events, 0.4 us)
Async XLA Ops:
  0.0 20.1 %collective-permute-start.4 = (bf16[1024,2048]{1,0:T(8,128)(2,1)}, bf16[1024,2048]{1,0:T(8,128)(2,1)}, u32[]{:S(2)}, u32[]{:S(2)}) collective-permute-start(bf16[1024,2048]{1,0:T(8,128)(2,1)} %bitcast.7), channel_id=1, source_target_pairs={{0,1},{1,0},{2,3},{3,2},{4,5},{5,4},{6,7},{7,6},{8,9},{9,8},{10,11... | collective-permute-start | bytes 12582920 | tf_op jit(solution)/shard_map/ppermute | solution.py:255
  1.8 6.4 %collective-permute-start.1 = (s32[65]{0:T(128)S(1)}, s32[65]{0:T(128)S(1)}, u32[]{:S(2)}, u32[]{:S(2)}) collective-permute-start(s32[65]{0:T(128)S(1)} %pad_add_fusion), channel_id=1, source_target_pairs={{0,4},{4,0},{8,12},{12,8},{1,5},{5,1},{9,13},{13,9},{2,6},{6,2},{1... | collective-permute-start | bytes 788 | tf_op jit(solution)/shard_map/ppermute | solution.py:255
  4.4 4.4 %collective-permute-start.2 = (s32[65]{0:T(128)S(1)}, s32[65]{0:T(128)S(1)}, u32[]{:S(2)}, u32[]{:S(2)}) collective-permute-start(s32[65]{0:T(128)S(1)} %pad_add_fusion), channel_id=1, source_target_pairs={{0,8},{4,12},{8,0},{12,4},{1,9},{5,13},{9,1},{13,5},{2,10},{6,14},... | collective-permute-start | bytes 788 | tf_op jit(solution)/shard_map/ppermute | solution.py:255
  7.0 5.3 %collective-permute-start.3 = (s32[65]{0:T(128)S(1)}, s32[65]{0:T(128)S(1)}, u32[]{:S(2)}, u32[]{:S(2)}) collective-permute-start(s32[65]{0:T(128)S(1)} %pad_add_fusion), channel_id=1, source_target_pairs={{0,12},{4,8},{8,4},{12,0},{1,13},{5,9},{9,5},{13,1},{2,14},{6,10},... | collective-permute-start | bytes 788 | tf_op jit(solution)/shard_map/ppermute | solution.py:255
  7.0 1.3 %collective-permute-start = (s32[16]{0:T(128)}, s32[16]{0:T(128)S(1)}, u32[]{:S(2)}, u32[]{:S(2)}) collective-permute-start(s32[16]{0:T(128)} %bitcast.12), channel_id=1, source_target_pairs={{0,1},{1,0},{2,3},{3,2},{4,5},{5,4},{6,7},{7,6},{8,9},{9,8},{10,11... | collective-permute-start | bytes 200 | tf_op jit(solution)/shard_map/ppermute | solution.py:255
  26.7 20.0 %collective-permute-start.5 = (bf16[16,128,128]{2,1,0:T(8,128)(2,1)}, bf16[16,128,128]{2,1,0:T(8,128)(2,1)S(1)}, u32[]{:S(2)}, u32[]{:S(2)}) collective-permute-start(bf16[16,128,128]{2,1,0:T(8,128)(2,1)} %get-tuple-element.20), channel_id=1, source_target_pairs={{0,2},{1,3},{2,0},{3,1},{4,6},{5,7},{6,4},{7,5},{8,10},{9,11},{10,... | collective-permute-start | bytes 1572872 | tf_op jit(solution)/shard_map/ppermute | solution.py:255
  36.9 9.9 %copy-start.2 = (f32[16,128,128]{2,1,0:T(8,128)S(1)}, f32[16,128,128]{2,1,0:T(8,128)}, u32[]{:S(2)}) copy-start(f32[16,128,128]{2,1,0:T(8,128)} %get-tuple-element.19) | copy-start | bytes 3145732
  36.9 15.3 %copy-start.1 = (f32[16,128,128]{2,1,0:T(8,128)S(1)}, f32[16,128,128]{2,1,0:T(8,128)}, u32[]{:S(2)}) copy-start(f32[16,128,128]{2,1,0:T(8,128)} %get-tuple-element.24) | copy-start | bytes 3145732
  36.9 15.3 %collective-permute-start.7 = (bf16[16,128,128]{2,1,0:T(8,128)(2,1)}, bf16[16,128,128]{2,1,0:T(8,128)(2,1)S(1)}, u32[]{:S(2)}, u32[]{:S(2)}) collective-permute-start(bf16[16,128,128]{2,1,0:T(8,128)(2,1)} %get-tuple-element.25), channel_id=1, source_target_pairs={{0,2},{1,3},{2,0},{3,1},{4,6},{5,7},{6,4},{7,5},{8,10},{9,11},{10,... | collective-permute-start | bytes 1572872 | tf_op jit(solution)/shard_map/ppermute | solution.py:255
  45.3 20.5 %collective-permute-start.9 = (bf16[16,128,128]{2,1,0:T(8,128)(2,1)}, bf16[16,128,128]{2,1,0:T(8,128)(2,1)S(1)}, u32[]{:S(2)}, u32[]{:S(2)}) collective-permute-start(bf16[16,128,128]{2,1,0:T(8,128)(2,1)} %get-tuple-element.27), channel_id=1, source_target_pairs={{0,2},{1,3},{2,0},{3,1},{4,6},{5,7},{6,4},{7,5},{8,10},{9,11},{10,... | collective-permute-start | bytes 1572872 | tf_op jit(solution)/shard_map/ppermute | solution.py:255
  46.9 18.9 %collective-permute-start.10 = (bf16[16,128,128]{2,1,0:T(8,128)(2,1)S(1)}, bf16[16,128,128]{2,1,0:T(8,128)(2,1)S(1)}, u32[]{:S(2)}, u32[]{:S(2)}) collective-permute-start(bf16[16,128,128]{2,1,0:T(8,128)(2,1)S(1)} %add_convert_fusion.3), channel_id=1, source_target_pairs={{0,4},{4,0},{8,12},{12,8},{1,5},{5,1},{9,13},{13,9},{2,6},{6,2},{1... | collective-permute-start | bytes 1572872 | tf_op jit(solution)/shard_map/ppermute | solution.py:255
  52.3 13.4 %copy-start = (f32[16,128,128]{2,1,0:T(8,128)S(1)}, f32[16,128,128]{2,1,0:T(8,128)}, u32[]{:S(2)}) copy-start(f32[16,128,128]{2,1,0:T(8,128)} %get-tuple-element.26) | copy-start | bytes 3145732
  52.3 26.0 %collective-permute-start.8 = (bf16[16,128,128]{2,1,0:T(8,128)(2,1)S(1)}, bf16[16,128,128]{2,1,0:T(8,128)(2,1)S(1)}, u32[]{:S(2)}, u32[]{:S(2)}) collective-permute-start(bf16[16,128,128]{2,1,0:T(8,128)(2,1)S(1)} %add_convert_fusion.2), channel_id=1, source_target_pairs={{0,4},{4,0},{8,12},{12,8},{1,5},{5,1},{9,13},{13,9},{2,6},{6,2},{1... | collective-permute-start | bytes 1572872 | tf_op jit(solution)/shard_map/ppermute | solution.py:255
  63.7 14.7 %collective-permute-start.6 = (bf16[16,128,128]{2,1,0:T(8,128)(2,1)}, bf16[16,128,128]{2,1,0:T(8,128)(2,1)S(1)}, u32[]{:S(2)}, u32[]{:S(2)}) collective-permute-start(bf16[16,128,128]{2,1,0:T(8,128)(2,1)} %get-tuple-element.23), channel_id=1, source_target_pairs={{0,2},{1,3},{2,0},{3,1},{4,6},{5,7},{6,4},{7,5},{8,10},{9,11},{10,... | collective-permute-start | bytes 1572872 | tf_op jit(solution)/shard_map/ppermute | solution.py:255
  66.0 21.4 %collective-permute-start.11 = (bf16[16,128,128]{2,1,0:T(8,128)(2,1)S(1)}, bf16[16,128,128]{2,1,0:T(8,128)(2,1)S(1)}, u32[]{:S(2)}, u32[]{:S(2)}) collective-permute-start(bf16[16,128,128]{2,1,0:T(8,128)(2,1)S(1)} %add_convert_fusion.1), channel_id=1, source_target_pairs={{0,8},{4,12},{8,0},{12,4},{1,9},{5,13},{9,1},{13,5},{2,10},{6,14},... | collective-permute-start | bytes 1572872 | tf_op jit(solution)/shard_map/ppermute | solution.py:255

commit v4 on v3

--- a/solution.py
+++ b/solution.py
@@ -77,12 +77,10 @@
     return mine[None]
 
 
-def chunk_kernel(bits, sources, started, occ_local, info, table, *refs):
-    slabs, refs = refs[:sources], refs[sources:]
-    before, refs = (refs[:2], refs[2:]) if started else (None, refs)
-    send_ref, keep_ref, stage, packed_rows, turned, pick, arrived = refs[:7]
-    started_tiles, started_arrived = refs[7:] if started else (None, None)
-    share = send_ref.shape[0]
+def chunk_kernel(bits, occ_local, share, info, table, *refs):
+    slabs, (send_out, keep_out) = refs[:2], refs[2:4]
+    stage, packed_rows, turned, pick, send_ref, keep_ref, arrived, left_off = refs[4:]
+    sources = len(slabs)
     rows_total, domain = slabs[0].shape
     groups = rows_total // GROUP
     per_group = GROUP // occ_local
@@ -92,7 +90,7 @@
     send_first = (info[1] ^ 2) * share
     keep_first = info[1] * share
     owner_at = 2
-    codes_at = owner_at + 2 * occ_local + bits * (pair_total + 1)
+    codes_at = owner_at + sources * occ_local + bits * (pair_total + 1)
     live = info[codes_at + pair_total]
 
     def slab_copy(source, group):
@@ -106,17 +104,10 @@
     for source in range(sources):
         for group in range(groups):
             slab_copy(source, group).start()
-    if started:
-        start_copies = [
-            pltpu.make_async_copy(before[i], started_tiles.at[i], started_arrived.at[i])
-            for i in range(2)
-        ]
-        for copy in start_copies:
-            copy.start()
 
     first = jnp.int32(0)
     for source in range(sources):
-        owners = owner_at + (source + (0 if sources == 2 else int(started))) * occ_local
+        owners = owner_at + source * occ_local
         mine = [info[owners + orbital] == batch for orbital in range(occ_local)]
         number = sum(each.astype(jnp.int32) for each in mine)
 
@@ -136,13 +127,20 @@
             slab_copy(source, group).wait()
             staged = pl.multiple_of((source * groups + group) * GROUP, GROUP)
             start = pl.multiple_of((first + group * number) * per_group, per_group)
-            for column in range(0, domain, 2 * TILE):
-                columns = slice(column, column + 2 * TILE)
-                packed = jnp.dot(
-                    pick[...], stage[pl.ds(staged, GROUP), columns],
-                    preferred_element_type=jnp.float32,
-                )
-                packed_rows[pl.ds(start, held), columns] = packed.astype(jnp.bfloat16)
+            for batch_of in range(0, domain, 8 * TILE):
+                pieces = [
+                    slice(column, column + 2 * TILE)
+                    for column in range(batch_of, batch_of + 8 * TILE, 2 * TILE)
+                ]
+                packed = [
+                    jnp.dot(
+                        pick[...], stage[pl.ds(staged, GROUP), columns],
+                        preferred_element_type=jnp.float32,
+                    ).astype(jnp.bfloat16)
+                    for columns in pieces
+                ]
+                for columns, piece in zip(pieces, packed):
+                    packed_rows[pl.ds(start, held), columns] = piece
             return carry
 
         lax.fori_loop(0, groups, pack, 0)
@@ -154,40 +152,53 @@
 
     def turn(part, carry):
         at = pl.multiple_of(part * GROUP, GROUP)
-        for column in range(0, domain, TILE):
-            columns = slice(column, column + TILE)
-            turned[columns, pl.ds(at, GROUP)] = packed_rows[pl.ds(at, GROUP), columns].T
+        for batch_of in range(0, domain, 4 * TILE):
+            pieces = [
+                slice(column, column + TILE)
+                for column in range(batch_of, batch_of + 4 * TILE, TILE)
+            ]
+            blocks = [packed_rows[pl.ds(at, GROUP), columns].T for columns in pieces]
+            for columns, block in zip(pieces, blocks):
+                turned[columns, pl.ds(at, GROUP)] = block
         return carry
 
     lax.fori_loop(0, parts, turn, 0)
-    if started:
-        for copy in start_copies:
-            copy.wait()
+
+    width = math.gcd(2, share)
+
+    def out_copies(turn_at):
+        at = pl.ds(turn_at * width, width)
+        return [
+            pltpu.make_async_copy(held_tiles.at[at], out.at[at], left_off.at[side, turn_at])
+            for side, (held_tiles, out) in enumerate(
+                ((send_ref, send_out), (keep_ref, keep_out))
+            )
+        ]
 
     def tiles(depth):
-        def tile(pair, out, at, side):
-            value = jnp.zeros((TILE, TILE), jnp.float32)
-            if depth:
-                code = info[codes_at + pair]
-                left = pl.multiple_of(table[2 * code], TILE)
-                right = pl.multiple_of(table[2 * code + 1], TILE)
-                product = jnp.dot(
-                    turned[pl.ds(left, TILE), :depth],
-                    packed_rows[:depth, pl.ds(right, TILE)],
-                    preferred_element_type=jnp.float32,
-                )
-                value = jnp.where(pair < live, product, value)
-            if started:
-                value = value + started_tiles[side, at]
-            out[at] = value.astype(out.dtype)
-
-        width = math.gcd(4, share)
+        def tile(pair):
+            zero = jnp.zeros((TILE, TILE), jnp.float32)
+            if not depth:
+                return zero
+            code = info[codes_at + pair]
+            left = pl.multiple_of(table[2 * code], TILE)
+            right = pl.multiple_of(table[2 * code + 1], TILE)
+            product = jnp.dot(
+                turned[pl.ds(left, TILE), :depth],
+                packed_rows[:depth, pl.ds(right, TILE)],
+                preferred_element_type=jnp.float32,
+            )
+            return jnp.where(pair < live, product, zero)
 
         def several(turn_at, carry):
-            for offset in range(width):
-                at = turn_at * width + offset
-                tile(send_first + at, send_ref, at, 0)
-                tile(keep_first + at, keep_ref, at, 1)
+            ats = [turn_at * width + offset for offset in range(width)]
+            sends = [tile(send_first + at).astype(send_ref.dtype) for at in ats]
+            keeps = [tile(keep_first + at) for at in ats]
+            for at, send, keep in zip(ats, sends, keeps):
+                send_ref[at] = send
+                keep_ref[at] = keep
+            for copy in out_copies(turn_at):
+                copy.start()
             return carry
 
         lax.fori_loop(0, share // width, several, 0)
@@ -195,8 +206,15 @@
     for part_count in range(turned.shape[1] // GROUP + 1):
         pl.when(parts == part_count)(functools.partial(tiles, part_count * GROUP))
 
-
-def tile_chunk(bits, info, table, slabs, occ_local, share, send_type, before=()):
+    def drain(turn_at, carry):
+        for copy in out_copies(turn_at):
+            copy.wait()
+        return carry
+
+    lax.fori_loop(0, share // width, drain, 0)
+
+
+def tile_chunk(bits, info, table, slabs, occ_local, share):
     sources = len(slabs)
     rows_total, domain = slabs[0].shape
     groups = rows_total // GROUP
@@ -204,24 +222,23 @@
     depth = -(-sources * groups * held // GROUP) * GROUP
     tiles = (share, TILE, TILE)
     anywhere = pl.BlockSpec(memory_space=pl.ANY)
-    in_vmem = pl.BlockSpec(memory_space=pltpu.VMEM)
     in_smem = pl.BlockSpec(memory_space=pltpu.SMEM)
-    scratch = [
-        pltpu.VMEM((sources * rows_total, domain), jnp.bfloat16),
-        pltpu.VMEM((depth + GROUP, domain), jnp.bfloat16),
-        pltpu.VMEM((domain, depth), jnp.bfloat16),
-        pltpu.VMEM((held, GROUP), jnp.bfloat16),
-        pltpu.SemaphoreType.DMA((sources * groups,)),
-    ]
-    if before:
-        scratch += [pltpu.VMEM((2, *tiles), jnp.float32), pltpu.SemaphoreType.DMA((2,))]
     return pl.pallas_call(
-        functools.partial(chunk_kernel, bits, sources, bool(before), occ_local),
-        in_specs=[in_smem, in_smem] + [anywhere] * (sources + len(before)),
-        out_specs=[in_vmem, in_vmem],
-        scratch_shapes=scratch,
+        functools.partial(chunk_kernel, bits, occ_local, share),
+        in_specs=[in_smem, in_smem] + [anywhere] * sources,
+        out_specs=[anywhere, anywhere],
+        scratch_shapes=[
+            pltpu.VMEM((sources * rows_total, domain), jnp.bfloat16),
+            pltpu.VMEM((depth + GROUP, domain), jnp.bfloat16),
+            pltpu.VMEM((domain, depth), jnp.bfloat16),
+            pltpu.VMEM((held, GROUP), jnp.bfloat16),
+            pltpu.VMEM(tiles, jnp.bfloat16),
+            pltpu.VMEM(tiles, jnp.float32),
+            pltpu.SemaphoreType.DMA((sources * groups,)),
+            pltpu.SemaphoreType.DMA((2, share)),
+        ],
         out_shape=[
-            jax.ShapeDtypeStruct(tiles, send_type),
+            jax.ShapeDtypeStruct(tiles, jnp.bfloat16),
             jax.ShapeDtypeStruct(tiles, jnp.float32),
         ],
         compiler_params=pltpu.CompilerParams(vmem_limit_bytes=56 * 1024 * 1024),
@@ -231,7 +248,7 @@
             transcendentals=0,
         ),
         name="tile_chunk",
-    )(info, table, *slabs, *before)
+    )(info, table, *slabs)
 
 
 def pair_table(blocks):
@@ -264,8 +281,8 @@
     )
     table = pair_table(domain // TILE)
 
-    def chunk(bits, slabs, send_type=jnp.bfloat16, before=()):
-        return tile_chunk(bits, info, table, slabs, occ_local, share, send_type, before)
+    def chunk(bits):
+        return tile_chunk(bits, info, table, (own_rows, other_rows), occ_local, share)
 
     def over_x(send, keep):
         return keep + exchange(send, "row", 2).astype(jnp.float32)
@@ -273,14 +290,13 @@
     def after(array, earlier):
         return lax.optimization_barrier((array, earlier))
 
-    started = chunk(3, (own_rows,), jnp.float32)
-    send_3, keep_3 = chunk(3, (other_rows,), before=started)
-    send_2, keep_2 = chunk(2, (own_rows, other_rows))
-    send_1, keep_1 = chunk(1, (own_rows, other_rows))
+    send_3, keep_3 = chunk(3)
+    send_2, keep_2 = chunk(2)
+    send_1, keep_1 = chunk(1)
     far = over_x(send_3, keep_3).astype(jnp.bfloat16)
     other_rows, far = after(other_rows, far)
     far = exchange(far, "orb", 1)
-    send_0, keep_0 = chunk(0, (own_rows, other_rows))
+    send_0, keep_0 = chunk(0)
     term_2 = over_x(send_2, keep_2)
     across = exchange((term_2 + far.astype(jnp.float32)).astype(jnp.bfloat16), "orb", 2)
     near = exchange(over_x(send_1, keep_1).astype(jnp.bfloat16), "orb", 1)

time: 91 us -> 87.2 us (0.958)
  Pallas kernels: 40.2 us -> 37.5 us
  starting transfers between devices: 13.6 us -> 11.7 us
  waiting for transfers between devices: 30.3 us -> 31.7 us
    pallas_call x5 -> x4, Pallas kernels: 40.2 us -> 37.5 us  [tile_chunk(): pl.pallas_call(functools.partial(chunk_kernel, bits, occ_local, share), i...]
    ppermute x12, starting transfers between devices: 13.6 us -> 11.7 us  [exchange(): return lax.ppermute(array, axis, [(i, i ^ bits) for i in range(size)])]
    ppermute x12, waiting for transfers between devices: 30.3 us -> 31.7 us  [exchange(): return lax.ppermute(array, axis, [(i, i ^ bits) for i in range(size)])]
  transfers between devices with their start and end apart: 12 -> 12, of which waited for: 6 -> 6; matrix products, arithmetic and copies ran while one was open for 3% -> 3% of each run, Pallas kernels for 37% -> 33%
where the time goes in v4:
time: 87.2 us; the launch traced here: 86.6 us
  Pallas kernels  37.5 us (43%)
  waiting for transfers between devices  31.7 us (36%)
  starting transfers between devices  11.7 us (13%)
  other arithmetic  3.48 us (4%)
  local copies, waits for them, and re-layouts  1.35 us (2%)
    pallas_call x4, Pallas kernels, tile_chunk(): pl.pallas_call(functools.partial(chunk_kernel, bits, occ_local, share), i...  37.5 us
    ppermute x12, waiting for transfers between devices, exchange(): return lax.ppermute(array, axis, [(i, i ^ bits) for i in range(size)])  31.7 us
    ppermute x12, starting transfers between devices, exchange(): return lax.ppermute(array, axis, [(i, i ^ bits) for i in range(size)])  11.7 us
    broadcast_in_dim x1, other arithmetic, tile_plan(): return total.astype(jnp.bfloat16)[None]  2.3 us
  transfers between devices with their start and end apart: 12, of which 6 were waited for; matrix products, arithmetic and copies ran while one was open for 3% of the time, Pallas kernels for 33%

profile of v4, /device:TPU:0, one launch (start us, length us, event | category | flops | bytes accessed | tf_op | source)
XLA Modules:
  0.0 86.6 jit_solution(10592860654691494184)
XLA Ops:
  0.0 0.5 collective-permute-start.4
  1.1 0.7 pad_add_fusion
  1.8 2.6 %collective-permute-start.1 = (s32[65]{0:T(128)S(1)}, s32[65]{0:T(128)S(1)}, u32[]{:S(2)}, u32[]{:S(2)}) collective-permute-start(s32[65]{0:T(128)S(1)} %pad_add_fusion), channel_id=1, source_target_pairs={{0,4},{4,0},{8,12},{12,8},{1,5},{5,1},{9,13},{13,9},{2,6},{6,2},{1... | collective-permute-start | bytes 788 | tf_op jit(solution)/shard_map/ppermute | solution.py:272
  4.4 2.6 %collective-permute-start.2 = (s32[65]{0:T(128)S(1)}, s32[65]{0:T(128)S(1)}, u32[]{:S(2)}, u32[]{:S(2)}) collective-permute-start(s32[65]{0:T(128)S(1)} %pad_add_fusion), channel_id=1, source_target_pairs={{0,8},{4,12},{8,0},{12,4},{1,9},{5,13},{9,1},{13,5},{2,10},{6,14},... | collective-permute-start | bytes 788 | tf_op jit(solution)/shard_map/ppermute | solution.py:272
  7.0 1.3 %collective-permute-done = s32[16]{0:T(128)S(1)} collective-permute-done((s32[16]{0:T(128)}, s32[16]{0:T(128)S(1)}, u32[]{:S(2)}, u32[]{:S(2)}) %collective-permute-start) | collective-permute-done | bytes 96 | tf_op jit(solution)/shard_map/ppermute | solution.py:272
  8.3 0.6 collective-permute-done.2
  8.9 3.5 %collective-permute-done.3 = s32[65]{0:T(128)S(1)} collective-permute-done((s32[65]{0:T(128)S(1)}, s32[65]{0:T(128)S(1)}, u32[]{:S(2)}, u32[]{:S(2)}) %collective-permute-start.3) | collective-permute-done | bytes 292 | tf_op jit(solution)/shard_map/ppermute | solution.py:272
  12.3 1.3 %concatenate.8.info = s32[294]{0:T(512)} concatenate(s32[1]{0:T(128)} %bitcast, s32[1]{0:T(128)} %bitcast.1, s32[16]{0:T(128)} %bitcast.13, s32[16]{0:T(128)S(1)} %collective-permute-done, s32[64]{0:T(128)} %bitcast.15, s32[1]{0:T(128)S(6)} %copy.6, s32[65]{0:T(128)S(1)} %collective-permute-done.1, s32[65]{0:T(128)S(1)} %collective-permute-done.2, s32[65]{0:T(128)S(1)} %collective-permute-done.3), dimensions={0} | concatenate | bytes 2352 | tf_op jit(solution)/shard_map/concatenate | solution.py:278
  13.7 9.1 %tile_chunk.4 = (bf16[16,128,128]{2,1,0:T(8,128)(2,1)}, f32[16,128,128]{2,1,0:T(8,128)}) custom-call(s32[294]{0:T(512)} %concatenate.8.info, s32[272]{0:T(512)} %constant.9.clone.table, bf16[1024,2048]{1,0:T(8,128)(2,1)} %bitcast.8, bf16[1024,2048]{1,0:T(8,128)(2,1)} %collective-permute-done.4.refs_1_), custom_call_target="tpu_custom_call" | custom-call | flops 2147483648 | bytes 9961472 | tf_op jit(solution)/shard_map/tile_chunk/pallas_call | solution.py:226
  22.8 1.6 %collective-permute-start.5 = (bf16[16,128,128]{2,1,0:T(8,128)(2,1)}, bf16[16,128,128]{2,1,0:T(8,128)(2,1)S(1)}, u32[]{:S(2)}, u32[]{:S(2)}) collective-permute-start(bf16[16,128,128]{2,1,0:T(8,128)(2,1)} %get-tuple-element.16), channel_id=1, source_target_pairs={{0,2},{1,3},{2,0},{3,1},{4,6},{5,7},{6,4},{7,5},{8,10},{9,11},{10,... | collective-permute-start | bytes 1572872 | tf_op jit(solution)/shard_map/ppermute | solution.py:272
  24.3 9.1 %tile_chunk.6 = (bf16[16,128,128]{2,1,0:T(8,128)(2,1)}, f32[16,128,128]{2,1,0:T(8,128)}) custom-call(s32[294]{0:T(512)} %concatenate.8.info, s32[272]{0:T(512)} %constant.9.clone.table, bf16[1024,2048]{1,0:T(8,128)(2,1)} %bitcast.9, bf16[1024,2048]{1,0:T(8,128)(2,1)} %collective-permute-done.4.refs_1_), custom_call_target="tpu_custom_call" | custom-call | flops 2147483648 | bytes 9961472 | tf_op jit(solution)/shard_map/tile_chunk/pallas_call | solution.py:226
  33.4 0.6 collective-permute-start.7
  34.0 8.2 %tile_chunk.7 = (bf16[16,128,128]{2,1,0:T(8,128)(2,1)}, f32[16,128,128]{2,1,0:T(8,128)}) custom-call(s32[294]{0:T(512)} %concatenate.8.info, s32[272]{0:T(512)} %constant.9.clone.table, bf16[1024,2048]{1,0:T(8,128)(2,1)} %bitcast.10, bf16[1024,2048]{1,0:T(8,128)(2,1)} %collective-permute-done.4.refs_1_), custom_call_target="tpu_custom_call" | custom-call | flops 2147483648 | bytes 9961472 | tf_op jit(solution)/shard_map/tile_chunk/pallas_call | solution.py:226
  42.2 1.4 %collective-permute-start.9 = (bf16[16,128,128]{2,1,0:T(8,128)(2,1)}, bf16[16,128,128]{2,1,0:T(8,128)(2,1)S(1)}, u32[]{:S(2)}, u32[]{:S(2)}) collective-permute-start(bf16[16,128,128]{2,1,0:T(8,128)(2,1)} %get-tuple-element.23), channel_id=1, source_target_pairs={{0,2},{1,3},{2,0},{3,1},{4,6},{5,7},{6,4},{7,5},{8,10},{9,11},{10,... | collective-permute-start | bytes 1572872 | tf_op jit(solution)/shard_map/ppermute | solution.py:272
  43.6 0.1 add_convert_fusion.3
  43.8 0.7 collective-permute-start.10
  44.5 4.1 %collective-permute-done.7 = bf16[16,128,128]{2,1,0:T(8,128)(2,1)S(1)} collective-permute-done((bf16[16,128,128]{2,1,0:T(8,128)(2,1)}, bf16[16,128,128]{2,1,0:T(8,128)(2,1)S(1)}, u32[]{:S(2)}, u32[]{:S(2)}) %collective-permute-start.7) | collective-permute-done | bytes 524320 | tf_op jit(solution)/shard_map/ppermute | solution.py:272
  48.5 0.1 add_convert_fusion.2
  48.8 11.2 %tile_chunk.5 = (bf16[16,128,128]{2,1,0:T(8,128)(2,1)}, f32[16,128,128]{2,1,0:T(8,128)}) custom-call(s32[294]{0:T(512)} %concatenate.8.info, s32[272]{0:T(512)} %constant.9.clone.table, bf16[1024,2048]{1,0:T(8,128)(2,1)} %bitcast.11, bf16[1024,2048]{1,0:T(8,128)(2,1)} %collective-permute-done.4.refs_1_), custom_call_target="tpu_custom_call" | custom-call | flops 2147483648 | bytes 9961472 | tf_op jit(solution)/shard_map/tile_chunk/pallas_call | solution.py:226
  60.0 1.7 %collective-permute-start.6 = (bf16[16,128,128]{2,1,0:T(8,128)(2,1)}, bf16[16,128,128]{2,1,0:T(8,128)(2,1)S(1)}, u32[]{:S(2)}, u32[]{:S(2)}) collective-permute-start(bf16[16,128,128]{2,1,0:T(8,128)(2,1)} %get-tuple-element.19), channel_id=1, source_target_pairs={{0,2},{1,3},{2,0},{3,1},{4,6},{5,7},{6,4},{7,5},{8,10},{9,11},{10,... | collective-permute-start | bytes 1572872 | tf_op jit(solution)/shard_map/ppermute | solution.py:272
  61.7 0.2 add_convert_fusion.1
  62.0 12.8 %collective-permute-done.8 = bf16[16,128,128]{2,1,0:T(8,128)(2,1)S(1)} collective-permute-done((bf16[16,128,128]{2,1,0:T(8,128)(2,1)S(1)}, bf16[16,128,128]{2,1,0:T(8,128)(2,1)S(1)}, u32[]{:S(2)}, u32[]{:S(2)}) %collective-permute-start.8) | collective-permute-done | bytes 524320 | tf_op jit(solution)/shard_map/ppermute | solution.py:272
  74.8 9.5 %collective-permute-done.11 = bf16[16,128,128]{2,1,0:T(8,128)(2,1)S(1)} collective-permute-done((bf16[16,128,128]{2,1,0:T(8,128)(2,1)S(1)}, bf16[16,128,128]{2,1,0:T(8,128)(2,1)S(1)}, u32[]{:S(2)}, u32[]{:S(2)}) %collective-permute-start.11) | collective-permute-done | bytes 524320 | tf_op jit(solution)/shard_map/ppermute | solution.py:272
  84.3 2.3 %fusion = bf16[1,16,128,128]{3,2,1,0:T(8,128)(2,1)} fusion(bf16[16,128,128]{2,1,0:T(8,128)(2,1)S(1)} %collective-permute-done.11, bf16[16,128,128]{2,1,0:T(8,128)(2,1)S(1)} %collective-permute-done.8, f32[16,128,128]{2,1,0:T(8,128)} %get-tuple-element.18, bf16[16,128,128]{2,1,0:T(8,128)(2,1)S(1)} %collective-permute-done.6), kind=kLoop, calls=%fused_computation.4 | loop fusion | flops 1835008 | bytes 3145728 | tf_op jit(solution)/shard_map/broadcast_in_dim | solution.py:304
  (16 shorter events, 0.2 us)
Async XLA Ops:
  0.0 13.7 %collective-permute-start.4 = (bf16[1024,2048]{1,0:T(8,128)(2,1)}, bf16[1024,2048]{1,0:T(8,128)(2,1)}, u32[]{:S(2)}, u32[]{:S(2)}) collective-permute-start(bf16[1024,2048]{1,0:T(8,128)(2,1)} %bitcast.7), channel_id=1, source_target_pairs={{0,1},{1,0},{2,3},{3,2},{4,5},{5,4},{6,7},{7,6},{8,9},{9,8},{10,11... | collective-permute-start | bytes 12582920 | tf_op jit(solution)/shard_map/ppermute | solution.py:272
  1.8 6.4 %collective-permute-start.1 = (s32[65]{0:T(128)S(1)}, s32[65]{0:T(128)S(1)}, u32[]{:S(2)}, u32[]{:S(2)}) collective-permute-start(s32[65]{0:T(128)S(1)} %pad_add_fusion), channel_id=1, source_target_pairs={{0,4},{4,0},{8,12},{12,8},{1,5},{5,1},{9,13},{13,9},{2,6},{6,2},{1... | collective-permute-start | bytes 788 | tf_op jit(solution)/shard_map/ppermute | solution.py:272
  4.4 4.4 %collective-permute-start.2 = (s32[65]{0:T(128)S(1)}, s32[65]{0:T(128)S(1)}, u32[]{:S(2)}, u32[]{:S(2)}) collective-permute-start(s32[65]{0:T(128)S(1)} %pad_add_fusion), channel_id=1, source_target_pairs={{0,8},{4,12},{8,0},{12,4},{1,9},{5,13},{9,1},{13,5},{2,10},{6,14},... | collective-permute-start | bytes 788 | tf_op jit(solution)/shard_map/ppermute | solution.py:272
  7.0 5.3 %collective-permute-start.3 = (s32[65]{0:T(128)S(1)}, s32[65]{0:T(128)S(1)}, u32[]{:S(2)}, u32[]{:S(2)}) collective-permute-start(s32[65]{0:T(128)S(1)} %pad_add_fusion), channel_id=1, source_target_pairs={{0,12},{4,8},{8,4},{12,0},{1,13},{5,9},{9,5},{13,1},{2,14},{6,10},... | collective-permute-start | bytes 788 | tf_op jit(solution)/shard_map/ppermute | solution.py:272
  7.0 1.3 %collective-permute-start = (s32[16]{0:T(128)}, s32[16]{0:T(128)S(1)}, u32[]{:S(2)}, u32[]{:S(2)}) collective-permute-start(s32[16]{0:T(128)} %bitcast.12), channel_id=1, source_target_pairs={{0,1},{1,0},{2,3},{3,2},{4,5},{5,4},{6,7},{7,6},{8,9},{9,8},{10,11... | collective-permute-start | bytes 200 | tf_op jit(solution)/shard_map/ppermute | solution.py:272
  22.8 20.9 %collective-permute-start.5 = (bf16[16,128,128]{2,1,0:T(8,128)(2,1)}, bf16[16,128,128]{2,1,0:T(8,128)(2,1)S(1)}, u32[]{:S(2)}, u32[]{:S(2)}) collective-permute-start(bf16[16,128,128]{2,1,0:T(8,128)(2,1)} %get-tuple-element.16), channel_id=1, source_target_pairs={{0,2},{1,3},{2,0},{3,1},{4,6},{5,7},{6,4},{7,5},{8,10},{9,11},{10,... | collective-permute-start | bytes 1572872 | tf_op jit(solution)/shard_map/ppermute | solution.py:272
  33.4 10.3 %copy-start.2 = (f32[16,128,128]{2,1,0:T(8,128)S(1)}, f32[16,128,128]{2,1,0:T(8,128)}, u32[]{:S(2)}) copy-start(f32[16,128,128]{2,1,0:T(8,128)} %get-tuple-element.15) | copy-start | bytes 3145732
  33.4 15.1 %copy-start.1 = (f32[16,128,128]{2,1,0:T(8,128)S(1)}, f32[16,128,128]{2,1,0:T(8,128)}, u32[]{:S(2)}) copy-start(f32[16,128,128]{2,1,0:T(8,128)} %get-tuple-element.20) | copy-start | bytes 3145732
  33.4 15.1 %collective-permute-start.7 = (bf16[16,128,128]{2,1,0:T(8,128)(2,1)}, bf16[16,128,128]{2,1,0:T(8,128)(2,1)S(1)}, u32[]{:S(2)}, u32[]{:S(2)}) collective-permute-start(bf16[16,128,128]{2,1,0:T(8,128)(2,1)} %get-tuple-element.21), channel_id=1, source_target_pairs={{0,2},{1,3},{2,0},{3,1},{4,6},{5,7},{6,4},{7,5},{8,10},{9,11},{10,... | collective-permute-start | bytes 1572872 | tf_op jit(solution)/shard_map/ppermute | solution.py:272
  42.2 19.5 %collective-permute-start.9 = (bf16[16,128,128]{2,1,0:T(8,128)(2,1)}, bf16[16,128,128]{2,1,0:T(8,128)(2,1)S(1)}, u32[]{:S(2)}, u32[]{:S(2)}) collective-permute-start(bf16[16,128,128]{2,1,0:T(8,128)(2,1)} %get-tuple-element.23), channel_id=1, source_target_pairs={{0,2},{1,3},{2,0},{3,1},{4,6},{5,7},{6,4},{7,5},{8,10},{9,11},{10,... | collective-permute-start | bytes 1572872 | tf_op jit(solution)/shard_map/ppermute | solution.py:272
  43.8 17.9 %collective-permute-start.10 = (bf16[16,128,128]{2,1,0:T(8,128)(2,1)S(1)}, bf16[16,128,128]{2,1,0:T(8,128)(2,1)S(1)}, u32[]{:S(2)}, u32[]{:S(2)}) collective-permute-start(bf16[16,128,128]{2,1,0:T(8,128)(2,1)S(1)} %add_convert_fusion.3), channel_id=1, source_target_pairs={{0,4},{4,0},{8,12},{12,8},{1,5},{5,1},{9,13},{13,9},{2,6},{6,2},{1... | collective-permute-start | bytes 1572872 | tf_op jit(solution)/shard_map/ppermute | solution.py:272
  48.7 13.0 %copy-start = (f32[16,128,128]{2,1,0:T(8,128)S(1)}, f32[16,128,128]{2,1,0:T(8,128)}, u32[]{:S(2)}) copy-start(f32[16,128,128]{2,1,0:T(8,128)} %get-tuple-element.22) | copy-start | bytes 3145732
  48.7 26.1 %collective-permute-start.8 = (bf16[16,128,128]{2,1,0:T(8,128)(2,1)S(1)}, bf16[16,128,128]{2,1,0:T(8,128)(2,1)S(1)}, u32[]{:S(2)}, u32[]{:S(2)}) collective-permute-start(bf16[16,128,128]{2,1,0:T(8,128)(2,1)S(1)} %add_convert_fusion.2), channel_id=1, source_target_pairs={{0,4},{4,0},{8,12},{12,8},{1,5},{5,1},{9,13},{13,9},{2,6},{6,2},{1... | collective-permute-start | bytes 1572872 | tf_op jit(solution)/shard_map/ppermute | solution.py:272
  60.0 14.8 %collective-permute-start.6 = (bf16[16,128,128]{2,1,0:T(8,128)(2,1)}, bf16[16,128,128]{2,1,0:T(8,128)(2,1)S(1)}, u32[]{:S(2)}, u32[]{:S(2)}) collective-permute-start(bf16[16,128,128]{2,1,0:T(8,128)(2,1)} %get-tuple-element.19), channel_id=1, source_target_pairs={{0,2},{1,3},{2,0},{3,1},{4,6},{5,7},{6,4},{7,5},{8,10},{9,11},{10,... | collective-permute-start | bytes 1572872 | tf_op jit(solution)/shard_map/ppermute | solution.py:272
  61.9 22.4 %collective-permute-start.11 = (bf16[16,128,128]{2,1,0:T(8,128)(2,1)S(1)}, bf16[16,128,128]{2,1,0:T(8,128)(2,1)S(1)}, u32[]{:S(2)}, u32[]{:S(2)}) collective-permute-start(bf16[16,128,128]{2,1,0:T(8,128)(2,1)S(1)} %add_convert_fusion.1), channel_id=1, source_target_pairs={{0,8},{4,12},{8,0},{12,4},{1,9},{5,13},{9,1},{13,5},{2,10},{6,14},... | collective-permute-start | bytes 1572872 | tf_op jit(solution)/shard_map/ppermute | solution.py:272

commit v5 on v4

--- a/solution.py
+++ b/solution.py
@@ -77,78 +77,172 @@
     return mine[None]
 
 
-def chunk_kernel(bits, occ_local, share, info, table, *refs):
-    slabs, (send_out, keep_out) = refs[:2], refs[2:4]
-    stage, packed_rows, turned, pick, send_ref, keep_ref, arrived, left_off = refs[4:]
-    sources = len(slabs)
-    rows_total, domain = slabs[0].shape
+def lane_targets(positions, occ_local, stride, step):
+    lane = lax.broadcasted_iota(jnp.int32, (1, GROUP), 1)
+    orbital_of = lane & (occ_local - 1)
+    base = (lane >> (occ_local.bit_length() - 1)) * step
+    target = jnp.full((1, GROUP), -1, jnp.int32)
+    for orbital in range(occ_local):
+        target = jnp.where(orbital_of == orbital, base + positions[orbital] * stride, target)
+    return target
+
+
+def one_hot(target, height):
+    slot = lax.broadcasted_iota(jnp.int32, (height, GROUP), 0)
+    return (slot == target).astype(jnp.bfloat16)
+
+
+def sort_kernel(batches, occ_local, owner, slab, sorted_out, stage, ordered, pick, arrived, left):
+    rows_total, domain = slab.shape
     groups = rows_total // GROUP
     per_group = GROUP // occ_local
+    piece = 2 * TILE
+
+    def slab_copy(group):
+        rows = pl.ds(group * GROUP, GROUP)
+        return pltpu.make_async_copy(slab.at[rows, :], stage.at[rows, :], arrived.at[group])
+
+    def out_copy(column):
+        columns = pl.ds(column * piece, piece)
+        return pltpu.make_async_copy(
+            ordered.at[:, columns], sorted_out.at[:, columns], left.at[column]
+        )
+
+    for group in range(groups):
+        slab_copy(group).start()
+    owners = [owner[orbital] for orbital in range(occ_local)]
+    positions = [jnp.int32(0)] * occ_local
+    rank = jnp.int32(0)
+    for batch in range(batches):
+        for orbital in range(occ_local):
+            mine = owners[orbital] == batch
+            positions[orbital] = jnp.where(mine, rank, positions[orbital])
+            rank = rank + mine.astype(jnp.int32)
+    pick[...] = one_hot(lane_targets(positions, occ_local, per_group, 1), GROUP)
+    for group in range(groups):
+        slab_copy(group).wait()
+
+    for column in range(domain // piece):
+        columns = slice(column * piece, (column + 1) * piece)
+        for group in range(groups):
+            moved = jnp.dot(
+                pick[...], stage[group * GROUP:(group + 1) * GROUP, columns],
+                preferred_element_type=jnp.float32,
+            ).astype(jnp.bfloat16)
+            for unit in range(occ_local):
+                to = (unit * groups + group) * per_group
+                ordered[to:to + per_group, columns] = (
+                    moved[unit * per_group:(unit + 1) * per_group]
+                )
+        out_copy(column).start()
+    for column in range(domain // piece):
+        out_copy(column).wait()
+
+
+def sort_rows(owner, slab, batches):
+    occ_local, = owner.shape
+    rows_total, domain = slab.shape
+    anywhere = pl.BlockSpec(memory_space=pl.ANY)
+    return pl.pallas_call(
+        functools.partial(sort_kernel, batches, occ_local),
+        in_specs=[pl.BlockSpec(memory_space=pltpu.SMEM), anywhere],
+        out_specs=anywhere,
+        scratch_shapes=[
+            pltpu.VMEM((rows_total, domain), jnp.bfloat16),
+            pltpu.VMEM((rows_total, domain), jnp.bfloat16),
+            pltpu.VMEM((GROUP, GROUP), jnp.bfloat16),
+            pltpu.SemaphoreType.DMA((rows_total // GROUP,)),
+            pltpu.SemaphoreType.DMA((domain // (2 * TILE),)),
+        ],
+        out_shape=jax.ShapeDtypeStruct((rows_total, domain), jnp.bfloat16),
+        compiler_params=pltpu.CompilerParams(vmem_limit_bytes=56 * 1024 * 1024),
+        cost_estimate=pl.CostEstimate(
+            flops=2 * rows_total * GROUP * domain,
+            bytes_accessed=4 * rows_total * domain,
+            transcendentals=0,
+        ),
+        name="sort_rows",
+    )(owner, slab)
+
+
+def chunk_kernel(bits, occ_local, share, info, codes, table, own_sorted, other_rows, *refs):
+    send_out, keep_out = refs[:2]
+    stage, packed_rows, turned, pick, send_ref, keep_ref = refs[2:8]
+    own_arrived, other_arrived, left_off = refs[8:]
+    rows_total, domain = other_rows.shape
+    groups = rows_total // GROUP
+    per_group = GROUP // occ_local
+    per_orbital = rows_total // occ_local
     held = per_group * CAP
-    pair_total = share * ROWS
     batch = info[0] ^ bits
     send_first = (info[1] ^ 2) * share
     keep_first = info[1] * share
-    owner_at = 2
-    codes_at = owner_at + sources * occ_local + bits * (pair_total + 1)
-    live = info[codes_at + pair_total]
-
-    def slab_copy(source, group):
+    live = codes[share * ROWS]
+
+    def other_copy(group):
         rows = pl.ds(pl.multiple_of(group * GROUP, GROUP), GROUP)
-        place = source * groups + group
-        staged = pl.ds(pl.multiple_of(place * GROUP, GROUP), GROUP)
         return pltpu.make_async_copy(
-            slabs[source].at[rows, :], stage.at[staged, :], arrived.at[place]
+            other_rows.at[rows, :], stage.at[rows, :], other_arrived.at[group]
         )
 
-    for source in range(sources):
-        for group in range(groups):
-            slab_copy(source, group).start()
-
-    first = jnp.int32(0)
-    for source in range(sources):
-        owners = owner_at + source * occ_local
-        mine = [info[owners + orbital] == batch for orbital in range(occ_local)]
-        number = sum(each.astype(jnp.int32) for each in mine)
-
-        lane = lax.broadcasted_iota(jnp.int32, (1, GROUP), 1)
-        orbital_of = lane & (occ_local - 1)
-        base = (lane >> (occ_local.bit_length() - 1)) * number
-        target = jnp.full((1, GROUP), -1, jnp.int32)
-        rank = jnp.int32(0)
-        for orbital in range(occ_local):
-            shift = jnp.where(mine[orbital], rank, -GROUP * CAP)
-            target = jnp.where(orbital_of == orbital, base + shift, target)
-            rank = rank + mine[orbital].astype(jnp.int32)
-        slot = lax.broadcasted_iota(jnp.int32, (held, GROUP), 0)
-        pick[...] = (slot == target).astype(jnp.bfloat16)
-
-        def pack(group, carry, source=source, number=number, first=first):
-            slab_copy(source, group).wait()
-            staged = pl.multiple_of((source * groups + group) * GROUP, GROUP)
-            start = pl.multiple_of((first + group * number) * per_group, per_group)
-            for batch_of in range(0, domain, 8 * TILE):
-                pieces = [
-                    slice(column, column + 2 * TILE)
-                    for column in range(batch_of, batch_of + 8 * TILE, 2 * TILE)
-                ]
-                packed = [
-                    jnp.dot(
-                        pick[...], stage[pl.ds(staged, GROUP), columns],
-                        preferred_element_type=jnp.float32,
-                    ).astype(jnp.bfloat16)
-                    for columns in pieces
-                ]
-                for columns, piece in zip(pieces, packed):
-                    packed_rows[pl.ds(start, held), columns] = piece
-            return carry
-
-        lax.fori_loop(0, groups, pack, 0)
-        first = first + groups * number
-
-    filled = pl.multiple_of(first * per_group, per_group)
+    for group in range(groups):
+        other_copy(group).start()
+
+    owners = [info[2 + orbital] for orbital in range(occ_local)]
+    earlier = sum((owner < batch).astype(jnp.int32) for owner in owners)
+    own_count = sum((owner == batch).astype(jnp.int32) for owner in owners)
+
+    def own_copy(orbital):
+        rows = pl.ds(pl.multiple_of((earlier + orbital) * per_orbital, per_orbital), per_orbital)
+        to = pl.ds(pl.multiple_of(orbital * per_orbital, per_orbital), per_orbital)
+        return pltpu.make_async_copy(
+            own_sorted.at[rows, :], packed_rows.at[to, :], own_arrived.at[orbital]
+        )
+
+    def own_start(orbital, carry):
+        own_copy(orbital).start()
+        return carry
+
+    def own_wait(orbital, carry):
+        own_copy(orbital).wait()
+        return carry
+
+    lax.fori_loop(0, own_count, own_start, 0)
+
+    mine = [info[2 + occ_local + orbital] == batch for orbital in range(occ_local)]
+    positions = []
+    other_count = jnp.int32(0)
+    for each in mine:
+        positions.append(jnp.where(each, other_count, -GROUP * CAP))
+        other_count = other_count + each.astype(jnp.int32)
+    pick[...] = one_hot(lane_targets(positions, occ_local, 1, other_count), held)
+
+    def pack(group, carry):
+        other_copy(group).wait()
+        staged = pl.multiple_of(group * GROUP, GROUP)
+        start = own_count * per_orbital + group * other_count * per_group
+        start = pl.multiple_of(start, per_group)
+        for batch_of in range(0, domain, 8 * TILE):
+            pieces = [
+                slice(column, column + 2 * TILE)
+                for column in range(batch_of, batch_of + 8 * TILE, 2 * TILE)
+            ]
+            packed = [
+                jnp.dot(
+                    pick[...], stage[pl.ds(staged, GROUP), columns],
+                    preferred_element_type=jnp.float32,
+                ).astype(jnp.bfloat16)
+                for columns in pieces
+            ]
+            for columns, piece in zip(pieces, packed):
+                packed_rows[pl.ds(start, held), columns] = piece
+        return carry
+
+    lax.fori_loop(0, groups, pack, 0)
+    filled = pl.multiple_of((own_count + other_count) * per_orbital, per_orbital)
     packed_rows[pl.ds(filled, GROUP), :] = jnp.zeros((GROUP, domain), jnp.bfloat16)
     parts = (filled + GROUP - 1) // GROUP
+    lax.fori_loop(0, own_count, own_wait, 0)
 
     def turn(part, carry):
         at = pl.multiple_of(part * GROUP, GROUP)
@@ -180,7 +274,7 @@
             zero = jnp.zeros((TILE, TILE), jnp.float32)
             if not depth:
                 return zero
-            code = info[codes_at + pair]
+            code = codes[pair]
             left = pl.multiple_of(table[2 * code], TILE)
             right = pl.multiple_of(table[2 * code + 1], TILE)
             product = jnp.dot(
@@ -214,27 +308,27 @@
     lax.fori_loop(0, share // width, drain, 0)
 
 
-def tile_chunk(bits, info, table, slabs, occ_local, share):
-    sources = len(slabs)
-    rows_total, domain = slabs[0].shape
+def tile_chunk(bits, info, codes, table, own_sorted, other_rows, occ_local, share):
+    rows_total, domain = other_rows.shape
     groups = rows_total // GROUP
     held = GROUP // occ_local * CAP
-    depth = -(-sources * groups * held // GROUP) * GROUP
+    depth = 2 * groups * held
     tiles = (share, TILE, TILE)
     anywhere = pl.BlockSpec(memory_space=pl.ANY)
     in_smem = pl.BlockSpec(memory_space=pltpu.SMEM)
     return pl.pallas_call(
         functools.partial(chunk_kernel, bits, occ_local, share),
-        in_specs=[in_smem, in_smem] + [anywhere] * sources,
+        in_specs=[in_smem] * 3 + [anywhere] * 2,
         out_specs=[anywhere, anywhere],
         scratch_shapes=[
-            pltpu.VMEM((sources * rows_total, domain), jnp.bfloat16),
+            pltpu.VMEM((rows_total, domain), jnp.bfloat16),
             pltpu.VMEM((depth + GROUP, domain), jnp.bfloat16),
             pltpu.VMEM((domain, depth), jnp.bfloat16),
             pltpu.VMEM((held, GROUP), jnp.bfloat16),
             pltpu.VMEM(tiles, jnp.bfloat16),
             pltpu.VMEM(tiles, jnp.float32),
-            pltpu.SemaphoreType.DMA((sources * groups,)),
+            pltpu.SemaphoreType.DMA((CAP,)),
+            pltpu.SemaphoreType.DMA((groups,)),
             pltpu.SemaphoreType.DMA((2, share)),
         ],
         out_shape=[
@@ -243,12 +337,12 @@
         ],
         compiler_params=pltpu.CompilerParams(vmem_limit_bytes=56 * 1024 * 1024),
         cost_estimate=pl.CostEstimate(
-            flops=4 * share * TILE * TILE * depth + 2 * depth * GROUP * domain,
-            bytes_accessed=2 * sources * rows_total * domain + 6 * share * TILE * TILE,
+            flops=4 * share * TILE * TILE * depth + depth * GROUP * domain,
+            bytes_accessed=3 * rows_total * domain + 6 * share * TILE * TILE,
             transcendentals=0,
         ),
         name="tile_chunk",
-    )(info, table, *slabs)
+    )(info, codes, table, own_sorted, other_rows)
 
 
 def pair_table(blocks):
@@ -271,24 +365,27 @@
         size = lax.axis_size(axis)
         return lax.ppermute(array, axis, [(i, i ^ bits) for i in range(size)])
 
+    def after(array, earlier):
+        return lax.optimization_barrier((array, earlier))
+
     own_rows = half_tensor.reshape(aux_local * occ_local, domain)
     other_rows = exchange(own_rows, "row", 1)
     own_owner = batch_owner[:, 0]
-    own_pairs = jnp.concatenate([pair_list[0], live_pairs])
-    info = jnp.concatenate(
-        [jnp.stack([orb_at, row_at]), own_owner, exchange(own_owner, "row", 1), own_pairs]
-        + [exchange(own_pairs, "orb", bits) for bits in range(1, batches)]
-    )
+    other_owner = exchange(own_owner, "row", 1)
+    info = jnp.concatenate([jnp.stack([orb_at, row_at]), own_owner, other_owner])
+    own_sorted = sort_rows(own_owner, own_rows, batches)
+    own_codes = jnp.concatenate([pair_list[0], live_pairs])
+    own_codes, own_sorted = after(own_codes, own_sorted)
+    codes = {bits: exchange(own_codes, "orb", bits) for bits in (3, 2, 1)} | {0: own_codes}
     table = pair_table(domain // TILE)
 
     def chunk(bits):
-        return tile_chunk(bits, info, table, (own_rows, other_rows), occ_local, share)
+        return tile_chunk(
+            bits, info, codes[bits], table, own_sorted, other_rows, occ_local, share
+        )
 
     def over_x(send, keep):
         return keep + exchange(send, "row", 2).astype(jnp.float32)
-
-    def after(array, earlier):
-        return lax.optimization_barrier((array, earlier))
 
     send_3, keep_3 = chunk(3)
     send_2, keep_2 = chunk(2)

time: 87.2 us -> 90.6 us (1.039)
  starting transfers between devices: 11.7 us -> 24.7 us
  waiting for transfers between devices: 31.7 us -> 21.4 us
  Pallas kernels: 37.5 us -> 38.6 us
    ppermute x12, starting transfers between devices: 11.7 us -> 24.7 us  [exchange(): return lax.ppermute(array, axis, [(i, i ^ bits) for i in range(size)])]
    ppermute x12, waiting for transfers between devices: 31.7 us -> 21.4 us  [exchange(): return lax.ppermute(array, axis, [(i, i ^ bits) for i in range(size)])]
    pallas_call x0 -> x1, Pallas kernels: none -> 5.37 us  [sort_rows(): pl.pallas_call(functools.partial(sort_kernel, batches, occ_local), in_spe...]
    pallas_call x4, Pallas kernels: 37.5 us -> 33.3 us  [tile_chunk(): pl.pallas_call(functools.partial(chunk_kernel, bits, occ_local, share), i...]
    unnamed x6 -> x18, local copies, waits for them, and re-layouts: 0.01 us -> 1.58 us
    concatenate x1 -> x0, local copies, waits for them, and re-layouts: 1.33 us -> none  [tile_plan(): jnp.concatenate([jnp.stack([orb_at, row_at]), own_owner, exchange(own_own...]
  transfers between devices with their start and end apart: 12 -> 12, of which waited for: 6 -> 4; matrix products, arithmetic and copies ran while one was open for 3% -> 1% of each run, Pallas kernels for 33% -> 34%
where the time goes in v5:
time: 90.6 us; the launch traced here: 90.5 us
  Pallas kernels  38.6 us (43%)
  starting transfers between devices  24.7 us (27%)
  waiting for transfers between devices  21.4 us (24%)
  other arithmetic  3.41 us (4%)
  local copies, waits for them, and re-layouts  1.58 us (2%)
    pallas_call x4, Pallas kernels, tile_chunk(): pl.pallas_call(functools.partial(chunk_kernel, bits, occ_local, share), i...  33.3 us
    ppermute x12, starting transfers between devices, exchange(): return lax.ppermute(array, axis, [(i, i ^ bits) for i in range(size)])  24.7 us
    ppermute x12, waiting for transfers between devices, exchange(): return lax.ppermute(array, axis, [(i, i ^ bits) for i in range(size)])  21.4 us
    pallas_call x1, Pallas kernels, sort_rows(): pl.pallas_call(functools.partial(sort_kernel, batches, occ_local), in_spe...  5.37 us
    broadcast_in_dim x1, other arithmetic, tile_plan(): return total.astype(jnp.bfloat16)[None]  2.3 us
  transfers between devices with their start and end apart: 12, of which 4 were waited for; matrix products, arithmetic and copies ran while one was open for 1% of the time, Pallas kernels for 34%

profile of v5, /device:TPU:0, one launch (start us, length us, event | category | flops | bytes accessed | tf_op | source)
XLA Modules:
  0.0 90.5 jit_solution(2450790320919693243)
XLA Ops:
  1.2 5.4 %sort_rows.1.own_sorted = bf16[1024,2048]{1,0:T(8,128)(2,1)} custom-call(s32[16]{0:T(128)} %bitcast.10, bf16[1024,2048]{1,0:T(8,128)(2,1)} %bitcast.8), custom_call_target="tpu_custom_call" | custom-call | flops 1073741824 | bytes 8388608 | tf_op jit(solution)/shard_map/sort_rows/pallas_call | solution.py:146
  6.6 5.1 %collective-permute-start.2 = (s32[65]{0:T(128)S(1)}, s32[65]{0:T(128)S(1)}, u32[]{:S(2)}, u32[]{:S(2)}) collective-permute-start(s32[65]{0:T(128)S(1)} %pad_add_fusion.1.codes), channel_id=1, source_target_pairs={{0,12},{4,8},{8,4},{12,0},{1,13},{5,9},{9,5},{13,1},{2,14},{6,10},... | collective-permute-start | bytes 788 | tf_op jit(solution)/shard_map/ppermute | solution.py:366
  11.7 0.6 pad_add_fusion.info
  12.3 0.9 %collective-permute-done.2.codes = s32[65]{0:T(128)S(1)} collective-permute-done((s32[65]{0:T(128)S(1)}, s32[65]{0:T(128)S(1)}, u32[]{:S(2)}, u32[]{:S(2)}) %collective-permute-start.2) | collective-permute-done | bytes 292 | tf_op jit(solution)/shard_map/ppermute | solution.py:366
  13.2 0.5 copy-done.5
  13.7 7.8 %tile_chunk.4 = (bf16[16,128,128]{2,1,0:T(8,128)(2,1)}, f32[16,128,128]{2,1,0:T(8,128)}) custom-call(s32[34]{0:T(128)} %pad_add_fusion.info, s32[65]{0:T(128)} %copy-done.5, s32[272]{0:T(512)} %constant.9.clone.table, bf16[1024,2048]{1,0:T(8,128)(2,1)} %sort_rows.1.own_sorted, bf16[1024,2048]{1,0:T(8,128)(2,1)} %collective-permute-done.1.other_rows), custom_call_target="tpu_custom_call" | custom-call | flops 1610612736 | bytes 7864320 | tf_op jit(solution)/shard_map/tile_chunk/pallas_call | solution.py:319
  21.5 0.8 collective-permute-start.3
  22.3 0.8 collective-permute-start.5
  23.1 6.5 %collective-permute-start.8 = (s32[65]{0:T(128)S(1)}, s32[65]{0:T(128)S(1)}, u32[]{:S(2)}, u32[]{:S(2)}) collective-permute-start(s32[65]{0:T(128)S(1)} %pad_add_fusion.1.codes), channel_id=1, source_target_pairs={{0,8},{4,12},{8,0},{12,4},{1,9},{5,13},{9,1},{13,5},{2,10},{6,14},... | collective-permute-start | bytes 788 | tf_op jit(solution)/shard_map/ppermute | solution.py:366
  29.6 0.5 copy-done.7
  30.2 7.8 %tile_chunk.6 = (bf16[16,128,128]{2,1,0:T(8,128)(2,1)}, f32[16,128,128]{2,1,0:T(8,128)}) custom-call(s32[34]{0:T(128)} %pad_add_fusion.info, s32[65]{0:T(128)} %copy-done.7, s32[272]{0:T(512)} %constant.9.clone.table, bf16[1024,2048]{1,0:T(8,128)(2,1)} %sort_rows.1.own_sorted, bf16[1024,2048]{1,0:T(8,128)(2,1)} %collective-permute-done.1.other_rows), custom_call_target="tpu_custom_call" | custom-call | flops 1610612736 | bytes 7864320 | tf_op jit(solution)/shard_map/tile_chunk/pallas_call | solution.py:319
  38.0 0.6 collective-permute-start.6
  38.6 0.5 copy-done.6
  39.1 7.8 %tile_chunk.7 = (bf16[16,128,128]{2,1,0:T(8,128)(2,1)}, f32[16,128,128]{2,1,0:T(8,128)}) custom-call(s32[34]{0:T(128)} %pad_add_fusion.info, s32[65]{0:T(128)} %copy-done.6, s32[272]{0:T(512)} %constant.9.clone.table, bf16[1024,2048]{1,0:T(8,128)(2,1)} %sort_rows.1.own_sorted, bf16[1024,2048]{1,0:T(8,128)(2,1)} %collective-permute-done.1.other_rows), custom_call_target="tpu_custom_call" | custom-call | flops 1610612736 | bytes 7864320 | tf_op jit(solution)/shard_map/tile_chunk/pallas_call | solution.py:319
  46.9 1.5 %collective-permute-start.9 = (bf16[16,128,128]{2,1,0:T(8,128)(2,1)}, bf16[16,128,128]{2,1,0:T(8,128)(2,1)S(1)}, u32[]{:S(2)}, u32[]{:S(2)}) collective-permute-start(bf16[16,128,128]{2,1,0:T(8,128)(2,1)} %get-tuple-element.27), channel_id=1, source_target_pairs={{0,2},{1,3},{2,0},{3,1},{4,6},{5,7},{6,4},{7,5},{8,10},{9,11},{10,... | collective-permute-start | bytes 1572872 | tf_op jit(solution)/shard_map/ppermute | solution.py:366
  48.6 1.2 %collective-permute-start.10 = (bf16[16,128,128]{2,1,0:T(8,128)(2,1)S(1)}, bf16[16,128,128]{2,1,0:T(8,128)(2,1)S(1)}, u32[]{:S(2)}, u32[]{:S(2)}) collective-permute-start(bf16[16,128,128]{2,1,0:T(8,128)(2,1)S(1)} %add_convert_fusion.3), channel_id=1, source_target_pairs={{0,4},{4,0},{8,12},{12,8},{1,5},{5,1},{9,13},{13,9},{2,6},{6,2},{1... | collective-permute-start | bytes 1572872 | tf_op jit(solution)/shard_map/ppermute | solution.py:366
  49.8 2.8 %collective-permute-done.6 = bf16[16,128,128]{2,1,0:T(8,128)(2,1)S(1)} collective-permute-done((bf16[16,128,128]{2,1,0:T(8,128)(2,1)}, bf16[16,128,128]{2,1,0:T(8,128)(2,1)S(1)}, u32[]{:S(2)}, u32[]{:S(2)}) %collective-permute-start.6) | collective-permute-done | bytes 524320 | tf_op jit(solution)/shard_map/ppermute | solution.py:366
  52.7 2.7 %collective-permute-start.7 = (bf16[16,128,128]{2,1,0:T(8,128)(2,1)S(1)}, bf16[16,128,128]{2,1,0:T(8,128)(2,1)S(1)}, u32[]{:S(2)}, u32[]{:S(2)}) collective-permute-start(bf16[16,128,128]{2,1,0:T(8,128)(2,1)S(1)} %add_convert_fusion.2), channel_id=1, source_target_pairs={{0,4},{4,0},{8,12},{12,8},{1,5},{5,1},{9,13},{13,9},{2,6},{6,2},{1... | collective-permute-start | bytes 1572872 | tf_op jit(solution)/shard_map/ppermute | solution.py:366
  55.4 9.9 %tile_chunk.5 = (bf16[16,128,128]{2,1,0:T(8,128)(2,1)}, f32[16,128,128]{2,1,0:T(8,128)}) custom-call(s32[34]{0:T(128)} %pad_add_fusion.info, s32[65]{0:T(128)} %copy-done.4, s32[272]{0:T(512)} %constant.9.clone.table, bf16[1024,2048]{1,0:T(8,128)(2,1)} %sort_rows.1.own_sorted, bf16[1024,2048]{1,0:T(8,128)(2,1)} %collective-permute-done.1.other_rows), custom_call_target="tpu_custom_call" | custom-call | flops 1610612736 | bytes 7864320 | tf_op jit(solution)/shard_map/tile_chunk/pallas_call | solution.py:319
  65.3 0.7 collective-permute-start.4
  66.2 4.4 %collective-permute-start.11 = (bf16[16,128,128]{2,1,0:T(8,128)(2,1)S(1)}, bf16[16,128,128]{2,1,0:T(8,128)(2,1)S(1)}, u32[]{:S(2)}, u32[]{:S(2)}) collective-permute-start(bf16[16,128,128]{2,1,0:T(8,128)(2,1)S(1)} %add_convert_fusion.1), channel_id=1, source_target_pairs={{0,8},{4,12},{8,0},{12,4},{1,9},{5,13},{9,1},{13,5},{2,10},{6,14},... | collective-permute-start | bytes 1572872 | tf_op jit(solution)/shard_map/ppermute | solution.py:366
  70.6 9.2 %collective-permute-done.7 = bf16[16,128,128]{2,1,0:T(8,128)(2,1)S(1)} collective-permute-done((bf16[16,128,128]{2,1,0:T(8,128)(2,1)S(1)}, bf16[16,128,128]{2,1,0:T(8,128)(2,1)S(1)}, u32[]{:S(2)}, u32[]{:S(2)}) %collective-permute-start.7) | collective-permute-done | bytes 524320 | tf_op jit(solution)/shard_map/ppermute | solution.py:366
  79.8 8.4 %collective-permute-done.11 = bf16[16,128,128]{2,1,0:T(8,128)(2,1)S(1)} collective-permute-done((bf16[16,128,128]{2,1,0:T(8,128)(2,1)S(1)}, bf16[16,128,128]{2,1,0:T(8,128)(2,1)S(1)}, u32[]{:S(2)}, u32[]{:S(2)}) %collective-permute-start.11) | collective-permute-done | bytes 524320 | tf_op jit(solution)/shard_map/ppermute | solution.py:366
  88.2 2.3 %fusion = bf16[1,16,128,128]{3,2,1,0:T(8,128)(2,1)} fusion(bf16[16,128,128]{2,1,0:T(8,128)(2,1)S(1)} %collective-permute-done.11, bf16[16,128,128]{2,1,0:T(8,128)(2,1)S(1)} %collective-permute-done.7, f32[16,128,128]{2,1,0:T(8,128)} %get-tuple-element.22, bf16[16,128,128]{2,1,0:T(8,128)(2,1)S(1)} %collective-permute-done.4), kind=kLoop, calls=%fused_computation.4 | loop fusion | flops 1835008 | bytes 3145728 | tf_op jit(solution)/shard_map/broadcast_in_dim | solution.py:401
  (29 shorter events, 1.1 us)
Async XLA Ops:
  0.0 13.2 %collective-permute-start.1 = (bf16[1024,2048]{1,0:T(8,128)(2,1)}, bf16[1024,2048]{1,0:T(8,128)(2,1)}, u32[]{:S(2)}, u32[]{:S(2)}) collective-permute-start(bf16[1024,2048]{1,0:T(8,128)(2,1)} %bitcast.7), channel_id=1, source_target_pairs={{0,1},{1,0},{2,3},{3,2},{4,5},{5,4},{6,7},{7,6},{8,9},{9,8},{10,11... | collective-permute-start | bytes 12582920 | tf_op jit(solution)/shard_map/ppermute | solution.py:366
  0.5 11.3 %collective-permute-start = (s32[16]{0:T(128)}, s32[16]{0:T(128)S(1)}, u32[]{:S(2)}, u32[]{:S(2)}) collective-permute-start(s32[16]{0:T(128)} %bitcast.9), channel_id=1, source_target_pairs={{0,1},{1,0},{2,3},{3,2},{4,5},{5,4},{6,7},{7,6},{8,9},{9,8},{10,11... | collective-permute-start | bytes 200 | tf_op jit(solution)/shard_map/ppermute | solution.py:366
  1.2 5.4 %copy-start.8 = (s32[1,64]{1,0:T(1,128)S(1)}, s32[1,64]{1,0:T(1,128)}, u32[]{:S(2)}) copy-start(s32[1,64]{1,0:T(1,128)} %param.7) | copy-start | bytes 772
  1.2 10.5 %copy-start.3 = (s32[16,1]{0,1:T(1,128)S(1)}, s32[16,1]{0,1:T(1,128)}, u32[]{:S(2)}) copy-start(s32[16,1]{0,1:T(1,128)} %param.6) | copy-start | bytes 196
  6.6 16.4 %copy-start.4 = (s32[65]{0:T(128)}, s32[65]{0:T(128)S(1)}, u32[]{:S(2)}) copy-start(s32[65]{0:T(128)S(1)} %pad_add_fusion.1.codes) | copy-start | bytes 784
  6.6 6.6 %collective-permute-start.2 = (s32[65]{0:T(128)S(1)}, s32[65]{0:T(128)S(1)}, u32[]{:S(2)}, u32[]{:S(2)}) collective-permute-start(s32[65]{0:T(128)S(1)} %pad_add_fusion.1.codes), channel_id=1, source_target_pairs={{0,12},{4,8},{8,4},{12,0},{1,13},{5,9},{9,5},{13,1},{2,14},{6,10},... | collective-permute-start | bytes 788 | tf_op jit(solution)/shard_map/ppermute | solution.py:366
  13.2 0.5 copy-start.5
  21.5 27.0 %collective-permute-start.3 = (bf16[16,128,128]{2,1,0:T(8,128)(2,1)}, bf16[16,128,128]{2,1,0:T(8,128)(2,1)S(1)}, u32[]{:S(2)}, u32[]{:S(2)}) collective-permute-start(bf16[16,128,128]{2,1,0:T(8,128)(2,1)} %get-tuple-element.20), channel_id=1, source_target_pairs={{0,2},{1,3},{2,0},{3,1},{4,6},{5,7},{6,4},{7,5},{8,10},{9,11},{10,... | collective-permute-start | bytes 1572872 | tf_op jit(solution)/shard_map/ppermute | solution.py:366
  22.3 7.3 %collective-permute-start.5 = (s32[65]{0:T(128)S(1)}, s32[65]{0:T(128)S(1)}, u32[]{:S(2)}, u32[]{:S(2)}) collective-permute-start(s32[65]{0:T(128)S(1)} %pad_add_fusion.1.codes), channel_id=1, source_target_pairs={{0,4},{4,0},{8,12},{12,8},{1,5},{5,1},{9,13},{13,9},{2,6},{6,2},{1... | collective-permute-start | bytes 788 | tf_op jit(solution)/shard_map/ppermute | solution.py:366
  23.1 15.5 %collective-permute-start.8 = (s32[65]{0:T(128)S(1)}, s32[65]{0:T(128)S(1)}, u32[]{:S(2)}, u32[]{:S(2)}) collective-permute-start(s32[65]{0:T(128)S(1)} %pad_add_fusion.1.codes), channel_id=1, source_target_pairs={{0,8},{4,12},{8,0},{12,4},{1,9},{5,13},{9,1},{13,5},{2,10},{6,14},... | collective-permute-start | bytes 788 | tf_op jit(solution)/shard_map/ppermute | solution.py:366
  29.6 0.5 copy-start.7
  38.0 10.5 %copy-start.1 = (f32[16,128,128]{2,1,0:T(8,128)S(1)}, f32[16,128,128]{2,1,0:T(8,128)}, u32[]{:S(2)}) copy-start(f32[16,128,128]{2,1,0:T(8,128)} %get-tuple-element.19) | copy-start | bytes 3145732
  38.0 14.6 %copy-start.2 = (f32[16,128,128]{2,1,0:T(8,128)S(1)}, f32[16,128,128]{2,1,0:T(8,128)}, u32[]{:S(2)}) copy-start(f32[16,128,128]{2,1,0:T(8,128)} %get-tuple-element.24) | copy-start | bytes 3145732
  38.0 14.6 %collective-permute-start.6 = (bf16[16,128,128]{2,1,0:T(8,128)(2,1)}, bf16[16,128,128]{2,1,0:T(8,128)(2,1)S(1)}, u32[]{:S(2)}, u32[]{:S(2)}) collective-permute-start(bf16[16,128,128]{2,1,0:T(8,128)(2,1)} %get-tuple-element.25), channel_id=1, source_target_pairs={{0,2},{1,3},{2,0},{3,1},{4,6},{5,7},{6,4},{7,5},{8,10},{9,11},{10,... | collective-permute-start | bytes 1572872 | tf_op jit(solution)/shard_map/ppermute | solution.py:366
  38.6 0.5 copy-start.6
  46.9 19.1 %collective-permute-start.9 = (bf16[16,128,128]{2,1,0:T(8,128)(2,1)}, bf16[16,128,128]{2,1,0:T(8,128)(2,1)S(1)}, u32[]{:S(2)}, u32[]{:S(2)}) collective-permute-start(bf16[16,128,128]{2,1,0:T(8,128)(2,1)} %get-tuple-element.27), channel_id=1, source_target_pairs={{0,2},{1,3},{2,0},{3,1},{4,6},{5,7},{6,4},{7,5},{8,10},{9,11},{10,... | collective-permute-start | bytes 1572872 | tf_op jit(solution)/shard_map/ppermute | solution.py:366
  48.6 17.4 %collective-permute-start.10 = (bf16[16,128,128]{2,1,0:T(8,128)(2,1)S(1)}, bf16[16,128,128]{2,1,0:T(8,128)(2,1)S(1)}, u32[]{:S(2)}, u32[]{:S(2)}) collective-permute-start(bf16[16,128,128]{2,1,0:T(8,128)(2,1)S(1)} %add_convert_fusion.3), channel_id=1, source_target_pairs={{0,4},{4,0},{8,12},{12,8},{1,5},{5,1},{9,13},{13,9},{2,6},{6,2},{1... | collective-permute-start | bytes 1572872 | tf_op jit(solution)/shard_map/ppermute | solution.py:366
  52.7 13.3 %copy-start = (f32[16,128,128]{2,1,0:T(8,128)S(1)}, f32[16,128,128]{2,1,0:T(8,128)}, u32[]{:S(2)}) copy-start(f32[16,128,128]{2,1,0:T(8,128)} %get-tuple-element.26) | copy-start | bytes 3145732
  52.7 27.1 %collective-permute-start.7 = (bf16[16,128,128]{2,1,0:T(8,128)(2,1)S(1)}, bf16[16,128,128]{2,1,0:T(8,128)(2,1)S(1)}, u32[]{:S(2)}, u32[]{:S(2)}) collective-permute-start(bf16[16,128,128]{2,1,0:T(8,128)(2,1)S(1)} %add_convert_fusion.2), channel_id=1, source_target_pairs={{0,4},{4,0},{8,12},{12,8},{1,5},{5,1},{9,13},{13,9},{2,6},{6,2},{1... | collective-permute-start | bytes 1572872 | tf_op jit(solution)/shard_map/ppermute | solution.py:366
  65.3 14.5 %collective-permute-start.4 = (bf16[16,128,128]{2,1,0:T(8,128)(2,1)}, bf16[16,128,128]{2,1,0:T(8,128)(2,1)S(1)}, u32[]{:S(2)}, u32[]{:S(2)}) collective-permute-start(bf16[16,128,128]{2,1,0:T(8,128)(2,1)} %get-tuple-element.23), channel_id=1, source_target_pairs={{0,2},{1,3},{2,0},{3,1},{4,6},{5,7},{6,4},{7,5},{8,10},{9,11},{10,... | collective-permute-start | bytes 1572872 | tf_op jit(solution)/shard_map/ppermute | solution.py:366
  66.2 22.1 %collective-permute-start.11 = (bf16[16,128,128]{2,1,0:T(8,128)(2,1)S(1)}, bf16[16,128,128]{2,1,0:T(8,128)(2,1)S(1)}, u32[]{:S(2)}, u32[]{:S(2)}) collective-permute-start(bf16[16,128,128]{2,1,0:T(8,128)(2,1)S(1)} %add_convert_fusion.1), channel_id=1, source_target_pairs={{0,8},{4,12},{8,0},{12,4},{1,9},{5,13},{9,1},{13,5},{2,10},{6,14},... | collective-permute-start | bytes 1572872 | tf_op jit(solution)/shard_map/ppermute | solution.py:366

commit v6 on v0

--- a/solution.py
+++ b/solution.py
@@ -1,12 +1,17 @@
+import functools
 import math
 
 import jax
 import jax.numpy as jnp
 from jax import lax
+from jax.experimental import pallas as pl
+from jax.experimental.pallas import tpu as pltpu
 from jax.sharding import PartitionSpec as P
 
 TILE = 128
 CAP = 8
+GROUP = 256
+ROWS = 4
 
 
 def block_pairs(pair_codes, blocks):
@@ -35,46 +40,274 @@
     return jnp.where(filled, source_row, local_count)
 
 
-def per_device(half_tensor, batch_owner, pair_list, live_pairs):
+def slab_plan(half_tensor, batch_owner, pair_list, live_pairs):
     batches = lax.axis_size("orb")
     aux_local, occ_local, domain = half_tensor.shape
-    tile_width = TILE
-    blocks = domain // tile_width
+    blocks = domain // TILE
     sources = slot_sources(batch_owner[:, 0], batches, CAP)
-    block_major = half_tensor.reshape(aux_local, occ_local, blocks, tile_width).transpose(
-        2, 1, 0, 3
-    )
+    block_major = half_tensor.reshape(aux_local, occ_local, blocks, TILE).transpose(2, 1, 0, 3)
     outgoing = jnp.take(block_major, sources, axis=1, mode="fill", fill_value=0)
     arrived = lax.all_to_all(outgoing, "orb", split_axis=1, concat_axis=2, tiled=True)
-    pieces = [arrived.reshape(blocks, -1, tile_width)]
+    stacked_rows = arrived.reshape(blocks, -1, TILE)
     first_blocks, second_blocks = block_pairs(pair_list[0], blocks)
     live_count = live_pairs[0]
     pair_total = pair_list.shape[1]
     contract = (((0,), (0,)), ((), ()))
     group_size = math.gcd(4, pair_total)
-    group_turns = pair_total // group_size
 
     def one_group(group_index):
-        pair_start = 0 + group_index * group_size
+        pair_start = group_index * group_size
         tiles = []
         for offset in range(group_size):
-            left_block = first_blocks[pair_start + offset]
-            right_block = second_blocks[pair_start + offset]
-            stacked_rows = pieces[0]
-            left_part = lax.dynamic_index_in_dim(stacked_rows, left_block, 0, keepdims=False)
-            right_part = lax.dynamic_index_in_dim(stacked_rows, right_block, 0, keepdims=False)
-            tile_one = lax.dot_general(
-                left_part, right_part, contract, preferred_element_type=jnp.float32
+            left = lax.dynamic_index_in_dim(
+                stacked_rows, first_blocks[pair_start + offset], 0, keepdims=False
             )
-            tiles.append(tile_one)
-        tile_block = jnp.stack(tiles, axis=0)
+            right = lax.dynamic_index_in_dim(
+                stacked_rows, second_blocks[pair_start + offset], 0, keepdims=False
+            )
+            tiles.append(
+                lax.dot_general(left, right, contract, preferred_element_type=jnp.float32)
+            )
         keep_mask = pair_start + lax.iota(jnp.int32, group_size) < live_count
-        return jnp.where(keep_mask[:, None, None], tile_block, jnp.float32(0.0))
-
-    grouped = lax.map(one_group, jnp.arange(group_turns, dtype=jnp.int32))
-    terms = grouped.reshape(pair_total, tile_width, tile_width)
+        return jnp.where(keep_mask[:, None, None], jnp.stack(tiles, axis=0), jnp.float32(0.0))
+
+    grouped = lax.map(one_group, jnp.arange(pair_total // group_size, dtype=jnp.int32))
+    terms = grouped.reshape(pair_total, TILE, TILE)
     mine = lax.psum_scatter(terms.astype(jnp.bfloat16), "row", scatter_dimension=0, tiled=True)
     return mine[None]
+
+
+def chunk_kernel(occ_local, share, info, codes, own_rows, other_rows, *refs):
+    send_out, keep_out = refs[:2]
+    stage, packed_rows, turned, pick, sums, send_ref, left_at, right_at = refs[2:10]
+    arrived, left_off = refs[10:]
+    rows_total, domain = own_rows.shape
+    blocks = domain // TILE
+    groups = rows_total // GROUP
+    per_group = GROUP // occ_local
+    held = per_group * CAP
+    pair_total = share * ROWS
+    live, batch = codes[pair_total], codes[pair_total + 1]
+
+    def slab_copy(place):
+        slab = own_rows if place < groups else other_rows
+        return pltpu.make_async_copy(
+            slab.at[pl.ds(place % groups * GROUP, GROUP), :],
+            stage.at[pl.ds(place * GROUP, GROUP), :],
+            arrived.at[place],
+        )
+
+    for place in range(2 * groups):
+        slab_copy(place).start()
+
+    lane = lax.broadcasted_iota(jnp.int32, (1, GROUP), 1)
+    orbital_of = lane & (occ_local - 1)
+    turn_of = lane >> (occ_local.bit_length() - 1)
+    slot = lax.broadcasted_iota(jnp.int32, (held, GROUP), 0)
+    counts = []
+    for source in range(2):
+        count = jnp.int32(0)
+        rank = jnp.full((1, GROUP), -GROUP * CAP, jnp.int32)
+        for orbital in range(occ_local):
+            mine = info[1 + source * occ_local + orbital] == batch
+            rank = jnp.where(orbital_of == orbital, jnp.where(mine, count, -GROUP * CAP), rank)
+            count = count + mine.astype(jnp.int32)
+        pick[source] = (slot == turn_of * count + rank).astype(jnp.bfloat16)
+        counts.append(count)
+
+    def decode(at, carry):
+        first = jnp.where(at < share, info[0] ^ 2, info[0]) * share
+        pair = first + jnp.where(at < share, at, at - share)
+        code = codes[pair]
+        left = jnp.int32(0)
+        start = jnp.int32(0)
+        for block in range(1, blocks):
+            past = code >= block * blocks - block * (block - 1) // 2
+            left = left + past.astype(jnp.int32)
+            start = start + jnp.where(past, blocks - block + 1, 0)
+        left_at[at] = jnp.where(pair < live, left * TILE, -1)
+        right_at[at] = (code - start + left) * TILE
+        return carry
+
+    lax.fori_loop(0, 2 * share, decode, 0)
+
+    def pack(place, carry):
+        rows = pl.ds(pl.multiple_of(place * GROUP, GROUP), GROUP)
+        pltpu.make_async_copy(
+            own_rows.at[pl.ds(0, GROUP), :], stage.at[rows, :], arrived.at[place]
+        ).wait()
+        source = place // groups
+        before = jnp.minimum(place, groups) * counts[0]
+        before = before + jnp.maximum(place - groups, 0) * counts[1]
+        start = pl.multiple_of(before * per_group, per_group)
+        for column in range(0, domain, 2 * TILE):
+            columns = slice(column, column + 2 * TILE)
+            packed = jnp.dot(
+                pick[source], stage[rows, columns], preferred_element_type=jnp.float32
+            )
+            packed_rows[pl.ds(start, held), columns] = packed.astype(jnp.bfloat16)
+        return carry
+
+    lax.fori_loop(0, 2 * groups, pack, 0)
+    filled = pl.multiple_of((counts[0] + counts[1]) * groups * per_group, per_group)
+    packed_rows[pl.ds(filled, GROUP), :] = jnp.zeros((GROUP, domain), jnp.bfloat16)
+    parts = jnp.maximum((filled + GROUP - 1) // GROUP, 1)
+
+    width = math.gcd(4, share)
+
+    def out_copies(turn_at):
+        sends = pl.ds(turn_at * width, width)
+        keeps = pl.ds(share + turn_at * width, width)
+        return (
+            pltpu.make_async_copy(send_ref.at[sends], send_out.at[sends], left_off.at[0, turn_at]),
+            pltpu.make_async_copy(sums.at[keeps], keep_out.at[sends], left_off.at[1, turn_at]),
+        )
+
+    def add_part(part, carry):
+        rows = pl.ds(pl.multiple_of(part * GROUP, GROUP), GROUP)
+        for column in range(0, domain, TILE):
+            columns = slice(column, column + TILE)
+            turned[columns, :] = packed_rows[rows, columns].T
+
+        def several(turn_at, carry):
+            for offset in range(2 * width):
+                at = turn_at * width + offset % width + offset // width * share
+                left = left_at[at]
+                known = pl.multiple_of(jnp.maximum(left, 0), TILE)
+                right = pl.multiple_of(right_at[at], TILE)
+                product = jnp.dot(
+                    turned[pl.ds(known, TILE), :],
+                    packed_rows[rows, pl.ds(right, TILE)],
+                    preferred_element_type=jnp.float32,
+                )
+                product = jnp.where(left >= 0, product, jnp.float32(0.0))
+                sums[at] = jnp.where(part > 0, sums[at], jnp.float32(0.0)) + product
+
+            @pl.when(part == parts - 1)
+            def _():
+                sends = pl.ds(turn_at * width, width)
+                send_ref[sends] = sums[sends].astype(send_ref.dtype)
+                for copy in out_copies(turn_at):
+                    copy.start()
+
+            return carry
+
+        lax.fori_loop(0, share // width, several, 0)
+        return carry
+
+    lax.fori_loop(0, parts, add_part, 0)
+    for turn_at in range(share // width):
+        for copy in out_copies(turn_at):
+            copy.wait()
+
+
+def tile_chunk(info, codes, own_rows, other_rows, occ_local, share):
+    rows_total, domain = own_rows.shape
+    groups = rows_total // GROUP
+    held = GROUP // occ_local * CAP
+    depth = 2 * groups * held
+    tiles = (share, TILE, TILE)
+    anywhere = pl.BlockSpec(memory_space=pl.ANY)
+    in_smem = pl.BlockSpec(memory_space=pltpu.SMEM)
+    return pl.pallas_call(
+        functools.partial(chunk_kernel, occ_local, share),
+        in_specs=[in_smem, in_smem, anywhere, anywhere],
+        out_specs=[anywhere, anywhere],
+        scratch_shapes=[
+            pltpu.VMEM((2 * rows_total, domain), jnp.bfloat16),
+            pltpu.VMEM((depth + GROUP, domain), jnp.bfloat16),
+            pltpu.VMEM((domain, GROUP), jnp.bfloat16),
+            pltpu.VMEM((2, held, GROUP), jnp.bfloat16),
+            pltpu.VMEM((2 * share, TILE, TILE), jnp.float32),
+            pltpu.VMEM(tiles, jnp.bfloat16),
+            pltpu.SMEM((2 * share,), jnp.int32),
+            pltpu.SMEM((2 * share,), jnp.int32),
+            pltpu.SemaphoreType.DMA((2 * groups,)),
+            pltpu.SemaphoreType.DMA((2, share)),
+        ],
+        out_shape=[
+            jax.ShapeDtypeStruct(tiles, jnp.bfloat16),
+            jax.ShapeDtypeStruct(tiles, jnp.float32),
+        ],
+        compiler_params=pltpu.CompilerParams(vmem_limit_bytes=56 * 1024 * 1024),
+        cost_estimate=pl.CostEstimate(
+            flops=4 * share * TILE * TILE * depth + 2 * depth * GROUP * domain,
+            bytes_accessed=4 * rows_total * domain + 6 * share * TILE * TILE,
+            transcendentals=0,
+        ),
+        name="tile_chunk",
+    )(info, codes, own_rows, other_rows)
+
+
+def tile_plan(half_tensor, batch_owner, pair_list, live_pairs):
+    batches = lax.axis_size("orb")
+    rows = lax.axis_size("row")
+    aux_local, occ_local, domain = half_tensor.shape
+    share = pair_list.shape[1] // rows
+    row_at = lax.axis_index("row")
+    orb_at = lax.axis_index("orb")
+
+    def exchange(array, axis, bits):
+        size = lax.axis_size(axis)
+        return lax.ppermute(array, axis, [(i, i ^ bits) for i in range(size)])
+
+    def after(array, earlier):
+        return lax.optimization_barrier((array, earlier))
+
+    def after(array, earlier):
+        return lax.optimization_barrier((array, earlier))
+
+    own_rows = half_tensor.reshape(aux_local * occ_local, domain)
+    other_rows = exchange(own_rows, "row", 1)
+    own_owner = batch_owner[:, 0]
+    other_owner = exchange(own_owner, "row", 1)
+    info = jnp.concatenate([row_at[None], own_owner, other_owner])
+    own_codes = jnp.concatenate([pair_list[0], live_pairs, orb_at[None]])
+    codes = [exchange(own_codes, "orb", bits) for bits in (3, 2, 1)]
+    codes = lax.optimization_barrier(tuple(codes))[::-1]
+    codes = (own_codes, *codes)
+
+    def chunk(bits):
+        return tile_chunk(info, codes[bits], own_rows, other_rows, occ_local, share)
+
+    def over_x(send, keep):
+        return keep + exchange(send, "row", 2).astype(jnp.float32)
+
+    send_3, keep_3 = chunk(3)
+    send_2, keep_2 = chunk(2)
+    far = over_x(send_3, keep_3).astype(jnp.bfloat16)
+    other_rows, far = after(other_rows, far)
+    far = exchange(far, "orb", 1)
+    send_1, keep_1 = chunk(1)
+    across = (over_x(send_2, keep_2) + far.astype(jnp.float32)).astype(jnp.bfloat16)
+    other_rows, across = after(other_rows, across)
+    across = exchange(across, "orb", 2)
+    send_0, keep_0 = chunk(0)
+    near = exchange(over_x(send_1, keep_1).astype(jnp.bfloat16), "orb", 1)
+    beside = near.astype(jnp.float32) + across.astype(jnp.float32)
+    beside, keep_0 = after(beside, keep_0)
+    total = over_x(send_0, keep_0) + beside
+    return total.astype(jnp.bfloat16)[None]
+
+
+def per_device(half_tensor, batch_owner, pair_list, live_pairs):
+    batches = lax.axis_size("orb")
+    rows = lax.axis_size("row")
+    aux_local, occ_local, domain = half_tensor.shape
+    pair_total = pair_list.shape[1]
+    tile_elements = batches * pair_total * TILE * TILE
+    slab_elements = batches * CAP * aux_local * domain
+    fits = (
+        rows == ROWS
+        and batches == 4
+        and pair_total % rows == 0
+        and occ_local & (occ_local - 1) == 0
+        and GROUP % occ_local == 0
+        and aux_local * occ_local % GROUP == 0
+        and tile_elements <= slab_elements
+    )
+    plan = tile_plan if fits else slab_plan
+    return plan(half_tensor, batch_owner, pair_list, live_pairs)
 
 
 def solution(mesh):

time: 663 us -> 90.2 us (0.14)
  loops' own time: 245 us -> 0 us
  waiting for transfers between devices: 215 us -> 19.9 us
  matrix products: 98.7 us -> 0 us
  local copies, waits for them, and re-layouts: 46.1 us -> 0.02 us
  Pallas kernels: 0 us -> 38.8 us
  other arithmetic: 32.4 us -> 6.01 us
  starting transfers between devices: 6.45 us -> 24.3 us
  between operations: 13.4 us -> 0.79 us
    another operation x1 -> x0, loops' own time: 245 us -> none  [per_device(): grouped = lax.map(one_group, jnp.arange(group_turns, dtype=jnp.int32))]
    all_to_all x1 -> x0, waiting for transfers between devices: 184 us -> none  [per_device(): lax.all_to_all(outgoing, 'orb', split_axis=1, concat_axis=2, tiled=True)]
    dot_general x64 -> x0, matrix products: 98.7 us -> none  [one_group(): lax.dot_general(left_part, right_part, contract, preferred_element_type=j...]
    pallas_call x0 -> x4, Pallas kernels: none -> 38.8 us  [tile_chunk(): pl.pallas_call(functools.partial(chunk_kernel, occ_local, share), in_spec...]
    reduce_scatter x1 -> x0, waiting for transfers between devices: 30.9 us -> none  [per_device(): lax.psum_scatter(terms.astype(jnp.bfloat16), 'row', scatter_dimension=0,...]
    ppermute x0 -> x12, starting transfers between devices: none -> 24.3 us  [exchange(): return lax.ppermute(array, axis, [(i, i ^ bits) for i in range(size)])]
    dynamic_slice x32 -> x0, local copies, waits for them, and re-layouts: 21.1 us -> none  [the longest x16 10.8 us: one_group(): left_block = first_blocks[pair_start + offset]]
    ppermute x0 -> x12, waiting for transfers between devices: none -> 19.9 us  [exchange(): return lax.ppermute(array, axis, [(i, i ^ bits) for i in range(size)])]
  transfers between devices with their start and end apart: 2 -> 12, of which waited for: 2 -> 6; matrix products, arithmetic and copies ran while one was open for 0% -> 4% of each run, Pallas kernels for 0% -> 35%
where the time goes in v6:
time: 90.2 us; the launch traced here: 89.8 us
  Pallas kernels  38.8 us (43%)
  starting transfers between devices  24.3 us (27%)
  waiting for transfers between devices  19.9 us (22%)
  other arithmetic  6.01 us (7%)
    pallas_call x4, Pallas kernels, tile_chunk(): pl.pallas_call(functools.partial(chunk_kernel, occ_local, share), in_spec...  38.8 us
    ppermute x12, starting transfers between devices, exchange(): return lax.ppermute(array, axis, [(i, i ^ bits) for i in range(size)])  24.3 us
    ppermute x12, waiting for transfers between devices, exchange(): return lax.ppermute(array, axis, [(i, i ^ bits) for i in range(size)])  19.9 us
    broadcast_in_dim x1, other arithmetic, tile_plan(): return total.astype(jnp.bfloat16)[None]  2.21 us
  transfers between devices with their start and end apart: 12, of which 6 were waited for; matrix products, arithmetic and copies ran while one was open for 4% of the time, Pallas kernels for 35%

profile of v6, /device:TPU:0, one launch (start us, length us, event | category | flops | bytes accessed | tf_op | source)
XLA Modules:
  0.0 89.8 jit_solution(404252646289557934)
XLA Ops:
  0.0 0.5 collective-permute-start.4
  1.1 0.7 pad_add_fusion.1.codes
  1.8 4.6 %collective-permute-start.1 = (s32[66]{0:T(128)S(1)}, s32[66]{0:T(128)S(1)}, u32[]{:S(2)}, u32[]{:S(2)}) collective-permute-start(s32[66]{0:T(128)S(1)} %pad_add_fusion.1.codes), channel_id=1, source_target_pairs={{0,12},{4,8},{8,4},{12,0},{1,13},{5,9},{9,5},{13,1},{2,14},{6,10},... | collective-permute-start | bytes 800 | tf_op jit(solution)/shard_map/ppermute | solution.py:252
  6.4 0.6 collective-permute-start.3
  7.1 1.3 %collective-permute-done = s32[16]{0:T(128)S(1)} collective-permute-done((s32[16]{0:T(128)}, s32[16]{0:T(128)S(1)}, u32[]{:S(2)}, u32[]{:S(2)}) %collective-permute-start) | collective-permute-done | bytes 96 | tf_op jit(solution)/shard_map/ppermute | solution.py:252
  8.3 1.3 %pad_add_fusion.info = s32[33]{0:T(128)} fusion(s32[16]{0:T(128)S(1)} %collective-permute-done, s32[16]{0:T(128)} %bitcast.14, s32[1]{0:T(128)} %bitcast), kind=kLoop, calls=%fused_computation.6 | loop fusion | flops 66 | bytes 264 | tf_op jit(solution)/shard_map/concatenate | solution.py:264
  9.6 1.3 %collective-permute-done.2.codes = s32[66]{0:T(128)S(1)} collective-permute-done((s32[66]{0:T(128)S(1)}, s32[66]{0:T(128)S(1)}, u32[]{:S(2)}, u32[]{:S(2)}) %collective-permute-start.2) | collective-permute-done | bytes 296 | tf_op jit(solution)/shard_map/ppermute | solution.py:252
  10.9 7.6 %tile_chunk.4 = (bf16[16,128,128]{2,1,0:T(8,128)(2,1)}, f32[16,128,128]{2,1,0:T(8,128)}) custom-call(s32[33]{0:T(128)} %pad_add_fusion.info, s32[66]{0:T(128)} %copy-done.5, bf16[1024,2048]{1,0:T(8,128)(2,1)} %bitcast.8, bf16[1024,2048]{1,0:T(8,128)(2,1)} %collective-permute-done.4.other_rows), custom_call_target="tpu_custom_call" | custom-call | flops 2147483648 | bytes 9961472 | tf_op jit(solution)/shard_map/tile_chunk/pallas_call | solution.py:212
  18.5 3.3 %collective-permute-start.5 = (bf16[16,128,128]{2,1,0:T(8,128)(2,1)}, bf16[16,128,128]{2,1,0:T(8,128)(2,1)S(1)}, u32[]{:S(2)}, u32[]{:S(2)}) collective-permute-start(bf16[16,128,128]{2,1,0:T(8,128)(2,1)} %get-tuple-element.25), channel_id=1, source_target_pairs={{0,2},{1,3},{2,0},{3,1},{4,6},{5,7},{6,4},{7,5},{8,10},{9,11},{10,... | collective-permute-start | bytes 1572872 | tf_op jit(solution)/shard_map/ppermute | solution.py:252
  21.8 9.3 %tile_chunk.6 = (bf16[16,128,128]{2,1,0:T(8,128)(2,1)}, f32[16,128,128]{2,1,0:T(8,128)}) custom-call(s32[33]{0:T(128)} %pad_add_fusion.info, s32[66]{0:T(128)} %copy-done.4, bf16[1024,2048]{1,0:T(8,128)(2,1)} %bitcast.9, bf16[1024,2048]{1,0:T(8,128)(2,1)} %collective-permute-done.4.other_rows), custom_call_target="tpu_custom_call" | custom-call | flops 2147483648 | bytes 9961472 | tf_op jit(solution)/shard_map/tile_chunk/pallas_call | solution.py:212
  31.0 0.2 collective-permute-start.8
  31.3 3.2 %collective-permute-done.5 = bf16[16,128,128]{2,1,0:T(8,128)(2,1)S(1)} collective-permute-done((bf16[16,128,128]{2,1,0:T(8,128)(2,1)}, bf16[16,128,128]{2,1,0:T(8,128)(2,1)S(1)}, u32[]{:S(2)}, u32[]{:S(2)}) %collective-permute-start.5) | collective-permute-done | bytes 524320 | tf_op jit(solution)/shard_map/ppermute | solution.py:252
  34.6 2.0 %collective-permute-start.9 = (bf16[16,128,128]{2,1,0:T(8,128)(2,1)S(1)}, bf16[16,128,128]{2,1,0:T(8,128)(2,1)S(1)}, u32[]{:S(2)}, u32[]{:S(2)}) collective-permute-start(bf16[16,128,128]{2,1,0:T(8,128)(2,1)S(1)} %add_convert_fusion.3), channel_id=1, source_target_pairs={{0,4},{4,0},{8,12},{12,8},{1,5},{5,1},{9,13},{13,9},{2,6},{6,2},{1... | collective-permute-start | bytes 1572872 | tf_op jit(solution)/shard_map/ppermute | solution.py:252
  36.6 9.3 %tile_chunk.5 = (bf16[16,128,128]{2,1,0:T(8,128)(2,1)}, f32[16,128,128]{2,1,0:T(8,128)}) custom-call(s32[33]{0:T(128)} %pad_add_fusion.info, s32[66]{0:T(128)} %copy-done.3, bf16[1024,2048]{1,0:T(8,128)(2,1)} %bitcast.10, bf16[1024,2048]{1,0:T(8,128)(2,1)} %collective-permute-done.4.other_rows), custom_call_target="tpu_custom_call" | custom-call | flops 2147483648 | bytes 9961472 | tf_op jit(solution)/shard_map/tile_chunk/pallas_call | solution.py:212
  45.9 1.6 %collective-permute-start.6 = (bf16[16,128,128]{2,1,0:T(8,128)(2,1)}, bf16[16,128,128]{2,1,0:T(8,128)(2,1)S(1)}, u32[]{:S(2)}, u32[]{:S(2)}) collective-permute-start(bf16[16,128,128]{2,1,0:T(8,128)(2,1)} %get-tuple-element.28), channel_id=1, source_target_pairs={{0,2},{1,3},{2,0},{3,1},{4,6},{5,7},{6,4},{7,5},{8,10},{9,11},{10,... | collective-permute-start | bytes 1572872 | tf_op jit(solution)/shard_map/ppermute | solution.py:252
  47.7 6.1 %collective-permute-start.10 = (bf16[16,128,128]{2,1,0:T(8,128)(2,1)S(1)}, bf16[16,128,128]{2,1,0:T(8,128)(2,1)S(1)}, u32[]{:S(2)}, u32[]{:S(2)}) collective-permute-start(bf16[16,128,128]{2,1,0:T(8,128)(2,1)S(1)} %add_convert_fusion.1), channel_id=1, source_target_pairs={{0,8},{4,12},{8,0},{12,4},{1,9},{5,13},{9,1},{13,5},{2,10},{6,14},... | collective-permute-start | bytes 1572872 | tf_op jit(solution)/shard_map/ppermute | solution.py:252
  53.8 4.5 %collective-permute-done.6 = bf16[16,128,128]{2,1,0:T(8,128)(2,1)S(1)} collective-permute-done((bf16[16,128,128]{2,1,0:T(8,128)(2,1)}, bf16[16,128,128]{2,1,0:T(8,128)(2,1)S(1)}, u32[]{:S(2)}, u32[]{:S(2)}) %collective-permute-start.6) | collective-permute-done | bytes 524320 | tf_op jit(solution)/shard_map/ppermute | solution.py:252
  58.3 1.3 %add_convert_fusion.2 = bf16[16,128,128]{2,1,0:T(8,128)(2,1)S(1)} fusion(f32[16,128,128]{2,1,0:T(8,128)} %get-tuple-element.27, bf16[16,128,128]{2,1,0:T(8,128)(2,1)S(1)} %collective-permute-done.6), kind=kLoop, calls=%fused_computation.3 | loop fusion | flops 786432 | bytes 2097152 | tf_op jit(solution)/shard_map/convert_element_type | solution.py:286
  59.7 3.9 %collective-permute-start.7 = (bf16[16,128,128]{2,1,0:T(8,128)(2,1)S(1)}, bf16[16,128,128]{2,1,0:T(8,128)(2,1)S(1)}, u32[]{:S(2)}, u32[]{:S(2)}) collective-permute-start(bf16[16,128,128]{2,1,0:T(8,128)(2,1)S(1)} %add_convert_fusion.2), channel_id=1, source_target_pairs={{0,4},{4,0},{8,12},{12,8},{1,5},{5,1},{9,13},{13,9},{2,6},{6,2},{1... | collective-permute-start | bytes 1572872 | tf_op jit(solution)/shard_map/ppermute | solution.py:252
  63.6 12.8 %tile_chunk.7 = (bf16[16,128,128]{2,1,0:T(8,128)(2,1)}, f32[16,128,128]{2,1,0:T(8,128)}) custom-call(s32[33]{0:T(128)} %pad_add_fusion.info, s32[66]{0:T(128)} %copy-done.2, bf16[1024,2048]{1,0:T(8,128)(2,1)} %bitcast.11, bf16[1024,2048]{1,0:T(8,128)(2,1)} %collective-permute-done.4.other_rows), custom_call_target="tpu_custom_call" | custom-call | flops 2147483648 | bytes 9961472 | tf_op jit(solution)/shard_map/tile_chunk/pallas_call | solution.py:212
  76.4 1.5 %collective-permute-start.11 = (bf16[16,128,128]{2,1,0:T(8,128)(2,1)}, bf16[16,128,128]{2,1,0:T(8,128)(2,1)S(1)}, u32[]{:S(2)}, u32[]{:S(2)}) collective-permute-start(bf16[16,128,128]{2,1,0:T(8,128)(2,1)} %get-tuple-element.37), channel_id=1, source_target_pairs={{0,2},{1,3},{2,0},{3,1},{4,6},{5,7},{6,4},{7,5},{8,10},{9,11},{10,... | collective-permute-start | bytes 1572872 | tf_op jit(solution)/shard_map/ppermute | solution.py:252
  77.8 5.7 %collective-permute-done.7 = bf16[16,128,128]{2,1,0:T(8,128)(2,1)S(1)} collective-permute-done((bf16[16,128,128]{2,1,0:T(8,128)(2,1)S(1)}, bf16[16,128,128]{2,1,0:T(8,128)(2,1)S(1)}, u32[]{:S(2)}, u32[]{:S(2)}) %collective-permute-start.7) | collective-permute-done | bytes 524320 | tf_op jit(solution)/shard_map/ppermute | solution.py:252
  83.6 3.9 %collective-permute-done.11 = bf16[16,128,128]{2,1,0:T(8,128)(2,1)S(1)} collective-permute-done((bf16[16,128,128]{2,1,0:T(8,128)(2,1)}, bf16[16,128,128]{2,1,0:T(8,128)(2,1)S(1)}, u32[]{:S(2)}, u32[]{:S(2)}) %collective-permute-start.11) | collective-permute-done | bytes 524320 | tf_op jit(solution)/shard_map/ppermute | solution.py:252
  87.6 2.2 %fusion = bf16[1,16,128,128]{3,2,1,0:T(8,128)(2,1)} fusion(f32[16,128,128]{2,1,0:T(8,128)S(1)} %convert_add_fusion, f32[16,128,128]{2,1,0:T(8,128)} %get-tuple-element.36, bf16[16,128,128]{2,1,0:T(8,128)(2,1)S(1)} %collective-permute-done.11), kind=kLoop, calls=%fused_computation.5 | loop fusion | flops 1048576 | bytes 3145728 | tf_op jit(solution)/shard_map/broadcast_in_dim | solution.py:290
  (23 shorter events, 0.5 us)
Async XLA Ops:
  0.0 10.9 %collective-permute-start.4 = (bf16[1024,2048]{1,0:T(8,128)(2,1)}, bf16[1024,2048]{1,0:T(8,128)(2,1)}, u32[]{:S(2)}, u32[]{:S(2)}) collective-permute-start(bf16[1024,2048]{1,0:T(8,128)(2,1)} %bitcast.7), channel_id=1, source_target_pairs={{0,1},{1,0},{2,3},{3,2},{4,5},{5,4},{6,7},{7,6},{8,9},{9,8},{10,11... | collective-permute-start | bytes 12582920 | tf_op jit(solution)/shard_map/ppermute | solution.py:252
  1.8 16.6 %copy-start.2 = (s32[66]{0:T(128)}, s32[66]{0:T(128)S(1)}, u32[]{:S(2)}) copy-start(s32[66]{0:T(128)S(1)} %pad_add_fusion.1.codes) | copy-start | bytes 796
  1.8 7.8 %collective-permute-start.1 = (s32[66]{0:T(128)S(1)}, s32[66]{0:T(128)S(1)}, u32[]{:S(2)}, u32[]{:S(2)}) collective-permute-start(s32[66]{0:T(128)S(1)} %pad_add_fusion.1.codes), channel_id=1, source_target_pairs={{0,12},{4,8},{8,4},{12,0},{1,13},{5,9},{9,5},{13,1},{2,14},{6,10},... | collective-permute-start | bytes 800 | tf_op jit(solution)/shard_map/ppermute | solution.py:252
  6.4 4.4 %collective-permute-start.2 = (s32[66]{0:T(128)S(1)}, s32[66]{0:T(128)S(1)}, u32[]{:S(2)}, u32[]{:S(2)}) collective-permute-start(s32[66]{0:T(128)S(1)} %pad_add_fusion.1.codes), channel_id=1, source_target_pairs={{0,8},{4,12},{8,0},{12,4},{1,9},{5,13},{9,1},{13,5},{2,10},{6,14},... | collective-permute-start | bytes 800 | tf_op jit(solution)/shard_map/ppermute | solution.py:252
  6.4 4.4 %collective-permute-start.3 = (s32[66]{0:T(128)S(1)}, s32[66]{0:T(128)S(1)}, u32[]{:S(2)}, u32[]{:S(2)}) collective-permute-start(s32[66]{0:T(128)S(1)} %pad_add_fusion.1.codes), channel_id=1, source_target_pairs={{0,4},{4,0},{8,12},{12,8},{1,5},{5,1},{9,13},{13,9},{2,6},{6,2},{1... | collective-permute-start | bytes 800 | tf_op jit(solution)/shard_map/ppermute | solution.py:252
  7.1 1.3 %collective-permute-start = (s32[16]{0:T(128)}, s32[16]{0:T(128)S(1)}, u32[]{:S(2)}, u32[]{:S(2)}) collective-permute-start(s32[16]{0:T(128)} %bitcast.13), channel_id=1, source_target_pairs={{0,1},{1,0},{2,3},{3,2},{4,5},{5,4},{6,7},{7,6},{8,9},{9,8},{10,11... | collective-permute-start | bytes 200 | tf_op jit(solution)/shard_map/ppermute | solution.py:252
  9.6 1.3 %copy-start.5 = (s32[66]{0:T(128)}, s32[66]{0:T(128)S(1)}, u32[]{:S(2)}) copy-start(s32[66]{0:T(128)S(1)} %collective-permute-done.1.codes) | copy-start | bytes 796
  10.9 7.6 %copy-start.4 = (s32[66]{0:T(128)}, s32[66]{0:T(128)S(1)}, u32[]{:S(2)}) copy-start(s32[66]{0:T(128)S(1)} %collective-permute-done.2.codes) | copy-start | bytes 796
  10.9 7.6 %copy-start.3 = (s32[66]{0:T(128)}, s32[66]{0:T(128)S(1)}, u32[]{:S(2)}) copy-start(s32[66]{0:T(128)S(1)} %collective-permute-done.3.codes) | copy-start | bytes 796
  18.5 15.9 %copy-start.1 = (f32[16,128,128]{2,1,0:T(8,128)S(1)}, f32[16,128,128]{2,1,0:T(8,128)}, u32[]{:S(2)}) copy-start(f32[16,128,128]{2,1,0:T(8,128)} %get-tuple-element.24) | copy-start | bytes 3145732
  18.5 15.9 %collective-permute-start.5 = (bf16[16,128,128]{2,1,0:T(8,128)(2,1)}, bf16[16,128,128]{2,1,0:T(8,128)(2,1)S(1)}, u32[]{:S(2)}, u32[]{:S(2)}) collective-permute-start(bf16[16,128,128]{2,1,0:T(8,128)(2,1)} %get-tuple-element.25), channel_id=1, source_target_pairs={{0,2},{1,3},{2,0},{3,1},{4,6},{5,7},{6,4},{7,5},{8,10},{9,11},{10,... | collective-permute-start | bytes 1572872 | tf_op jit(solution)/shard_map/ppermute | solution.py:252
  31.0 16.4 %collective-permute-start.8 = (bf16[16,128,128]{2,1,0:T(8,128)(2,1)}, bf16[16,128,128]{2,1,0:T(8,128)(2,1)S(1)}, u32[]{:S(2)}, u32[]{:S(2)}) collective-permute-start(bf16[16,128,128]{2,1,0:T(8,128)(2,1)} %get-tuple-element.31), channel_id=1, source_target_pairs={{0,2},{1,3},{2,0},{3,1},{4,6},{5,7},{6,4},{7,5},{8,10},{9,11},{10,... | collective-permute-start | bytes 1572872 | tf_op jit(solution)/shard_map/ppermute | solution.py:252
  34.6 12.9 %copy-start = (f32[16,128,128]{2,1,0:T(8,128)S(1)}, f32[16,128,128]{2,1,0:T(8,128)}, u32[]{:S(2)}) copy-start(f32[16,128,128]{2,1,0:T(8,128)} %get-tuple-element.30) | copy-start | bytes 3145732
  34.6 12.9 %collective-permute-start.9 = (bf16[16,128,128]{2,1,0:T(8,128)(2,1)S(1)}, bf16[16,128,128]{2,1,0:T(8,128)(2,1)S(1)}, u32[]{:S(2)}, u32[]{:S(2)}) collective-permute-start(bf16[16,128,128]{2,1,0:T(8,128)(2,1)S(1)} %add_convert_fusion.3), channel_id=1, source_target_pairs={{0,4},{4,0},{8,12},{12,8},{1,5},{5,1},{9,13},{13,9},{2,6},{6,2},{1... | collective-permute-start | bytes 1572872 | tf_op jit(solution)/shard_map/ppermute | solution.py:252
  45.9 12.4 %collective-permute-start.6 = (bf16[16,128,128]{2,1,0:T(8,128)(2,1)}, bf16[16,128,128]{2,1,0:T(8,128)(2,1)S(1)}, u32[]{:S(2)}, u32[]{:S(2)}) collective-permute-start(bf16[16,128,128]{2,1,0:T(8,128)(2,1)} %get-tuple-element.28), channel_id=1, source_target_pairs={{0,2},{1,3},{2,0},{3,1},{4,6},{5,7},{6,4},{7,5},{8,10},{9,11},{10,... | collective-permute-start | bytes 1572872 | tf_op jit(solution)/shard_map/ppermute | solution.py:252
  47.7 30.2 %collective-permute-start.10 = (bf16[16,128,128]{2,1,0:T(8,128)(2,1)S(1)}, bf16[16,128,128]{2,1,0:T(8,128)(2,1)S(1)}, u32[]{:S(2)}, u32[]{:S(2)}) collective-permute-start(bf16[16,128,128]{2,1,0:T(8,128)(2,1)S(1)} %add_convert_fusion.1), channel_id=1, source_target_pairs={{0,8},{4,12},{8,0},{12,4},{1,9},{5,13},{9,1},{13,5},{2,10},{6,14},... | collective-permute-start | bytes 1572872 | tf_op jit(solution)/shard_map/ppermute | solution.py:252
  59.7 23.8 %collective-permute-start.7 = (bf16[16,128,128]{2,1,0:T(8,128)(2,1)S(1)}, bf16[16,128,128]{2,1,0:T(8,128)(2,1)S(1)}, u32[]{:S(2)}, u32[]{:S(2)}) collective-permute-start(bf16[16,128,128]{2,1,0:T(8,128)(2,1)S(1)} %add_convert_fusion.2), channel_id=1, source_target_pairs={{0,4},{4,0},{8,12},{12,8},{1,5},{5,1},{9,13},{13,9},{2,6},{6,2},{1... | collective-permute-start | bytes 1572872 | tf_op jit(solution)/shard_map/ppermute | solution.py:252
  76.4 11.2 %collective-permute-start.11 = (bf16[16,128,128]{2,1,0:T(8,128)(2,1)}, bf16[16,128,128]{2,1,0:T(8,128)(2,1)S(1)}, u32[]{:S(2)}, u32[]{:S(2)}) collective-permute-start(bf16[16,128,128]{2,1,0:T(8,128)(2,1)} %get-tuple-element.37), channel_id=1, source_target_pairs={{0,2},{1,3},{2,0},{3,1},{4,6},{5,7},{6,4},{7,5},{8,10},{9,11},{10,... | collective-permute-start | bytes 1572872 | tf_op jit(solution)/shard_map/ppermute | solution.py:252

commit v7 on v6

--- a/solution.py
+++ b/solution.py
@@ -77,7 +77,7 @@
     return mine[None]
 
 
-def chunk_kernel(occ_local, share, info, codes, own_rows, other_rows, *refs):
+def chunk_kernel(occ_local, share, own_owner, other_owner, codes, own_rows, other_rows, *refs):
     send_out, keep_out = refs[:2]
     stage, packed_rows, turned, pick, sums, send_ref, left_at, right_at = refs[2:10]
     arrived, left_off = refs[10:]
@@ -105,18 +105,20 @@
     turn_of = lane >> (occ_local.bit_length() - 1)
     slot = lax.broadcasted_iota(jnp.int32, (held, GROUP), 0)
     counts = []
-    for source in range(2):
+    for source, owner in enumerate((own_owner, other_owner)):
         count = jnp.int32(0)
         rank = jnp.full((1, GROUP), -GROUP * CAP, jnp.int32)
         for orbital in range(occ_local):
-            mine = info[1 + source * occ_local + orbital] == batch
+            mine = owner[orbital] == batch
             rank = jnp.where(orbital_of == orbital, jnp.where(mine, count, -GROUP * CAP), rank)
             count = count + mine.astype(jnp.int32)
         pick[source] = (slot == turn_of * count + rank).astype(jnp.bfloat16)
         counts.append(count)
 
+    row_at = lax.axis_index("row")
+
     def decode(at, carry):
-        first = jnp.where(at < share, info[0] ^ 2, info[0]) * share
+        first = jnp.where(at < share, row_at ^ 2, row_at) * share
         pair = first + jnp.where(at < share, at, at - share)
         code = codes[pair]
         left = jnp.int32(0)
@@ -125,11 +127,13 @@
             past = code >= block * blocks - block * (block - 1) // 2
             left = left + past.astype(jnp.int32)
             start = start + jnp.where(past, blocks - block + 1, 0)
-        left_at[at] = jnp.where(pair < live, left * TILE, -1)
+        left_at[at] = jnp.where(pair < live, left * TILE, domain)
         right_at[at] = (code - start + left) * TILE
         return carry
 
     lax.fori_loop(0, 2 * share, decode, 0)
+    sums[...] = jnp.zeros(sums.shape, jnp.float32)
+    turned[domain:, :] = jnp.zeros((TILE, GROUP), jnp.bfloat16)
 
     def pack(place, carry):
         rows = pl.ds(pl.multiple_of(place * GROUP, GROUP), GROUP)
@@ -169,30 +173,24 @@
             columns = slice(column, column + TILE)
             turned[columns, :] = packed_rows[rows, columns].T
 
-        def several(turn_at, carry):
-            for offset in range(2 * width):
-                at = turn_at * width + offset % width + offset // width * share
-                left = left_at[at]
-                known = pl.multiple_of(jnp.maximum(left, 0), TILE)
-                right = pl.multiple_of(right_at[at], TILE)
-                product = jnp.dot(
-                    turned[pl.ds(known, TILE), :],
-                    packed_rows[rows, pl.ds(right, TILE)],
-                    preferred_element_type=jnp.float32,
-                )
-                product = jnp.where(left >= 0, product, jnp.float32(0.0))
-                sums[at] = jnp.where(part > 0, sums[at], jnp.float32(0.0)) + product
+        for turn_at in range(share // width):
+            sends = slice(turn_at * width, (turn_at + 1) * width)
+            for offset in range(width):
+                for at in (sends.start + offset, share + sends.start + offset):
+                    left = pl.multiple_of(left_at[at], TILE)
+                    right = pl.multiple_of(right_at[at], TILE)
+                    sums[at] += jnp.dot(
+                        turned[pl.ds(left, TILE), :],
+                        packed_rows[rows, pl.ds(right, TILE)],
+                        preferred_element_type=jnp.float32,
+                    )
 
             @pl.when(part == parts - 1)
-            def _():
-                sends = pl.ds(turn_at * width, width)
+            def _(turn_at=turn_at, sends=sends):
                 send_ref[sends] = sums[sends].astype(send_ref.dtype)
                 for copy in out_copies(turn_at):
                     copy.start()
 
-            return carry
-
-        lax.fori_loop(0, share // width, several, 0)
         return carry
 
     lax.fori_loop(0, parts, add_part, 0)
@@ -201,7 +199,7 @@
             copy.wait()
 
 
-def tile_chunk(info, codes, own_rows, other_rows, occ_local, share):
+def tile_chunk(owners, codes, own_rows, other_rows, occ_local, share):
     rows_total, domain = own_rows.shape
     groups = rows_total // GROUP
     held = GROUP // occ_local * CAP
@@ -211,12 +209,12 @@
     in_smem = pl.BlockSpec(memory_space=pltpu.SMEM)
     return pl.pallas_call(
         functools.partial(chunk_kernel, occ_local, share),
-        in_specs=[in_smem, in_smem, anywhere, anywhere],
+        in_specs=[in_smem] * 3 + [anywhere] * 2,
         out_specs=[anywhere, anywhere],
         scratch_shapes=[
             pltpu.VMEM((2 * rows_total, domain), jnp.bfloat16),
             pltpu.VMEM((depth + GROUP, domain), jnp.bfloat16),
-            pltpu.VMEM((domain, GROUP), jnp.bfloat16),
+            pltpu.VMEM((domain + TILE, GROUP), jnp.bfloat16),
             pltpu.VMEM((2, held, GROUP), jnp.bfloat16),
             pltpu.VMEM((2 * share, TILE, TILE), jnp.float32),
             pltpu.VMEM(tiles, jnp.bfloat16),
@@ -236,7 +234,7 @@
             transcendentals=0,
         ),
         name="tile_chunk",
-    )(info, codes, own_rows, other_rows)
+    )(*owners, codes, own_rows, other_rows)
 
 
 def tile_plan(half_tensor, batch_owner, pair_list, live_pairs):
@@ -244,7 +242,6 @@
     rows = lax.axis_size("row")
     aux_local, occ_local, domain = half_tensor.shape
     share = pair_list.shape[1] // rows
-    row_at = lax.axis_index("row")
     orb_at = lax.axis_index("orb")
 
     def exchange(array, axis, bits):
@@ -260,15 +257,14 @@
     own_rows = half_tensor.reshape(aux_local * occ_local, domain)
     other_rows = exchange(own_rows, "row", 1)
     own_owner = batch_owner[:, 0]
-    other_owner = exchange(own_owner, "row", 1)
-    info = jnp.concatenate([row_at[None], own_owner, other_owner])
+    owners = own_owner, exchange(own_owner, "row", 1)
     own_codes = jnp.concatenate([pair_list[0], live_pairs, orb_at[None]])
     codes = [exchange(own_codes, "orb", bits) for bits in (3, 2, 1)]
     codes = lax.optimization_barrier(tuple(codes))[::-1]
     codes = (own_codes, *codes)
 
     def chunk(bits):
-        return tile_chunk(info, codes[bits], own_rows, other_rows, occ_local, share)
+        return tile_chunk(owners, codes[bits], own_rows, other_rows, occ_local, share)
 
     def over_x(send, keep):
         return keep + exchange(send, "row", 2).astype(jnp.float32)
@@ -283,6 +279,7 @@
     other_rows, across = after(other_rows, across)
     across = exchange(across, "orb", 2)
     send_0, keep_0 = chunk(0)
+    keep_1, send_0 = after(keep_1, send_0)
     near = exchange(over_x(send_1, keep_1).astype(jnp.bfloat16), "orb", 1)
     beside = near.astype(jnp.float32) + across.astype(jnp.float32)
     beside, keep_0 = after(beside, keep_0)

time: 90.2 us -> 85.9 us (0.952)
  starting transfers between devices: 24.3 us -> 17.5 us
  waiting for transfers between devices: 19.9 us -> 23.8 us
  other arithmetic: 6.01 us -> 2.28 us
  Pallas kernels: 38.8 us -> 40.4 us
    ppermute x12, starting transfers between devices: 24.3 us -> 17.5 us  [exchange(): return lax.ppermute(array, axis, [(i, i ^ bits) for i in range(size)])]
    ppermute x12, waiting for transfers between devices: 19.9 us -> 23.8 us  [exchange(): return lax.ppermute(array, axis, [(i, i ^ bits) for i in range(size)])]
    pallas_call x4, Pallas kernels: 38.8 us -> 40.4 us  [tile_chunk(): pl.pallas_call(functools.partial(chunk_kernel, occ_local, share), in_spec...]
    concatenate x1 -> x0, other arithmetic: 1.27 us -> none  [tile_plan(): info = jnp.concatenate([row_at[None], own_owner, other_owner])]
    broadcast_in_dim x1, other arithmetic: 2.21 us -> 0.97 us  [tile_plan(): return total.astype(jnp.bfloat16)[None]]
    convert_element_type x1, other arithmetic: 1.35 us -> 0.13 us  [tile_plan(): near = exchange(over_x(send_1, keep_1).astype(jnp.bfloat16), 'orb', 1)]
  transfers between devices with their start and end apart: 12 -> 12, of which waited for: 6 -> 5; matrix products, arithmetic and copies ran while one was open for 4% -> 2% of each run, Pallas kernels for 35% -> 36%
where the time goes in v7:
time: 85.9 us; the launch traced here: 85.4 us
  Pallas kernels  40.4 us (47%)
  waiting for transfers between devices  23.8 us (28%)
  starting transfers between devices  17.5 us (20%)
  other arithmetic  2.28 us (3%)
    pallas_call x4, Pallas kernels, tile_chunk(): pl.pallas_call(functools.partial(chunk_kernel, occ_local, share), in_spec...  40.4 us
    ppermute x12, waiting for transfers between devices, exchange(): return lax.ppermute(array, axis, [(i, i ^ bits) for i in range(size)])  23.8 us
    ppermute x12, starting transfers between devices, exchange(): return lax.ppermute(array, axis, [(i, i ^ bits) for i in range(size)])  17.5 us
  transfers between devices with their start and end apart: 12, of which 5 were waited for; matrix products, arithmetic and copies ran while one was open for 2% of the time, Pallas kernels for 36%

profile of v7, /device:TPU:0, one launch (start us, length us, event | category | flops | bytes accessed | tf_op | source)
XLA Modules:
  0.0 85.4 jit_solution(225319798894676794)
XLA Ops:
  0.0 0.5 collective-permute-start.4
  1.1 0.7 pad_add_fusion.codes
  1.8 4.6 %collective-permute-start.1 = (s32[66]{0:T(128)S(1)}, s32[66]{0:T(128)S(1)}, u32[]{:S(2)}, u32[]{:S(2)}) collective-permute-start(s32[66]{0:T(128)S(1)} %pad_add_fusion.codes), channel_id=1, source_target_pairs={{0,12},{4,8},{8,4},{12,0},{1,13},{5,9},{9,5},{13,1},{2,14},{6,10},... | collective-permute-start | bytes 800 | tf_op jit(solution)/shard_map/ppermute | solution.py:249
  6.4 0.6 collective-permute-start.3
  7.1 0.9 %collective-permute-done.1.codes = s32[66]{0:T(128)S(1)} collective-permute-done((s32[66]{0:T(128)S(1)}, s32[66]{0:T(128)S(1)}, u32[]{:S(2)}, u32[]{:S(2)}) %collective-permute-start.1) | collective-permute-done | bytes 296 | tf_op jit(solution)/shard_map/ppermute | solution.py:249
  8.0 2.9 %collective-permute-done.2.codes = s32[66]{0:T(128)S(1)} collective-permute-done((s32[66]{0:T(128)S(1)}, s32[66]{0:T(128)S(1)}, u32[]{:S(2)}, u32[]{:S(2)}) %collective-permute-start.2) | collective-permute-done | bytes 296 | tf_op jit(solution)/shard_map/ppermute | solution.py:249
  10.9 0.5 copy-done.4
  11.4 9.3 %tile_chunk.4 = (bf16[16,128,128]{2,1,0:T(8,128)(2,1)}, f32[16,128,128]{2,1,0:T(8,128)}) custom-call(s32[16]{0:T(128)} %bitcast.12, s32[16]{0:T(128)} %copy-done.4, s32[66]{0:T(128)} %copy-done.8, bf16[1024,2048]{1,0:T(8,128)(2,1)} %bitcast.7, bf16[1024,2048]{1,0:T(8,128)(2,1)} %collective-permute-done.4.other_rows), custom_call_target="tpu_custom_call" | custom-call | flops 2147483648 | bytes 9961472 | tf_op jit(solution)/shard_map/tile_chunk/pallas_call | solution.py:210
  20.8 1.5 %collective-permute-start.5 = (bf16[16,128,128]{2,1,0:T(8,128)(2,1)}, bf16[16,128,128]{2,1,0:T(8,128)(2,1)S(1)}, u32[]{:S(2)}, u32[]{:S(2)}) collective-permute-start(bf16[16,128,128]{2,1,0:T(8,128)(2,1)} %get-tuple-element.27), channel_id=1, source_target_pairs={{0,2},{1,3},{2,0},{3,1},{4,6},{5,7},{6,4},{7,5},{8,10},{9,11},{10,... | collective-permute-start | bytes 1572872 | tf_op jit(solution)/shard_map/ppermute | solution.py:249
  22.3 9.2 %tile_chunk.6 = (bf16[16,128,128]{2,1,0:T(8,128)(2,1)}, f32[16,128,128]{2,1,0:T(8,128)}) custom-call(s32[16]{0:T(128)} %bitcast.13, s32[16]{0:T(128)} %copy-done.4, s32[66]{0:T(128)} %copy-done.7, bf16[1024,2048]{1,0:T(8,128)(2,1)} %bitcast.8, bf16[1024,2048]{1,0:T(8,128)(2,1)} %collective-permute-done.4.other_rows), custom_call_target="tpu_custom_call" | custom-call | flops 2147483648 | bytes 9961472 | tf_op jit(solution)/shard_map/tile_chunk/pallas_call | solution.py:210
  31.6 0.6 collective-permute-start.6
  32.2 2.4 %collective-permute-done.5 = bf16[16,128,128]{2,1,0:T(8,128)(2,1)S(1)} collective-permute-done((bf16[16,128,128]{2,1,0:T(8,128)(2,1)}, bf16[16,128,128]{2,1,0:T(8,128)(2,1)S(1)}, u32[]{:S(2)}, u32[]{:S(2)}) %collective-permute-start.5) | collective-permute-done | bytes 524320 | tf_op jit(solution)/shard_map/ppermute | solution.py:249
  34.7 0.5 collective-permute-start.7
  35.2 12.6 %tile_chunk.5 = (bf16[16,128,128]{2,1,0:T(8,128)(2,1)}, f32[16,128,128]{2,1,0:T(8,128)}) custom-call(s32[16]{0:T(128)} %bitcast.14, s32[16]{0:T(128)} %copy-done.4, s32[66]{0:T(128)} %copy-done.6, bf16[1024,2048]{1,0:T(8,128)(2,1)} %bitcast.9, bf16[1024,2048]{1,0:T(8,128)(2,1)} %collective-permute-done.4.other_rows), custom_call_target="tpu_custom_call" | custom-call | flops 2147483648 | bytes 9961472 | tf_op jit(solution)/shard_map/tile_chunk/pallas_call | solution.py:210
  47.8 2.3 %collective-permute-start.8 = (bf16[16,128,128]{2,1,0:T(8,128)(2,1)}, bf16[16,128,128]{2,1,0:T(8,128)(2,1)S(1)}, u32[]{:S(2)}, u32[]{:S(2)}) collective-permute-start(bf16[16,128,128]{2,1,0:T(8,128)(2,1)} %get-tuple-element.37), channel_id=1, source_target_pairs={{0,2},{1,3},{2,0},{3,1},{4,6},{5,7},{6,4},{7,5},{8,10},{9,11},{10,... | collective-permute-start | bytes 1572872 | tf_op jit(solution)/shard_map/ppermute | solution.py:249
  50.1 0.2 add_convert_fusion.2
  50.3 1.7 %collective-permute-start.10 = (bf16[16,128,128]{2,1,0:T(8,128)(2,1)S(1)}, bf16[16,128,128]{2,1,0:T(8,128)(2,1)S(1)}, u32[]{:S(2)}, u32[]{:S(2)}) collective-permute-start(bf16[16,128,128]{2,1,0:T(8,128)(2,1)S(1)} %add_convert_fusion.2), channel_id=1, source_target_pairs={{0,8},{4,12},{8,0},{12,4},{1,9},{5,13},{9,1},{13,5},{2,10},{6,14},... | collective-permute-start | bytes 1572872 | tf_op jit(solution)/shard_map/ppermute | solution.py:249
  52.0 9.2 %tile_chunk.7 = (bf16[16,128,128]{2,1,0:T(8,128)(2,1)}, f32[16,128,128]{2,1,0:T(8,128)}) custom-call(s32[16]{0:T(128)} %bitcast.15, s32[16]{0:T(128)} %copy-done.4, s32[66]{0:T(128)} %copy-done.5, bf16[1024,2048]{1,0:T(8,128)(2,1)} %bitcast.10, bf16[1024,2048]{1,0:T(8,128)(2,1)} %collective-permute-done.4.other_rows), custom_call_target="tpu_custom_call" | custom-call | flops 2147483648 | bytes 9961472 | tf_op jit(solution)/shard_map/tile_chunk/pallas_call | solution.py:210
  61.2 0.1 add_convert_fusion.1
  61.4 5.2 %collective-permute-start.9 = (bf16[16,128,128]{2,1,0:T(8,128)(2,1)S(1)}, bf16[16,128,128]{2,1,0:T(8,128)(2,1)S(1)}, u32[]{:S(2)}, u32[]{:S(2)}) collective-permute-start(bf16[16,128,128]{2,1,0:T(8,128)(2,1)S(1)} %add_convert_fusion.1), channel_id=1, source_target_pairs={{0,4},{4,0},{8,12},{12,8},{1,5},{5,1},{9,13},{13,9},{2,6},{6,2},{1... | collective-permute-start | bytes 1572872 | tf_op jit(solution)/shard_map/ppermute | solution.py:249
  66.7 6.5 %collective-permute-done.10 = bf16[16,128,128]{2,1,0:T(8,128)(2,1)S(1)} collective-permute-done((bf16[16,128,128]{2,1,0:T(8,128)(2,1)S(1)}, bf16[16,128,128]{2,1,0:T(8,128)(2,1)S(1)}, u32[]{:S(2)}, u32[]{:S(2)}) %collective-permute-start.10) | collective-permute-done | bytes 524320 | tf_op jit(solution)/shard_map/ppermute | solution.py:249
  73.1 11.1 %collective-permute-done.9 = bf16[16,128,128]{2,1,0:T(8,128)(2,1)S(1)} collective-permute-done((bf16[16,128,128]{2,1,0:T(8,128)(2,1)S(1)}, bf16[16,128,128]{2,1,0:T(8,128)(2,1)S(1)}, u32[]{:S(2)}, u32[]{:S(2)}) %collective-permute-start.9) | collective-permute-done | bytes 524320 | tf_op jit(solution)/shard_map/ppermute | solution.py:249
  84.2 0.1 convert_add_fusion
  84.4 1.0 %fusion = bf16[1,16,128,128]{3,2,1,0:T(8,128)(2,1)} fusion(f32[16,128,128]{2,1,0:T(8,128)S(1)} %convert_add_fusion, f32[16,128,128]{2,1,0:T(8,128)S(1)} %copy-done, bf16[16,128,128]{2,1,0:T(8,128)(2,1)S(1)} %collective-permute-done.11), kind=kLoop, calls=%fused_computation.5 | loop fusion | flops 1048576 | bytes 3145728 | tf_op jit(solution)/shard_map/broadcast_in_dim | solution.py:287
  (28 shorter events, 0.2 us)
Async XLA Ops:
  0.0 10.9 %collective-permute-start.4 = (bf16[1024,2048]{1,0:T(8,128)(2,1)}, bf16[1024,2048]{1,0:T(8,128)(2,1)}, u32[]{:S(2)}, u32[]{:S(2)}) collective-permute-start(bf16[1024,2048]{1,0:T(8,128)(2,1)} %bitcast.6), channel_id=1, source_target_pairs={{0,1},{1,0},{2,3},{3,2},{4,5},{5,4},{6,7},{7,6},{8,9},{9,8},{10,11... | collective-permute-start | bytes 12582920 | tf_op jit(solution)/shard_map/ppermute | solution.py:249
  1.8 18.9 %copy-start.5 = (s32[66]{0:T(128)}, s32[66]{0:T(128)S(1)}, u32[]{:S(2)}) copy-start(s32[66]{0:T(128)S(1)} %pad_add_fusion.codes) | copy-start | bytes 796
  1.8 6.1 %collective-permute-start.1 = (s32[66]{0:T(128)S(1)}, s32[66]{0:T(128)S(1)}, u32[]{:S(2)}, u32[]{:S(2)}) collective-permute-start(s32[66]{0:T(128)S(1)} %pad_add_fusion.codes), channel_id=1, source_target_pairs={{0,12},{4,8},{8,4},{12,0},{1,13},{5,9},{9,5},{13,1},{2,14},{6,10},... | collective-permute-start | bytes 800 | tf_op jit(solution)/shard_map/ppermute | solution.py:249
  6.4 4.4 %collective-permute-start.2 = (s32[66]{0:T(128)S(1)}, s32[66]{0:T(128)S(1)}, u32[]{:S(2)}, u32[]{:S(2)}) collective-permute-start(s32[66]{0:T(128)S(1)} %pad_add_fusion.codes), channel_id=1, source_target_pairs={{0,8},{4,12},{8,0},{12,4},{1,9},{5,13},{9,1},{13,5},{2,10},{6,14},... | collective-permute-start | bytes 800 | tf_op jit(solution)/shard_map/ppermute | solution.py:249
  6.4 4.4 %collective-permute-start.3 = (s32[66]{0:T(128)S(1)}, s32[66]{0:T(128)S(1)}, u32[]{:S(2)}, u32[]{:S(2)}) collective-permute-start(s32[66]{0:T(128)S(1)} %pad_add_fusion.codes), channel_id=1, source_target_pairs={{0,4},{4,0},{8,12},{12,8},{1,5},{5,1},{9,13},{13,9},{2,6},{6,2},{1... | collective-permute-start | bytes 800 | tf_op jit(solution)/shard_map/ppermute | solution.py:249
  7.1 3.8 %collective-permute-start = (s32[16]{0:T(128)}, s32[16]{0:T(128)S(1)}, u32[]{:S(2)}, u32[]{:S(2)}) collective-permute-start(s32[16]{0:T(128)} %bitcast.11), channel_id=1, source_target_pairs={{0,1},{1,0},{2,3},{3,2},{4,5},{5,4},{6,7},{7,6},{8,9},{9,8},{10,11... | collective-permute-start | bytes 200 | tf_op jit(solution)/shard_map/ppermute | solution.py:249
  8.0 3.0 %copy-start.8 = (s32[66]{0:T(128)}, s32[66]{0:T(128)S(1)}, u32[]{:S(2)}) copy-start(s32[66]{0:T(128)S(1)} %collective-permute-done.1.codes) | copy-start | bytes 796
  10.9 11.4 %copy-start.7 = (s32[66]{0:T(128)}, s32[66]{0:T(128)S(1)}, u32[]{:S(2)}) copy-start(s32[66]{0:T(128)S(1)} %collective-permute-done.2.codes) | copy-start | bytes 796
  10.9 24.4 %copy-start.6 = (s32[66]{0:T(128)}, s32[66]{0:T(128)S(1)}, u32[]{:S(2)}) copy-start(s32[66]{0:T(128)S(1)} %collective-permute-done.3.codes) | copy-start | bytes 796
  10.9 0.5 copy-start.4
  20.7 13.8 %copy-start.3 = (f32[16,128,128]{2,1,0:T(8,128)S(1)}, f32[16,128,128]{2,1,0:T(8,128)}, u32[]{:S(2)}) copy-start(f32[16,128,128]{2,1,0:T(8,128)} %get-tuple-element.26) | copy-start | bytes 3145732
  20.8 13.8 %collective-permute-start.5 = (bf16[16,128,128]{2,1,0:T(8,128)(2,1)}, bf16[16,128,128]{2,1,0:T(8,128)(2,1)S(1)}, u32[]{:S(2)}, u32[]{:S(2)}) collective-permute-start(bf16[16,128,128]{2,1,0:T(8,128)(2,1)} %get-tuple-element.27), channel_id=1, source_target_pairs={{0,2},{1,3},{2,0},{3,1},{4,6},{5,7},{6,4},{7,5},{8,10},{9,11},{10,... | collective-permute-start | bytes 1572872 | tf_op jit(solution)/shard_map/ppermute | solution.py:249
  31.6 18.5 %collective-permute-start.6 = (bf16[16,128,128]{2,1,0:T(8,128)(2,1)}, bf16[16,128,128]{2,1,0:T(8,128)(2,1)S(1)}, u32[]{:S(2)}, u32[]{:S(2)}) collective-permute-start(bf16[16,128,128]{2,1,0:T(8,128)(2,1)} %get-tuple-element.32), channel_id=1, source_target_pairs={{0,2},{1,3},{2,0},{3,1},{4,6},{5,7},{6,4},{7,5},{8,10},{9,11},{10,... | collective-permute-start | bytes 1572872 | tf_op jit(solution)/shard_map/ppermute | solution.py:249
  34.7 15.4 %copy-start.1 = (f32[16,128,128]{2,1,0:T(8,128)S(1)}, f32[16,128,128]{2,1,0:T(8,128)}, u32[]{:S(2)}) copy-start(f32[16,128,128]{2,1,0:T(8,128)} %get-tuple-element.31) | copy-start | bytes 3145732
  34.7 15.4 %collective-permute-start.7 = (bf16[16,128,128]{2,1,0:T(8,128)(2,1)S(1)}, bf16[16,128,128]{2,1,0:T(8,128)(2,1)S(1)}, u32[]{:S(2)}, u32[]{:S(2)}) collective-permute-start(bf16[16,128,128]{2,1,0:T(8,128)(2,1)S(1)} %add_convert_fusion.3), channel_id=1, source_target_pairs={{0,4},{4,0},{8,12},{12,8},{1,5},{5,1},{9,13},{13,9},{2,6},{6,2},{1... | collective-permute-start | bytes 1572872 | tf_op jit(solution)/shard_map/ppermute | solution.py:249
  47.8 13.4 %collective-permute-start.8 = (bf16[16,128,128]{2,1,0:T(8,128)(2,1)}, bf16[16,128,128]{2,1,0:T(8,128)(2,1)S(1)}, u32[]{:S(2)}, u32[]{:S(2)}) collective-permute-start(bf16[16,128,128]{2,1,0:T(8,128)(2,1)} %get-tuple-element.37), channel_id=1, source_target_pairs={{0,2},{1,3},{2,0},{3,1},{4,6},{5,7},{6,4},{7,5},{8,10},{9,11},{10,... | collective-permute-start | bytes 1572872 | tf_op jit(solution)/shard_map/ppermute | solution.py:249
  50.3 10.9 %copy-start.2 = (f32[16,128,128]{2,1,0:T(8,128)S(1)}, f32[16,128,128]{2,1,0:T(8,128)}, u32[]{:S(2)}) copy-start(f32[16,128,128]{2,1,0:T(8,128)} %get-tuple-element.36) | copy-start | bytes 3145732
  50.3 22.8 %collective-permute-start.10 = (bf16[16,128,128]{2,1,0:T(8,128)(2,1)S(1)}, bf16[16,128,128]{2,1,0:T(8,128)(2,1)S(1)}, u32[]{:S(2)}, u32[]{:S(2)}) collective-permute-start(bf16[16,128,128]{2,1,0:T(8,128)(2,1)S(1)} %add_convert_fusion.2), channel_id=1, source_target_pairs={{0,8},{4,12},{8,0},{12,4},{1,9},{5,13},{9,1},{13,5},{2,10},{6,14},... | collective-permute-start | bytes 1572872 | tf_op jit(solution)/shard_map/ppermute | solution.py:249
  61.2 23.2 %copy-start = (f32[16,128,128]{2,1,0:T(8,128)S(1)}, f32[16,128,128]{2,1,0:T(8,128)}, u32[]{:S(2)}) copy-start(f32[16,128,128]{2,1,0:T(8,128)} %get-tuple-element.40) | copy-start | bytes 3145732
  61.4 22.9 %collective-permute-start.9 = (bf16[16,128,128]{2,1,0:T(8,128)(2,1)S(1)}, bf16[16,128,128]{2,1,0:T(8,128)(2,1)S(1)}, u32[]{:S(2)}, u32[]{:S(2)}) collective-permute-start(bf16[16,128,128]{2,1,0:T(8,128)(2,1)S(1)} %add_convert_fusion.1), channel_id=1, source_target_pairs={{0,4},{4,0},{8,12},{12,8},{1,5},{5,1},{9,13},{13,9},{2,6},{6,2},{1... | collective-permute-start | bytes 1572872 | tf_op jit(solution)/shard_map/ppermute | solution.py:249
  66.6 17.8 %collective-permute-start.11 = (bf16[16,128,128]{2,1,0:T(8,128)(2,1)}, bf16[16,128,128]{2,1,0:T(8,128)(2,1)S(1)}, u32[]{:S(2)}, u32[]{:S(2)}) collective-permute-start(bf16[16,128,128]{2,1,0:T(8,128)(2,1)} %get-tuple-element.41), channel_id=1, source_target_pairs={{0,2},{1,3},{2,0},{3,1},{4,6},{5,7},{6,4},{7,5},{8,10},{9,11},{10,... | collective-permute-start | bytes 1572872 | tf_op jit(solution)/shard_map/ppermute | solution.py:249

commit v8 on v7

--- a/solution.py
+++ b/solution.py
@@ -11,6 +11,7 @@
 TILE = 128
 CAP = 8
 GROUP = 256
+PART = 512
 ROWS = 4
 
 
@@ -78,9 +79,7 @@
 
 
 def chunk_kernel(occ_local, share, own_owner, other_owner, codes, own_rows, other_rows, *refs):
-    send_out, keep_out = refs[:2]
-    stage, packed_rows, turned, pick, sums, send_ref, left_at, right_at = refs[2:10]
-    arrived, left_off = refs[10:]
+    send_ref, keep_ref, packed_rows, turned, pick, partial_send, left_at, right_at = refs
     rows_total, domain = own_rows.shape
     blocks = domain // TILE
     groups = rows_total // GROUP
@@ -88,17 +87,6 @@
     held = per_group * CAP
     pair_total = share * ROWS
     live, batch = codes[pair_total], codes[pair_total + 1]
-
-    def slab_copy(place):
-        slab = own_rows if place < groups else other_rows
-        return pltpu.make_async_copy(
-            slab.at[pl.ds(place % groups * GROUP, GROUP), :],
-            stage.at[pl.ds(place * GROUP, GROUP), :],
-            arrived.at[place],
-        )
-
-    for place in range(2 * groups):
-        slab_copy(place).start()
 
     lane = lax.broadcasted_iota(jnp.int32, (1, GROUP), 1)
     orbital_of = lane & (occ_local - 1)
@@ -132,71 +120,65 @@
         return carry
 
     lax.fori_loop(0, 2 * share, decode, 0)
-    sums[...] = jnp.zeros(sums.shape, jnp.float32)
-    turned[domain:, :] = jnp.zeros((TILE, GROUP), jnp.bfloat16)
-
-    def pack(place, carry):
-        rows = pl.ds(pl.multiple_of(place * GROUP, GROUP), GROUP)
-        pltpu.make_async_copy(
-            own_rows.at[pl.ds(0, GROUP), :], stage.at[rows, :], arrived.at[place]
-        ).wait()
-        source = place // groups
-        before = jnp.minimum(place, groups) * counts[0]
-        before = before + jnp.maximum(place - groups, 0) * counts[1]
-        start = pl.multiple_of(before * per_group, per_group)
-        for column in range(0, domain, 2 * TILE):
-            columns = slice(column, column + 2 * TILE)
-            packed = jnp.dot(
-                pick[source], stage[rows, columns], preferred_element_type=jnp.float32
-            )
-            packed_rows[pl.ds(start, held), columns] = packed.astype(jnp.bfloat16)
-        return carry
-
-    lax.fori_loop(0, 2 * groups, pack, 0)
-    filled = pl.multiple_of((counts[0] + counts[1]) * groups * per_group, per_group)
-    packed_rows[pl.ds(filled, GROUP), :] = jnp.zeros((GROUP, domain), jnp.bfloat16)
-    parts = jnp.maximum((filled + GROUP - 1) // GROUP, 1)
+    turned[domain:, :] = jnp.zeros((TILE, PART), jnp.bfloat16)
+
+    before = jnp.int32(0)
+    for source, slab in enumerate((own_rows, other_rows)):
+        def pack(group, carry, source=source, slab=slab, before=before):
+            rows = pl.ds(pl.multiple_of(group * GROUP, GROUP), GROUP)
+            start = pl.multiple_of((before + group * counts[source]) * per_group, per_group)
+            for column in range(0, domain, 2 * TILE):
+                columns = slice(column, column + 2 * TILE)
+                packed = jnp.dot(
+                    pick[source], slab[rows, columns], preferred_element_type=jnp.float32
+                )
+                packed_rows[pl.ds(start, held), columns] = packed.astype(jnp.bfloat16)
+            return carry
+
+        lax.fori_loop(0, groups, pack, 0)
+        before = before + groups * counts[source]
+
+    filled = pl.multiple_of(before * per_group, per_group)
+    packed_rows[pl.ds(filled, PART), :] = jnp.zeros((PART, domain), jnp.bfloat16)
+    parts = jnp.maximum((filled + PART - 1) // PART, 1)
 
     width = math.gcd(4, share)
 
-    def out_copies(turn_at):
-        sends = pl.ds(turn_at * width, width)
-        keeps = pl.ds(share + turn_at * width, width)
-        return (
-            pltpu.make_async_copy(send_ref.at[sends], send_out.at[sends], left_off.at[0, turn_at]),
-            pltpu.make_async_copy(sums.at[keeps], keep_out.at[sends], left_off.at[1, turn_at]),
-        )
-
-    def add_part(part, carry):
-        rows = pl.ds(pl.multiple_of(part * GROUP, GROUP), GROUP)
+    def add_part(part, fresh):
+        rows = pl.ds(pl.multiple_of(part * PART, PART), PART)
         for column in range(0, domain, TILE):
             columns = slice(column, column + TILE)
             turned[columns, :] = packed_rows[rows, columns].T
 
-        for turn_at in range(share // width):
-            sends = slice(turn_at * width, (turn_at + 1) * width)
+        def product(at):
+            left = pl.multiple_of(left_at[at], TILE)
+            right = pl.multiple_of(right_at[at], TILE)
+            return jnp.dot(
+                turned[pl.ds(left, TILE), :],
+                packed_rows[rows, pl.ds(right, TILE)],
+                preferred_element_type=jnp.float32,
+            )
+
+        def several(turn_at, carry):
             for offset in range(width):
-                for at in (sends.start + offset, share + sends.start + offset):
-                    left = pl.multiple_of(left_at[at], TILE)
-                    right = pl.multiple_of(right_at[at], TILE)
-                    sums[at] += jnp.dot(
-                        turned[pl.ds(left, TILE), :],
-                        packed_rows[rows, pl.ds(right, TILE)],
-                        preferred_element_type=jnp.float32,
-                    )
-
-            @pl.when(part == parts - 1)
-            def _(turn_at=turn_at, sends=sends):
-                send_ref[sends] = sums[sends].astype(send_ref.dtype)
-                for copy in out_copies(turn_at):
-                    copy.start()
-
+                at = turn_at * width + offset
+                sent, kept = product(at), product(share + at)
+                if not fresh:
+                    sent, kept = sent + partial_send[at], kept + keep_ref[at]
+                send_ref[at] = sent.astype(send_ref.dtype)
+                partial_send[at] = sent
+                keep_ref[at] = kept
+            return carry
+
+        lax.fori_loop(0, share // width, several, 0)
+
+    add_part(0, True)
+
+    def more(part, carry):
+        add_part(part, False)
         return carry
 
-    lax.fori_loop(0, parts, add_part, 0)
-    for turn_at in range(share // width):
-        for copy in out_copies(turn_at):
-            copy.wait()
+    lax.fori_loop(1, parts, more, 0)
 
 
 def tile_chunk(owners, codes, own_rows, other_rows, occ_local, share):
@@ -205,29 +187,25 @@
     held = GROUP // occ_local * CAP
     depth = 2 * groups * held
     tiles = (share, TILE, TILE)
-    anywhere = pl.BlockSpec(memory_space=pl.ANY)
+    in_vmem = pl.BlockSpec(memory_space=pltpu.VMEM)
     in_smem = pl.BlockSpec(memory_space=pltpu.SMEM)
     return pl.pallas_call(
         functools.partial(chunk_kernel, occ_local, share),
-        in_specs=[in_smem] * 3 + [anywhere] * 2,
-        out_specs=[anywhere, anywhere],
+        in_specs=[in_smem] * 3 + [in_vmem] * 2,
+        out_specs=[in_vmem, in_vmem],
         scratch_shapes=[
-            pltpu.VMEM((2 * rows_total, domain), jnp.bfloat16),
-            pltpu.VMEM((depth + GROUP, domain), jnp.bfloat16),
-            pltpu.VMEM((domain + TILE, GROUP), jnp.bfloat16),
+            pltpu.VMEM((depth + PART, domain), jnp.bfloat16),
+            pltpu.VMEM((domain + TILE, PART), jnp.bfloat16),
             pltpu.VMEM((2, held, GROUP), jnp.bfloat16),
-            pltpu.VMEM((2 * share, TILE, TILE), jnp.float32),
-            pltpu.VMEM(tiles, jnp.bfloat16),
+            pltpu.VMEM(tiles, jnp.float32),
             pltpu.SMEM((2 * share,), jnp.int32),
             pltpu.SMEM((2 * share,), jnp.int32),
-            pltpu.SemaphoreType.DMA((2 * groups,)),
-            pltpu.SemaphoreType.DMA((2, share)),
         ],
         out_shape=[
             jax.ShapeDtypeStruct(tiles, jnp.bfloat16),
             jax.ShapeDtypeStruct(tiles, jnp.float32),
         ],
-        compiler_params=pltpu.CompilerParams(vmem_limit_bytes=56 * 1024 * 1024),
+        compiler_params=pltpu.CompilerParams(vmem_limit_bytes=24 * 1024 * 1024),
         cost_estimate=pl.CostEstimate(
             flops=4 * share * TILE * TILE * depth + 2 * depth * GROUP * domain,
             bytes_accessed=4 * rows_total * domain + 6 * share * TILE * TILE,

time: 85.9 us -> 85.5 us (level); the launches traced: 85.4 us -> 86.4 us
  local copies, waits for them, and re-layouts: 0.55 us -> 2.84 us
  Pallas kernels: 40.4 us -> 38.5 us
  waiting for transfers between devices: 23.8 us -> 25.1 us
    unnamed x18 -> x6, local copies, waits for them, and re-layouts: 0.55 us -> 2.84 us
    pallas_call x4, Pallas kernels: 40.4 us -> 38.5 us  [tile_chunk(): pl.pallas_call(functools.partial(chunk_kernel, occ_local, share), in_spec...]
    ppermute x12, waiting for transfers between devices: 23.8 us -> 25.1 us  [exchange(): return lax.ppermute(array, axis, [(i, i ^ bits) for i in range(size)])]
  transfers between devices with their start and end apart: 12 -> 12, of which waited for: 5 -> 5; matrix products, arithmetic and copies ran while one was open for 2% -> 2% of each run, Pallas kernels for 36% -> 34%
where the time goes in v8:
time: 85.5 us; the launch traced here: 86.4 us
  Pallas kernels  38.5 us (45%)
  waiting for transfers between devices  25.1 us (29%)
  starting transfers between devices  16.9 us (20%)
  local copies, waits for them, and re-layouts  2.84 us (3%)
  other arithmetic  2.31 us (3%)
    pallas_call x4, Pallas kernels, tile_chunk(): pl.pallas_call(functools.partial(chunk_kernel, occ_local, share), in_spec...  38.5 us
    ppermute x12, waiting for transfers between devices, exchange(): return lax.ppermute(array, axis, [(i, i ^ bits) for i in range(size)])  25.1 us
    ppermute x12, starting transfers between devices, exchange(): return lax.ppermute(array, axis, [(i, i ^ bits) for i in range(size)])  16.9 us
    unnamed x6, local copies, waits for them, and re-layouts  2.84 us
  transfers between devices with their start and end apart: 12, of which 5 were waited for; matrix products, arithmetic and copies ran while one was open for 2% of the time, Pallas kernels for 34%

profile of v8, /device:TPU:0, one launch (start us, length us, event | category | flops | bytes accessed | tf_op | source)
XLA Modules:
  0.0 86.4 jit_solution(3719447724919951166)
XLA Ops:
  0.0 0.5 collective-permute-start.4
  1.1 0.7 pad_add_fusion.codes
  1.8 4.6 %collective-permute-start.1 = (s32[66]{0:T(128)S(1)}, s32[66]{0:T(128)S(1)}, u32[]{:S(2)}, u32[]{:S(2)}) collective-permute-start(s32[66]{0:T(128)S(1)} %pad_add_fusion.codes), channel_id=1, source_target_pairs={{0,12},{4,8},{8,4},{12,0},{1,13},{5,9},{9,5},{13,1},{2,14},{6,10},... | collective-permute-start | bytes 800 | tf_op jit(solution)/shard_map/ppermute | solution.py:227
  6.4 0.6 collective-permute-start.3
  7.0 0.9 %collective-permute-done.1.codes = s32[66]{0:T(128)S(1)} collective-permute-done((s32[66]{0:T(128)S(1)}, s32[66]{0:T(128)S(1)}, u32[]{:S(2)}, u32[]{:S(2)}) %collective-permute-start.1) | collective-permute-done | bytes 296 | tf_op jit(solution)/shard_map/ppermute | solution.py:227
  8.0 2.9 %collective-permute-done.2.codes = s32[66]{0:T(128)S(1)} collective-permute-done((s32[66]{0:T(128)S(1)}, s32[66]{0:T(128)S(1)}, u32[]{:S(2)}, u32[]{:S(2)}) %collective-permute-start.2) | collective-permute-done | bytes 296 | tf_op jit(solution)/shard_map/ppermute | solution.py:227
  10.9 2.2 %copy-done = bf16[64,16,2048]{2,1,0:T(8,128)(2,1)S(1)} copy-done((bf16[64,16,2048]{2,1,0:T(8,128)(2,1)S(1)}, bf16[64,16,2048]{2,1,0:T(8,128)(2,1)}, u32[]{:S(2)}) %copy-start) | copy-done | bytes 4194328
  13.1 0.7 copy-done.2
  13.7 9.0 %tile_chunk.4 = (bf16[16,128,128]{2,1,0:T(8,128)(2,1)S(1)}, f32[16,128,128]{2,1,0:T(8,128)S(1)}) custom-call(s32[16]{0:T(128)S(1)} %bitcast.12, s32[16]{0:T(128)S(1)} %collective-permute-done.other_owner, s32[66]{0:T(128)S(1)} %collective-permute-done.1.codes, bf16[1024,2048]{1,0:T(8,128)(2,1)S(1)} %bitcast.7, ...), custom_call_target="tpu_custom_call" | custom-call | flops 2147483648 | bytes 9961472 | tf_op jit(solution)/shard_map/tile_chunk/pallas_call | solution.py:192
  22.8 1.6 %collective-permute-start.5 = (bf16[16,128,128]{2,1,0:T(8,128)(2,1)S(1)}, bf16[16,128,128]{2,1,0:T(8,128)(2,1)S(1)}, u32[]{:S(2)}, u32[]{:S(2)}) collective-permute-start(bf16[16,128,128]{2,1,0:T(8,128)(2,1)S(1)} %get-tuple-element.27), channel_id=1, source_target_pairs={{0,2},{1,3},{2,0},{3,1},{4,6},{5,7},{6,4},{7,5},{8,10},{9,11},{10,... | collective-permute-start | bytes 1572872 | tf_op jit(solution)/shard_map/ppermute | solution.py:227
  24.3 8.9 %tile_chunk.6 = (bf16[16,128,128]{2,1,0:T(8,128)(2,1)S(1)}, f32[16,128,128]{2,1,0:T(8,128)S(1)}) custom-call(s32[16]{0:T(128)S(1)} %bitcast.13, s32[16]{0:T(128)S(1)} %collective-permute-done.other_owner, s32[66]{0:T(128)S(1)} %collective-permute-done.2.codes, bf16[1024,2048]{1,0:T(8,128)(2,1)S(1)} %bitcast.8, ...), custom_call_target="tpu_custom_call" | custom-call | flops 2147483648 | bytes 9961472 | tf_op jit(solution)/shard_map/tile_chunk/pallas_call | solution.py:192
  33.2 0.6 collective-permute-start.6
  33.8 3.0 %collective-permute-done.5 = bf16[16,128,128]{2,1,0:T(8,128)(2,1)S(1)} collective-permute-done((bf16[16,128,128]{2,1,0:T(8,128)(2,1)S(1)}, bf16[16,128,128]{2,1,0:T(8,128)(2,1)S(1)}, u32[]{:S(2)}, u32[]{:S(2)}) %collective-permute-start.5) | collective-permute-done | bytes 524320 | tf_op jit(solution)/shard_map/ppermute | solution.py:227
  36.9 0.6 collective-permute-start.7
  37.5 11.7 %tile_chunk.5 = (bf16[16,128,128]{2,1,0:T(8,128)(2,1)S(1)}, f32[16,128,128]{2,1,0:T(8,128)S(1)}) custom-call(s32[16]{0:T(128)S(1)} %bitcast.14, s32[16]{0:T(128)S(1)} %collective-permute-done.other_owner, s32[66]{0:T(128)S(1)} %collective-permute-done.3.codes, bf16[1024,2048]{1,0:T(8,128)(2,1)S(1)} %bitcast.9, ...), custom_call_target="tpu_custom_call" | custom-call | flops 2147483648 | bytes 9961472 | tf_op jit(solution)/shard_map/tile_chunk/pallas_call | solution.py:192
  49.2 2.0 %collective-permute-start.8 = (bf16[16,128,128]{2,1,0:T(8,128)(2,1)S(1)}, bf16[16,128,128]{2,1,0:T(8,128)(2,1)S(1)}, u32[]{:S(2)}, u32[]{:S(2)}) collective-permute-start(bf16[16,128,128]{2,1,0:T(8,128)(2,1)S(1)} %get-tuple-element.37), channel_id=1, source_target_pairs={{0,2},{1,3},{2,0},{3,1},{4,6},{5,7},{6,4},{7,5},{8,10},{9,11},{10,... | collective-permute-start | bytes 1572872 | tf_op jit(solution)/shard_map/ppermute | solution.py:227
  51.2 0.2 add_convert_fusion.2
  51.4 1.8 %collective-permute-start.10 = (bf16[16,128,128]{2,1,0:T(8,128)(2,1)S(1)}, bf16[16,128,128]{2,1,0:T(8,128)(2,1)S(1)}, u32[]{:S(2)}, u32[]{:S(2)}) collective-permute-start(bf16[16,128,128]{2,1,0:T(8,128)(2,1)S(1)} %add_convert_fusion.2), channel_id=1, source_target_pairs={{0,8},{4,12},{8,0},{12,4},{1,9},{5,13},{9,1},{13,5},{2,10},{6,14},... | collective-permute-start | bytes 1572872 | tf_op jit(solution)/shard_map/ppermute | solution.py:227
  53.3 8.9 %tile_chunk.7 = (bf16[16,128,128]{2,1,0:T(8,128)(2,1)S(1)}, f32[16,128,128]{2,1,0:T(8,128)S(1)}) custom-call(s32[16]{0:T(128)S(1)} %bitcast.15, s32[16]{0:T(128)S(1)} %collective-permute-done.other_owner, s32[66]{0:T(128)S(1)} %pad_add_fusion.codes, bf16[1024,2048]{1,0:T(8,128)(2,1)S(1)} %bitcast.10, bf16[1024,2048]{1,0:T(8,128)(2,1)} %collective-permute-done.4.other_rows), custom_call_target="tpu_custom_call" | custom-call | flops 2147483648 | bytes 9961472 | tf_op jit(solution)/shard_map/tile_chunk/pallas_call | solution.py:192
  62.2 0.1 add_convert_fusion.1
  62.3 4.7 %collective-permute-start.9 = (bf16[16,128,128]{2,1,0:T(8,128)(2,1)S(1)}, bf16[16,128,128]{2,1,0:T(8,128)(2,1)S(1)}, u32[]{:S(2)}, u32[]{:S(2)}) collective-permute-start(bf16[16,128,128]{2,1,0:T(8,128)(2,1)S(1)} %add_convert_fusion.1), channel_id=1, source_target_pairs={{0,4},{4,0},{8,12},{12,8},{1,5},{5,1},{9,13},{13,9},{2,6},{6,2},{1... | collective-permute-start | bytes 1572872 | tf_op jit(solution)/shard_map/ppermute | solution.py:227
  67.1 7.1 %collective-permute-done.10 = bf16[16,128,128]{2,1,0:T(8,128)(2,1)S(1)} collective-permute-done((bf16[16,128,128]{2,1,0:T(8,128)(2,1)S(1)}, bf16[16,128,128]{2,1,0:T(8,128)(2,1)S(1)}, u32[]{:S(2)}, u32[]{:S(2)}) %collective-permute-start.10) | collective-permute-done | bytes 524320 | tf_op jit(solution)/shard_map/ppermute | solution.py:227
  74.1 11.1 %collective-permute-done.9 = bf16[16,128,128]{2,1,0:T(8,128)(2,1)S(1)} collective-permute-done((bf16[16,128,128]{2,1,0:T(8,128)(2,1)S(1)}, bf16[16,128,128]{2,1,0:T(8,128)(2,1)S(1)}, u32[]{:S(2)}, u32[]{:S(2)}) %collective-permute-start.9) | collective-permute-done | bytes 524320 | tf_op jit(solution)/shard_map/ppermute | solution.py:227
  85.4 1.0 %fusion = bf16[1,16,128,128]{3,2,1,0:T(8,128)(2,1)} fusion(f32[16,128,128]{2,1,0:T(8,128)S(1)} %convert_add_fusion, f32[16,128,128]{2,1,0:T(8,128)S(1)} %get-tuple-element.40, bf16[16,128,128]{2,1,0:T(8,128)(2,1)S(1)} %collective-permute-done.11), kind=kLoop, calls=%fused_computation.5 | loop fusion | flops 1048576 | bytes 3145728 | tf_op jit(solution)/shard_map/broadcast_in_dim | solution.py:265
  (16 shorter events, 0.3 us)
Async XLA Ops:
  0.0 10.9 %collective-permute-start.4 = (bf16[1024,2048]{1,0:T(8,128)(2,1)}, bf16[1024,2048]{1,0:T(8,128)(2,1)}, u32[]{:S(2)}, u32[]{:S(2)}) collective-permute-start(bf16[1024,2048]{1,0:T(8,128)(2,1)} %bitcast.6), channel_id=1, source_target_pairs={{0,1},{1,0},{2,3},{3,2},{4,5},{5,4},{6,7},{7,6},{8,9},{9,8},{10,11... | collective-permute-start | bytes 12582920 | tf_op jit(solution)/shard_map/ppermute | solution.py:227
  1.8 6.1 %collective-permute-start.1 = (s32[66]{0:T(128)S(1)}, s32[66]{0:T(128)S(1)}, u32[]{:S(2)}, u32[]{:S(2)}) collective-permute-start(s32[66]{0:T(128)S(1)} %pad_add_fusion.codes), channel_id=1, source_target_pairs={{0,12},{4,8},{8,4},{12,0},{1,13},{5,9},{9,5},{13,1},{2,14},{6,10},... | collective-permute-start | bytes 800 | tf_op jit(solution)/shard_map/ppermute | solution.py:227
  6.4 4.4 %collective-permute-start.2 = (s32[66]{0:T(128)S(1)}, s32[66]{0:T(128)S(1)}, u32[]{:S(2)}, u32[]{:S(2)}) collective-permute-start(s32[66]{0:T(128)S(1)} %pad_add_fusion.codes), channel_id=1, source_target_pairs={{0,8},{4,12},{8,0},{12,4},{1,9},{5,13},{9,1},{13,5},{2,10},{6,14},... | collective-permute-start | bytes 800 | tf_op jit(solution)/shard_map/ppermute | solution.py:227
  6.4 4.4 %collective-permute-start.3 = (s32[66]{0:T(128)S(1)}, s32[66]{0:T(128)S(1)}, u32[]{:S(2)}, u32[]{:S(2)}) collective-permute-start(s32[66]{0:T(128)S(1)} %pad_add_fusion.codes), channel_id=1, source_target_pairs={{0,4},{4,0},{8,12},{12,8},{1,5},{5,1},{9,13},{13,9},{2,6},{6,2},{1... | collective-permute-start | bytes 800 | tf_op jit(solution)/shard_map/ppermute | solution.py:227
  7.0 3.9 %collective-permute-start = (s32[16]{0:T(128)}, s32[16]{0:T(128)S(1)}, u32[]{:S(2)}, u32[]{:S(2)}) collective-permute-start(s32[16]{0:T(128)} %bitcast.11), channel_id=1, source_target_pairs={{0,1},{1,0},{2,3},{3,2},{4,5},{5,4},{6,7},{7,6},{8,9},{9,8},{10,11... | collective-permute-start | bytes 200 | tf_op jit(solution)/shard_map/ppermute | solution.py:227
  10.9 2.2 %copy-start = (bf16[64,16,2048]{2,1,0:T(8,128)(2,1)S(1)}, bf16[64,16,2048]{2,1,0:T(8,128)(2,1)}, u32[]{:S(2)}) copy-start(bf16[64,16,2048]{2,1,0:T(8,128)(2,1)} %param.4) | copy-start | bytes 12582916
  13.1 0.7 copy-start.2
  13.7 10.6 %copy-start.1 = (bf16[64,16,2048]{2,1,0:T(8,128)(2,1)S(1)}, bf16[64,16,2048]{2,1,0:T(8,128)(2,1)}, u32[]{:S(2)}) copy-start(bf16[64,16,2048]{2,1,0:T(8,128)(2,1)} %param.4) | copy-start | bytes 12582916
  22.8 14.0 %collective-permute-start.5 = (bf16[16,128,128]{2,1,0:T(8,128)(2,1)S(1)}, bf16[16,128,128]{2,1,0:T(8,128)(2,1)S(1)}, u32[]{:S(2)}, u32[]{:S(2)}) collective-permute-start(bf16[16,128,128]{2,1,0:T(8,128)(2,1)S(1)} %get-tuple-element.27), channel_id=1, source_target_pairs={{0,2},{1,3},{2,0},{3,1},{4,6},{5,7},{6,4},{7,5},{8,10},{9,11},{10,... | collective-permute-start | bytes 1572872 | tf_op jit(solution)/shard_map/ppermute | solution.py:227
  33.2 18.0 %collective-permute-start.6 = (bf16[16,128,128]{2,1,0:T(8,128)(2,1)S(1)}, bf16[16,128,128]{2,1,0:T(8,128)(2,1)S(1)}, u32[]{:S(2)}, u32[]{:S(2)}) collective-permute-start(bf16[16,128,128]{2,1,0:T(8,128)(2,1)S(1)} %get-tuple-element.32), channel_id=1, source_target_pairs={{0,2},{1,3},{2,0},{3,1},{4,6},{5,7},{6,4},{7,5},{8,10},{9,11},{10,... | collective-permute-start | bytes 1572872 | tf_op jit(solution)/shard_map/ppermute | solution.py:227
  36.9 14.3 %collective-permute-start.7 = (bf16[16,128,128]{2,1,0:T(8,128)(2,1)S(1)}, bf16[16,128,128]{2,1,0:T(8,128)(2,1)S(1)}, u32[]{:S(2)}, u32[]{:S(2)}) collective-permute-start(bf16[16,128,128]{2,1,0:T(8,128)(2,1)S(1)} %add_convert_fusion.3), channel_id=1, source_target_pairs={{0,4},{4,0},{8,12},{12,8},{1,5},{5,1},{9,13},{13,9},{2,6},{6,2},{1... | collective-permute-start | bytes 1572872 | tf_op jit(solution)/shard_map/ppermute | solution.py:227
  49.2 12.9 %collective-permute-start.8 = (bf16[16,128,128]{2,1,0:T(8,128)(2,1)S(1)}, bf16[16,128,128]{2,1,0:T(8,128)(2,1)S(1)}, u32[]{:S(2)}, u32[]{:S(2)}) collective-permute-start(bf16[16,128,128]{2,1,0:T(8,128)(2,1)S(1)} %get-tuple-element.37), channel_id=1, source_target_pairs={{0,2},{1,3},{2,0},{3,1},{4,6},{5,7},{6,4},{7,5},{8,10},{9,11},{10,... | collective-permute-start | bytes 1572872 | tf_op jit(solution)/shard_map/ppermute | solution.py:227
  51.4 22.7 %collective-permute-start.10 = (bf16[16,128,128]{2,1,0:T(8,128)(2,1)S(1)}, bf16[16,128,128]{2,1,0:T(8,128)(2,1)S(1)}, u32[]{:S(2)}, u32[]{:S(2)}) collective-permute-start(bf16[16,128,128]{2,1,0:T(8,128)(2,1)S(1)} %add_convert_fusion.2), channel_id=1, source_target_pairs={{0,8},{4,12},{8,0},{12,4},{1,9},{5,13},{9,1},{13,5},{2,10},{6,14},... | collective-permute-start | bytes 1572872 | tf_op jit(solution)/shard_map/ppermute | solution.py:227
  62.3 23.0 %collective-permute-start.9 = (bf16[16,128,128]{2,1,0:T(8,128)(2,1)S(1)}, bf16[16,128,128]{2,1,0:T(8,128)(2,1)S(1)}, u32[]{:S(2)}, u32[]{:S(2)}) collective-permute-start(bf16[16,128,128]{2,1,0:T(8,128)(2,1)S(1)} %add_convert_fusion.1), channel_id=1, source_target_pairs={{0,4},{4,0},{8,12},{12,8},{1,5},{5,1},{9,13},{13,9},{2,6},{6,2},{1... | collective-permute-start | bytes 1572872 | tf_op jit(solution)/shard_map/ppermute | solution.py:227
  67.0 18.4 %collective-permute-start.11 = (bf16[16,128,128]{2,1,0:T(8,128)(2,1)S(1)}, bf16[16,128,128]{2,1,0:T(8,128)(2,1)S(1)}, u32[]{:S(2)}, u32[]{:S(2)}) collective-permute-start(bf16[16,128,128]{2,1,0:T(8,128)(2,1)S(1)} %get-tuple-element.41), channel_id=1, source_target_pairs={{0,2},{1,3},{2,0},{3,1},{4,6},{5,7},{6,4},{7,5},{8,10},{9,11},{10,... | collective-permute-start | bytes 1572872 | tf_op jit(solution)/shard_map/ppermute | solution.py:227

commit v9 on v7

--- a/solution.py
+++ b/solution.py
@@ -11,7 +11,9 @@
 TILE = 128
 CAP = 8
 GROUP = 256
+PART = 512
 ROWS = 4
+SHIFT = 16
 
 
 def block_pairs(pair_codes, blocks):
@@ -79,15 +81,12 @@
 
 def chunk_kernel(occ_local, share, own_owner, other_owner, codes, own_rows, other_rows, *refs):
     send_out, keep_out = refs[:2]
-    stage, packed_rows, turned, pick, sums, send_ref, left_at, right_at = refs[2:10]
-    arrived, left_off = refs[10:]
+    stage, packed_rows, turned, pick, sums, send_ref, arrived, left_off = refs[2:]
     rows_total, domain = own_rows.shape
-    blocks = domain // TILE
     groups = rows_total // GROUP
     per_group = GROUP // occ_local
     held = per_group * CAP
-    pair_total = share * ROWS
-    live, batch = codes[pair_total], codes[pair_total + 1]
+    batch = codes[share * ROWS]
 
     def slab_copy(place):
         slab = own_rows if place < groups else other_rows
@@ -114,33 +113,14 @@
             count = count + mine.astype(jnp.int32)
         pick[source] = (slot == turn_of * count + rank).astype(jnp.bfloat16)
         counts.append(count)
-
-    row_at = lax.axis_index("row")
-
-    def decode(at, carry):
-        first = jnp.where(at < share, row_at ^ 2, row_at) * share
-        pair = first + jnp.where(at < share, at, at - share)
-        code = codes[pair]
-        left = jnp.int32(0)
-        start = jnp.int32(0)
-        for block in range(1, blocks):
-            past = code >= block * blocks - block * (block - 1) // 2
-            left = left + past.astype(jnp.int32)
-            start = start + jnp.where(past, blocks - block + 1, 0)
-        left_at[at] = jnp.where(pair < live, left * TILE, domain)
-        right_at[at] = (code - start + left) * TILE
-        return carry
-
-    lax.fori_loop(0, 2 * share, decode, 0)
-    sums[...] = jnp.zeros(sums.shape, jnp.float32)
-    turned[domain:, :] = jnp.zeros((TILE, GROUP), jnp.bfloat16)
+    turned[domain:, :] = jnp.zeros((TILE, PART), jnp.bfloat16)
 
     def pack(place, carry):
         rows = pl.ds(pl.multiple_of(place * GROUP, GROUP), GROUP)
         pltpu.make_async_copy(
             own_rows.at[pl.ds(0, GROUP), :], stage.at[rows, :], arrived.at[place]
         ).wait()
-        source = place // groups
+        source = (place >= groups).astype(jnp.int32)
         before = jnp.minimum(place, groups) * counts[0]
         before = before + jnp.maximum(place - groups, 0) * counts[1]
         start = pl.multiple_of(before * per_group, per_group)
@@ -154,9 +134,12 @@
 
     lax.fori_loop(0, 2 * groups, pack, 0)
     filled = pl.multiple_of((counts[0] + counts[1]) * groups * per_group, per_group)
-    packed_rows[pl.ds(filled, GROUP), :] = jnp.zeros((GROUP, domain), jnp.bfloat16)
-    parts = jnp.maximum((filled + GROUP - 1) // GROUP, 1)
-
+    packed_rows[pl.ds(filled, PART), :] = jnp.zeros((PART, domain), jnp.bfloat16)
+    parts = jnp.maximum((filled + PART - 1) // PART, 1)
+
+    row_at = lax.axis_index("row")
+    send_first = (row_at ^ 2) * share
+    keep_first = row_at * share
     width = math.gcd(4, share)
 
     def out_copies(turn_at):
@@ -167,33 +150,44 @@
             pltpu.make_async_copy(sums.at[keeps], keep_out.at[sends], left_off.at[1, turn_at]),
         )
 
-    def add_part(part, carry):
-        rows = pl.ds(pl.multiple_of(part * GROUP, GROUP), GROUP)
+    def add_part(part, fresh):
+        rows = pl.ds(pl.multiple_of(part * PART, PART), PART)
         for column in range(0, domain, TILE):
             columns = slice(column, column + TILE)
             turned[columns, :] = packed_rows[rows, columns].T
 
-        for turn_at in range(share // width):
-            sends = slice(turn_at * width, (turn_at + 1) * width)
+        def several(turn_at, carry):
             for offset in range(width):
-                for at in (sends.start + offset, share + sends.start + offset):
-                    left = pl.multiple_of(left_at[at], TILE)
-                    right = pl.multiple_of(right_at[at], TILE)
-                    sums[at] += jnp.dot(
+                at = turn_at * width + offset
+                for pair, to in ((send_first + at, at), (keep_first + at, share + at)):
+                    code = codes[pair]
+                    left = pl.multiple_of(code >> SHIFT, TILE)
+                    right = pl.multiple_of(code & ((1 << SHIFT) - 1), TILE)
+                    product = jnp.dot(
                         turned[pl.ds(left, TILE), :],
                         packed_rows[rows, pl.ds(right, TILE)],
                         preferred_element_type=jnp.float32,
                     )
+                    sums[to] = product if fresh else sums[to] + product
 
             @pl.when(part == parts - 1)
-            def _(turn_at=turn_at, sends=sends):
+            def _():
+                sends = pl.ds(turn_at * width, width)
                 send_ref[sends] = sums[sends].astype(send_ref.dtype)
                 for copy in out_copies(turn_at):
                     copy.start()
 
+            return carry
+
+        lax.fori_loop(0, share // width, several, 0)
+
+    add_part(jnp.int32(0), True)
+
+    def more(part, carry):
+        add_part(part, False)
         return carry
 
-    lax.fori_loop(0, parts, add_part, 0)
+    lax.fori_loop(1, parts, more, 0)
     for turn_at in range(share // width):
         for copy in out_copies(turn_at):
             copy.wait()
@@ -213,13 +207,11 @@
         out_specs=[anywhere, anywhere],
         scratch_shapes=[
             pltpu.VMEM((2 * rows_total, domain), jnp.bfloat16),
-            pltpu.VMEM((depth + GROUP, domain), jnp.bfloat16),
-            pltpu.VMEM((domain + TILE, GROUP), jnp.bfloat16),
+            pltpu.VMEM((depth + PART, domain), jnp.bfloat16),
+            pltpu.VMEM((domain + TILE, PART), jnp.bfloat16),
             pltpu.VMEM((2, held, GROUP), jnp.bfloat16),
             pltpu.VMEM((2 * share, TILE, TILE), jnp.float32),
             pltpu.VMEM(tiles, jnp.bfloat16),
-            pltpu.SMEM((2 * share,), jnp.int32),
-            pltpu.SMEM((2 * share,), jnp.int32),
             pltpu.SemaphoreType.DMA((2 * groups,)),
             pltpu.SemaphoreType.DMA((2, share)),
         ],
@@ -237,53 +229,67 @@
     )(*owners, codes, own_rows, other_rows)
 
 
+def block_columns(pair_codes, live, blocks):
+    left = jnp.zeros_like(pair_codes)
+    start = jnp.zeros_like(pair_codes)
+    for block in range(1, blocks):
+        first = block * blocks - block * (block - 1) // 2
+        left = jnp.where(pair_codes >= first, block, left)
+        start = jnp.where(pair_codes >= first, first, start)
+    right = pair_codes - start + left
+    left = jnp.where(lax.iota(jnp.int32, pair_codes.shape[0]) < live, left, blocks)
+    return ((left << SHIFT) + right) * TILE
+
+
 def tile_plan(half_tensor, batch_owner, pair_list, live_pairs):
-    batches = lax.axis_size("orb")
     rows = lax.axis_size("row")
     aux_local, occ_local, domain = half_tensor.shape
     share = pair_list.shape[1] // rows
     orb_at = lax.axis_index("orb")
-
-    def exchange(array, axis, bits):
-        size = lax.axis_size(axis)
-        return lax.ppermute(array, axis, [(i, i ^ bits) for i in range(size)])
+    inner = (orb_at == 1) | (orb_at == 2)
+    swap = [(i, i ^ 1) for i in range(4)]
+    step_a = [(0, 1), (3, 2), (1, 3), (2, 0)]
+    step_b = [(0, 2), (3, 1), (1, 0), (2, 3)]
+
+    def exchange(array, bits):
+        return lax.ppermute(array, "row", [(i, i ^ bits) for i in range(rows)])
 
     def after(array, earlier):
         return lax.optimization_barrier((array, earlier))
 
-    def after(array, earlier):
-        return lax.optimization_barrier((array, earlier))
+    def over_x(send, keep):
+        return keep + exchange(send, 2).astype(jnp.float32)
 
     own_rows = half_tensor.reshape(aux_local * occ_local, domain)
-    other_rows = exchange(own_rows, "row", 1)
+    other_rows = exchange(own_rows, 1)
     own_owner = batch_owner[:, 0]
-    owners = own_owner, exchange(own_owner, "row", 1)
-    own_codes = jnp.concatenate([pair_list[0], live_pairs, orb_at[None]])
-    codes = [exchange(own_codes, "orb", bits) for bits in (3, 2, 1)]
-    codes = lax.optimization_barrier(tuple(codes))[::-1]
-    codes = (own_codes, *codes)
-
-    def chunk(bits):
-        return tile_chunk(owners, codes[bits], own_rows, other_rows, occ_local, share)
-
-    def over_x(send, keep):
-        return keep + exchange(send, "row", 2).astype(jnp.float32)
-
-    send_3, keep_3 = chunk(3)
-    send_2, keep_2 = chunk(2)
-    far = over_x(send_3, keep_3).astype(jnp.bfloat16)
+    owners = own_owner, exchange(own_owner, 1)
+    columns = block_columns(pair_list[0], live_pairs[0], domain // TILE)
+    own_codes = jnp.concatenate([columns, orb_at[None]])
+    far_codes = lax.ppermute(own_codes, "orb", [(i, i ^ 3) for i in range(4)])
+    a_codes = lax.ppermute(own_codes, "orb", [(to, at) for at, to in step_a])
+    b_codes = lax.ppermute(own_codes, "orb", [(to, at) for at, to in step_b])
+    far_codes, a_codes, b_codes = lax.optimization_barrier((far_codes, a_codes, b_codes))
+
+    def chunk(codes, other_rows):
+        return tile_chunk(owners, codes, own_rows, other_rows, occ_local, share)
+
+    far_send, far_keep = chunk(far_codes, other_rows)
+    a_send, a_keep = chunk(a_codes, other_rows)
+    far = over_x(far_send, far_keep).astype(jnp.bfloat16)
     other_rows, far = after(other_rows, far)
-    far = exchange(far, "orb", 1)
-    send_1, keep_1 = chunk(1)
-    across = (over_x(send_2, keep_2) + far.astype(jnp.float32)).astype(jnp.bfloat16)
-    other_rows, across = after(other_rows, across)
-    across = exchange(across, "orb", 2)
-    send_0, keep_0 = chunk(0)
-    keep_1, send_0 = after(keep_1, send_0)
-    near = exchange(over_x(send_1, keep_1).astype(jnp.bfloat16), "orb", 1)
-    beside = near.astype(jnp.float32) + across.astype(jnp.float32)
-    beside, keep_0 = after(beside, keep_0)
-    total = over_x(send_0, keep_0) + beside
+    far = lax.ppermute(far, "orb", swap).astype(jnp.float32)
+    b_send, b_keep = chunk(b_codes, other_rows)
+    a_term = over_x(a_send, a_keep) + jnp.where(inner, far, 0.0)
+    other_rows, a_term = after(other_rows, a_term.astype(jnp.bfloat16))
+    a_term = lax.ppermute(a_term, "orb", step_a)
+    own_send, own_keep = chunk(own_codes, other_rows)
+    b_keep, own_send = after(b_keep, own_send)
+    b_term = over_x(b_send, b_keep) + jnp.where(inner, 0.0, far)
+    b_term = lax.ppermute(b_term.astype(jnp.bfloat16), "orb", step_b)
+    beside = a_term.astype(jnp.float32) + b_term.astype(jnp.float32)
+    beside, own_keep = after(beside, own_keep)
+    total = over_x(own_send, own_keep) + beside
     return total.astype(jnp.bfloat16)[None]
 
 

time: 85.9 us -> 75.7 us (0.88)
  waiting for transfers between devices: 23.8 us -> 18.2 us
  Pallas kernels: 40.4 us -> 36 us
    ppermute x12, waiting for transfers between devices: 23.8 us -> 18.2 us  [the longest x1 12.7 us: tile_plan(): b_term = lax.ppermute(b_term.astype(jnp.bfloat16), 'orb', step_b)]
    pallas_call x4, Pallas kernels: 40.4 us -> 36 us  [tile_chunk(): pl.pallas_call(functools.partial(chunk_kernel, occ_local, share), in_spec...]
  transfers between devices with their start and end apart: 12 -> 12, of which waited for: 5 -> 5; matrix products, arithmetic and copies ran while one was open for 2% -> 2% of each run, Pallas kernels for 36% -> 37%
where the time goes in v9:
time: 75.7 us; the launch traced here: 75.3 us
  Pallas kernels  36 us (48%)
  waiting for transfers between devices  18.2 us (24%)
  starting transfers between devices  17.3 us (23%)
  other arithmetic  2.44 us (3%)
  between operations  0.82 us (1%)
    pallas_call x4, Pallas kernels, tile_chunk(): pl.pallas_call(functools.partial(chunk_kernel, occ_local, share), in_spec...  36 us
    ppermute x1, waiting for transfers between devices, tile_plan(): b_term = lax.ppermute(b_term.astype(jnp.bfloat16), 'orb', step_b)  12.7 us
    ppermute x6, starting transfers between devices, exchange(): return lax.ppermute(array, 'row', [(i, i ^ bits) for i in range(rows)])  5.94 us
    ppermute x6, waiting for transfers between devices, exchange(): return lax.ppermute(array, 'row', [(i, i ^ bits) for i in range(rows)])  3.98 us
    ppermute x1, starting transfers between devices, tile_plan(): far_codes = lax.ppermute(own_codes, 'orb', [(i, i ^ 3) for i in range(4)])  3.87 us
    ppermute x1, starting transfers between devices, tile_plan(): b_codes = lax.ppermute(own_codes, 'orb', [(to, at) for at, to in step_b])  2.57 us
    ppermute x1, starting transfers between devices, tile_plan(): b_term = lax.ppermute(b_term.astype(jnp.bfloat16), 'orb', step_b)  2.32 us
  transfers between devices with their start and end apart: 12, of which 5 were waited for; matrix products, arithmetic and copies ran while one was open for 2% of the time, Pallas kernels for 37%

profile of v9, /device:TPU:0, one launch (start us, length us, event | category | flops | bytes accessed | tf_op | source)
XLA Modules:
  0.0 75.3 jit_solution(1651097062026727742)
XLA Ops:
  0.0 0.5 collective-permute-start
  1.1 0.7 fusion.9
  1.9 2.6 %collective-permute-start.4 = (s32[65]{0:T(128)S(1)}, s32[65]{0:T(128)S(1)}, u32[]{:S(2)}, u32[]{:S(2)}) collective-permute-start(s32[65]{0:T(128)S(1)} %pad_add_fusion.codes), channel_id=1, source_target_pairs={{8,0},{4,12},{0,4},{12,8},{9,1},{5,13},{1,5},{13,9},{10,2},{6,14},... | collective-permute-start | bytes 788 | tf_op jit(solution)/shard_map/ppermute | solution.py:271
  4.4 1.1 %collective-permute-start.3 = (s32[65]{0:T(128)S(1)}, s32[65]{0:T(128)S(1)}, u32[]{:S(2)}, u32[]{:S(2)}) collective-permute-start(s32[65]{0:T(128)S(1)} %pad_add_fusion.codes), channel_id=1, source_target_pairs={{4,0},{8,12},{12,4},{0,8},{5,1},{9,13},{13,5},{1,9},{6,2},{10,14},... | collective-permute-start | bytes 788 | tf_op jit(solution)/shard_map/ppermute | solution.py:270
  5.5 3.9 %collective-permute-start.2 = (s32[65]{0:T(128)S(1)}, s32[65]{0:T(128)S(1)}, u32[]{:S(2)}, u32[]{:S(2)}) collective-permute-start(s32[65]{0:T(128)S(1)} %pad_add_fusion.codes), channel_id=1, source_target_pairs={{0,12},{4,8},{8,4},{12,0},{1,13},{5,9},{9,5},{13,1},{2,14},{6,10},... | collective-permute-start | bytes 788 | tf_op jit(solution)/shard_map/ppermute | solution.py:269
  9.4 1.5 %collective-permute-done.2.codes = s32[65]{0:T(128)S(1)} collective-permute-done((s32[65]{0:T(128)S(1)}, s32[65]{0:T(128)S(1)}, u32[]{:S(2)}, u32[]{:S(2)}) %collective-permute-start.2) | collective-permute-done | bytes 292 | tf_op jit(solution)/shard_map/ppermute | solution.py:269
  10.9 0.5 copy-done.8
  11.5 8.3 %tile_chunk.4 = (bf16[16,128,128]{2,1,0:T(8,128)(2,1)}, f32[16,128,128]{2,1,0:T(8,128)}) custom-call(s32[16]{0:T(128)} %bitcast.17, s32[16]{0:T(128)} %copy-done.4, s32[65]{0:T(128)} %copy-done.8, bf16[1024,2048]{1,0:T(8,128)(2,1)} %bitcast.12, bf16[1024,2048]{1,0:T(8,128)(2,1)} %collective-permute-done.other_rows), custom_call_target="tpu_custom_call" | custom-call | flops 2147483648 | bytes 9961472 | tf_op jit(solution)/shard_map/tile_chunk/pallas_call | solution.py:204
  19.8 1.8 %collective-permute-start.5 = (bf16[16,128,128]{2,1,0:T(8,128)(2,1)}, bf16[16,128,128]{2,1,0:T(8,128)(2,1)S(1)}, u32[]{:S(2)}, u32[]{:S(2)}) collective-permute-start(bf16[16,128,128]{2,1,0:T(8,128)(2,1)} %get-tuple-element.26), channel_id=1, source_target_pairs={{0,2},{1,3},{2,0},{3,1},{4,6},{5,7},{6,4},{7,5},{8,10},{9,11},{10,... | collective-permute-start | bytes 1572872 | tf_op jit(solution)/shard_map/ppermute | solution.py:255
  21.6 10.9 %tile_chunk.5 = (bf16[16,128,128]{2,1,0:T(8,128)(2,1)}, f32[16,128,128]{2,1,0:T(8,128)}) custom-call(s32[16]{0:T(128)} %bitcast.18, s32[16]{0:T(128)} %copy-done.4, s32[65]{0:T(128)} %copy-done.7, bf16[1024,2048]{1,0:T(8,128)(2,1)} %bitcast.13, bf16[1024,2048]{1,0:T(8,128)(2,1)} %collective-permute-done.other_rows), custom_call_target="tpu_custom_call" | custom-call | flops 2147483648 | bytes 9961472 | tf_op jit(solution)/shard_map/tile_chunk/pallas_call | solution.py:204
  32.5 0.4 collective-permute-start.6
  32.9 0.9 %collective-permute-done.5 = bf16[16,128,128]{2,1,0:T(8,128)(2,1)S(1)} collective-permute-done((bf16[16,128,128]{2,1,0:T(8,128)(2,1)}, bf16[16,128,128]{2,1,0:T(8,128)(2,1)S(1)}, u32[]{:S(2)}, u32[]{:S(2)}) %collective-permute-start.5) | collective-permute-done | bytes 524320 | tf_op jit(solution)/shard_map/ppermute | solution.py:255
  34.0 1.4 %collective-permute-start.7 = (bf16[16,128,128]{2,1,0:T(8,128)(2,1)S(1)}, bf16[16,128,128]{2,1,0:T(8,128)(2,1)S(1)}, u32[]{:S(2)}, u32[]{:S(2)}) collective-permute-start(bf16[16,128,128]{2,1,0:T(8,128)(2,1)S(1)} %add_convert_fusion.1), channel_id=1, source_target_pairs={{0,4},{4,0},{8,12},{12,8},{1,5},{5,1},{9,13},{13,9},{2,6},{6,2},{1... | collective-permute-start | bytes 1572872 | tf_op jit(solution)/shard_map/ppermute | solution.py:281
  35.4 8.3 %tile_chunk.6 = (bf16[16,128,128]{2,1,0:T(8,128)(2,1)}, f32[16,128,128]{2,1,0:T(8,128)}) custom-call(s32[16]{0:T(128)} %bitcast.19, s32[16]{0:T(128)} %copy-done.4, s32[65]{0:T(128)} %copy-done.6, bf16[1024,2048]{1,0:T(8,128)(2,1)} %bitcast.14, bf16[1024,2048]{1,0:T(8,128)(2,1)} %collective-permute-done.other_rows), custom_call_target="tpu_custom_call" | custom-call | flops 2147483648 | bytes 9961472 | tf_op jit(solution)/shard_map/tile_chunk/pallas_call | solution.py:204
  43.7 1.8 %collective-permute-start.9 = (bf16[16,128,128]{2,1,0:T(8,128)(2,1)}, bf16[16,128,128]{2,1,0:T(8,128)(2,1)S(1)}, u32[]{:S(2)}, u32[]{:S(2)}) collective-permute-start(bf16[16,128,128]{2,1,0:T(8,128)(2,1)} %get-tuple-element.38), channel_id=1, source_target_pairs={{0,2},{1,3},{2,0},{3,1},{4,6},{5,7},{6,4},{7,5},{8,10},{9,11},{10,... | collective-permute-start | bytes 1572872 | tf_op jit(solution)/shard_map/ppermute | solution.py:255
  45.6 2.1 %collective-permute-done.6 = bf16[16,128,128]{2,1,0:T(8,128)(2,1)S(1)} collective-permute-done((bf16[16,128,128]{2,1,0:T(8,128)(2,1)}, bf16[16,128,128]{2,1,0:T(8,128)(2,1)S(1)}, u32[]{:S(2)}, u32[]{:S(2)}) %collective-permute-start.6) | collective-permute-done | bytes 524320 | tf_op jit(solution)/shard_map/ppermute | solution.py:255
  47.7 0.2 fusion.1
  48.0 8.4 %tile_chunk.7 = (bf16[16,128,128]{2,1,0:T(8,128)(2,1)}, f32[16,128,128]{2,1,0:T(8,128)}) custom-call(s32[16]{0:T(128)} %bitcast.20, s32[16]{0:T(128)} %copy-done.4, s32[65]{0:T(128)} %copy-done.5, bf16[1024,2048]{1,0:T(8,128)(2,1)} %bitcast.15, bf16[1024,2048]{1,0:T(8,128)(2,1)} %collective-permute-done.other_rows), custom_call_target="tpu_custom_call" | custom-call | flops 2147483648 | bytes 9961472 | tf_op jit(solution)/shard_map/tile_chunk/pallas_call | solution.py:204
  56.4 0.9 %collective-permute-done.9 = bf16[16,128,128]{2,1,0:T(8,128)(2,1)S(1)} collective-permute-done((bf16[16,128,128]{2,1,0:T(8,128)(2,1)}, bf16[16,128,128]{2,1,0:T(8,128)(2,1)S(1)}, u32[]{:S(2)}, u32[]{:S(2)}) %collective-permute-start.9) | collective-permute-done | bytes 524320 | tf_op jit(solution)/shard_map/ppermute | solution.py:255
  57.3 0.2 fusion.3
  57.5 2.3 %collective-permute-start.10 = (bf16[16,128,128]{2,1,0:T(8,128)(2,1)S(1)}, bf16[16,128,128]{2,1,0:T(8,128)(2,1)S(1)}, u32[]{:S(2)}, u32[]{:S(2)}) collective-permute-start(bf16[16,128,128]{2,1,0:T(8,128)(2,1)S(1)} %fusion.3), channel_id=1, source_target_pairs={{0,8},{12,4},{4,0},{8,12},{1,9},{13,5},{5,1},{9,13},{2,10},{14,6},... | collective-permute-start | bytes 1572872 | tf_op jit(solution)/shard_map/ppermute | solution.py:289
  59.9 1.5 %collective-permute-start.11 = (bf16[16,128,128]{2,1,0:T(8,128)(2,1)}, bf16[16,128,128]{2,1,0:T(8,128)(2,1)S(1)}, u32[]{:S(2)}, u32[]{:S(2)}) collective-permute-start(bf16[16,128,128]{2,1,0:T(8,128)(2,1)} %get-tuple-element.41), channel_id=1, source_target_pairs={{0,2},{1,3},{2,0},{3,1},{4,6},{5,7},{6,4},{7,5},{8,10},{9,11},{10,... | collective-permute-start | bytes 1572872 | tf_op jit(solution)/shard_map/ppermute | solution.py:255
  61.4 12.7 %collective-permute-done.10 = bf16[16,128,128]{2,1,0:T(8,128)(2,1)S(1)} collective-permute-done((bf16[16,128,128]{2,1,0:T(8,128)(2,1)S(1)}, bf16[16,128,128]{2,1,0:T(8,128)(2,1)S(1)}, u32[]{:S(2)}, u32[]{:S(2)}) %collective-permute-start.10) | collective-permute-done | bytes 524320 | tf_op jit(solution)/shard_map/ppermute | solution.py:289
  74.3 1.0 %fusion.4 = bf16[1,16,128,128]{3,2,1,0:T(8,128)(2,1)} fusion(f32[16,128,128]{2,1,0:T(8,128)S(1)} %convert_add_fusion, f32[16,128,128]{2,1,0:T(8,128)S(1)} %copy-done, bf16[16,128,128]{2,1,0:T(8,128)(2,1)S(1)} %collective-permute-done.11), kind=kLoop, calls=%fused_computation.9 | loop fusion | flops 1048576 | bytes 3145728 | tf_op jit(solution)/shard_map/broadcast_in_dim | solution.py:293
  (29 shorter events, 0.5 us)
Async XLA Ops:
  0.0 10.9 %collective-permute-start = (bf16[1024,2048]{1,0:T(8,128)(2,1)}, bf16[1024,2048]{1,0:T(8,128)(2,1)}, u32[]{:S(2)}, u32[]{:S(2)}) collective-permute-start(bf16[1024,2048]{1,0:T(8,128)(2,1)} %bitcast.11), channel_id=1, source_target_pairs={{0,1},{1,0},{2,3},{3,2},{4,5},{5,4},{6,7},{7,6},{8,9},{9,8},{10,11... | collective-permute-start | bytes 12582920 | tf_op jit(solution)/shard_map/ppermute | solution.py:255
  1.9 17.9 %copy-start.5 = (s32[65]{0:T(128)}, s32[65]{0:T(128)S(1)}, u32[]{:S(2)}) copy-start(s32[65]{0:T(128)S(1)} %pad_add_fusion.codes) | copy-start | bytes 784
  1.9 7.5 %collective-permute-start.4 = (s32[65]{0:T(128)S(1)}, s32[65]{0:T(128)S(1)}, u32[]{:S(2)}, u32[]{:S(2)}) collective-permute-start(s32[65]{0:T(128)S(1)} %pad_add_fusion.codes), channel_id=1, source_target_pairs={{8,0},{4,12},{0,4},{12,8},{9,1},{5,13},{1,5},{13,9},{10,2},{6,14},... | collective-permute-start | bytes 788 | tf_op jit(solution)/shard_map/ppermute | solution.py:271
  4.4 5.0 %collective-permute-start.3 = (s32[65]{0:T(128)S(1)}, s32[65]{0:T(128)S(1)}, u32[]{:S(2)}, u32[]{:S(2)}) collective-permute-start(s32[65]{0:T(128)S(1)} %pad_add_fusion.codes), channel_id=1, source_target_pairs={{4,0},{8,12},{12,4},{0,8},{5,1},{9,13},{13,5},{1,9},{6,2},{10,14},... | collective-permute-start | bytes 788 | tf_op jit(solution)/shard_map/ppermute | solution.py:270
  5.5 5.4 %collective-permute-start.2 = (s32[65]{0:T(128)S(1)}, s32[65]{0:T(128)S(1)}, u32[]{:S(2)}, u32[]{:S(2)}) collective-permute-start(s32[65]{0:T(128)S(1)} %pad_add_fusion.codes), channel_id=1, source_target_pairs={{0,12},{4,8},{8,4},{12,0},{1,13},{5,9},{9,5},{13,1},{2,14},{6,10},... | collective-permute-start | bytes 788 | tf_op jit(solution)/shard_map/ppermute | solution.py:269
  9.4 1.5 %collective-permute-start.1 = (s32[16]{0:T(128)}, s32[16]{0:T(128)S(1)}, u32[]{:S(2)}, u32[]{:S(2)}) collective-permute-start(s32[16]{0:T(128)} %bitcast.16), channel_id=1, source_target_pairs={{0,1},{1,0},{2,3},{3,2},{4,5},{5,4},{6,7},{7,6},{8,9},{9,8},{10,11... | collective-permute-start | bytes 200 | tf_op jit(solution)/shard_map/ppermute | solution.py:255
  9.4 26.0 %copy-start.6 = (s32[65]{0:T(128)}, s32[65]{0:T(128)S(1)}, u32[]{:S(2)}) copy-start(s32[65]{0:T(128)S(1)} %collective-permute-done.4.codes) | copy-start | bytes 784
  9.4 12.2 %copy-start.7 = (s32[65]{0:T(128)}, s32[65]{0:T(128)S(1)}, u32[]{:S(2)}) copy-start(s32[65]{0:T(128)S(1)} %collective-permute-done.3.codes) | copy-start | bytes 784
  10.9 0.5 copy-start.8
  10.9 0.5 copy-start.4
  19.8 14.1 %copy-start.3 = (f32[16,128,128]{2,1,0:T(8,128)S(1)}, f32[16,128,128]{2,1,0:T(8,128)}, u32[]{:S(2)}) copy-start(f32[16,128,128]{2,1,0:T(8,128)} %get-tuple-element.25) | copy-start | bytes 3145732
  19.8 14.0 %collective-permute-start.5 = (bf16[16,128,128]{2,1,0:T(8,128)(2,1)}, bf16[16,128,128]{2,1,0:T(8,128)(2,1)S(1)}, u32[]{:S(2)}, u32[]{:S(2)}) collective-permute-start(bf16[16,128,128]{2,1,0:T(8,128)(2,1)} %get-tuple-element.26), channel_id=1, source_target_pairs={{0,2},{1,3},{2,0},{3,1},{4,6},{5,7},{6,4},{7,5},{8,10},{9,11},{10,... | collective-permute-start | bytes 1572872 | tf_op jit(solution)/shard_map/ppermute | solution.py:255
  32.5 15.1 %collective-permute-start.6 = (bf16[16,128,128]{2,1,0:T(8,128)(2,1)}, bf16[16,128,128]{2,1,0:T(8,128)(2,1)S(1)}, u32[]{:S(2)}, u32[]{:S(2)}) collective-permute-start(bf16[16,128,128]{2,1,0:T(8,128)(2,1)} %get-tuple-element.30), channel_id=1, source_target_pairs={{0,2},{1,3},{2,0},{3,1},{4,6},{5,7},{6,4},{7,5},{8,10},{9,11},{10,... | collective-permute-start | bytes 1572872 | tf_op jit(solution)/shard_map/ppermute | solution.py:255
  34.0 13.7 %copy-start.1 = (f32[16,128,128]{2,1,0:T(8,128)S(1)}, f32[16,128,128]{2,1,0:T(8,128)}, u32[]{:S(2)}) copy-start(f32[16,128,128]{2,1,0:T(8,128)} %get-tuple-element.29) | copy-start | bytes 3145732
  34.0 13.7 %collective-permute-start.7 = (bf16[16,128,128]{2,1,0:T(8,128)(2,1)S(1)}, bf16[16,128,128]{2,1,0:T(8,128)(2,1)S(1)}, u32[]{:S(2)}, u32[]{:S(2)}) collective-permute-start(bf16[16,128,128]{2,1,0:T(8,128)(2,1)S(1)} %add_convert_fusion.1), channel_id=1, source_target_pairs={{0,4},{4,0},{8,12},{12,8},{1,5},{5,1},{9,13},{13,9},{2,6},{6,2},{1... | collective-permute-start | bytes 1572872 | tf_op jit(solution)/shard_map/ppermute | solution.py:281
  43.7 13.6 %collective-permute-start.9 = (bf16[16,128,128]{2,1,0:T(8,128)(2,1)}, bf16[16,128,128]{2,1,0:T(8,128)(2,1)S(1)}, u32[]{:S(2)}, u32[]{:S(2)}) collective-permute-start(bf16[16,128,128]{2,1,0:T(8,128)(2,1)} %get-tuple-element.38), channel_id=1, source_target_pairs={{0,2},{1,3},{2,0},{3,1},{4,6},{5,7},{6,4},{7,5},{8,10},{9,11},{10,... | collective-permute-start | bytes 1572872 | tf_op jit(solution)/shard_map/ppermute | solution.py:255
  47.9 9.4 %copy-start.2 = (f32[16,128,128]{2,1,0:T(8,128)S(1)}, f32[16,128,128]{2,1,0:T(8,128)}, u32[]{:S(2)}) copy-start(f32[16,128,128]{2,1,0:T(8,128)} %get-tuple-element.37) | copy-start | bytes 3145732
  47.9 13.5 %collective-permute-start.8 = (bf16[16,128,128]{2,1,0:T(8,128)(2,1)S(1)}, bf16[16,128,128]{2,1,0:T(8,128)(2,1)S(1)}, u32[]{:S(2)}, u32[]{:S(2)}) collective-permute-start(bf16[16,128,128]{2,1,0:T(8,128)(2,1)S(1)} %fusion.1), channel_id=1, source_target_pairs={{0,4},{12,8},{4,12},{8,0},{1,5},{13,9},{5,13},{9,1},{2,6},{14,10},... | collective-permute-start | bytes 1572872 | tf_op jit(solution)/shard_map/ppermute | solution.py:285
  56.4 17.9 %copy-start = (f32[16,128,128]{2,1,0:T(8,128)S(1)}, f32[16,128,128]{2,1,0:T(8,128)}, u32[]{:S(2)}) copy-start(f32[16,128,128]{2,1,0:T(8,128)} %get-tuple-element.40) | copy-start | bytes 3145732
  57.5 16.6 %collective-permute-start.10 = (bf16[16,128,128]{2,1,0:T(8,128)(2,1)S(1)}, bf16[16,128,128]{2,1,0:T(8,128)(2,1)S(1)}, u32[]{:S(2)}, u32[]{:S(2)}) collective-permute-start(bf16[16,128,128]{2,1,0:T(8,128)(2,1)S(1)} %fusion.3), channel_id=1, source_target_pairs={{0,8},{12,4},{4,0},{8,12},{1,9},{13,5},{5,1},{9,13},{2,10},{14,6},... | collective-permute-start | bytes 1572872 | tf_op jit(solution)/shard_map/ppermute | solution.py:289
  59.9 14.4 %collective-permute-start.11 = (bf16[16,128,128]{2,1,0:T(8,128)(2,1)}, bf16[16,128,128]{2,1,0:T(8,128)(2,1)S(1)}, u32[]{:S(2)}, u32[]{:S(2)}) collective-permute-start(bf16[16,128,128]{2,1,0:T(8,128)(2,1)} %get-tuple-element.41), channel_id=1, source_target_pairs={{0,2},{1,3},{2,0},{3,1},{4,6},{5,7},{6,4},{7,5},{8,10},{9,11},{10,... | collective-permute-start | bytes 1572872 | tf_op jit(solution)/shard_map/ppermute | solution.py:255

commit v10 on v9

--- a/solution.py
+++ b/solution.py
@@ -79,63 +79,135 @@
     return mine[None]
 
 
-def chunk_kernel(occ_local, share, own_owner, other_owner, codes, own_rows, other_rows, *refs):
-    send_out, keep_out = refs[:2]
-    stage, packed_rows, turned, pick, sums, send_ref, arrived, left_off = refs[2:]
-    rows_total, domain = own_rows.shape
+def sort_kernel(batches, occ_local, first, owner, slab, sorted_out, stage, ordered, pick, arrived, left):
+    rows_total, width = sorted_out.shape
     groups = rows_total // GROUP
     per_group = GROUP // occ_local
-    held = per_group * CAP
-    batch = codes[share * ROWS]
-
-    def slab_copy(place):
-        slab = own_rows if place < groups else other_rows
+    piece = 2 * TILE
+
+    def slab_copy(group):
+        rows = pl.ds(group * GROUP, GROUP)
         return pltpu.make_async_copy(
-            slab.at[pl.ds(place % groups * GROUP, GROUP), :],
-            stage.at[pl.ds(place * GROUP, GROUP), :],
-            arrived.at[place],
+            slab.at[rows, pl.ds(first, width)], stage.at[rows, :], arrived.at[group]
         )
 
-    for place in range(2 * groups):
-        slab_copy(place).start()
-
+    def out_copy(column):
+        columns = pl.ds(column * piece, piece)
+        return pltpu.make_async_copy(
+            ordered.at[:, columns], sorted_out.at[:, columns], left.at[column]
+        )
+
+    for group in range(groups):
+        slab_copy(group).start()
+    owners = [owner[orbital] for orbital in range(occ_local)]
+    positions = [jnp.int32(0)] * occ_local
+    rank = jnp.int32(0)
+    for batch in range(batches):
+        for orbital in range(occ_local):
+            mine = owners[orbital] == batch
+            positions[orbital] = jnp.where(mine, rank, positions[orbital])
+            rank = rank + mine.astype(jnp.int32)
     lane = lax.broadcasted_iota(jnp.int32, (1, GROUP), 1)
     orbital_of = lane & (occ_local - 1)
-    turn_of = lane >> (occ_local.bit_length() - 1)
-    slot = lax.broadcasted_iota(jnp.int32, (held, GROUP), 0)
-    counts = []
+    target = lane >> (occ_local.bit_length() - 1)
+    for orbital in range(occ_local):
+        target = target + jnp.where(orbital_of == orbital, positions[orbital] * per_group, 0)
+    slot = lax.broadcasted_iota(jnp.int32, (GROUP, GROUP), 0)
+    pick[...] = (slot == target).astype(jnp.bfloat16)
+    for group in range(groups):
+        slab_copy(group).wait()
+
+    for column in range(width // piece):
+        columns = slice(column * piece, (column + 1) * piece)
+        for group in range(groups):
+            moved = jnp.dot(
+                pick[...], stage[group * GROUP:(group + 1) * GROUP, columns],
+                preferred_element_type=jnp.float32,
+            ).astype(jnp.bfloat16)
+            for unit in range(occ_local):
+                to = (unit * groups + group) * per_group
+                ordered[to:to + per_group, columns] = (
+                    moved[unit * per_group:(unit + 1) * per_group]
+                )
+        out_copy(column).start()
+    for column in range(width // piece):
+        out_copy(column).wait()
+
+
+def sort_rows(owner, slab, first, width, batches):
+    occ_local, = owner.shape
+    rows_total = slab.shape[0]
+    anywhere = pl.BlockSpec(memory_space=pl.ANY)
+    return pl.pallas_call(
+        functools.partial(sort_kernel, batches, occ_local, first),
+        in_specs=[pl.BlockSpec(memory_space=pltpu.SMEM), anywhere],
+        out_specs=anywhere,
+        scratch_shapes=[
+            pltpu.VMEM((rows_total, width), jnp.bfloat16),
+            pltpu.VMEM((rows_total, width), jnp.bfloat16),
+            pltpu.VMEM((GROUP, GROUP), jnp.bfloat16),
+            pltpu.SemaphoreType.DMA((rows_total // GROUP,)),
+            pltpu.SemaphoreType.DMA((width // (2 * TILE),)),
+        ],
+        out_shape=jax.ShapeDtypeStruct((rows_total, width), jnp.bfloat16),
+        compiler_params=pltpu.CompilerParams(vmem_limit_bytes=56 * 1024 * 1024),
+        cost_estimate=pl.CostEstimate(
+            flops=2 * rows_total * GROUP * width,
+            bytes_accessed=4 * rows_total * width,
+            transcendentals=0,
+        ),
+        name="sort_rows",
+    )(owner, slab)
+
+
+def chunk_kernel(occ_local, share, own_owner, other_owner, codes, *refs):
+    slabs = refs[:2], refs[2:4]
+    send_out, keep_out = refs[4:6]
+    packed_rows, turned, sums, send_ref, arrived, left_off = refs[6:]
+    rows_total, half = refs[0].shape
+    domain = 2 * half
+    per_orbital = rows_total // occ_local
+    batch = codes[share * ROWS]
+
+    filled = jnp.int32(0)
+    pieces = []
     for source, owner in enumerate((own_owner, other_owner)):
-        count = jnp.int32(0)
-        rank = jnp.full((1, GROUP), -GROUP * CAP, jnp.int32)
-        for orbital in range(occ_local):
-            mine = owner[orbital] == batch
-            rank = jnp.where(orbital_of == orbital, jnp.where(mine, count, -GROUP * CAP), rank)
-            count = count + mine.astype(jnp.int32)
-        pick[source] = (slot == turn_of * count + rank).astype(jnp.bfloat16)
-        counts.append(count)
+        owners = [owner[orbital] for orbital in range(occ_local)]
+        earlier = sum((each < batch).astype(jnp.int32) for each in owners)
+        count = sum((each == batch).astype(jnp.int32) for each in owners)
+
+        def copies(orbital, source=source, earlier=earlier, filled=filled):
+            at = pl.multiple_of((earlier + orbital) * per_orbital, per_orbital)
+            to = pl.multiple_of((filled + orbital) * per_orbital, per_orbital)
+            return [
+                pltpu.make_async_copy(
+                    slabs[source][side].at[pl.ds(at, per_orbital), :],
+                    packed_rows.at[pl.ds(to, per_orbital), pl.ds(side * half, half)],
+                    arrived.at[source, side, orbital],
+                )
+                for side in range(2)
+            ]
+
+        def start(orbital, carry, copies=copies):
+            for copy in copies(orbital):
+                copy.start()
+            return carry
+
+        lax.fori_loop(0, count, start, 0)
+        pieces.append((copies, count))
+        filled = filled + count
+
+    end = pl.multiple_of(filled * per_orbital, per_orbital)
+    packed_rows[pl.ds(end, PART), :] = jnp.zeros((PART, domain), jnp.bfloat16)
     turned[domain:, :] = jnp.zeros((TILE, PART), jnp.bfloat16)
-
-    def pack(place, carry):
-        rows = pl.ds(pl.multiple_of(place * GROUP, GROUP), GROUP)
-        pltpu.make_async_copy(
-            own_rows.at[pl.ds(0, GROUP), :], stage.at[rows, :], arrived.at[place]
-        ).wait()
-        source = (place >= groups).astype(jnp.int32)
-        before = jnp.minimum(place, groups) * counts[0]
-        before = before + jnp.maximum(place - groups, 0) * counts[1]
-        start = pl.multiple_of(before * per_group, per_group)
-        for column in range(0, domain, 2 * TILE):
-            columns = slice(column, column + 2 * TILE)
-            packed = jnp.dot(
-                pick[source], stage[rows, columns], preferred_element_type=jnp.float32
-            )
-            packed_rows[pl.ds(start, held), columns] = packed.astype(jnp.bfloat16)
-        return carry
-
-    lax.fori_loop(0, 2 * groups, pack, 0)
-    filled = pl.multiple_of((counts[0] + counts[1]) * groups * per_group, per_group)
-    packed_rows[pl.ds(filled, PART), :] = jnp.zeros((PART, domain), jnp.bfloat16)
-    parts = jnp.maximum((filled + PART - 1) // PART, 1)
+    parts = jnp.maximum((end + PART - 1) // PART, 1)
+    for copies, count in pieces:
+        def wait(orbital, carry, copies=copies):
+            for copy in copies(orbital):
+                copy.wait()
+            return carry
+
+        lax.fori_loop(0, count, wait, 0)
 
     row_at = lax.axis_index("row")
     send_first = (row_at ^ 2) * share
@@ -193,26 +265,24 @@
             copy.wait()
 
 
-def tile_chunk(owners, codes, own_rows, other_rows, occ_local, share):
-    rows_total, domain = own_rows.shape
-    groups = rows_total // GROUP
-    held = GROUP // occ_local * CAP
-    depth = 2 * groups * held
+def tile_chunk(owners, codes, slabs, share):
+    occ_local, = owners[0].shape
+    rows_total, half = slabs[0].shape
+    domain = 2 * half
+    depth = 2 * CAP * (rows_total // occ_local)
     tiles = (share, TILE, TILE)
     anywhere = pl.BlockSpec(memory_space=pl.ANY)
     in_smem = pl.BlockSpec(memory_space=pltpu.SMEM)
     return pl.pallas_call(
         functools.partial(chunk_kernel, occ_local, share),
-        in_specs=[in_smem] * 3 + [anywhere] * 2,
+        in_specs=[in_smem] * 3 + [anywhere] * 4,
         out_specs=[anywhere, anywhere],
         scratch_shapes=[
-            pltpu.VMEM((2 * rows_total, domain), jnp.bfloat16),
             pltpu.VMEM((depth + PART, domain), jnp.bfloat16),
             pltpu.VMEM((domain + TILE, PART), jnp.bfloat16),
-            pltpu.VMEM((2, held, GROUP), jnp.bfloat16),
             pltpu.VMEM((2 * share, TILE, TILE), jnp.float32),
             pltpu.VMEM(tiles, jnp.bfloat16),
-            pltpu.SemaphoreType.DMA((2 * groups,)),
+            pltpu.SemaphoreType.DMA((2, 2, CAP)),
             pltpu.SemaphoreType.DMA((2, share)),
         ],
         out_shape=[
@@ -221,12 +291,12 @@
         ],
         compiler_params=pltpu.CompilerParams(vmem_limit_bytes=56 * 1024 * 1024),
         cost_estimate=pl.CostEstimate(
-            flops=4 * share * TILE * TILE * depth + 2 * depth * GROUP * domain,
-            bytes_accessed=4 * rows_total * domain + 6 * share * TILE * TILE,
+            flops=4 * share * TILE * TILE * depth,
+            bytes_accessed=2 * depth * domain + 6 * share * TILE * TILE,
             transcendentals=0,
         ),
         name="tile_chunk",
-    )(*owners, codes, own_rows, other_rows)
+    )(*owners, codes, *slabs)
 
 
 def block_columns(pair_codes, live, blocks):
@@ -261,29 +331,35 @@
         return keep + exchange(send, 2).astype(jnp.float32)
 
     own_rows = half_tensor.reshape(aux_local * occ_local, domain)
-    other_rows = exchange(own_rows, 1)
     own_owner = batch_owner[:, 0]
-    owners = own_owner, exchange(own_owner, 1)
+    half = domain // 2
+    own_halves = [sort_rows(own_owner, own_rows, first, half, 4) for first in (0, half)]
+    other_halves = [exchange(each, 1) for each in own_halves]
+    other_owner = exchange(own_owner, 1)
     columns = block_columns(pair_list[0], live_pairs[0], domain // TILE)
     own_codes = jnp.concatenate([columns, orb_at[None]])
+    own_codes, own_halves[1] = after(own_codes, own_halves[1])
+    slabs = (*own_halves, *other_halves)
     far_codes = lax.ppermute(own_codes, "orb", [(i, i ^ 3) for i in range(4)])
+    own_codes, other_owner = after(own_codes, other_owner)
     a_codes = lax.ppermute(own_codes, "orb", [(to, at) for at, to in step_a])
     b_codes = lax.ppermute(own_codes, "orb", [(to, at) for at, to in step_b])
     far_codes, a_codes, b_codes = lax.optimization_barrier((far_codes, a_codes, b_codes))
-
-    def chunk(codes, other_rows):
-        return tile_chunk(owners, codes, own_rows, other_rows, occ_local, share)
-
-    far_send, far_keep = chunk(far_codes, other_rows)
-    a_send, a_keep = chunk(a_codes, other_rows)
+    owners = own_owner, other_owner
+
+    def chunk(codes):
+        return tile_chunk(owners, codes, slabs, share)
+
+    far_send, far_keep = chunk(far_codes)
+    a_send, a_keep = chunk(a_codes)
     far = over_x(far_send, far_keep).astype(jnp.bfloat16)
-    other_rows, far = after(other_rows, far)
+    b_codes, far = after(b_codes, far)
     far = lax.ppermute(far, "orb", swap).astype(jnp.float32)
-    b_send, b_keep = chunk(b_codes, other_rows)
+    b_send, b_keep = chunk(b_codes)
     a_term = over_x(a_send, a_keep) + jnp.where(inner, far, 0.0)
-    other_rows, a_term = after(other_rows, a_term.astype(jnp.bfloat16))
+    own_codes, a_term = after(own_codes, a_term.astype(jnp.bfloat16))
     a_term = lax.ppermute(a_term, "orb", step_a)
-    own_send, own_keep = chunk(own_codes, other_rows)
+    own_send, own_keep = chunk(own_codes)
     b_keep, own_send = after(b_keep, own_send)
     b_term = over_x(b_send, b_keep) + jnp.where(inner, 0.0, far)
     b_term = lax.ppermute(b_term.astype(jnp.bfloat16), "orb", step_b)
@@ -306,6 +382,7 @@
         and pair_total % rows == 0
         and occ_local & (occ_local - 1) == 0
         and GROUP % occ_local == 0
+        and domain % (4 * TILE) == 0
         and aux_local * occ_local % GROUP == 0
         and tile_elements <= slab_elements
     )

time: 75.7 us -> 81.6 us (1.078)
  starting transfers between devices: 17.3 us -> 27.3 us
  waiting for transfers between devices: 18.2 us -> 14.2 us
  local copies, waits for them, and re-layouts: 0.57 us -> 1.43 us
    pallas_call x4, Pallas kernels: 36 us -> 27.9 us  [tile_chunk(): pl.pallas_call(functools.partial(chunk_kernel, occ_local, share), in_spec...]
    pallas_call x0 -> x2, Pallas kernels: none -> 7.85 us  [sort_rows(): pl.pallas_call(functools.partial(sort_kernel, batches, occ_local, first),...]
    ppermute x1, starting transfers between devices: 1.43 us -> 6.76 us  [tile_plan(): far = lax.ppermute(far, 'orb', swap).astype(jnp.float32)]
    ppermute x6 -> x7, starting transfers between devices: 5.94 us -> 10.9 us  [exchange(): return lax.ppermute(array, 'row', [(i, i ^ bits) for i in range(rows)])]
    ppermute x1, waiting for transfers between devices: 12.7 us -> 9 us  [tile_plan(): b_term = lax.ppermute(b_term.astype(jnp.bfloat16), 'orb', step_b)]
    ppermute x1, starting transfers between devices: 2.57 us -> 0.74 us  [tile_plan(): b_codes = lax.ppermute(own_codes, 'orb', [(to, at) for at, to in step_b])]
    ppermute x1, waiting for transfers between devices: 0.01 us -> 1.51 us  [tile_plan(): b_codes = lax.ppermute(own_codes, 'orb', [(to, at) for at, to in step_b])]
    ppermute x1, waiting for transfers between devices: 1.49 us -> 0.01 us  [tile_plan(): far_codes = lax.ppermute(own_codes, 'orb', [(i, i ^ 3) for i in range(4)])]
  transfers between devices with their start and end apart: 12 -> 13, of which waited for: 5 -> 5; matrix products, arithmetic and copies ran while one was open for 2% -> 1% of each run, Pallas kernels for 37% -> 32%
where the time goes in v10:
time: 81.6 us; the launch traced here: 81.3 us
  Pallas kernels  35.7 us (44%)
  starting transfers between devices  27.3 us (33%)
  waiting for transfers between devices  14.2 us (17%)
  other arithmetic  1.78 us (2%)
  local copies, waits for them, and re-layouts  1.43 us (2%)
  between operations  0.88 us (1%)
    pallas_call x4, Pallas kernels, tile_chunk(): pl.pallas_call(functools.partial(chunk_kernel, occ_local, share), in_spec...  27.9 us
    ppermute x7, starting transfers between devices, exchange(): return lax.ppermute(array, 'row', [(i, i ^ bits) for i in range(rows)])  10.9 us
    ppermute x1, waiting for transfers between devices, tile_plan(): b_term = lax.ppermute(b_term.astype(jnp.bfloat16), 'orb', step_b)  9 us
    pallas_call x2, Pallas kernels, sort_rows(): pl.pallas_call(functools.partial(sort_kernel, batches, occ_local, first),...  7.85 us
    ppermute x1, starting transfers between devices, tile_plan(): far = lax.ppermute(far, 'orb', swap).astype(jnp.float32)  6.76 us
    ppermute x1, starting transfers between devices, tile_plan(): far_codes = lax.ppermute(own_codes, 'orb', [(i, i ^ 3) for i in range(4)])  4.69 us
    ppermute x7, waiting for transfers between devices, exchange(): return lax.ppermute(array, 'row', [(i, i ^ bits) for i in range(rows)])  3.28 us
    ppermute x1, starting transfers between devices, tile_plan(): a_codes = lax.ppermute(own_codes, 'orb', [(to, at) for at, to in step_a])  2.19 us
  transfers between devices with their start and end apart: 13, of which 5 were waited for; matrix products, arithmetic and copies ran while one was open for 1% of the time, Pallas kernels for 32%

profile of v10, /device:TPU:0, one launch (start us, length us, event | category | flops | bytes accessed | tf_op | source)
XLA Modules:
  0.0 81.3 jit_solution(263044827137339589)
XLA Ops:
  0.0 3.9 %sort_rows.2.refs_1_ = bf16[1024,1024]{1,0:T(8,128)(2,1)} custom-call(s32[16]{0:T(128)} %bitcast.13, bf16[1024,2048]{1,0:T(8,128)(2,1)} %bitcast.11), custom_call_target="tpu_custom_call" | custom-call | flops 536870912 | bytes 4194304 | tf_op jit(solution)/shard_map/sort_rows/pallas_call | solution.py:141
  4.0 0.5 collective-permute-start.5
  4.5 3.9 %sort_rows.3.refs_0_ = bf16[1024,1024]{1,0:T(8,128)(2,1)} custom-call(s32[16]{0:T(128)} %bitcast.14, bf16[1024,2048]{1,0:T(8,128)(2,1)} %bitcast.12), custom_call_target="tpu_custom_call" | custom-call | flops 536870912 | bytes 4194304 | tf_op jit(solution)/shard_map/sort_rows/pallas_call | solution.py:141
  8.6 0.4 collective-permute-start
  9.8 4.7 %collective-permute-start.1 = (s32[65]{0:T(128)S(1)}, s32[65]{0:T(128)S(1)}, u32[]{:S(2)}, u32[]{:S(2)}) collective-permute-start(s32[65]{0:T(128)S(1)} %pad_add_fusion.codes), channel_id=1, source_target_pairs={{0,12},{4,8},{8,4},{12,0},{1,13},{5,9},{9,5},{13,1},{2,14},{6,10},... | collective-permute-start | bytes 788 | tf_op jit(solution)/shard_map/ppermute | solution.py:343
  14.4 0.7 collective-permute-start.3
  15.2 2.2 %collective-permute-start.2 = (s32[65]{0:T(128)S(1)}, s32[65]{0:T(128)S(1)}, u32[]{:S(2)}, u32[]{:S(2)}) collective-permute-start(s32[65]{0:T(128)S(1)} %pad_add_fusion.codes), channel_id=1, source_target_pairs={{4,0},{8,12},{12,4},{0,8},{5,1},{9,13},{13,5},{1,9},{6,2},{10,14},... | collective-permute-start | bytes 788 | tf_op jit(solution)/shard_map/ppermute | solution.py:345
  17.4 1.5 %collective-permute-done.3.codes = s32[65]{0:T(128)S(1)} collective-permute-done((s32[65]{0:T(128)S(1)}, s32[65]{0:T(128)S(1)}, u32[]{:S(2)}, u32[]{:S(2)}) %collective-permute-start.3) | collective-permute-done | bytes 292 | tf_op jit(solution)/shard_map/ppermute | solution.py:346
  18.9 0.4 collective-permute-done.2.codes
  19.3 1.4 %copy-done = bf16[1024,1024]{1,0:T(8,128)(2,1)} copy-done((bf16[1024,1024]{1,0:T(8,128)(2,1)}, bf16[1024,1024]{1,0:T(8,128)(2,1)S(1)}, u32[]{:S(2)}) %copy-start) | copy-done | bytes 2097176
  20.7 6.1 %tile_chunk.5 = (bf16[16,128,128]{2,1,0:T(8,128)(2,1)}, f32[16,128,128]{2,1,0:T(8,128)}) custom-call(s32[16]{0:T(128)} %bitcast.15, s32[16]{0:T(128)} %copy-done.6, s32[65]{0:T(128)} %copy-done.9, bf16[1024,1024]{1,0:T(8,128)(2,1)} %sort_rows.3.refs_0_, bf16[1024,1024]{1,0:T(8,128)(2,1)} %sort_rows.2.refs_1_, ...), custom_call_target="tpu_custom_call" | custom-call | flops 1073741824 | bytes 5767168 | tf_op jit(solution)/shard_map/tile_chunk/pallas_call | solution.py:276
  26.8 1.4 %collective-permute-start.7 = (bf16[16,128,128]{2,1,0:T(8,128)(2,1)}, bf16[16,128,128]{2,1,0:T(8,128)(2,1)S(1)}, u32[]{:S(2)}, u32[]{:S(2)}) collective-permute-start(bf16[16,128,128]{2,1,0:T(8,128)(2,1)} %get-tuple-element.38), channel_id=1, source_target_pairs={{0,2},{1,3},{2,0},{3,1},{4,6},{5,7},{6,4},{7,5},{8,10},{9,11},{10,... | collective-permute-start | bytes 1572872 | tf_op jit(solution)/shard_map/ppermute | solution.py:325
  28.2 9.4 %tile_chunk.4 = (bf16[16,128,128]{2,1,0:T(8,128)(2,1)}, f32[16,128,128]{2,1,0:T(8,128)}) custom-call(s32[16]{0:T(128)} %bitcast.16, s32[16]{0:T(128)} %copy-done.6, s32[65]{0:T(128)} %copy-done.10, bf16[1024,1024]{1,0:T(8,128)(2,1)} %sort_rows.3.refs_0_, bf16[1024,1024]{1,0:T(8,128)(2,1)} %sort_rows.2.refs_1_, ...), custom_call_target="tpu_custom_call" | custom-call | flops 1073741824 | bytes 5767168 | tf_op jit(solution)/shard_map/tile_chunk/pallas_call | solution.py:276
  37.7 0.8 %collective-permute-start.6 = (bf16[16,128,128]{2,1,0:T(8,128)(2,1)}, bf16[16,128,128]{2,1,0:T(8,128)(2,1)S(1)}, u32[]{:S(2)}, u32[]{:S(2)}) collective-permute-start(bf16[16,128,128]{2,1,0:T(8,128)(2,1)} %get-tuple-element.34), channel_id=1, source_target_pairs={{0,2},{1,3},{2,0},{3,1},{4,6},{5,7},{6,4},{7,5},{8,10},{9,11},{10,... | collective-permute-start | bytes 1572872 | tf_op jit(solution)/shard_map/ppermute | solution.py:325
  38.5 2.1 %collective-permute-done.7 = bf16[16,128,128]{2,1,0:T(8,128)(2,1)S(1)} collective-permute-done((bf16[16,128,128]{2,1,0:T(8,128)(2,1)}, bf16[16,128,128]{2,1,0:T(8,128)(2,1)S(1)}, u32[]{:S(2)}, u32[]{:S(2)}) %collective-permute-start.7) | collective-permute-done | bytes 524320 | tf_op jit(solution)/shard_map/ppermute | solution.py:325
  40.7 6.8 %collective-permute-start.8 = (bf16[16,128,128]{2,1,0:T(8,128)(2,1)S(1)}, bf16[16,128,128]{2,1,0:T(8,128)(2,1)S(1)}, u32[]{:S(2)}, u32[]{:S(2)}) collective-permute-start(bf16[16,128,128]{2,1,0:T(8,128)(2,1)S(1)} %add_convert_fusion.1), channel_id=1, source_target_pairs={{0,4},{4,0},{8,12},{12,8},{1,5},{5,1},{9,13},{13,9},{2,6},{6,2},{1... | collective-permute-start | bytes 1572872 | tf_op jit(solution)/shard_map/ppermute | solution.py:357
  47.5 6.3 %tile_chunk.6 = (bf16[16,128,128]{2,1,0:T(8,128)(2,1)}, f32[16,128,128]{2,1,0:T(8,128)}) custom-call(s32[16]{0:T(128)} %bitcast.17, s32[16]{0:T(128)} %copy-done.6, s32[65]{0:T(128)} %copy-done.8, bf16[1024,1024]{1,0:T(8,128)(2,1)} %sort_rows.3.refs_0_, bf16[1024,1024]{1,0:T(8,128)(2,1)} %sort_rows.2.refs_1_, ...), custom_call_target="tpu_custom_call" | custom-call | flops 1073741824 | bytes 5767168 | tf_op jit(solution)/shard_map/tile_chunk/pallas_call | solution.py:276
  53.8 4.8 %collective-permute-start.10 = (bf16[16,128,128]{2,1,0:T(8,128)(2,1)}, bf16[16,128,128]{2,1,0:T(8,128)(2,1)S(1)}, u32[]{:S(2)}, u32[]{:S(2)}) collective-permute-start(bf16[16,128,128]{2,1,0:T(8,128)(2,1)} %get-tuple-element.46), channel_id=1, source_target_pairs={{0,2},{1,3},{2,0},{3,1},{4,6},{5,7},{6,4},{7,5},{8,10},{9,11},{10,... | collective-permute-start | bytes 1572872 | tf_op jit(solution)/shard_map/ppermute | solution.py:325
  58.9 6.1 %tile_chunk.7 = (bf16[16,128,128]{2,1,0:T(8,128)(2,1)}, f32[16,128,128]{2,1,0:T(8,128)}) custom-call(s32[16]{0:T(128)} %bitcast.18, s32[16]{0:T(128)} %copy-done.6, s32[65]{0:T(128)} %copy-done.7, bf16[1024,1024]{1,0:T(8,128)(2,1)} %sort_rows.3.refs_0_, bf16[1024,1024]{1,0:T(8,128)(2,1)} %sort_rows.2.refs_1_, ...), custom_call_target="tpu_custom_call" | custom-call | flops 1073741824 | bytes 5767168 | tf_op jit(solution)/shard_map/tile_chunk/pallas_call | solution.py:276
  65.0 1.2 %collective-permute-done.10 = bf16[16,128,128]{2,1,0:T(8,128)(2,1)S(1)} collective-permute-done((bf16[16,128,128]{2,1,0:T(8,128)(2,1)}, bf16[16,128,128]{2,1,0:T(8,128)(2,1)S(1)}, u32[]{:S(2)}, u32[]{:S(2)}) %collective-permute-start.10) | collective-permute-done | bytes 524320 | tf_op jit(solution)/shard_map/ppermute | solution.py:325
  66.4 2.0 %collective-permute-start.11 = (bf16[16,128,128]{2,1,0:T(8,128)(2,1)S(1)}, bf16[16,128,128]{2,1,0:T(8,128)(2,1)S(1)}, u32[]{:S(2)}, u32[]{:S(2)}) collective-permute-start(bf16[16,128,128]{2,1,0:T(8,128)(2,1)S(1)} %fusion.3), channel_id=1, source_target_pairs={{0,8},{12,4},{4,0},{8,12},{1,9},{13,5},{5,1},{9,13},{2,10},{14,6},... | collective-permute-start | bytes 1572872 | tf_op jit(solution)/shard_map/ppermute | solution.py:365
  68.4 2.8 %collective-permute-start.12 = (bf16[16,128,128]{2,1,0:T(8,128)(2,1)S(1)}, bf16[16,128,128]{2,1,0:T(8,128)(2,1)S(1)}, u32[]{:S(2)}, u32[]{:S(2)}) collective-permute-start(bf16[16,128,128]{2,1,0:T(8,128)(2,1)S(1)} %copy-done.11), channel_id=1, source_target_pairs={{0,2},{1,3},{2,0},{3,1},{4,6},{5,7},{6,4},{7,5},{8,10},{9,11},{10,... | collective-permute-start | bytes 1572872 | tf_op jit(solution)/shard_map/ppermute | solution.py:325
  71.2 9.0 %collective-permute-done.11 = bf16[16,128,128]{2,1,0:T(8,128)(2,1)S(1)} collective-permute-done((bf16[16,128,128]{2,1,0:T(8,128)(2,1)S(1)}, bf16[16,128,128]{2,1,0:T(8,128)(2,1)S(1)}, u32[]{:S(2)}, u32[]{:S(2)}) %collective-permute-start.11) | collective-permute-done | bytes 524320 | tf_op jit(solution)/shard_map/ppermute | solution.py:365
  80.3 1.0 %fusion.4 = bf16[1,16,128,128]{3,2,1,0:T(8,128)(2,1)} fusion(f32[16,128,128]{2,1,0:T(8,128)S(1)} %convert_add_fusion, f32[16,128,128]{2,1,0:T(8,128)S(1)} %copy-done.1, bf16[16,128,128]{2,1,0:T(8,128)(2,1)S(1)} %collective-permute-done.12), kind=kLoop, calls=%fused_computation.9 | loop fusion | flops 1048576 | bytes 3145728 | tf_op jit(solution)/shard_map/broadcast_in_dim | solution.py:369
  (41 shorter events, 1.0 us)
Async XLA Ops:
  3.9 4.6 %copy-start.5 = (s32[16,1]{0,1:T(1,128)S(1)}, s32[16,1]{0,1:T(1,128)}, u32[]{:S(2)}) copy-start(s32[16,1]{0,1:T(1,128)} %param.5) | copy-start | bytes 196
  3.9 5.7 %copy-start.12 = (s32[1,64]{1,0:T(1,128)S(1)}, s32[1,64]{1,0:T(1,128)}, u32[]{:S(2)}) copy-start(s32[1,64]{1,0:T(1,128)} %param.6) | copy-start | bytes 772
  4.0 15.3 %collective-permute-start.5 = (bf16[1024,1024]{1,0:T(8,128)(2,1)}, bf16[1024,1024]{1,0:T(8,128)(2,1)S(1)}, u32[]{:S(2)}, u32[]{:S(2)}) collective-permute-start(bf16[1024,1024]{1,0:T(8,128)(2,1)} %sort_rows.2.refs_1_), channel_id=1, source_target_pairs={{0,1},{1,0},{2,3},{3,2},{4,5},{5,4},{6,7},{7,6},{8,9},{9,8},{10,11... | collective-permute-start | bytes 6291464 | tf_op jit(solution)/shard_map/ppermute | solution.py:325
  8.4 10.9 %collective-permute-start.4 = (bf16[1024,1024]{1,0:T(8,128)(2,1)}, bf16[1024,1024]{1,0:T(8,128)(2,1)}, u32[]{:S(2)}, u32[]{:S(2)}) collective-permute-start(bf16[1024,1024]{1,0:T(8,128)(2,1)} %sort_rows.3.refs_0_), channel_id=1, source_target_pairs={{0,1},{1,0},{2,3},{3,2},{4,5},{5,4},{6,7},{7,6},{8,9},{9,8},{10,11... | collective-permute-start | bytes 6291464 | tf_op jit(solution)/shard_map/ppermute | solution.py:325
  8.6 5.9 %collective-permute-start = (s32[16]{0:T(128)S(1)}, s32[16]{0:T(128)S(1)}, u32[]{:S(2)}, u32[]{:S(2)}) collective-permute-start(s32[16]{0:T(128)S(1)} %bitcast.19), channel_id=1, source_target_pairs={{0,1},{1,0},{2,3},{3,2},{4,5},{5,4},{6,7},{7,6},{8,9},{9,8},{10,11... | collective-permute-start | bytes 200 | tf_op jit(solution)/shard_map/ppermute | solution.py:325
  9.8 27.9 %copy-start.7 = (s32[65]{0:T(128)}, s32[65]{0:T(128)S(1)}, u32[]{:S(2)}) copy-start(s32[65]{0:T(128)S(1)} %pad_add_fusion.codes) | copy-start | bytes 784
  9.8 7.6 %collective-permute-start.1 = (s32[65]{0:T(128)S(1)}, s32[65]{0:T(128)S(1)}, u32[]{:S(2)}, u32[]{:S(2)}) collective-permute-start(s32[65]{0:T(128)S(1)} %pad_add_fusion.codes), channel_id=1, source_target_pairs={{0,12},{4,8},{8,4},{12,0},{1,13},{5,9},{9,5},{13,1},{2,14},{6,10},... | collective-permute-start | bytes 788 | tf_op jit(solution)/shard_map/ppermute | solution.py:343
  14.4 4.9 %copy-start.6 = (s32[16]{0:T(128)}, s32[16]{0:T(128)S(1)}, u32[]{:S(2)}) copy-start(s32[16]{0:T(128)S(1)} %collective-permute-done.other_owner) | copy-start | bytes 196
  14.4 4.4 %collective-permute-start.3 = (s32[65]{0:T(128)S(1)}, s32[65]{0:T(128)S(1)}, u32[]{:S(2)}, u32[]{:S(2)}) collective-permute-start(s32[65]{0:T(128)S(1)} %pad_add_fusion.codes), channel_id=1, source_target_pairs={{8,0},{4,12},{0,4},{12,8},{9,1},{5,13},{1,5},{13,9},{10,2},{6,14},... | collective-permute-start | bytes 788 | tf_op jit(solution)/shard_map/ppermute | solution.py:346
  15.2 4.1 %collective-permute-start.2 = (s32[65]{0:T(128)S(1)}, s32[65]{0:T(128)S(1)}, u32[]{:S(2)}, u32[]{:S(2)}) collective-permute-start(s32[65]{0:T(128)S(1)} %pad_add_fusion.codes), channel_id=1, source_target_pairs={{4,0},{8,12},{12,4},{0,8},{5,1},{9,13},{13,5},{1,9},{6,2},{10,14},... | collective-permute-start | bytes 788 | tf_op jit(solution)/shard_map/ppermute | solution.py:345
  18.9 18.8 %copy-start.8 = (s32[65]{0:T(128)}, s32[65]{0:T(128)S(1)}, u32[]{:S(2)}) copy-start(s32[65]{0:T(128)S(1)} %collective-permute-done.3.codes) | copy-start | bytes 784
  19.3 8.9 %copy-start.10 = (s32[65]{0:T(128)}, s32[65]{0:T(128)S(1)}, u32[]{:S(2)}) copy-start(s32[65]{0:T(128)S(1)} %collective-permute-done.2.codes) | copy-start | bytes 784
  26.8 13.8 %copy-start.4 = (f32[16,128,128]{2,1,0:T(8,128)S(1)}, f32[16,128,128]{2,1,0:T(8,128)}, u32[]{:S(2)}) copy-start(f32[16,128,128]{2,1,0:T(8,128)} %get-tuple-element.37) | copy-start | bytes 3145732
  26.8 13.7 %collective-permute-start.7 = (bf16[16,128,128]{2,1,0:T(8,128)(2,1)}, bf16[16,128,128]{2,1,0:T(8,128)(2,1)S(1)}, u32[]{:S(2)}, u32[]{:S(2)}) collective-permute-start(bf16[16,128,128]{2,1,0:T(8,128)(2,1)} %get-tuple-element.38), channel_id=1, source_target_pairs={{0,2},{1,3},{2,0},{3,1},{4,6},{5,7},{6,4},{7,5},{8,10},{9,11},{10,... | collective-permute-start | bytes 1572872 | tf_op jit(solution)/shard_map/ppermute | solution.py:325
  37.7 20.9 %collective-permute-start.6 = (bf16[16,128,128]{2,1,0:T(8,128)(2,1)}, bf16[16,128,128]{2,1,0:T(8,128)(2,1)S(1)}, u32[]{:S(2)}, u32[]{:S(2)}) collective-permute-start(bf16[16,128,128]{2,1,0:T(8,128)(2,1)} %get-tuple-element.34), channel_id=1, source_target_pairs={{0,2},{1,3},{2,0},{3,1},{4,6},{5,7},{6,4},{7,5},{8,10},{9,11},{10,... | collective-permute-start | bytes 1572872 | tf_op jit(solution)/shard_map/ppermute | solution.py:325
  40.7 17.9 %copy-start.3 = (f32[16,128,128]{2,1,0:T(8,128)S(1)}, f32[16,128,128]{2,1,0:T(8,128)}, u32[]{:S(2)}) copy-start(f32[16,128,128]{2,1,0:T(8,128)} %get-tuple-element.33) | copy-start | bytes 3145732
  40.7 17.9 %collective-permute-start.8 = (bf16[16,128,128]{2,1,0:T(8,128)(2,1)S(1)}, bf16[16,128,128]{2,1,0:T(8,128)(2,1)S(1)}, u32[]{:S(2)}, u32[]{:S(2)}) collective-permute-start(bf16[16,128,128]{2,1,0:T(8,128)(2,1)S(1)} %add_convert_fusion.1), channel_id=1, source_target_pairs={{0,4},{4,0},{8,12},{12,8},{1,5},{5,1},{9,13},{13,9},{2,6},{6,2},{1... | collective-permute-start | bytes 1572872 | tf_op jit(solution)/shard_map/ppermute | solution.py:357
  53.8 12.5 %collective-permute-start.10 = (bf16[16,128,128]{2,1,0:T(8,128)(2,1)}, bf16[16,128,128]{2,1,0:T(8,128)(2,1)S(1)}, u32[]{:S(2)}, u32[]{:S(2)}) collective-permute-start(bf16[16,128,128]{2,1,0:T(8,128)(2,1)} %get-tuple-element.46), channel_id=1, source_target_pairs={{0,2},{1,3},{2,0},{3,1},{4,6},{5,7},{6,4},{7,5},{8,10},{9,11},{10,... | collective-permute-start | bytes 1572872 | tf_op jit(solution)/shard_map/ppermute | solution.py:325
  58.8 7.4 %copy-start.2 = (f32[16,128,128]{2,1,0:T(8,128)S(1)}, f32[16,128,128]{2,1,0:T(8,128)}, u32[]{:S(2)}) copy-start(f32[16,128,128]{2,1,0:T(8,128)} %get-tuple-element.45) | copy-start | bytes 3145732
  58.8 12.4 %collective-permute-start.9 = (bf16[16,128,128]{2,1,0:T(8,128)(2,1)S(1)}, bf16[16,128,128]{2,1,0:T(8,128)(2,1)S(1)}, u32[]{:S(2)}, u32[]{:S(2)}) collective-permute-start(bf16[16,128,128]{2,1,0:T(8,128)(2,1)S(1)} %fusion.1), channel_id=1, source_target_pairs={{0,4},{12,8},{4,12},{8,0},{1,5},{13,9},{5,13},{9,1},{2,6},{14,10},... | collective-permute-start | bytes 1572872 | tf_op jit(solution)/shard_map/ppermute | solution.py:361
  65.0 3.4 %copy-start.11 = (bf16[16,128,128]{2,1,0:T(8,128)(2,1)S(1)}, bf16[16,128,128]{2,1,0:T(8,128)(2,1)}, u32[]{:S(2)}) copy-start(bf16[16,128,128]{2,1,0:T(8,128)(2,1)} %get-tuple-element.49) | copy-start | bytes 1572868
  65.0 15.3 %copy-start.1 = (f32[16,128,128]{2,1,0:T(8,128)S(1)}, f32[16,128,128]{2,1,0:T(8,128)}, u32[]{:S(2)}) copy-start(f32[16,128,128]{2,1,0:T(8,128)} %get-tuple-element.48) | copy-start | bytes 3145732
  66.4 13.7 %collective-permute-start.11 = (bf16[16,128,128]{2,1,0:T(8,128)(2,1)S(1)}, bf16[16,128,128]{2,1,0:T(8,128)(2,1)S(1)}, u32[]{:S(2)}, u32[]{:S(2)}) collective-permute-start(bf16[16,128,128]{2,1,0:T(8,128)(2,1)S(1)} %fusion.3), channel_id=1, source_target_pairs={{0,8},{12,4},{4,0},{8,12},{1,9},{13,5},{5,1},{9,13},{2,10},{14,6},... | collective-permute-start | bytes 1572872 | tf_op jit(solution)/shard_map/ppermute | solution.py:365
  68.4 11.9 %collective-permute-start.12 = (bf16[16,128,128]{2,1,0:T(8,128)(2,1)S(1)}, bf16[16,128,128]{2,1,0:T(8,128)(2,1)S(1)}, u32[]{:S(2)}, u32[]{:S(2)}) collective-permute-start(bf16[16,128,128]{2,1,0:T(8,128)(2,1)S(1)} %copy-done.11), channel_id=1, source_target_pairs={{0,2},{1,3},{2,0},{3,1},{4,6},{5,7},{6,4},{7,5},{8,10},{9,11},{10,... | collective-permute-start | bytes 1572872 | tf_op jit(solution)/shard_map/ppermute | solution.py:325
  (2 other events, 3.3 us)

commit v11 on v9

--- a/solution.py
+++ b/solution.py
@@ -141,6 +141,7 @@
     send_first = (row_at ^ 2) * share
     keep_first = row_at * share
     width = math.gcd(4, share)
+    blocks_at_once = math.gcd(4, domain // TILE)
 
     def out_copies(turn_at):
         sends = pl.ds(turn_at * width, width)
@@ -152,9 +153,15 @@
 
     def add_part(part, fresh):
         rows = pl.ds(pl.multiple_of(part * PART, PART), PART)
-        for column in range(0, domain, TILE):
-            columns = slice(column, column + TILE)
-            turned[columns, :] = packed_rows[rows, columns].T
+
+        def turn(group, carry):
+            for block in range(blocks_at_once):
+                column = pl.multiple_of((group * blocks_at_once + block) * TILE, TILE)
+                columns = pl.ds(column, TILE)
+                turned[columns, :] = packed_rows[rows, columns].T
+            return carry
+
+        lax.fori_loop(0, domain // TILE // blocks_at_once, turn, 0)
 
         def several(turn_at, carry):
             for offset in range(width):
@@ -263,13 +270,15 @@
     own_rows = half_tensor.reshape(aux_local * occ_local, domain)
     other_rows = exchange(own_rows, 1)
     own_owner = batch_owner[:, 0]
-    owners = own_owner, exchange(own_owner, 1)
+    other_owner = exchange(own_owner, 1)
     columns = block_columns(pair_list[0], live_pairs[0], domain // TILE)
     own_codes = jnp.concatenate([columns, orb_at[None]])
     far_codes = lax.ppermute(own_codes, "orb", [(i, i ^ 3) for i in range(4)])
+    own_codes, other_owner = after(own_codes, other_owner)
     a_codes = lax.ppermute(own_codes, "orb", [(to, at) for at, to in step_a])
     b_codes = lax.ppermute(own_codes, "orb", [(to, at) for at, to in step_b])
     far_codes, a_codes, b_codes = lax.optimization_barrier((far_codes, a_codes, b_codes))
+    owners = own_owner, other_owner
 
     def chunk(codes, other_rows):
         return tile_chunk(owners, codes, own_rows, other_rows, occ_local, share)
@@ -287,9 +296,9 @@
     b_keep, own_send = after(b_keep, own_send)
     b_term = over_x(b_send, b_keep) + jnp.where(inner, 0.0, far)
     b_term = lax.ppermute(b_term.astype(jnp.bfloat16), "orb", step_b)
-    beside = a_term.astype(jnp.float32) + b_term.astype(jnp.float32)
-    beside, own_keep = after(beside, own_keep)
-    total = over_x(own_send, own_keep) + beside
+    beside = over_x(own_send, own_keep) + a_term.astype(jnp.float32)
+    beside, b_term = after(beside, b_term)
+    total = beside + b_term.astype(jnp.float32)
     return total.astype(jnp.bfloat16)[None]
 
 

time: 75.7 us -> 75.9 us (level)
  waiting for transfers between devices: 18.2 us -> 16.2 us
  other arithmetic: 2.44 us -> 3.62 us
  Pallas kernels: 36 us -> 36.8 us
    ppermute x1, waiting for transfers between devices: 12.7 us -> 1.07 us  [tile_plan(): b_term = lax.ppermute(b_term.astype(jnp.bfloat16), 'orb', step_b)]
    ppermute x6, waiting for transfers between devices: 3.98 us -> 12 us  [exchange(): return lax.ppermute(array, 'row', [(i, i ^ bits) for i in range(rows)])]
    ppermute x1, starting transfers between devices: 0.06 us -> 1.86 us  [tile_plan(): a_term = lax.ppermute(a_term, 'orb', step_a)]
    ppermute x1, waiting for transfers between devices: 0.01 us -> 1.57 us  [tile_plan(): a_codes = lax.ppermute(own_codes, 'orb', [(to, at) for at, to in step_a])]
    ppermute x1, waiting for transfers between devices: 0.01 us -> 1.51 us  [tile_plan(): b_codes = lax.ppermute(own_codes, 'orb', [(to, at) for at, to in step_b])]
    ppermute x1, waiting for transfers between devices: 1.49 us -> 0.01 us  [tile_plan(): far_codes = lax.ppermute(own_codes, 'orb', [(i, i ^ 3) for i in range(4)])]
    ppermute x1, starting transfers between devices: 1.43 us -> 0.07 us  [tile_plan(): far = lax.ppermute(far, 'orb', swap).astype(jnp.float32)]
    add x1, other arithmetic: 0.12 us -> 1.39 us  [tile_plan(): beside = over_x(own_send, own_keep) + a_term.astype(jnp.float32)]
  transfers between devices with their start and end apart: 12 -> 12, of which waited for: 5 -> 7; matrix products, arithmetic and copies ran while one was open for 2% -> 4% of each run, Pallas kernels for 37% -> 34%
where the time goes in v11:
time: 75.9 us; the launch traced here: 74.9 us
  Pallas kernels  36.8 us (48%)
  starting transfers between devices  17.4 us (23%)
  waiting for transfers between devices  16.2 us (21%)
  other arithmetic  3.62 us (5%)
  between operations  0.8 us (1%)
    pallas_call x4, Pallas kernels, tile_chunk(): pl.pallas_call(functools.partial(chunk_kernel, occ_local, share), in_spec...  36.8 us
    ppermute x6, waiting for transfers between devices, exchange(): return lax.ppermute(array, 'row', [(i, i ^ bits) for i in range(rows)])  12 us
    ppermute x1, starting transfers between devices, tile_plan(): far_codes = lax.ppermute(own_codes, 'orb', [(i, i ^ 3) for i in range(4)])  5.06 us
    ppermute x6, starting transfers between devices, exchange(): return lax.ppermute(array, 'row', [(i, i ^ bits) for i in range(rows)])  4.84 us
    ppermute x1, starting transfers between devices, tile_plan(): b_term = lax.ppermute(b_term.astype(jnp.bfloat16), 'orb', step_b)  2.52 us
    ppermute x1, starting transfers between devices, tile_plan(): b_codes = lax.ppermute(own_codes, 'orb', [(to, at) for at, to in step_b])  2.05 us
    ppermute x1, starting transfers between devices, tile_plan(): a_term = lax.ppermute(a_term, 'orb', step_a)  1.86 us
    ppermute x1, waiting for transfers between devices, tile_plan(): a_codes = lax.ppermute(own_codes, 'orb', [(to, at) for at, to in step_a])  1.57 us
  transfers between devices with their start and end apart: 12, of which 7 were waited for; matrix products, arithmetic and copies ran while one was open for 4% of the time, Pallas kernels for 34%

profile of v11, /device:TPU:0, one launch (start us, length us, event | category | flops | bytes accessed | tf_op | source)
XLA Modules:
  0.0 74.9 jit_solution(16172364983391658077)
XLA Ops:
  0.0 0.5 collective-permute-start.1
  1.2 0.7 fusion.9
  1.9 5.1 %collective-permute-start.2 = (s32[65]{0:T(128)S(1)}, s32[65]{0:T(128)S(1)}, u32[]{:S(2)}, u32[]{:S(2)}) collective-permute-start(s32[65]{0:T(128)S(1)} %pad_add_fusion.codes), channel_id=1, source_target_pairs={{0,12},{4,8},{8,4},{12,0},{1,13},{5,9},{9,5},{13,1},{2,14},{6,10},... | collective-permute-start | bytes 788 | tf_op jit(solution)/shard_map/ppermute | solution.py:276
  7.0 2.0 %collective-permute-start.4 = (s32[65]{0:T(128)S(1)}, s32[65]{0:T(128)S(1)}, u32[]{:S(2)}, u32[]{:S(2)}) collective-permute-start(s32[65]{0:T(128)S(1)} %pad_add_fusion.codes), channel_id=1, source_target_pairs={{8,0},{4,12},{0,4},{12,8},{9,1},{5,13},{1,5},{13,9},{10,2},{6,14},... | collective-permute-start | bytes 788 | tf_op jit(solution)/shard_map/ppermute | solution.py:279
  9.0 1.0 %collective-permute-start.3 = (s32[65]{0:T(128)S(1)}, s32[65]{0:T(128)S(1)}, u32[]{:S(2)}, u32[]{:S(2)}) collective-permute-start(s32[65]{0:T(128)S(1)} %pad_add_fusion.codes), channel_id=1, source_target_pairs={{4,0},{8,12},{12,4},{0,8},{5,1},{9,13},{13,5},{1,9},{6,2},{10,14},... | collective-permute-start | bytes 788 | tf_op jit(solution)/shard_map/ppermute | solution.py:278
  10.1 1.5 %collective-permute-done.4.codes = s32[65]{0:T(128)S(1)} collective-permute-done((s32[65]{0:T(128)S(1)}, s32[65]{0:T(128)S(1)}, u32[]{:S(2)}, u32[]{:S(2)}) %collective-permute-start.4) | collective-permute-done | bytes 292 | tf_op jit(solution)/shard_map/ppermute | solution.py:279
  11.6 1.6 %collective-permute-done.3.codes = s32[65]{0:T(128)S(1)} collective-permute-done((s32[65]{0:T(128)S(1)}, s32[65]{0:T(128)S(1)}, u32[]{:S(2)}, u32[]{:S(2)}) %collective-permute-start.3) | collective-permute-done | bytes 292 | tf_op jit(solution)/shard_map/ppermute | solution.py:278
  13.2 11.3 %tile_chunk.4 = (bf16[16,128,128]{2,1,0:T(8,128)(2,1)}, f32[16,128,128]{2,1,0:T(8,128)}) custom-call(s32[16]{0:T(128)} %bitcast.17, s32[16]{0:T(128)} %copy-done.3, s32[65]{0:T(128)} %copy-done.6, bf16[1024,2048]{1,0:T(8,128)(2,1)} %bitcast.12, bf16[1024,2048]{1,0:T(8,128)(2,1)} %collective-permute-done.1.other_rows), custom_call_target="tpu_custom_call" | custom-call | flops 2147483648 | bytes 9961472 | tf_op jit(solution)/shard_map/tile_chunk/pallas_call | solution.py:211
  24.5 1.6 %collective-permute-start.5 = (bf16[16,128,128]{2,1,0:T(8,128)(2,1)}, bf16[16,128,128]{2,1,0:T(8,128)(2,1)S(1)}, u32[]{:S(2)}, u32[]{:S(2)}) collective-permute-start(bf16[16,128,128]{2,1,0:T(8,128)(2,1)} %get-tuple-element.30), channel_id=1, source_target_pairs={{0,2},{1,3},{2,0},{3,1},{4,6},{5,7},{6,4},{7,5},{8,10},{9,11},{10,... | collective-permute-start | bytes 1572872 | tf_op jit(solution)/shard_map/ppermute | solution.py:262
  26.1 8.5 %tile_chunk.5 = (bf16[16,128,128]{2,1,0:T(8,128)(2,1)}, f32[16,128,128]{2,1,0:T(8,128)}) custom-call(s32[16]{0:T(128)} %bitcast.18, s32[16]{0:T(128)} %copy-done.3, s32[65]{0:T(128)} %copy-done.7, bf16[1024,2048]{1,0:T(8,128)(2,1)} %bitcast.13, bf16[1024,2048]{1,0:T(8,128)(2,1)} %collective-permute-done.1.other_rows), custom_call_target="tpu_custom_call" | custom-call | flops 2147483648 | bytes 9961472 | tf_op jit(solution)/shard_map/tile_chunk/pallas_call | solution.py:211
  34.5 0.6 collective-permute-start.6
  35.2 4.1 %collective-permute-done.5 = bf16[16,128,128]{2,1,0:T(8,128)(2,1)S(1)} collective-permute-done((bf16[16,128,128]{2,1,0:T(8,128)(2,1)}, bf16[16,128,128]{2,1,0:T(8,128)(2,1)S(1)}, u32[]{:S(2)}, u32[]{:S(2)}) %collective-permute-start.5) | collective-permute-done | bytes 524320 | tf_op jit(solution)/shard_map/ppermute | solution.py:262
  39.5 8.6 %tile_chunk.7 = (bf16[16,128,128]{2,1,0:T(8,128)(2,1)}, f32[16,128,128]{2,1,0:T(8,128)}) custom-call(s32[16]{0:T(128)} %bitcast.19, s32[16]{0:T(128)} %copy-done.3, s32[65]{0:T(128)} %copy-done.5, bf16[1024,2048]{1,0:T(8,128)(2,1)} %bitcast.14, bf16[1024,2048]{1,0:T(8,128)(2,1)} %collective-permute-done.1.other_rows), custom_call_target="tpu_custom_call" | custom-call | flops 2147483648 | bytes 9961472 | tf_op jit(solution)/shard_map/tile_chunk/pallas_call | solution.py:211
  48.1 2.0 %collective-permute-start.10 = (bf16[16,128,128]{2,1,0:T(8,128)(2,1)}, bf16[16,128,128]{2,1,0:T(8,128)(2,1)S(1)}, u32[]{:S(2)}, u32[]{:S(2)}) collective-permute-start(bf16[16,128,128]{2,1,0:T(8,128)(2,1)} %get-tuple-element.44), channel_id=1, source_target_pairs={{0,2},{1,3},{2,0},{3,1},{4,6},{5,7},{6,4},{7,5},{8,10},{9,11},{10,... | collective-permute-start | bytes 1572872 | tf_op jit(solution)/shard_map/ppermute | solution.py:262
  50.2 0.2 fusion.1
  50.4 1.9 %collective-permute-start.9 = (bf16[16,128,128]{2,1,0:T(8,128)(2,1)S(1)}, bf16[16,128,128]{2,1,0:T(8,128)(2,1)S(1)}, u32[]{:S(2)}, u32[]{:S(2)}) collective-permute-start(bf16[16,128,128]{2,1,0:T(8,128)(2,1)S(1)} %fusion.1), channel_id=1, source_target_pairs={{0,4},{12,8},{4,12},{8,0},{1,5},{13,9},{5,13},{9,1},{2,6},{14,10},... | collective-permute-start | bytes 1572872 | tf_op jit(solution)/shard_map/ppermute | solution.py:294
  52.3 8.4 %tile_chunk.6 = (bf16[16,128,128]{2,1,0:T(8,128)(2,1)}, f32[16,128,128]{2,1,0:T(8,128)}) custom-call(s32[16]{0:T(128)} %bitcast.20, s32[16]{0:T(128)} %copy-done.3, s32[65]{0:T(128)} %copy-done.4, bf16[1024,2048]{1,0:T(8,128)(2,1)} %bitcast.15, bf16[1024,2048]{1,0:T(8,128)(2,1)} %collective-permute-done.1.other_rows), custom_call_target="tpu_custom_call" | custom-call | flops 2147483648 | bytes 9961472 | tf_op jit(solution)/shard_map/tile_chunk/pallas_call | solution.py:211
  60.7 0.2 collective-permute-start.8
  60.9 0.2 fusion.3
  61.2 2.5 %collective-permute-start.11 = (bf16[16,128,128]{2,1,0:T(8,128)(2,1)S(1)}, bf16[16,128,128]{2,1,0:T(8,128)(2,1)S(1)}, u32[]{:S(2)}, u32[]{:S(2)}) collective-permute-start(bf16[16,128,128]{2,1,0:T(8,128)(2,1)S(1)} %fusion.3), channel_id=1, source_target_pairs={{0,8},{12,4},{4,0},{8,12},{1,9},{13,5},{5,1},{9,13},{2,10},{14,6},... | collective-permute-start | bytes 1572872 | tf_op jit(solution)/shard_map/ppermute | solution.py:298
  63.7 7.8 %collective-permute-done.8 = bf16[16,128,128]{2,1,0:T(8,128)(2,1)S(1)} collective-permute-done((bf16[16,128,128]{2,1,0:T(8,128)(2,1)}, bf16[16,128,128]{2,1,0:T(8,128)(2,1)S(1)}, u32[]{:S(2)}, u32[]{:S(2)}) %collective-permute-start.8) | collective-permute-done | bytes 524320 | tf_op jit(solution)/shard_map/ppermute | solution.py:262
  71.5 1.4 %convert_add_fusion = f32[16,128,128]{2,1,0:T(8,128)S(1)} fusion(bf16[16,128,128]{2,1,0:T(8,128)(2,1)S(1)} %collective-permute-done.9, f32[16,128,128]{2,1,0:T(8,128)} %get-tuple-element.37, bf16[16,128,128]{2,1,0:T(8,128)(2,1)S(1)} %collective-permute-done.8), kind=kLoop, calls=%fused_computation.7 | loop fusion | flops 1048576 | bytes 3145728 | tf_op jit(solution)/shard_map/add | solution.py:299
  72.9 1.1 %collective-permute-done.11 = bf16[16,128,128]{2,1,0:T(8,128)(2,1)S(1)} collective-permute-done((bf16[16,128,128]{2,1,0:T(8,128)(2,1)S(1)}, bf16[16,128,128]{2,1,0:T(8,128)(2,1)S(1)}, u32[]{:S(2)}, u32[]{:S(2)}) %collective-permute-start.11) | collective-permute-done | bytes 524320 | tf_op jit(solution)/shard_map/ppermute | solution.py:298
  74.0 0.9 %fusion.4 = bf16[1,16,128,128]{3,2,1,0:T(8,128)(2,1)} fusion(f32[16,128,128]{2,1,0:T(8,128)S(1)} %convert_add_fusion, bf16[16,128,128]{2,1,0:T(8,128)(2,1)S(1)} %collective-permute-done.11), kind=kLoop, calls=%fused_computation.9 | loop fusion | flops 786432 | bytes 2097152 | tf_op jit(solution)/shard_map/broadcast_in_dim | solution.py:302
  (27 shorter events, 0.5 us)
Async XLA Ops:
  0.0 13.1 %collective-permute-start.1 = (bf16[1024,2048]{1,0:T(8,128)(2,1)}, bf16[1024,2048]{1,0:T(8,128)(2,1)}, u32[]{:S(2)}, u32[]{:S(2)}) collective-permute-start(bf16[1024,2048]{1,0:T(8,128)(2,1)} %bitcast.11), channel_id=1, source_target_pairs={{0,1},{1,0},{2,3},{3,2},{4,5},{5,4},{6,7},{7,6},{8,9},{9,8},{10,11... | collective-permute-start | bytes 12582920 | tf_op jit(solution)/shard_map/ppermute | solution.py:262
  0.5 6.5 %collective-permute-start = (s32[16]{0:T(128)}, s32[16]{0:T(128)S(1)}, u32[]{:S(2)}, u32[]{:S(2)}) collective-permute-start(s32[16]{0:T(128)} %bitcast.16), channel_id=1, source_target_pairs={{0,1},{1,0},{2,3},{3,2},{4,5},{5,4},{6,7},{7,6},{8,9},{9,8},{10,11... | collective-permute-start | bytes 200 | tf_op jit(solution)/shard_map/ppermute | solution.py:262
  1.9 46.2 %copy-start.4 = (s32[65]{0:T(128)}, s32[65]{0:T(128)S(1)}, u32[]{:S(2)}) copy-start(s32[65]{0:T(128)S(1)} %pad_add_fusion.codes) | copy-start | bytes 784
  1.9 8.1 %collective-permute-start.2 = (s32[65]{0:T(128)S(1)}, s32[65]{0:T(128)S(1)}, u32[]{:S(2)}, u32[]{:S(2)}) collective-permute-start(s32[65]{0:T(128)S(1)} %pad_add_fusion.codes), channel_id=1, source_target_pairs={{0,12},{4,8},{8,4},{12,0},{1,13},{5,9},{9,5},{13,1},{2,14},{6,10},... | collective-permute-start | bytes 788 | tf_op jit(solution)/shard_map/ppermute | solution.py:276
  7.0 6.2 %copy-start.3 = (s32[16]{0:T(128)}, s32[16]{0:T(128)S(1)}, u32[]{:S(2)}) copy-start(s32[16]{0:T(128)S(1)} %collective-permute-done.other_owner) | copy-start | bytes 196
  7.0 4.6 %collective-permute-start.4 = (s32[65]{0:T(128)S(1)}, s32[65]{0:T(128)S(1)}, u32[]{:S(2)}, u32[]{:S(2)}) collective-permute-start(s32[65]{0:T(128)S(1)} %pad_add_fusion.codes), channel_id=1, source_target_pairs={{8,0},{4,12},{0,4},{12,8},{9,1},{5,13},{1,5},{13,9},{10,2},{6,14},... | collective-permute-start | bytes 788 | tf_op jit(solution)/shard_map/ppermute | solution.py:279
  9.0 4.1 %collective-permute-start.3 = (s32[65]{0:T(128)S(1)}, s32[65]{0:T(128)S(1)}, u32[]{:S(2)}, u32[]{:S(2)}) collective-permute-start(s32[65]{0:T(128)S(1)} %pad_add_fusion.codes), channel_id=1, source_target_pairs={{4,0},{8,12},{12,4},{0,8},{5,1},{9,13},{13,5},{1,9},{6,2},{10,14},... | collective-permute-start | bytes 788 | tf_op jit(solution)/shard_map/ppermute | solution.py:278
  10.1 3.1 %copy-start.6 = (s32[65]{0:T(128)}, s32[65]{0:T(128)S(1)}, u32[]{:S(2)}) copy-start(s32[65]{0:T(128)S(1)} %collective-permute-done.2.codes) | copy-start | bytes 784
  11.6 12.9 %copy-start.5 = (s32[65]{0:T(128)}, s32[65]{0:T(128)S(1)}, u32[]{:S(2)}) copy-start(s32[65]{0:T(128)S(1)} %collective-permute-done.4.codes) | copy-start | bytes 784
  13.1 11.4 %copy-start.7 = (s32[65]{0:T(128)}, s32[65]{0:T(128)S(1)}, u32[]{:S(2)}) copy-start(s32[65]{0:T(128)S(1)} %collective-permute-done.3.codes) | copy-start | bytes 784
  24.5 14.7 %copy-start.2 = (f32[16,128,128]{2,1,0:T(8,128)S(1)}, f32[16,128,128]{2,1,0:T(8,128)}, u32[]{:S(2)}) copy-start(f32[16,128,128]{2,1,0:T(8,128)} %get-tuple-element.29) | copy-start | bytes 3145732
  24.5 14.7 %collective-permute-start.5 = (bf16[16,128,128]{2,1,0:T(8,128)(2,1)}, bf16[16,128,128]{2,1,0:T(8,128)(2,1)S(1)}, u32[]{:S(2)}, u32[]{:S(2)}) collective-permute-start(bf16[16,128,128]{2,1,0:T(8,128)(2,1)} %get-tuple-element.30), channel_id=1, source_target_pairs={{0,2},{1,3},{2,0},{3,1},{4,6},{5,7},{6,4},{7,5},{8,10},{9,11},{10,... | collective-permute-start | bytes 1572872 | tf_op jit(solution)/shard_map/ppermute | solution.py:262
  34.5 15.6 %collective-permute-start.6 = (bf16[16,128,128]{2,1,0:T(8,128)(2,1)}, bf16[16,128,128]{2,1,0:T(8,128)(2,1)S(1)}, u32[]{:S(2)}, u32[]{:S(2)}) collective-permute-start(bf16[16,128,128]{2,1,0:T(8,128)(2,1)} %get-tuple-element.34), channel_id=1, source_target_pairs={{0,2},{1,3},{2,0},{3,1},{4,6},{5,7},{6,4},{7,5},{8,10},{9,11},{10,... | collective-permute-start | bytes 1572872 | tf_op jit(solution)/shard_map/ppermute | solution.py:262
  39.4 10.8 %copy-start.1 = (f32[16,128,128]{2,1,0:T(8,128)S(1)}, f32[16,128,128]{2,1,0:T(8,128)}, u32[]{:S(2)}) copy-start(f32[16,128,128]{2,1,0:T(8,128)} %get-tuple-element.33) | copy-start | bytes 3145732
  39.4 10.8 %collective-permute-start.7 = (bf16[16,128,128]{2,1,0:T(8,128)(2,1)S(1)}, bf16[16,128,128]{2,1,0:T(8,128)(2,1)S(1)}, u32[]{:S(2)}, u32[]{:S(2)}) collective-permute-start(bf16[16,128,128]{2,1,0:T(8,128)(2,1)S(1)} %add_convert_fusion.1), channel_id=1, source_target_pairs={{0,4},{4,0},{8,12},{12,8},{1,5},{5,1},{9,13},{13,9},{2,6},{6,2},{1... | collective-permute-start | bytes 1572872 | tf_op jit(solution)/shard_map/ppermute | solution.py:290
  48.1 12.9 %collective-permute-start.10 = (bf16[16,128,128]{2,1,0:T(8,128)(2,1)}, bf16[16,128,128]{2,1,0:T(8,128)(2,1)S(1)}, u32[]{:S(2)}, u32[]{:S(2)}) collective-permute-start(bf16[16,128,128]{2,1,0:T(8,128)(2,1)} %get-tuple-element.44), channel_id=1, source_target_pairs={{0,2},{1,3},{2,0},{3,1},{4,6},{5,7},{6,4},{7,5},{8,10},{9,11},{10,... | collective-permute-start | bytes 1572872 | tf_op jit(solution)/shard_map/ppermute | solution.py:262
  50.4 10.6 %copy-start = (f32[16,128,128]{2,1,0:T(8,128)S(1)}, f32[16,128,128]{2,1,0:T(8,128)}, u32[]{:S(2)}) copy-start(f32[16,128,128]{2,1,0:T(8,128)} %get-tuple-element.43) | copy-start | bytes 3145732
  50.4 13.3 %collective-permute-start.9 = (bf16[16,128,128]{2,1,0:T(8,128)(2,1)S(1)}, bf16[16,128,128]{2,1,0:T(8,128)(2,1)S(1)}, u32[]{:S(2)}, u32[]{:S(2)}) collective-permute-start(bf16[16,128,128]{2,1,0:T(8,128)(2,1)S(1)} %fusion.1), channel_id=1, source_target_pairs={{0,4},{12,8},{4,12},{8,0},{1,5},{13,9},{5,13},{9,1},{2,6},{14,10},... | collective-permute-start | bytes 1572872 | tf_op jit(solution)/shard_map/ppermute | solution.py:294
  60.7 10.8 %collective-permute-start.8 = (bf16[16,128,128]{2,1,0:T(8,128)(2,1)}, bf16[16,128,128]{2,1,0:T(8,128)(2,1)S(1)}, u32[]{:S(2)}, u32[]{:S(2)}) collective-permute-start(bf16[16,128,128]{2,1,0:T(8,128)(2,1)} %get-tuple-element.41), channel_id=1, source_target_pairs={{0,2},{1,3},{2,0},{3,1},{4,6},{5,7},{6,4},{7,5},{8,10},{9,11},{10,... | collective-permute-start | bytes 1572872 | tf_op jit(solution)/shard_map/ppermute | solution.py:262
  61.2 12.8 %collective-permute-start.11 = (bf16[16,128,128]{2,1,0:T(8,128)(2,1)S(1)}, bf16[16,128,128]{2,1,0:T(8,128)(2,1)S(1)}, u32[]{:S(2)}, u32[]{:S(2)}) collective-permute-start(bf16[16,128,128]{2,1,0:T(8,128)(2,1)S(1)} %fusion.3), channel_id=1, source_target_pairs={{0,8},{12,4},{4,0},{8,12},{1,9},{13,5},{5,1},{9,13},{2,10},{14,6},... | collective-permute-start | bytes 1572872 | tf_op jit(solution)/shard_map/ppermute | solution.py:298

commit v12 on v9

--- a/solution.py
+++ b/solution.py
@@ -269,7 +269,7 @@
     far_codes = lax.ppermute(own_codes, "orb", [(i, i ^ 3) for i in range(4)])
     a_codes = lax.ppermute(own_codes, "orb", [(to, at) for at, to in step_a])
     b_codes = lax.ppermute(own_codes, "orb", [(to, at) for at, to in step_b])
-    far_codes, a_codes, b_codes = lax.optimization_barrier((far_codes, a_codes, b_codes))
+    b_codes, a_codes, far_codes = lax.optimization_barrier((b_codes, a_codes, far_codes))
 
     def chunk(codes, other_rows):
         return tile_chunk(owners, codes, own_rows, other_rows, occ_local, share)
@@ -287,9 +287,10 @@
     b_keep, own_send = after(b_keep, own_send)
     b_term = over_x(b_send, b_keep) + jnp.where(inner, 0.0, far)
     b_term = lax.ppermute(b_term.astype(jnp.bfloat16), "orb", step_b)
-    beside = a_term.astype(jnp.float32) + b_term.astype(jnp.float32)
-    beside, own_keep = after(beside, own_keep)
-    total = over_x(own_send, own_keep) + beside
+    own_other = exchange(own_send, 2)
+    part = own_keep + a_term.astype(jnp.float32)
+    b_term, own_other, part = lax.optimization_barrier((b_term, own_other, part))
+    total = part + own_other.astype(jnp.float32) + b_term.astype(jnp.float32)
     return total.astype(jnp.bfloat16)[None]
 
 

time: 75.7 us -> 75.6 us (level)
  waiting for transfers between devices: 18.2 us -> 13.9 us
  starting transfers between devices: 17.3 us -> 20.8 us
  other arithmetic: 2.44 us -> 3.63 us
    ppermute x1, waiting for transfers between devices: 12.7 us -> 0.01 us  [tile_plan(): b_term = lax.ppermute(b_term.astype(jnp.bfloat16), 'orb', step_b)]
    ppermute x1, waiting for transfers between devices: 0.01 us -> 7.31 us  [tile_plan(): a_term = lax.ppermute(a_term, 'orb', step_a)]
    ppermute x1, starting transfers between devices: 2.32 us -> 5.46 us  [tile_plan(): b_term = lax.ppermute(b_term.astype(jnp.bfloat16), 'orb', step_b)]
    ppermute x1, starting transfers between devices: 1.43 us -> 3.02 us  [tile_plan(): far = lax.ppermute(far, 'orb', swap).astype(jnp.float32)]
    add x1, other arithmetic: 0.12 us -> 1.33 us  [tile_plan(): part = own_keep + a_term.astype(jnp.float32)]
    ppermute x6, starting transfers between devices: 5.94 us -> 4.76 us  [exchange(): return lax.ppermute(array, 'row', [(i, i ^ bits) for i in range(rows)])]
    ppermute x6, waiting for transfers between devices: 3.98 us -> 5.14 us  [exchange(): return lax.ppermute(array, 'row', [(i, i ^ bits) for i in range(rows)])]
  transfers between devices with their start and end apart: 12 -> 12, of which waited for: 5 -> 4; matrix products, arithmetic and copies ran while one was open for 2% -> 3% of each run, Pallas kernels for 37% -> 36%
where the time goes in v12:
time: 75.6 us; the launch traced here: 75.7 us
  Pallas kernels  35.9 us (47%)
  starting transfers between devices  20.8 us (28%)
  waiting for transfers between devices  13.9 us (18%)
  other arithmetic  3.63 us (5%)
  between operations  0.82 us (1%)
    pallas_call x4, Pallas kernels, tile_chunk(): pl.pallas_call(functools.partial(chunk_kernel, occ_local, share), in_spec...  35.9 us
    ppermute x1, waiting for transfers between devices, tile_plan(): a_term = lax.ppermute(a_term, 'orb', step_a)  7.31 us
    ppermute x1, starting transfers between devices, tile_plan(): b_term = lax.ppermute(b_term.astype(jnp.bfloat16), 'orb', step_b)  5.46 us
    ppermute x6, waiting for transfers between devices, exchange(): return lax.ppermute(array, 'row', [(i, i ^ bits) for i in range(rows)])  5.14 us
    ppermute x6, starting transfers between devices, exchange(): return lax.ppermute(array, 'row', [(i, i ^ bits) for i in range(rows)])  4.76 us
    ppermute x1, starting transfers between devices, tile_plan(): far_codes = lax.ppermute(own_codes, 'orb', [(i, i ^ 3) for i in range(4)])  3.87 us
    ppermute x1, starting transfers between devices, tile_plan(): far = lax.ppermute(far, 'orb', swap).astype(jnp.float32)  3.02 us
    ppermute x1, starting transfers between devices, tile_plan(): b_codes = lax.ppermute(own_codes, 'orb', [(to, at) for at, to in step_b])  2.57 us
  transfers between devices with their start and end apart: 12, of which 4 were waited for; matrix products, arithmetic and copies ran while one was open for 3% of the time, Pallas kernels for 36%

profile of v12, /device:TPU:0, one launch (start us, length us, event | category | flops | bytes accessed | tf_op | source)
XLA Modules:
  0.0 75.7 jit_solution(7913642218584919647)
XLA Ops:
  0.0 0.5 collective-permute-start.4
  1.1 0.7 fusion.9
  1.9 2.6 %collective-permute-start.1 = (s32[65]{0:T(128)S(1)}, s32[65]{0:T(128)S(1)}, u32[]{:S(2)}, u32[]{:S(2)}) collective-permute-start(s32[65]{0:T(128)S(1)} %pad_add_fusion.codes), channel_id=1, source_target_pairs={{8,0},{4,12},{0,4},{12,8},{9,1},{5,13},{1,5},{13,9},{10,2},{6,14},... | collective-permute-start | bytes 788 | tf_op jit(solution)/shard_map/ppermute | solution.py:271
  4.4 1.1 %collective-permute-start.2 = (s32[65]{0:T(128)S(1)}, s32[65]{0:T(128)S(1)}, u32[]{:S(2)}, u32[]{:S(2)}) collective-permute-start(s32[65]{0:T(128)S(1)} %pad_add_fusion.codes), channel_id=1, source_target_pairs={{4,0},{8,12},{12,4},{0,8},{5,1},{9,13},{13,5},{1,9},{6,2},{10,14},... | collective-permute-start | bytes 788 | tf_op jit(solution)/shard_map/ppermute | solution.py:270
  5.5 3.9 %collective-permute-start.3 = (s32[65]{0:T(128)S(1)}, s32[65]{0:T(128)S(1)}, u32[]{:S(2)}, u32[]{:S(2)}) collective-permute-start(s32[65]{0:T(128)S(1)} %pad_add_fusion.codes), channel_id=1, source_target_pairs={{0,12},{4,8},{8,4},{12,0},{1,13},{5,9},{9,5},{13,1},{2,14},{6,10},... | collective-permute-start | bytes 788 | tf_op jit(solution)/shard_map/ppermute | solution.py:269
  9.4 1.5 %collective-permute-done.3.codes = s32[65]{0:T(128)S(1)} collective-permute-done((s32[65]{0:T(128)S(1)}, s32[65]{0:T(128)S(1)}, u32[]{:S(2)}, u32[]{:S(2)}) %collective-permute-start.3) | collective-permute-done | bytes 292 | tf_op jit(solution)/shard_map/ppermute | solution.py:269
  10.9 0.6 copy-done.7
  11.5 8.3 %tile_chunk.4 = (bf16[16,128,128]{2,1,0:T(8,128)(2,1)}, f32[16,128,128]{2,1,0:T(8,128)}) custom-call(s32[16]{0:T(128)} %bitcast.17, s32[16]{0:T(128)} %copy-done.3, s32[65]{0:T(128)} %copy-done.7, bf16[1024,2048]{1,0:T(8,128)(2,1)} %bitcast.12, bf16[1024,2048]{1,0:T(8,128)(2,1)} %collective-permute-done.4.other_rows), custom_call_target="tpu_custom_call" | custom-call | flops 2147483648 | bytes 9961472 | tf_op jit(solution)/shard_map/tile_chunk/pallas_call | solution.py:204
  19.8 1.8 %collective-permute-start.5 = (bf16[16,128,128]{2,1,0:T(8,128)(2,1)}, bf16[16,128,128]{2,1,0:T(8,128)(2,1)S(1)}, u32[]{:S(2)}, u32[]{:S(2)}) collective-permute-start(bf16[16,128,128]{2,1,0:T(8,128)(2,1)} %get-tuple-element.28), channel_id=1, source_target_pairs={{0,2},{1,3},{2,0},{3,1},{4,6},{5,7},{6,4},{7,5},{8,10},{9,11},{10,... | collective-permute-start | bytes 1572872 | tf_op jit(solution)/shard_map/ppermute | solution.py:255
  21.6 8.3 %tile_chunk.6 = (bf16[16,128,128]{2,1,0:T(8,128)(2,1)}, f32[16,128,128]{2,1,0:T(8,128)}) custom-call(s32[16]{0:T(128)} %bitcast.18, s32[16]{0:T(128)} %copy-done.3, s32[65]{0:T(128)} %copy-done.6, bf16[1024,2048]{1,0:T(8,128)(2,1)} %bitcast.13, bf16[1024,2048]{1,0:T(8,128)(2,1)} %collective-permute-done.4.other_rows), custom_call_target="tpu_custom_call" | custom-call | flops 2147483648 | bytes 9961472 | tf_op jit(solution)/shard_map/tile_chunk/pallas_call | solution.py:204
  29.9 0.4 collective-permute-start.6
  30.3 4.6 %collective-permute-done.5 = bf16[16,128,128]{2,1,0:T(8,128)(2,1)S(1)} collective-permute-done((bf16[16,128,128]{2,1,0:T(8,128)(2,1)}, bf16[16,128,128]{2,1,0:T(8,128)(2,1)S(1)}, u32[]{:S(2)}, u32[]{:S(2)}) %collective-permute-start.5) | collective-permute-done | bytes 524320 | tf_op jit(solution)/shard_map/ppermute | solution.py:255
  35.0 3.0 %collective-permute-start.7 = (bf16[16,128,128]{2,1,0:T(8,128)(2,1)S(1)}, bf16[16,128,128]{2,1,0:T(8,128)(2,1)S(1)}, u32[]{:S(2)}, u32[]{:S(2)}) collective-permute-start(bf16[16,128,128]{2,1,0:T(8,128)(2,1)S(1)} %add_convert_fusion.1), channel_id=1, source_target_pairs={{0,4},{4,0},{8,12},{12,8},{1,5},{5,1},{9,13},{13,9},{2,6},{6,2},{1... | collective-permute-start | bytes 1572872 | tf_op jit(solution)/shard_map/ppermute | solution.py:281
  38.1 10.9 %tile_chunk.5 = (bf16[16,128,128]{2,1,0:T(8,128)(2,1)}, f32[16,128,128]{2,1,0:T(8,128)}) custom-call(s32[16]{0:T(128)} %bitcast.19, s32[16]{0:T(128)} %copy-done.3, s32[65]{0:T(128)} %copy-done.5, bf16[1024,2048]{1,0:T(8,128)(2,1)} %bitcast.14, bf16[1024,2048]{1,0:T(8,128)(2,1)} %collective-permute-done.4.other_rows), custom_call_target="tpu_custom_call" | custom-call | flops 2147483648 | bytes 9961472 | tf_op jit(solution)/shard_map/tile_chunk/pallas_call | solution.py:204
  49.0 1.9 %collective-permute-start.8 = (bf16[16,128,128]{2,1,0:T(8,128)(2,1)}, bf16[16,128,128]{2,1,0:T(8,128)(2,1)S(1)}, u32[]{:S(2)}, u32[]{:S(2)}) collective-permute-start(bf16[16,128,128]{2,1,0:T(8,128)(2,1)} %get-tuple-element.38), channel_id=1, source_target_pairs={{0,2},{1,3},{2,0},{3,1},{4,6},{5,7},{6,4},{7,5},{8,10},{9,11},{10,... | collective-permute-start | bytes 1572872 | tf_op jit(solution)/shard_map/ppermute | solution.py:255
  50.9 0.2 fusion.1
  51.2 8.4 %tile_chunk.7 = (bf16[16,128,128]{2,1,0:T(8,128)(2,1)}, f32[16,128,128]{2,1,0:T(8,128)}) custom-call(s32[16]{0:T(128)} %bitcast.20, s32[16]{0:T(128)} %copy-done.3, s32[65]{0:T(128)} %copy-done.4, bf16[1024,2048]{1,0:T(8,128)(2,1)} %bitcast.15, bf16[1024,2048]{1,0:T(8,128)(2,1)} %collective-permute-done.4.other_rows), custom_call_target="tpu_custom_call" | custom-call | flops 2147483648 | bytes 9961472 | tf_op jit(solution)/shard_map/tile_chunk/pallas_call | solution.py:204
  59.6 0.2 fusion.3
  59.9 5.5 %collective-permute-start.9 = (bf16[16,128,128]{2,1,0:T(8,128)(2,1)S(1)}, bf16[16,128,128]{2,1,0:T(8,128)(2,1)S(1)}, u32[]{:S(2)}, u32[]{:S(2)}) collective-permute-start(bf16[16,128,128]{2,1,0:T(8,128)(2,1)S(1)} %fusion.3), channel_id=1, source_target_pairs={{0,8},{12,4},{4,0},{8,12},{1,9},{13,5},{5,1},{9,13},{2,10},{14,6},... | collective-permute-start | bytes 1572872 | tf_op jit(solution)/shard_map/ppermute | solution.py:289
  65.3 0.2 collective-permute-start.10
  65.5 7.3 %collective-permute-done.11 = bf16[16,128,128]{2,1,0:T(8,128)(2,1)S(1)} collective-permute-done((bf16[16,128,128]{2,1,0:T(8,128)(2,1)S(1)}, bf16[16,128,128]{2,1,0:T(8,128)(2,1)S(1)}, u32[]{:S(2)}, u32[]{:S(2)}) %collective-permute-start.11) | collective-permute-done | bytes 524320 | tf_op jit(solution)/shard_map/ppermute | solution.py:285
  72.9 1.3 %convert_add_fusion = f32[16,128,128]{2,1,0:T(8,128)S(1)} fusion(f32[16,128,128]{2,1,0:T(8,128)} %get-tuple-element.40, bf16[16,128,128]{2,1,0:T(8,128)(2,1)S(1)} %collective-permute-done.11), kind=kLoop, calls=%fused_computation.7 | loop fusion | flops 524288 | bytes 2621440 | tf_op jit(solution)/shard_map/add | solution.py:291
  74.2 0.5 collective-permute-done.10
  74.7 1.0 %fusion.4 = bf16[1,16,128,128]{3,2,1,0:T(8,128)(2,1)} fusion(bf16[16,128,128]{2,1,0:T(8,128)(2,1)S(1)} %collective-permute-done.9, f32[16,128,128]{2,1,0:T(8,128)S(1)} %convert_add_fusion, bf16[16,128,128]{2,1,0:T(8,128)(2,1)S(1)} %collective-permute-done.10), kind=kLoop, calls=%fused_computation.9 | loop fusion | flops 1310720 | bytes 2621440 | tf_op jit(solution)/shard_map/broadcast_in_dim | solution.py:294
  (27 shorter events, 0.3 us)
Async XLA Ops:
  0.0 10.9 %collective-permute-start.4 = (bf16[1024,2048]{1,0:T(8,128)(2,1)}, bf16[1024,2048]{1,0:T(8,128)(2,1)}, u32[]{:S(2)}, u32[]{:S(2)}) collective-permute-start(bf16[1024,2048]{1,0:T(8,128)(2,1)} %bitcast.11), channel_id=1, source_target_pairs={{0,1},{1,0},{2,3},{3,2},{4,5},{5,4},{6,7},{7,6},{8,9},{9,8},{10,11... | collective-permute-start | bytes 12582920 | tf_op jit(solution)/shard_map/ppermute | solution.py:255
  1.9 17.9 %copy-start.4 = (s32[65]{0:T(128)}, s32[65]{0:T(128)S(1)}, u32[]{:S(2)}) copy-start(s32[65]{0:T(128)S(1)} %pad_add_fusion.codes) | copy-start | bytes 784
  1.9 7.5 %collective-permute-start.1 = (s32[65]{0:T(128)S(1)}, s32[65]{0:T(128)S(1)}, u32[]{:S(2)}, u32[]{:S(2)}) collective-permute-start(s32[65]{0:T(128)S(1)} %pad_add_fusion.codes), channel_id=1, source_target_pairs={{8,0},{4,12},{0,4},{12,8},{9,1},{5,13},{1,5},{13,9},{10,2},{6,14},... | collective-permute-start | bytes 788 | tf_op jit(solution)/shard_map/ppermute | solution.py:271
  4.4 5.0 %collective-permute-start.2 = (s32[65]{0:T(128)S(1)}, s32[65]{0:T(128)S(1)}, u32[]{:S(2)}, u32[]{:S(2)}) collective-permute-start(s32[65]{0:T(128)S(1)} %pad_add_fusion.codes), channel_id=1, source_target_pairs={{4,0},{8,12},{12,4},{0,8},{5,1},{9,13},{13,5},{1,9},{6,2},{10,14},... | collective-permute-start | bytes 788 | tf_op jit(solution)/shard_map/ppermute | solution.py:270
  5.5 5.4 %collective-permute-start.3 = (s32[65]{0:T(128)S(1)}, s32[65]{0:T(128)S(1)}, u32[]{:S(2)}, u32[]{:S(2)}) collective-permute-start(s32[65]{0:T(128)S(1)} %pad_add_fusion.codes), channel_id=1, source_target_pairs={{0,12},{4,8},{8,4},{12,0},{1,13},{5,9},{9,5},{13,1},{2,14},{6,10},... | collective-permute-start | bytes 788 | tf_op jit(solution)/shard_map/ppermute | solution.py:269
  9.4 1.5 %collective-permute-start = (s32[16]{0:T(128)}, s32[16]{0:T(128)S(1)}, u32[]{:S(2)}, u32[]{:S(2)}) collective-permute-start(s32[16]{0:T(128)} %bitcast.16), channel_id=1, source_target_pairs={{0,1},{1,0},{2,3},{3,2},{4,5},{5,4},{6,7},{7,6},{8,9},{9,8},{10,11... | collective-permute-start | bytes 200 | tf_op jit(solution)/shard_map/ppermute | solution.py:255
  9.4 28.7 %copy-start.5 = (s32[65]{0:T(128)}, s32[65]{0:T(128)S(1)}, u32[]{:S(2)}) copy-start(s32[65]{0:T(128)S(1)} %collective-permute-done.1.codes) | copy-start | bytes 784
  9.4 12.2 %copy-start.6 = (s32[65]{0:T(128)}, s32[65]{0:T(128)S(1)}, u32[]{:S(2)}) copy-start(s32[65]{0:T(128)S(1)} %collective-permute-done.2.codes) | copy-start | bytes 784
  10.9 0.6 copy-start.7
  10.9 0.6 copy-start.3
  19.8 15.1 %copy-start.2 = (f32[16,128,128]{2,1,0:T(8,128)S(1)}, f32[16,128,128]{2,1,0:T(8,128)}, u32[]{:S(2)}) copy-start(f32[16,128,128]{2,1,0:T(8,128)} %get-tuple-element.27) | copy-start | bytes 3145732
  19.8 15.1 %collective-permute-start.5 = (bf16[16,128,128]{2,1,0:T(8,128)(2,1)}, bf16[16,128,128]{2,1,0:T(8,128)(2,1)S(1)}, u32[]{:S(2)}, u32[]{:S(2)}) collective-permute-start(bf16[16,128,128]{2,1,0:T(8,128)(2,1)} %get-tuple-element.28), channel_id=1, source_target_pairs={{0,2},{1,3},{2,0},{3,1},{4,6},{5,7},{6,4},{7,5},{8,10},{9,11},{10,... | collective-permute-start | bytes 1572872 | tf_op jit(solution)/shard_map/ppermute | solution.py:255
  29.9 21.0 %collective-permute-start.6 = (bf16[16,128,128]{2,1,0:T(8,128)(2,1)}, bf16[16,128,128]{2,1,0:T(8,128)(2,1)S(1)}, u32[]{:S(2)}, u32[]{:S(2)}) collective-permute-start(bf16[16,128,128]{2,1,0:T(8,128)(2,1)} %get-tuple-element.33), channel_id=1, source_target_pairs={{0,2},{1,3},{2,0},{3,1},{4,6},{5,7},{6,4},{7,5},{8,10},{9,11},{10,... | collective-permute-start | bytes 1572872 | tf_op jit(solution)/shard_map/ppermute | solution.py:255
  35.0 15.9 %copy-start = (f32[16,128,128]{2,1,0:T(8,128)S(1)}, f32[16,128,128]{2,1,0:T(8,128)}, u32[]{:S(2)}) copy-start(f32[16,128,128]{2,1,0:T(8,128)} %get-tuple-element.32) | copy-start | bytes 3145732
  35.0 15.9 %collective-permute-start.7 = (bf16[16,128,128]{2,1,0:T(8,128)(2,1)S(1)}, bf16[16,128,128]{2,1,0:T(8,128)(2,1)S(1)}, u32[]{:S(2)}, u32[]{:S(2)}) collective-permute-start(bf16[16,128,128]{2,1,0:T(8,128)(2,1)S(1)} %add_convert_fusion.1), channel_id=1, source_target_pairs={{0,4},{4,0},{8,12},{12,8},{1,5},{5,1},{9,13},{13,9},{2,6},{6,2},{1... | collective-permute-start | bytes 1572872 | tf_op jit(solution)/shard_map/ppermute | solution.py:281
  49.0 10.6 %collective-permute-start.8 = (bf16[16,128,128]{2,1,0:T(8,128)(2,1)}, bf16[16,128,128]{2,1,0:T(8,128)(2,1)S(1)}, u32[]{:S(2)}, u32[]{:S(2)}) collective-permute-start(bf16[16,128,128]{2,1,0:T(8,128)(2,1)} %get-tuple-element.38), channel_id=1, source_target_pairs={{0,2},{1,3},{2,0},{3,1},{4,6},{5,7},{6,4},{7,5},{8,10},{9,11},{10,... | collective-permute-start | bytes 1572872 | tf_op jit(solution)/shard_map/ppermute | solution.py:255
  51.1 8.5 %copy-start.1 = (f32[16,128,128]{2,1,0:T(8,128)S(1)}, f32[16,128,128]{2,1,0:T(8,128)}, u32[]{:S(2)}) copy-start(f32[16,128,128]{2,1,0:T(8,128)} %get-tuple-element.37) | copy-start | bytes 3145732
  51.1 21.7 %collective-permute-start.11 = (bf16[16,128,128]{2,1,0:T(8,128)(2,1)S(1)}, bf16[16,128,128]{2,1,0:T(8,128)(2,1)S(1)}, u32[]{:S(2)}, u32[]{:S(2)}) collective-permute-start(bf16[16,128,128]{2,1,0:T(8,128)(2,1)S(1)} %fusion.1), channel_id=1, source_target_pairs={{0,4},{12,8},{4,12},{8,0},{1,5},{13,9},{5,13},{9,1},{2,6},{14,10},... | collective-permute-start | bytes 1572872 | tf_op jit(solution)/shard_map/ppermute | solution.py:285
  59.9 14.3 %collective-permute-start.9 = (bf16[16,128,128]{2,1,0:T(8,128)(2,1)S(1)}, bf16[16,128,128]{2,1,0:T(8,128)(2,1)S(1)}, u32[]{:S(2)}, u32[]{:S(2)}) collective-permute-start(bf16[16,128,128]{2,1,0:T(8,128)(2,1)S(1)} %fusion.3), channel_id=1, source_target_pairs={{0,8},{12,4},{4,0},{8,12},{1,9},{13,5},{5,1},{9,13},{2,10},{14,6},... | collective-permute-start | bytes 1572872 | tf_op jit(solution)/shard_map/ppermute | solution.py:289
  65.3 9.4 %collective-permute-start.10 = (bf16[16,128,128]{2,1,0:T(8,128)(2,1)}, bf16[16,128,128]{2,1,0:T(8,128)(2,1)S(1)}, u32[]{:S(2)}, u32[]{:S(2)}) collective-permute-start(bf16[16,128,128]{2,1,0:T(8,128)(2,1)} %get-tuple-element.39), channel_id=1, source_target_pairs={{0,2},{1,3},{2,0},{3,1},{4,6},{5,7},{6,4},{7,5},{8,10},{9,11},{10,... | collective-permute-start | bytes 1572872 | tf_op jit(solution)/shard_map/ppermute | solution.py:255
